TPU v7x, 32 devices: a whole 2x2x4 slice. The times are simulated.
32 devices in a mesh: dp: 4 (over z), tensor: 8 (over y, x, core).
Axes of the slice: x: 2, y: 2, z: 4, core: 2. Of those that a mesh axis runs over, the one named last changes fastest.
Arguments:
- tokens: bfloat16 [64, 128, 1536], P(('dp', 'tensor')), may hold values from -60 to 60
- cached: bfloat16 [64, 512, 1536], P(('dp', 'tensor')), may hold values from -60 to 60
- norm_gains: float32 [2, 1536], replicated, may hold values from 0.5 to 1.5
- w_qkv: bfloat16 [1536, 3072], replicated, may hold values from -0.15625 to 0.15625
- w_out: bfloat16 [1536, 1536], replicated, may hold values from -0.15625 to 0.15625
- mlp_weights: bfloat16 [3, 1536, 4096], P(None, None, 'tensor'), may hold values from -0.15625 to 0.15625
- request_order: int32 [64], replicated, may hold values from 0 to 63, as said below
- new_lengths: int32 [64], replicated, may hold values from 1 to 128, 5120 in all
- cached_lengths: int32 [64], replicated, may hold values from 0 to 384
- decode_slots: int32 [64], replicated, may hold values from 0 to 63, as said below
Outputs:
- layer_out: bfloat16 [64, 128, 1536], P(('dp', 'tensor'))
- kv_decode: bfloat16 [64, 512, 1536], P('dp', 'tensor')
Inputs may be any that keep to these rules, and one draw needn't show every extreme that they name: `request_order`: each value once; the device at index k of dp+tensor holds prefill slots k * 2 to (k + 1) * 2 - 1. `decode_slots`: each value once; the 16 requests held by the prefill slots of one index of dp take exactly 4 slots of every aligned block of 16 decode slots.
All inputs are finite; a program needn't handle non-finite values.
Results may differ from a plain program's by a relative error of at most 0.015.
Values may be sent and summed in bfloat16 or wider, within the bound.
No kernel may reach another device: no remote copies, remote signals or barrier semaphores. Data moves between devices by JAX's collectives and lax.ppermute only.
A program may use at most 192 MiB of HBM per device.

v0:
```python
import jax
import jax.numpy as jnp
from jax import lax
from jax.sharding import PartitionSpec as P

D = 1536
HEADS = 16
KV_HEADS = 8
HEAD_DIM = 96
NEW = 128
CTX = 512


epsilon = 1e-05
rope_base = 100000.0


def norm_rows(values, gain):
    widened = values.astype(jnp.float32)
    factor = lax.rsqrt(jnp.mean(widened * widened, axis=-1, keepdims=True) + epsilon)
    return (widened * factor * gain).astype(jnp.bfloat16)


def rotate(values, positions):
    half_dim = values.shape[-1] // 2
    frequency = rope_base ** (-2.0 * jnp.arange(half_dim, dtype=jnp.float32) / values.shape[-1])
    angles = positions[:, None, None] * frequency
    cosine = jnp.cos(angles)
    sine_part = jnp.sin(angles)
    leading = values[..., :half_dim]
    trailing = values[..., half_dim:]
    return jnp.concatenate(
        [leading * cosine - trailing * sine_part, trailing * cosine + leading * sine_part], axis=-1
    )


def place_context(fresh_rows, cached_rows, new_count, cached_count):
    offsets = jnp.arange(NEW, dtype=jnp.int32)
    kept = jnp.where((offsets < new_count)[:, None], fresh_rows, jnp.zeros_like(fresh_rows))
    canvas = jnp.zeros((CTX, fresh_rows.shape[1]), fresh_rows.dtype)
    placed = lax.dynamic_update_slice_in_dim(canvas, kept, cached_count, 0)
    spots = jnp.arange(CTX, dtype=jnp.int32)
    return jnp.where((spots < cached_count)[:, None], cached_rows, placed)


def attend(queries, context, cached_count):
    group_size = HEADS // KV_HEADS
    key_width = KV_HEADS * HEAD_DIM
    key_heads = context[:, :key_width].reshape(CTX, KV_HEADS, HEAD_DIM)
    value_heads = context[:, key_width:].reshape(CTX, KV_HEADS, HEAD_DIM)
    grouped = queries.reshape(NEW, KV_HEADS, group_size, HEAD_DIM)
    scores = jnp.einsum(
        "qkgd,pkd->kgqp", grouped, key_heads, preferred_element_type=jnp.float32
    ) * HEAD_DIM ** (-0.5)
    last_key = cached_count + jnp.arange(NEW, dtype=jnp.int32)
    allowed = jnp.arange(CTX, dtype=jnp.int32)[None, :] <= last_key[:, None]
    scores = jnp.where(allowed, scores, -jnp.inf)
    highest = jnp.max(scores, axis=-1, keepdims=True)
    exponent = jnp.exp(scores - highest)
    weights = (exponent / jnp.sum(exponent, axis=-1, keepdims=True)).astype(jnp.bfloat16)
    attended = jnp.einsum(
        "kgqp,pkd->qkgd", weights, value_heads, preferred_element_type=jnp.float32
    )
    return attended.reshape(NEW, D).astype(jnp.bfloat16)


def lookup(source_table, wanted):
    every_index = jnp.arange(source_table.shape[0], dtype=jnp.int32)
    matches = wanted[:, None] == every_index[None, :]
    return jnp.sum(jnp.where(matches, source_table[None, :], 0), axis=1)


def locate(source_table, wanted):
    every_index = jnp.arange(source_table.shape[0], dtype=jnp.int32)
    matches = source_table[None, :] == wanted[:, None]
    return jnp.sum(jnp.where(matches, every_index[None, :], 0), axis=1)


def block_sums(activated, down_part, unit_width):
    blocks = activated.shape[1] // unit_width
    spread = activated.reshape(activated.shape[0], blocks, unit_width)
    down_spread = down_part.reshape(down_part.shape[0], blocks, unit_width)
    partial_sums = jnp.einsum(
        "rmw,dmw->mrd", spread, down_spread, preferred_element_type=jnp.float32
    ).astype(jnp.bfloat16)
    return jnp.sum(partial_sums.astype(jnp.float32), axis=0)


def local(
    tokens,
    cached,
    norm_gains,
    w_qkv,
    w_out,
    mlp_weights,
    request_order,
    new_lengths,
    cached_lengths,
    decode_slots,
):
    tensor_size = lax.axis_size("tensor")
    group_total = lax.axis_size("dp")
    local_reqs = tokens.shape[0]
    group_reqs = local_reqs * tensor_size
    group_index = lax.axis_index("dp")
    device_index = group_index * tensor_size + lax.axis_index("tensor")
    local_order = lax.dynamic_slice_in_dim(request_order, device_index * local_reqs, local_reqs)
    new_counts = lookup(new_lengths, local_order)
    cached_counts = lookup(cached_lengths, local_order)
    key_width = KV_HEADS * HEAD_DIM
    row_count = local_reqs * NEW
    flattened = tokens.reshape(row_count, D)
    normed = norm_rows(flattened, norm_gains[0])
    projected = jnp.dot(normed, w_qkv, preferred_element_type=jnp.float32)
    positions = (
        (cached_counts[:, None] + jnp.arange(NEW, dtype=jnp.int32)[None, :])
        .reshape(row_count)
        .astype(jnp.float32)
    )
    queries = rotate(projected[:, :D].reshape(row_count, HEADS, HEAD_DIM), positions).astype(
        jnp.bfloat16
    )
    key_rows = rotate(
        projected[:, D : D + key_width].reshape(row_count, KV_HEADS, HEAD_DIM), positions
    ).reshape(row_count, key_width)
    fresh_rows = jnp.concatenate([key_rows, projected[:, D + key_width :]], axis=1).astype(
        jnp.bfloat16
    )
    fresh_rows = fresh_rows.reshape(local_reqs, NEW, 2 * key_width)
    contexts = jax.vmap(place_context)(fresh_rows, cached, new_counts, cached_counts)
    attended = lax.map(
        lambda inputs: attend(inputs[0], inputs[1], inputs[2]),
        (queries.reshape(local_reqs, NEW, HEADS, HEAD_DIM), contexts, cached_counts),
    )
    attended = attended.reshape(row_count, D)
    residual = (
        flattened.astype(jnp.float32) + jnp.dot(attended, w_out, preferred_element_type=jnp.float32)
    ).astype(jnp.bfloat16)
    post_norm = norm_rows(residual, norm_gains[1])
    unit_width = mlp_weights.shape[2]
    shards = lax.all_gather(mlp_weights, "tensor", axis=2, tiled=True)
    gate_out = jnp.dot(post_norm, shards[0], preferred_element_type=jnp.float32)
    up_out = jnp.dot(post_norm, shards[1], preferred_element_type=jnp.float32)
    activated = (jax.nn.silu(gate_out) * up_out).astype(jnp.bfloat16)
    mlp_sum = block_sums(activated, shards[2], unit_width)
    live = (jnp.arange(NEW, dtype=jnp.int32)[None, :] < new_counts[:, None]).reshape(row_count, 1)
    layer_out = (
        jnp.where(live, residual.astype(jnp.float32) + mlp_sum, 0.0)
        .astype(jnp.bfloat16)
        .reshape(local_reqs, NEW, D)
    )
    slot_ids = group_index * group_reqs + jnp.arange(group_reqs, dtype=jnp.int32)
    request_at = locate(decode_slots, slot_ids)
    prefill_at = locate(request_order, request_at)
    exchanged = lax.all_to_all(contexts, "tensor", split_axis=1, concat_axis=0, tiled=True)
    group_order = lax.dynamic_slice_in_dim(request_order, group_index * group_reqs, group_reqs)
    row_slots = lookup(decode_slots, group_order)
    arranged = exchanged[jnp.argsort(row_slots)]
    arrived = lax.all_to_all(arranged, "dp", split_axis=0, concat_axis=0, tiled=True)
    per_group = group_reqs // group_total
    owners = prefill_at // group_reqs
    ordinal = jnp.arange(group_reqs, dtype=jnp.int32)
    same_owner = (owners[:, None] == owners[None, :]) & (ordinal[None, :] < ordinal[:, None])
    source_rows = owners * per_group + jnp.sum(same_owner.astype(jnp.int32), axis=1)
    kv_decode = arrived[source_rows]
    return (layer_out, kv_decode)


def solution(mesh):
    in_specs = (
        P(("dp", "tensor"), None, None),
        P(("dp", "tensor"), None, None),
        P(),
        P(),
        P(),
        P(None, None, "tensor"),
        P(),
        P(),
        P(),
        P(),
    )
    out_specs = (P(("dp", "tensor"), None, None), P("dp", "tensor", None))
    return jax.shard_map(local, mesh=mesh, in_specs=in_specs, out_specs=out_specs, check_vma=False)
```

profile of v0, /device:TPU:0, one launch (start us, length us, event | category | flops | bytes accessed | tf_op | source)
XLA Modules:
  0.0 255.3 jit_solution(4751029765808565509)
XLA Ops:
  7.2 6.7 %copy.73 = bf16[3,1536,512]{1,2,0:T(8,128)(2,1)} copy(bf16[3,1536,512]{2,1,0:T(8,128)(2,1)} %param.17) | data formatting | bytes 9437184 | tf_op args[5]
  13.9 0.7 copy-done.6
  15.6 5.2 %fusion.27 = f32[256,3072]{1,0:T(8,128)S(1)} fusion(bf16[256,1536]{1,0:T(8,128)(2,1)S(1)} %fusion.20, bf16[1536,3072]{1,0:T(8,128)(2,1)} %param.15), kind=kOutput, calls=%fused_computation.94 | convolution fusion | flops 2415919104 | bytes 13369344 | tf_op jit(solution)/shard_map/dot_general | solution.py:114
  20.8 1.6 copy-done.1
  22.9 0.7 copy.64
  25.9 7.0 %broadcast_select_fusion.1 = bf16[2,128,1536]{1,0,2:T(2,128)(2,1)S(1)} fusion(pred[2,128]{1,0:T(4,128)(4,1)S(1)} %get-tuple-element.123, bf16[2,128,768]{1,0,2:T(2,128)(2,1)S(1)} %copy.63, bf16[2,128,768]{1,0,2:T(2,128)(2,1)S(1)} %concatenate.27), kind=kLoop, calls=%fused_computation.43 | loop fusion | flops 786432 | bytes 1573120 | tf_op jit(solution)/shard_map/vmap(jit(_where))/select_n | solution.py:39
  33.0 1.8 copy.65
  34.8 0.7 iota_compare_fusion.1
  35.7 20.4 %while.12 = (s32[]{:T(128)}, bf16[2,512,1536]{2,1,0:T(8,128)(2,1)S(1)}, s32[2,3]{1,0:T(2,128)}, bf16[2,128,1536]{2,1,0:T(8,128)(2,1)}, s32[]{:T(128)}, /*index=5*/s32[3]{0:T(128)S(1)}, s32[]{:T(128)}) while((s32[]{:T(128)}, bf16[2,512,1536]{2,1,0:T(8,128)(2,1)S(1)}, s32[2,3]{1,0:T(2,128)}, bf16[2,128,1536]{2,1,0:T(8,128)(2,1)}, s32[]{:T(128)}, ...), condition=%wide.while_cond, body=%wide.while_body.sunk | while | flops 196627 | bytes 1966259 | solution.py:41
  35.7 0.7 constant_dynamic-slice_fusion.5
  36.4 0.7 fusion.51
  37.0 2.5 and_reduce_fusion.2
  39.6 3.0 %dynamic-slice_select_fusion.2 = bf16[1,128,1536]{2,1,0:T(8,128)(2,1)S(1)} fusion(bf16[2,128,1536]{2,1,0:T(8,128)(2,1)} %get-tuple-element.213, s32[]{:T(128)S(6)} %copy.97, bf16[2,512,1536]{2,1,0:T(8,128)(2,1)S(1)} %get-tuple-element.204, s32[]{:T(128)} %bitcast.129, s32[]{:T(128)} %bitcast.130, pred[]{:T(512)} %and_reduce_fusion.2), kind=kLoop, calls=%fused_computation.20.clone.1 | loop fusion | flops 196608 | bytes 1179661 | tf_op jit(solution)/shard_map/vmap(vmap())/scatter
  42.6 3.3 %dynamic-update-slice.3 = bf16[2,512,1536]{2,1,0:T(8,128)(2,1)S(1)} dynamic-update-slice(bf16[2,512,1536]{2,1,0:T(8,128)(2,1)S(1)} %get-tuple-element.204, bf16[1,128,1536]{2,1,0:T(8,128)(2,1)S(1)} %dynamic-slice_select_fusion.2, s32[]{:T(128)} %bitcast.129, s32[]{:T(128)} %bitcast.130, s32[]{:T(128)} %constant.28.clone.1..sunk) | dynamic-update-slice | bytes 786436 | tf_op jit(solution)/shard_map/vmap(vmap())/scatter
  45.9 0.7 constant_dynamic-slice_fusion.5
  46.6 0.7 fusion.51
  47.2 2.5 and_reduce_fusion.2
  49.8 3.0 %dynamic-slice_select_fusion.2 = bf16[1,128,1536]{2,1,0:T(8,128)(2,1)S(1)} fusion(bf16[2,128,1536]{2,1,0:T(8,128)(2,1)} %get-tuple-element.213, s32[]{:T(128)S(6)} %copy.97, bf16[2,512,1536]{2,1,0:T(8,128)(2,1)S(1)} %get-tuple-element.204, s32[]{:T(128)} %bitcast.129, s32[]{:T(128)} %bitcast.130, pred[]{:T(512)} %and_reduce_fusion.2), kind=kLoop, calls=%fused_computation.20.clone.1 | loop fusion | flops 196608 | bytes 1179661 | tf_op jit(solution)/shard_map/vmap(vmap())/scatter
  52.8 3.3 %dynamic-update-slice.3 = bf16[2,512,1536]{2,1,0:T(8,128)(2,1)S(1)} dynamic-update-slice(bf16[2,512,1536]{2,1,0:T(8,128)(2,1)S(1)} %get-tuple-element.204, bf16[1,128,1536]{2,1,0:T(8,128)(2,1)S(1)} %dynamic-slice_select_fusion.2, s32[]{:T(128)} %bitcast.129, s32[]{:T(128)} %bitcast.130, s32[]{:T(128)} %constant.28.clone.1..sunk) | dynamic-update-slice | bytes 786436 | tf_op jit(solution)/shard_map/vmap(vmap())/scatter
  56.1 16.8 %broadcast_select_fusion = bf16[2,512,1536]{2,0,1:T(2,128)(2,1)} fusion(pred[2,512]{0,1:T(8,128)(4,1)} %iota_compare_fusion.1, bf16[2,512,1536]{2,1,0:T(8,128)(2,1)S(1)} %get-tuple-element.37, bf16[2,512,1536]{2,1,0:T(8,128)(2,1)} %param.13), kind=kLoop, calls=%fused_computation.28 | loop fusion | flops 1572864 | bytes 9438208 | tf_op jit(solution)/shard_map/vmap(jit(_where))/select_n | solution.py:43
  72.9 5.5 %all-to-all-start = ((bf16[2,512,1536]{2,0,1:T(2,128)(2,1)}), bf16[2,512,1536]{2,0,1:T(2,128)(2,1)}, u32[]{:S(2)}, u32[]{:S(2)}) async-start(bf16[2,512,1536]{2,0,1:T(2,128)(2,1)} %broadcast_select_fusion), calls=%async_computation | async-start | bytes 6291456 | tf_op jit(solution)/shard_map/all_to_all | solution.py:155
  78.4 1.3 slice.82
  79.6 7.0 %copy.70 = bf16[2,512,1536]{1,2,0:T(8,128)(2,1)S(1)} copy(bf16[2,512,1536]{2,0,1:T(2,128)(2,1)} %broadcast_select_fusion) | data formatting | bytes 6291456 | tf_op jit(solution)/shard_map/while | solution.py:131
  86.6 0.6 dynamic_slice.19
  87.3 3.1 %copy.68 = f32[256,1536]{0,1:T(8,128)} copy(f32[256,1536]{1,0:T(8,128)} %slice.82) | data formatting | bytes 3145728 | tf_op jit(solution)/shard_map/slice | solution.py:120
  90.4 2.4 subtract_convert_fusion
  92.7 1.8 concatenate.30
  94.6 0.9 concatenate.31
  95.4 2.1 pad_maximum_fusion
  97.6 1.0 copy.71
  98.6 0.8 select_reduce_fusion.1
  99.4 1.3 sort.17
  100.7 0.9 select_reduce_fusion
  101.8 31.6 %all-to-all-done = bf16[2,512,1536]{2,0,1:T(2,128)(2,1)} async-done(((bf16[2,512,1536]{2,0,1:T(2,128)(2,1)}), bf16[2,512,1536]{2,0,1:T(2,128)(2,1)}, u32[]{:S(2)}, u32[]{:S(2)}) %all-to-all-start) | async-done | bytes 3145760 | tf_op jit(solution)/shard_map/all_to_all | solution.py:155
  133.4 2.4 copy.76
  135.8 1.9 copy.77
  137.8 4.2 %gather_fusion = bf16[16,64,1536]{2,1,0:T(8,128)(2,1)} fusion(bf16[16,64,1536]{2,1,0:T(8,128)(2,1)} %bitcast.137, s32[1024]{0:T(1024)S(1)} %pad_clamp_fusion.1), kind=kCustom, calls=%fused_computation | custom fusion | bytes 6291520 | tf_op jit(solution)/shard_map/gather | solution.py:158
  142.0 5.8 %all-to-all-start.1 = ((bf16[16,64,1536]{2,1,0:T(8,128)(2,1)}), bf16[16,64,1536]{2,1,0:T(8,128)(2,1)}, u32[]{:S(2)}, u32[]{:S(2)}) async-start(bf16[16,64,1536]{2,1,0:T(8,128)(2,1)} %gather_fusion), calls=%async_computation.1 | async-start | bytes 6291456 | tf_op jit(solution)/shard_map/all_to_all | solution.py:159
  147.7 30.1 %while.11 = (s32[]{:T(128)}, bf16[2,128,1536]{2,1,0:T(8,128)(2,1)}, bf16[2,512,1536]{1,2,0:T(8,128)(2,1)S(1)}, s32[2]{0:T(128)S(1)}, bf16[2,128,16,96]{1,3,2,0:T(8,128)(2,1)}, /*index=5*/s32[]{:T(128)}) while((s32[]{:T(128)}, bf16[2,128,1536]{2,1,0:T(8,128)(2,1)}, bf16[2,512,1536]{1,2,0:T(8,128)(2,1)S(1)}, s32[2]{0:T(128)S(1)}, ...), condition=%wide.region_7.8_spmd, body=%wide.region_4.7_spmd.sunk | while | flops 409207424 | bytes 19547240 | solution.py:131
  148.3 0.6 iota_add_fusion.3
  149.0 0.7 iota_compare_fusion.7
  149.7 1.0 constant_dynamic-slice_fusion.4
  150.8 1.3 fusion.48
  152.1 5.1 %fusion.49 = (f32[8,2,128]{2,1,0:T(2,128)}, f32[8,2,128,512]{2,3,1,0:T(8,128)}) fusion(pred[128,512]{0,1:T(8,128)(4,1)} %iota_compare_fusion.7, bf16[512,8,96,1]{0,2,3,1:T(8,128)(2,1)} %bitcast.135, bf16[128,8,2,96]{0,3,2,1:T(8,128)(2,1)S(1)} %bitcast.140), kind=kOutput, calls=%fused_computation.92.clone.1 | convolution fusion | flops 205521408 | bytes 5447680 | tf_op jit(solution)/shard_map/while/body/eval_jaxpr/sub | solution.py:59
  157.2 3.6 %fusion.50 = bf16[8,96,2,128]{3,1,2,0:T(8,128)(2,1)} fusion(bf16[512,8,96,1]{0,2,3,1:T(8,128)(2,1)} %bitcast.134, f32[8,2,128,512]{2,3,1,0:T(8,128)} %get-tuple-element.187, f32[8,2,128]{2,1,0:T(2,128)} %get-tuple-element.188), kind=kOutput, calls=%fused_computation.12.clone.1 | convolution fusion | flops 203620352 | bytes 5382144 | tf_op jit(solution)/shard_map/while/body/eval_jaxpr/kgqp,pkd->qkgd/dot_general | solution.py:61
  160.8 1.2 copy.92
  162.0 0.8 constant_dynamic-update-slice_fusion.2
  163.4 0.6 iota_add_fusion.3
  164.0 0.7 iota_compare_fusion.7
  164.7 1.0 constant_dynamic-slice_fusion.4
  165.8 1.3 fusion.48
  167.1 5.1 %fusion.49 = (f32[8,2,128]{2,1,0:T(2,128)}, f32[8,2,128,512]{2,3,1,0:T(8,128)}) fusion(pred[128,512]{0,1:T(8,128)(4,1)} %iota_compare_fusion.7, bf16[512,8,96,1]{0,2,3,1:T(8,128)(2,1)} %bitcast.135, bf16[128,8,2,96]{0,3,2,1:T(8,128)(2,1)S(1)} %bitcast.140), kind=kOutput, calls=%fused_computation.92.clone.1 | convolution fusion | flops 205521408 | bytes 5447680 | tf_op jit(solution)/shard_map/while/body/eval_jaxpr/sub | solution.py:59
  172.2 3.6 %fusion.50 = bf16[8,96,2,128]{3,1,2,0:T(8,128)(2,1)} fusion(bf16[512,8,96,1]{0,2,3,1:T(8,128)(2,1)} %bitcast.134, f32[8,2,128,512]{2,3,1,0:T(8,128)} %get-tuple-element.187, f32[8,2,128]{2,1,0:T(2,128)} %get-tuple-element.188), kind=kOutput, calls=%fused_computation.12.clone.1 | convolution fusion | flops 203620352 | bytes 5382144 | tf_op jit(solution)/shard_map/while/body/eval_jaxpr/kgqp,pkd->qkgd/dot_general | solution.py:61
  175.8 1.2 copy.92
  177.0 0.8 constant_dynamic-update-slice_fusion.2
  177.8 4.2 %multiply_reduce_fusion = (f32[256]{0:T(256)S(1)}, f32[256,1536]{1,0:T(8,128)S(1)}) fusion(bf16[256,1536]{1,0:T(8,128)(2,1)} %bitcast.146, bf16[1536,1536]{1,0:T(8,128)(2,1)} %param.16, bf16[256,1536]{1,0:T(8,128)(2,1)} %bitcast.143), kind=kOutput, calls=%fused_computation.41 | convolution fusion | flops 1210318592 | bytes 7865344 | tf_op jit(solution)/shard_map/dot_general | solution.py:137
  182.1 32.3 %all-to-all-done.1 = bf16[16,64,1536]{2,1,0:T(8,128)(2,1)} async-done(((bf16[16,64,1536]{2,1,0:T(8,128)(2,1)}), bf16[16,64,1536]{2,1,0:T(8,128)(2,1)}, u32[]{:S(2)}, u32[]{:S(2)}) %all-to-all-start.1) | async-done | bytes 3145760 | tf_op jit(solution)/shard_map/all_to_all | solution.py:159
  214.4 4.3 %gather_fusion.1 = bf16[16,64,1536]{2,1,0:T(8,128)(2,1)} fusion(bf16[16,64,1536]{2,1,0:T(8,128)(2,1)} %all-to-all-done.1, s32[1024]{0:T(1024)S(1)} %pad_clamp_fusion), kind=kCustom, calls=%fused_computation.1 | custom fusion | bytes 6291520 | tf_op jit(solution)/shard_map/gather | solution.py:165
  218.7 3.0 %all-gather.2.cloned.1.call-done = bf16[3,1536,4096]{1,2,0:T(8,128)(2,1)} async-done(((bf16[3,1536,512]{1,2,0:T(8,128)(2,1)}), bf16[3,1536,4096]{1,2,0:T(8,128)(2,1)}) %all-gather.2.cloned.1.call-update) | async-done | bytes 37748752 | tf_op jit(solution)/shard_map/all_gather | solution.py:141
  221.7 10.0 %fusion.12 = f32[256,4096]{1,0:T(8,128)} fusion(bf16[3,1536,4096]{1,2,0:T(8,128)(2,1)} %all-gather.2.cloned.1.call-done, f32[256,1536]{1,0:T(8,128)S(1)} %get-tuple-element.125, f32[1536]{0:T(1024)S(1)} %get-tuple-element.85, f32[256]{0:T(256)S(1)} %add_rsqrt_fusion), kind=kOutput, calls=%fused_computation.26 | convolution fusion | flops 3222405120 | bytes 18357248 | tf_op jit(solution)/shard_map/dot_general | solution.py:142
  231.7 8.8 %fusion.14 = bf16[256,4096]{1,0:T(8,128)(2,1)} fusion(bf16[3,1536,4096]{1,2,0:T(8,128)(2,1)} %all-gather.2.cloned.1.call-done, f32[256,4096]{1,0:T(8,128)} %fusion.12, f32[256,1536]{1,0:T(8,128)S(1)} %get-tuple-element.125, f32[1536]{0:T(1024)S(1)} %get-tuple-element.85, f32[256]{0:T(256)S(1)} %add_rsqrt_fusion), kind=kOutput, calls=%fused_computation.30 | convolution fusion | flops 3228696576 | bytes 20454400 | tf_op jit(solution)/shard_map/dot_general | solution.py:143
  240.6 1.3 slice-done
  241.9 5.4 %convert_reduce_fusion = f32[256,1536]{1,0:T(8,128)S(1)} fusion(bf16[1536,8,512]{0,2,1:T(8,128)(2,1)S(1)} %bitcast.136, bf16[32,8,8,512]{3,2,1,0:T(8,128)(2,1)} %bitcast.147), kind=kOutput, calls=%fused_computation.27 | convolution fusion | flops 3230269440 | bytes 16252928 | tf_op jit(solution)/shard_map/rmw,dmw->mrd/dot_general | solution.py:83
  247.3 1.2 select_convert_fusion
  (65 shorter events, 5.7 us)
Async XLA Ops:
  7.2 214.6 %all-gather.2.cloned.1.call-start = ((), (), s32[]{:S(2)}) async-start(), calls=%async_computation.2 | async-start | bytes 42467328 | tf_op jit(solution)/shard_map/all_gather | solution.py:141
  13.9 0.7 copy-start.6
  13.9 1.1 copy-start
  15.5 6.9 %copy-start.12 = (s32[64]{0:T(128)S(1)}, s32[64]{0:T(128)}, u32[]{:S(2)}) copy-start(s32[64]{0:T(128)} %param.18) | copy-start | bytes 772
  15.5 7.0 %copy-start.8 = (s32[64]{0:T(128)S(1)}, s32[64]{0:T(128)}, u32[]{:S(2)}) copy-start(s32[64]{0:T(128)} %param.19) | copy-start | bytes 772
  15.6 7.0 %copy-start.9 = (s32[64]{0:T(128)S(1)}, s32[64]{0:T(128)}, u32[]{:S(2)}) copy-start(s32[64]{0:T(128)} %param.20) | copy-start | bytes 772
  15.6 7.2 %copy-start.11 = (s32[2]{0:T(128)S(1)}, s32[2]{0:T(128)}, u32[]{:S(2)}) copy-start(s32[2]{0:T(128)} %constant.74.clone.1) | copy-start | bytes 28
  20.8 1.6 copy-start.1
  24.5 0.6 copy-start.3
  24.6 0.6 copy-start.4
  25.9 9.7 %copy-start.5 = (s32[3]{0:T(128)S(1)}, s32[3]{0:T(128)}, u32[]{:S(2)}) copy-start(s32[3]{0:T(128)} %constant.166) | copy-start | bytes 40
  72.9 5.5 %copy-start.2 = (f32[256,3072]{1,0:T(8,128)S(1)}, f32[256,3072]{1,0:T(8,128)}, u32[]{:S(2)}) copy-start(f32[256,3072]{1,0:T(8,128)} %copy-done.1) | copy-start | bytes 9437188
  72.9 60.6 %all-to-all-start = ((bf16[2,512,1536]{2,0,1:T(2,128)(2,1)}), bf16[2,512,1536]{2,0,1:T(2,128)(2,1)}, u32[]{:S(2)}, u32[]{:S(2)}) async-start(bf16[2,512,1536]{2,0,1:T(2,128)(2,1)} %broadcast_select_fusion), calls=%async_computation | async-start | bytes 6291456 | tf_op jit(solution)/shard_map/all_to_all | solution.py:155
  79.6 7.0 %copy-start.13 = (s32[64]{0:T(128)S(1)}, s32[64]{0:T(128)}, u32[]{:S(2)}) copy-start(s32[64]{0:T(128)} %param.18) | copy-start | bytes 772
  90.4 8.2 %copy-start.10 = (s32[64]{0:T(128)S(1)}, s32[64]{0:T(128)}, u32[]{:S(2)}) copy-start(s32[64]{0:T(128)} %param.21) | copy-start | bytes 772
  142.0 72.4 %all-to-all-start.1 = ((bf16[16,64,1536]{2,1,0:T(8,128)(2,1)}), bf16[16,64,1536]{2,1,0:T(8,128)(2,1)}, u32[]{:S(2)}, u32[]{:S(2)}) async-start(bf16[16,64,1536]{2,1,0:T(8,128)(2,1)} %gather_fusion), calls=%async_computation.1 | async-start | bytes 6291456 | tf_op jit(solution)/shard_map/all_to_all | solution.py:159
  231.7 10.1 %slice-start = ((bf16[3,1536,4096]{1,2,0:T(8,128)(2,1)}), bf16[1,1536,4096]{1,2,0:T(8,128)(2,1)S(1)}, s32[]{:S(2)}) async-start(bf16[3,1536,4096]{1,2,0:T(8,128)(2,1)} %all-gather.2.cloned.1.call-done), calls=%async_computation.3 | async-start | bytes 25165824 | tf_op jit(solution)/shard_map/slice | solution.py:145
  241.9 5.4 %copy-start.7 = (pred[256]{0:T(512)(128)(4,1)S(1)}, pred[256]{0:T(512)(128)(4,1)}, u32[]{:S(2)}) copy-start(pred[256]{0:T(512)(128)(4,1)} %get-tuple-element.122) | copy-start | bytes 772
Sparse Core Ops, SparseCore 0:
  14.0 207.6 all-gather.1
where the time goes:
time: 257 us; the launch traced here: 255 us
  waiting for transfers between devices  67 us (26%)
  local copies, waits for them, and re-layouts  62.6 us (24%)
  matrix products  51.1 us (20%)
  other arithmetic  48.9 us (19%)
  between operations  14.3 us (6%)
  starting transfers between devices  11.3 us (4%)
    all_to_all x1, waiting for transfers between devices, local(): lax.all_to_all(arranged, 'dp', split_axis=0, concat_axis=0, tiled=True)  32.3 us
    all_to_all x1, waiting for transfers between devices, local(): lax.all_to_all(contexts, 'tensor', split_axis=1, concat_axis=0, tiled=True)  31.6 us
    select_n x1, other arithmetic, place_context(): return jnp.where((spots < cached_count)[:, None], cached_rows, placed)  16.8 us
    unnamed x32, local copies, waits for them, and re-layouts  12.3 us
    scatter x4, other arithmetic  11 us
    sub x2, matrix products, attend(): exponent = jnp.exp(scores - highest)  10.2 us
    dot_general x1, matrix products, local(): gate_out = jnp.dot(post_norm, shards[0], preferred_element_type=jnp.float32)  10 us
    scatter x6, local copies, waits for them, and re-layouts  9.31 us
  transfers between devices with their start and end apart: 3, of which 3 were waited for; matrix products, arithmetic and copies ran while one was open for 49% of the time, Pallas kernels for 0%

commit v1 on v0

v1 whole, which is shorter than its diff:
```python
import functools

import jax
import jax.numpy as jnp
import numpy as np
from jax import lax
from jax.experimental import pallas as pl
from jax.experimental.pallas import tpu as pltpu
from jax.sharding import PartitionSpec as P

HEADS = 16
KV_HEADS = 8
HEAD_DIM = 96
GROUP = 384
VMEM = 48 * 1024 * 1024

epsilon = 1e-05
rope_base = 100000.0
bf16 = jnp.bfloat16
f32 = jnp.float32


def frequencies():
    half = HEAD_DIM // 2
    steps = np.arange(half, dtype=np.float32)
    frequency = np.float32(rope_base) ** (np.float32(-2.0) * steps / np.float32(HEAD_DIM))
    row = np.zeros((1, 128), np.float32)
    row[0, :half] = frequency
    row[0, half:HEAD_DIM] = frequency
    return row


def norm_value(values, gain):
    factor = lax.rsqrt(jnp.mean(values * values, axis=-1, keepdims=True) + epsilon)
    return (values * factor * gain).astype(bf16)


def rotate(values, cosine, sine):
    width = values.shape[-1]
    half = HEAD_DIM // 2
    lane = lax.broadcasted_iota(jnp.int32, values.shape, 1)
    first = lax.rem(lane, HEAD_DIM) < half
    swapped = jnp.where(
        first, pltpu.roll(values, width - half, 1), pltpu.roll(values, half, 1)
    )
    return values * cosine + swapped * sine


def place(fresh, cached, new_count, cached_count):
    rows, new = cached.shape[0], fresh.shape[0]
    spot = lax.broadcasted_iota(jnp.int32, (rows, new), 0)
    token = lax.broadcasted_iota(jnp.int32, (rows, new), 1)
    chosen = (spot - cached_count == token) & (token < new_count)
    placed = jnp.dot(jnp.where(chosen, 1.0, 0.0).astype(bf16), fresh, preferred_element_type=f32)
    keep = lax.broadcasted_iota(jnp.int32, cached.shape, 0) < cached_count
    return jnp.where(keep, cached.astype(f32), placed).astype(bf16)


def key_kernel(
    order, news, olds, dev, tokens, gain, freq, weight, cached, context, normed, cosine, sine
):
    reqs, new, width = tokens.shape

    @pl.when(pl.program_id(0) == 0)
    def _():
        lane = lax.broadcasted_iota(jnp.int32, (new, 128), 1)
        row = lax.broadcasted_iota(jnp.int32, (new, 128), 0)
        sign = jnp.where(lane < HEAD_DIM // 2, -1.0, 1.0)
        for r in range(reqs):
            normed[r] = norm_value(tokens[r].astype(f32), gain[0:1, :])
            old = olds[order[dev[0] * reqs + r]]
            angles = (row + old).astype(f32) * freq[...]
            cos_part = jnp.cos(angles)[:, :HEAD_DIM]
            sin_part = (jnp.sin(angles) * sign)[:, :HEAD_DIM]
            cosine[r] = jnp.concatenate([cos_part] * 4, axis=1)
            sine[r] = jnp.concatenate([sin_part] * 4, axis=1)

    rows = normed[...].reshape(reqs * new, width)
    projected = jnp.dot(rows, weight[...], preferred_element_type=f32)
    turned = rotate(
        projected,
        cosine[...].reshape(reqs * new, GROUP),
        sine[...].reshape(reqs * new, GROUP),
    ).astype(bf16)
    parts, _, depth, _ = context.shape
    for r in range(reqs):
        request = order[dev[0] * reqs + r]
        merged = place(turned[r * new : (r + 1) * new], cached[r], news[request], olds[request])
        context[:, r] = merged.reshape(parts, depth, GROUP)


def value_kernel(order, news, olds, dev, normed, weight, cached, context):
    reqs, new, width = normed.shape
    rows = normed[...].reshape(reqs * new, width)
    projected = jnp.dot(rows, weight[...], preferred_element_type=f32).astype(bf16)
    parts, _, depth, _ = context.shape
    for r in range(reqs):
        request = order[dev[0] * reqs + r]
        merged = place(projected[r * new : (r + 1) * new], cached[r], news[request], olds[request])
        context[:, r] = merged.reshape(parts, depth, GROUP)


def attention_kernel(
    order, olds, dev, normed, cosine, sine, weight, keys, values, w_out, tokens, gain,
    residual, post, total, attended,
):
    step = pl.program_id(0)
    reqs, new, width = normed.shape
    parts, _, depth, _ = keys.shape
    ctx = parts * depth
    flat = reqs * new
    rows = normed[...].reshape(flat, width)
    projected = jnp.dot(rows, weight[...], preferred_element_type=f32)
    cos_part = cosine[...].reshape(flat, GROUP)
    sin_part = sine[...].reshape(flat, GROUP)
    queries = [
        rotate(projected[:, GROUP * i : GROUP * (i + 1)], cos_part, sin_part).astype(bf16)
        for i in range(2)
    ]
    spot = lax.broadcasted_iota(jnp.int32, (new, ctx), 1)
    token = lax.broadcasted_iota(jnp.int32, (new, ctx), 0)
    for r in range(reqs):
        old = olds[order[dev[0] * reqs + r]]
        key_rows = keys[:, r].reshape(ctx, GROUP)
        value_rows = values[:, r].reshape(ctx, GROUP)
        allowed = spot <= old + token
        pieces = []
        for k in range(4):
            key = key_rows[:, HEAD_DIM * k : HEAD_DIM * (k + 1)]
            value = value_rows[:, HEAD_DIM * k : HEAD_DIM * (k + 1)]
            for h in (2 * k, 2 * k + 1):
                place_at = HEAD_DIM * (h % 4)
                query = queries[h // 4][r * new : (r + 1) * new, place_at : place_at + HEAD_DIM]
                scores = lax.dot_general(
                    query, key, (((1,), (1,)), ((), ())), preferred_element_type=f32
                )
                scores = jnp.where(allowed, scores * HEAD_DIM ** (-0.5), -jnp.inf)
                highest = jnp.max(scores, axis=-1, keepdims=True)
                exponent = jnp.exp(scores - highest)
                weights = (exponent / jnp.sum(exponent, axis=-1, keepdims=True)).astype(bf16)
                pieces.append(jnp.dot(weights, value, preferred_element_type=f32))
        attended[r * new : (r + 1) * new, :] = jnp.concatenate(pieces, axis=1).astype(bf16)
    term = jnp.dot(attended[...], w_out[...], preferred_element_type=f32)

    @pl.when(step == 0)
    def _():
        total[...] = tokens[...].astype(f32).reshape(flat, width) + term

    @pl.when(step > 0)
    def _():
        total[...] += term

    @pl.when(step == pl.num_programs(0) - 1)
    def _():
        rounded = total[...].astype(bf16)
        residual[...] = rounded
        post[...] = norm_value(rounded.astype(f32), gain[1:2, :])


def mlp_kernel(rows, own, other, out, total):
    step = pl.program_id(0)
    values = rows[...]
    term = None
    for weights in (own, other):
        gate = jnp.dot(values, weights[0], preferred_element_type=f32)
        up = jnp.dot(values, weights[1], preferred_element_type=f32)
        hidden = (gate / (1.0 + jnp.exp(-gate)) * up).astype(bf16)
        product = lax.dot_general(
            hidden, weights[2], (((1,), (1,)), ((), ())), preferred_element_type=f32
        )
        term = product if term is None else term + product

    @pl.when(step == 0)
    def _():
        total[...] = term

    @pl.when(step > 0)
    def _():
        total[...] += term

    @pl.when(step == pl.num_programs(0) - 1)
    def _():
        out[...] = total[...].astype(bf16)


def pack_kernel(rank, source, target, sems):
    copies = [
        pltpu.make_async_copy(source.at[i], target.at[rank[i]], sems.at[i])
        for i in range(source.shape[0])
    ]
    for copy in copies:
        copy.start()
    for copy in copies:
        copy.wait()


def unpack_kernel(columns, rows, source, *rest):
    target, sems = rest[-2], rest[-1]
    width = source.shape[-1]
    copies = [
        pltpu.make_async_copy(
            source.at[rows[i]], target.at[i, :, pl.ds(columns, width)], sems.at[i]
        )
        for i in range(source.shape[0])
    ]
    for copy in copies:
        copy.start()
    for copy in copies:
        copy.wait()


def call(kernel, prefetched, grid, in_specs, out_specs, out_shape, scratch, operands, cost=None, aliases={}):
    return pl.pallas_call(
        kernel,
        out_shape=out_shape,
        grid_spec=pltpu.PrefetchScalarGridSpec(
            num_scalar_prefetch=len(prefetched),
            grid=grid,
            in_specs=in_specs,
            out_specs=out_specs,
            scratch_shapes=scratch,
        ),
        compiler_params=pltpu.CompilerParams(vmem_limit_bytes=VMEM),
        cost_estimate=cost,
        input_output_aliases=aliases,
    )(*prefetched, *operands)


def shape(dims, dtype=bf16):
    return jax.ShapeDtypeStruct(dims, dtype)


def whole(dims):
    return pl.BlockSpec(dims, lambda *_: (0,) * len(dims))


def local(
    tokens,
    cached,
    norm_gains,
    w_qkv,
    w_out,
    mlp_weights,
    request_order,
    new_lengths,
    cached_lengths,
    decode_slots,
):
    tensor_size = lax.axis_size("tensor")
    group_total = lax.axis_size("dp")
    reqs, new, width = tokens.shape
    ctx = cached.shape[1]
    depth = ctx // tensor_size
    flat = reqs * new
    group_reqs = reqs * tensor_size
    group_index = lax.axis_index("dp")
    device = group_index * tensor_size + lax.axis_index("tensor")
    dev = device.astype(jnp.int32).reshape(1)
    key_width = KV_HEADS * HEAD_DIM
    groups = key_width // GROUP
    scalars = (request_order, new_lengths, cached_lengths, dev)
    freq = jnp.asarray(frequencies())

    other_weights = lax.ppermute(
        mlp_weights, "tensor", [(t, t ^ 1) for t in range(tensor_size)]
    )

    context_shape = (tensor_size, reqs, depth, key_width)
    context_spec = pl.BlockSpec((tensor_size, reqs, depth, GROUP), lambda g, *_: (0, 0, 0, g))
    table = (reqs, new, GROUP)
    keys, normed, cosine, sine = call(
        key_kernel,
        scalars,
        (groups,),
        [
            whole(tokens.shape),
            whole(norm_gains.shape),
            whole((1, 128)),
            pl.BlockSpec((width, GROUP), lambda g, *_: (0, width // GROUP + g)),
            pl.BlockSpec((reqs, ctx, GROUP), lambda g, *_: (0, 0, g)),
        ],
        [context_spec, whole(tokens.shape), whole(table), whole(table)],
        [shape(context_shape), shape(tokens.shape), shape(table, f32), shape(table, f32)],
        [],
        (tokens, norm_gains, freq, w_qkv, cached),
        pl.CostEstimate(flops=2 * flat * width * key_width, bytes_accessed=8 << 20, transcendentals=0),
    )
    keys_moved = lax.all_to_all(keys, "tensor", split_axis=0, concat_axis=0, tiled=True)
    values = call(
        value_kernel,
        scalars,
        (groups,),
        [
            whole(tokens.shape),
            pl.BlockSpec((width, GROUP), lambda g, *_: (0, (width + key_width) // GROUP + g)),
            pl.BlockSpec((reqs, ctx, GROUP), lambda g, *_: (0, 0, groups + g)),
        ],
        context_spec,
        shape(context_shape),
        [],
        (normed, w_qkv, cached),
        pl.CostEstimate(flops=2 * flat * width * key_width, bytes_accessed=8 << 20, transcendentals=0),
    )
    values_moved = lax.all_to_all(values, "tensor", split_axis=0, concat_axis=0, tiled=True)

    residual, post = call(
        attention_kernel,
        (request_order, cached_lengths, dev),
        (groups,),
        [
            whole(tokens.shape),
            whole(table),
            whole(table),
            pl.BlockSpec((width, 2 * GROUP), lambda g, *_: (0, g)),
            context_spec,
            context_spec,
            pl.BlockSpec((2 * GROUP, width), lambda g, *_: (g, 0)),
            whole(tokens.shape),
            whole(norm_gains.shape),
        ],
        [whole((flat, width))] * 2,
        [shape((flat, width))] * 2,
        [pltpu.VMEM((flat, width), f32), pltpu.VMEM((flat, 2 * GROUP), bf16)],
        (normed, cosine, sine, w_qkv, keys, values, w_out, tokens, norm_gains),
        pl.CostEstimate(flops=12 * flat * width * width, bytes_accessed=16 << 20, transcendentals=0),
    )

    units = mlp_weights.shape[2]
    chunk = 256 if units % 256 == 0 else units

    def mlp(rows):
        return call(
            mlp_kernel,
            (),
            (units // chunk,),
            [
                whole((flat, width)),
                pl.BlockSpec((3, width, chunk), lambda c: (0, 0, c)),
                pl.BlockSpec((3, width, chunk), lambda c: (0, 0, c)),
            ],
            whole((flat, width)),
            shape((flat, width)),
            [pltpu.VMEM((flat, width), f32)],
            (rows, mlp_weights, other_weights),
            pl.CostEstimate(flops=12 * flat * width * units, bytes_accessed=12 * width * units, transcendentals=0),
        )

    partners = [
        [(t, t ^ (2 * s)) for t in range(tensor_size)] for s in range(1, tensor_size // 2)
    ]
    arrivals = [lax.ppermute(post, "tensor", pairs) for pairs in partners]
    partials = [mlp(post)]
    for pairs, rows in zip(partners, arrivals):
        partials.append(lax.ppermute(mlp(rows), "tensor", pairs))

    every = request_order.shape[0]
    indices = jnp.arange(every, dtype=jnp.int32)
    slot_of = jnp.sum(
        jnp.where(request_order[:, None] == indices[None, :], decode_slots[None, :], 0), axis=1
    )
    count_of = jnp.sum(
        jnp.where(request_order[:, None] == indices[None, :], new_lengths[None, :], 0), axis=1
    )
    own_slots = lax.dynamic_slice_in_dim(slot_of, group_index * group_reqs, group_reqs)
    rank = jnp.sum((own_slots[None, :] < own_slots[:, None]).astype(jnp.int32), axis=1)
    slot_ids = group_index * group_reqs + jnp.arange(group_reqs, dtype=jnp.int32)
    owners = jnp.sum(
        jnp.where(slot_of[None, :] == slot_ids[:, None], indices[None, :] // group_reqs, 0), axis=1
    )
    per_group = group_reqs // group_total
    ordinal = jnp.arange(group_reqs, dtype=jnp.int32)
    same_owner = (owners[:, None] == owners[None, :]) & (ordinal[None, :] < ordinal[:, None])
    source_rows = owners * per_group + jnp.sum(same_owner.astype(jnp.int32), axis=1)

    half_shape = (group_reqs, depth, key_width)
    anywhere = pl.BlockSpec(memory_space=pl.ANY)
    sems = [pltpu.SemaphoreType.DMA((group_reqs,))]

    def across(moved):
        packed = call(
            pack_kernel, (rank,), (1,), [anywhere], anywhere, shape(half_shape), sems,
            (moved.reshape(half_shape),),
            pl.CostEstimate(flops=0, bytes_accessed=6 << 20, transcendentals=0),
        )
        return lax.all_to_all(packed, "dp", split_axis=0, concat_axis=0, tiled=True)

    keys_arrived = across(keys_moved)
    values_arrived = across(values_moved)
    full_shape = shape((group_reqs, depth, 2 * key_width))
    kv_half = call(
        functools.partial(unpack_kernel, 0), (source_rows,), (1,), [anywhere], anywhere,
        full_shape, sems, (keys_arrived,),
        pl.CostEstimate(flops=0, bytes_accessed=6 << 20, transcendentals=0),
    )
    kv_decode = call(
        functools.partial(unpack_kernel, key_width), (source_rows,), (1,), [anywhere, anywhere],
        anywhere, full_shape, sems, (values_arrived, kv_half),
        pl.CostEstimate(flops=0, bytes_accessed=6 << 20, transcendentals=0), {2: 0},
    )

    own_counts = lax.dynamic_slice_in_dim(count_of, device * reqs, reqs)
    live = (jnp.arange(new, dtype=jnp.int32)[None, :] < own_counts[:, None]).reshape(flat, 1)
    total = residual.astype(f32)
    for partial in partials:
        total = total + partial.astype(f32)
    layer_out = jnp.where(live, total, 0.0).astype(bf16).reshape(reqs, new, width)
    return (layer_out, kv_decode)


def solution(mesh):
    in_specs = (
        P(("dp", "tensor"), None, None),
        P(("dp", "tensor"), None, None),
        P(),
        P(),
        P(),
        P(None, None, "tensor"),
        P(),
        P(),
        P(),
        P(),
    )
    out_specs = (P(("dp", "tensor"), None, None), P("dp", "tensor", None))
    return jax.shard_map(local, mesh=mesh, in_specs=in_specs, out_specs=out_specs, check_vma=False)
```

time: 257 us -> 215 us (0.84)
  Pallas kernels: 0 us -> 62.9 us
  matrix products: 51.1 us -> 0 us
  other arithmetic: 48.9 us -> 3.85 us
  local copies, waits for them, and re-layouts: 62.6 us -> 18.2 us
  waiting for transfers between devices: 67 us -> 102 us
  starting transfers between devices: 11.3 us -> 25.6 us
  between operations: 14.3 us -> 0.87 us
    pallas_call x0 -> x11, Pallas kernels: none -> 62.9 us  [call(): pl.pallas_call(kernel, out_shape=out_shape, grid_spec=pltpu.PrefetchScala...]
    dot_general x7 -> x0, matrix products: 40.9 us -> none  [the longest x1 10 us: local(): gate_out = jnp.dot(post_norm, shards[0], preferred_element_type=jnp.float32)]
    ppermute x0 -> x7, waiting for transfers between devices: none -> 38.5 us  [the longest x3 26 us: local(): arrivals = [lax.ppermute(post, 'tensor', pairs) for pairs in partners]]
    select_n x6 -> x1, other arithmetic: 23.9 us -> 0.01 us  [local(): indices[None, :] // group_reqs]
    scatter x5 -> x0, other arithmetic: 11.1 us -> none
    sub x2 -> x0, matrix products: 10.2 us -> none  [attend(): exponent = jnp.exp(scores - highest)]
    scatter x6 -> x0, local copies, waits for them, and re-layouts: 9.31 us -> none
    slice x10 -> x0, local copies, waits for them, and re-layouts: 8.61 us -> none  [the longest x2 4.33 us: local(): projected[:, :D].reshape(row_count, HEADS, HEAD_DIM)]
  transfers between devices with their start and end apart: 3 -> 11, of which waited for: 3 -> 6; matrix products, arithmetic and copies ran while one was open for 49% -> 0% of each run, Pallas kernels for 0% -> 27%
where the time goes in v1:
time: 215 us; the launch traced here: 214 us
  waiting for transfers between devices  102 us (47%)
  Pallas kernels  62.9 us (29%)
  starting transfers between devices  25.6 us (12%)
  local copies, waits for them, and re-layouts  18.2 us (8%)
  other arithmetic  3.85 us (2%)
    pallas_call x11, Pallas kernels, call(): pl.pallas_call(kernel, out_shape=out_shape, grid_spec=pltpu.PrefetchScala...  62.9 us
    all_to_all x2, waiting for transfers between devices, across(): return lax.all_to_all(packed, 'dp', split_axis=0, concat_axis=0, tiled=True)  32.2 us
    ppermute x3, waiting for transfers between devices, local(): arrivals = [lax.ppermute(post, 'tensor', pairs) for pairs in partners]  26 us
    unnamed x52, local copies, waits for them, and re-layouts  18.1 us
    all_to_all x1, waiting for transfers between devices, local(): lax.all_to_all(values, 'tensor', split_axis=0, concat_axis=0, tiled=True)  16.7 us
    all_to_all x1, waiting for transfers between devices, local(): lax.all_to_all(keys, 'tensor', split_axis=0, concat_axis=0, tiled=True)  15 us
    ppermute x3, waiting for transfers between devices, local(): partials.append(lax.ppermute(mlp(rows), 'tensor', pairs))  12.5 us
    all_to_all x2, starting transfers between devices, across(): return lax.all_to_all(packed, 'dp', split_axis=0, concat_axis=0, tiled=True)  9.09 us
  transfers between devices with their start and end apart: 11, of which 6 were waited for; matrix products, arithmetic and copies ran while one was open for 0% of the time, Pallas kernels for 27%

profile of v1, /device:TPU:0, one launch (start us, length us, event | category | flops | bytes accessed | tf_op | source)
XLA Modules:
  0.0 213.9 jit_solution(109775349204001837)
XLA Ops:
  0.6 0.0 copy-start.8
  0.6 1.1 copy-done.8
  1.8 0.7 copy-done.12
  2.5 0.7 copy-done.14
  3.1 0.7 copy-done.16
  3.8 0.7 copy-done.18
  4.4 0.7 copy-done.20
  5.1 5.3 %shard_map.122 = (bf16[8,2,64,768]{3,2,1,0:T(8,128)(2,1)S(1)}, bf16[2,128,1536]{2,1,0:T(8,128)(2,1)S(1)}, f32[2,128,384]{2,1,0:T(8,128)S(1)}, f32[2,128,384]{2,1,0:T(8,128)S(1)}) custom-call(s32[64]{0:T(128)S(1)} %copy-done.16, s32[64]{0:T(128)S(1)} %copy-done.14, s32[64]{0:T(128)S(1)} %copy-done.18, s32[1]{0:T(128)} %bitcast.1.dev, ...), custom_call_target="tpu_custom_call" | custom-call | flops 603979776 | bytes 8388608 | tf_op jit(solution)/shard_map/pallas_call | solution.py:213
  10.4 0.0 copy-start.3
  10.4 1.1 copy-done.3
  11.6 0.9 copy-done.5
  12.4 0.7 copy-done.21
  13.2 0.8 copy-done.23
  14.0 5.4 %all-to-all-start.2 = ((bf16[8,2,64,768]{3,2,1,0:T(8,128)(2,1)}), bf16[8,2,64,768]{3,2,1,0:T(8,128)(2,1)}, u32[]{:S(2)}, u32[]{:S(2)}) async-start(bf16[8,2,64,768]{3,2,1,0:T(8,128)(2,1)} %copy-done.3), calls=%async_computation.2 | async-start | bytes 3145728 | tf_op jit(solution)/shard_map/all_to_all | solution.py:288
  19.4 0.0 copy-start.6
  19.4 1.1 copy-done.6
  20.6 3.8 %shard_map.123.values = bf16[8,2,64,768]{3,2,1,0:T(8,128)(2,1)S(1)} custom-call(s32[64]{0:T(128)S(1)} %copy-done.17, s32[64]{0:T(128)S(1)} %copy-done.15, s32[64]{0:T(128)S(1)} %copy-done.19, s32[1]{0:T(128)} %bitcast.1.dev, bf16[2,128,1536]{2,1,0:T(8,128)(2,1)S(1)} %copy-done.6, bf16[1536,3072]{1,0:T(8,128)(2,1)} %weight.5, bf16[2,512,1536]{2,1,0:T(8,128)(2,1)S(1)} %copy-done), custom_call_target="tpu_custom_call" | custom-call | flops 603979776 | bytes 8388608 | tf_op jit(solution)/shard_map/pallas_call | solution.py:213
  24.4 1.1 copy-done.2
  25.5 15.0 %all-to-all-done.2 = bf16[8,2,64,768]{3,2,1,0:T(8,128)(2,1)} async-done(((bf16[8,2,64,768]{3,2,1,0:T(8,128)(2,1)}), bf16[8,2,64,768]{3,2,1,0:T(8,128)(2,1)}, u32[]{:S(2)}, u32[]{:S(2)}) %all-to-all-start.2) | async-done | bytes 1572896 | tf_op jit(solution)/shard_map/all_to_all | solution.py:288
  40.5 3.6 %all-to-all-start = ((bf16[8,2,64,768]{3,2,1,0:T(8,128)(2,1)}), bf16[8,2,64,768]{3,2,1,0:T(8,128)(2,1)S(1)}, u32[]{:S(2)}, u32[]{:S(2)}) async-start(bf16[8,2,64,768]{3,2,1,0:T(8,128)(2,1)} %copy-done.2), calls=%async_computation | async-start | bytes 3145728 | tf_op jit(solution)/shard_map/all_to_all | solution.py:304
  44.1 0.4 collective-permute-start
  44.5 0.2 select_reduce_fusion
  44.7 0.1 dynamic_slice.7
  44.8 0.2 convert_reduce_fusion.rank
  45.0 2.1 %shard_map.130 = bf16[16,64,768]{2,1,0:T(8,128)(2,1)S(1)} custom-call(s32[16]{0:T(128)S(1)} %convert_reduce_fusion.rank, bf16[16,64,768]{2,1,0:T(8,128)(2,1)} %bitcast.4.source), custom_call_target="tpu_custom_call" | custom-call | bytes 6291456 | tf_op jit(solution)/shard_map/pallas_call | solution.py:213
  47.1 1.2 copy-done.1
  48.4 16.7 %all-to-all-done = bf16[8,2,64,768]{3,2,1,0:T(8,128)(2,1)S(1)} async-done(((bf16[8,2,64,768]{3,2,1,0:T(8,128)(2,1)}), bf16[8,2,64,768]{3,2,1,0:T(8,128)(2,1)S(1)}, u32[]{:S(2)}, u32[]{:S(2)}) %all-to-all-start) | async-done | bytes 1572896 | tf_op jit(solution)/shard_map/all_to_all | solution.py:304
  65.1 5.3 %all-to-all-start.3 = ((bf16[16,64,768]{2,1,0:T(8,128)(2,1)}), bf16[16,64,768]{2,1,0:T(8,128)(2,1)S(1)}, u32[]{:S(2)}, u32[]{:S(2)}) async-start(bf16[16,64,768]{2,1,0:T(8,128)(2,1)} %copy-done.1), calls=%async_computation.3 | async-start | bytes 3145728 | tf_op jit(solution)/shard_map/all_to_all | solution.py:385
  70.4 1.9 shard_map.129
  72.3 0.0 copy-start.13
  72.3 32.2 %all-to-all-done.3.source = bf16[16,64,768]{2,1,0:T(8,128)(2,1)S(1)} async-done(((bf16[16,64,768]{2,1,0:T(8,128)(2,1)}), bf16[16,64,768]{2,1,0:T(8,128)(2,1)S(1)}, u32[]{:S(2)}, u32[]{:S(2)}) %all-to-all-start.3) | async-done | bytes 1572896 | tf_op jit(solution)/shard_map/all_to_all | solution.py:385
  104.5 3.7 %all-to-all-start.1 = ((bf16[16,64,768]{2,1,0:T(8,128)(2,1)}), bf16[16,64,768]{2,1,0:T(8,128)(2,1)S(1)}, u32[]{:S(2)}, u32[]{:S(2)}) async-start(bf16[16,64,768]{2,1,0:T(8,128)(2,1)} %shard_map.129), calls=%async_computation.1 | async-start | bytes 3145728 | tf_op jit(solution)/shard_map/all_to_all | solution.py:385
  108.3 0.0 copy-start.4
  108.3 1.4 copy-done.4
  109.7 1.1 copy-done.7
  110.8 1.1 copy-done.9
  112.0 1.0 copy-done.22
  113.0 1.0 copy-done.24
  114.0 20.0 %shard_map.124 = (bf16[256,1536]{1,0:T(8,128)(2,1)S(1)}, bf16[256,1536]{1,0:T(8,128)(2,1)}) custom-call(s32[64]{0:T(128)S(1)} %copy-done.17, s32[64]{0:T(128)S(1)} %copy-done.19, s32[1]{0:T(128)} %bitcast.1.dev, bf16[2,128,1536]{2,1,0:T(8,128)(2,1)S(1)} %copy-done.7, f32[2,128,384]{2,1,0:T(8,128)S(1)} %copy-done.22, f32[2,128,384]{2,1,0:T(8,128)S(1)} %copy-done.24, ...), custom_call_target="tpu_custom_call" | custom-call | flops 7247757312 | bytes 16777216 | tf_op jit(solution)/shard_map/pallas_call | solution.py:213
  133.9 0.9 copy-done.10
  134.8 3.6 %collective-permute-start.1 = (bf16[256,1536]{1,0:T(8,128)(2,1)}, bf16[256,1536]{1,0:T(8,128)(2,1)}, u32[]{:S(2)}, u32[]{:S(2)}) collective-permute-start(bf16[256,1536]{1,0:T(8,128)(2,1)} %get-tuple-element.13.rows), channel_id=1, source_target_pairs={{0,2},{1,3},{2,0},{3,1},{4,6},{5,7},{6,4},{7,5},{8,10},{9,11},{10,... | collective-permute-start | bytes 2359304 | tf_op jit(solution)/shard_map/ppermute | solution.py:351
  138.4 0.3 collective-permute-start.3
  138.8 1.1 collective-permute-start.5
  139.9 0.1 dynamic_slice.6
  140.0 0.2 select_reduce_fusion.2
  140.1 17.0 %collective-permute-done.1.rows = bf16[256,1536]{1,0:T(8,128)(2,1)} collective-permute-done((bf16[256,1536]{1,0:T(8,128)(2,1)}, bf16[256,1536]{1,0:T(8,128)(2,1)}, u32[]{:S(2)}, u32[]{:S(2)}) %collective-permute-start.1) | collective-permute-done | bytes 786464 | tf_op jit(solution)/shard_map/ppermute | solution.py:351
  157.2 0.0 collective-permute-done.other
  157.2 6.8 %shard_map.126 = bf16[256,1536]{1,0:T(8,128)(2,1)} custom-call(bf16[256,1536]{1,0:T(8,128)(2,1)} %collective-permute-done.1.rows, bf16[3,1536,512]{2,1,0:T(8,128)(2,1)} %own.7, bf16[3,1536,512]{2,1,0:T(8,128)(2,1)} %collective-permute-done.other), custom_call_target="tpu_custom_call" | custom-call | flops 2415919104 | bytes 9437184 | tf_op jit(solution)/shard_map/pallas_call | solution.py:213
  163.9 2.0 collective-permute-start.2
  166.0 8.9 %collective-permute-done.3.rows = bf16[256,1536]{1,0:T(8,128)(2,1)} collective-permute-done((bf16[256,1536]{1,0:T(8,128)(2,1)}, bf16[256,1536]{1,0:T(8,128)(2,1)}, u32[]{:S(2)}, u32[]{:S(2)}) %collective-permute-start.3) | collective-permute-done | bytes 786464 | tf_op jit(solution)/shard_map/ppermute | solution.py:351
  174.9 6.8 %shard_map.127 = bf16[256,1536]{1,0:T(8,128)(2,1)} custom-call(bf16[256,1536]{1,0:T(8,128)(2,1)} %collective-permute-done.3.rows, bf16[3,1536,512]{2,1,0:T(8,128)(2,1)} %own.7, bf16[3,1536,512]{2,1,0:T(8,128)(2,1)} %collective-permute-done.other), custom_call_target="tpu_custom_call" | custom-call | flops 2415919104 | bytes 9437184 | tf_op jit(solution)/shard_map/pallas_call | solution.py:213
  181.6 0.0 collective-permute-done.5.rows
  181.7 6.7 %shard_map.128 = bf16[256,1536]{1,0:T(8,128)(2,1)} custom-call(bf16[256,1536]{1,0:T(8,128)(2,1)} %collective-permute-done.5.rows, bf16[3,1536,512]{2,1,0:T(8,128)(2,1)} %own.7, bf16[3,1536,512]{2,1,0:T(8,128)(2,1)} %collective-permute-done.other), custom_call_target="tpu_custom_call" | custom-call | flops 2415919104 | bytes 9437184 | tf_op jit(solution)/shard_map/pallas_call | solution.py:213
  188.4 0.0 collective-permute-start.6
  188.4 0.2 convert_reduce_fusion.1
  188.6 0.1 compare_bitcast_fusion
  188.7 1.8 shard_map.131.rest_0_
  190.5 0.0 all-to-all-done.1.source
  190.5 1.8 shard_map.132
  192.3 5.9 %shard_map.125 = bf16[256,1536]{1,0:T(8,128)(2,1)S(1)} custom-call(bf16[256,1536]{1,0:T(8,128)(2,1)} %get-tuple-element.13.rows, bf16[3,1536,512]{2,1,0:T(8,128)(2,1)} %own.7, bf16[3,1536,512]{2,1,0:T(8,128)(2,1)} %collective-permute-done.other), custom_call_target="tpu_custom_call" | custom-call | flops 2415919104 | bytes 9437184 | tf_op jit(solution)/shard_map/pallas_call | solution.py:213
  198.3 0.0 collective-permute-done.2
  198.3 12.5 %collective-permute-done.4 = bf16[256,1536]{1,0:T(8,128)(2,1)} collective-permute-done((bf16[256,1536]{1,0:T(8,128)(2,1)}, bf16[256,1536]{1,0:T(8,128)(2,1)}, u32[]{:S(2)}, u32[]{:S(2)}) %collective-permute-start.4) | collective-permute-done | bytes 786464 | tf_op jit(solution)/shard_map/ppermute | solution.py:354
  210.8 0.0 collective-permute-done.6
  210.8 3.1 %select_convert_fusion = bf16[256,1536]{1,0:T(8,128)(2,1)} fusion(bf16[256,1536]{1,0:T(8,128)(2,1)} %collective-permute-done.6, bf16[256,1536]{1,0:T(8,128)(2,1)} %collective-permute-done.4, bf16[256,1536]{1,0:T(8,128)(2,1)} %collective-permute-done.2, bf16[256,1536]{1,0:T(8,128)(2,1)S(1)} %shard_map.125, bf16[256,1536]{1,0:T(8,128)(2,1)S(1)} %copy-done.11, ...), kind=kLoop, calls=%fused_computation | loop fusion | flops 4325376 | bytes 4718848 | tf_op jit(solution)/shard_map/convert_element_type | solution.py:406
  (32 shorter events, 0.1 us)
Async XLA Ops:
  0.6 1.1 copy-start.8
  1.8 0.7 copy-start.12
  2.5 0.7 copy-start.14
  3.1 0.7 copy-start.16
  3.8 0.7 copy-start.18
  4.4 0.7 copy-start.20
  10.4 1.1 copy-start.3
  11.6 0.9 copy-start.5
  12.4 0.7 copy-start.21
  13.2 0.8 copy-start.23
  13.9 5.5 %copy-start = (bf16[2,512,1536]{2,1,0:T(8,128)(2,1)S(1)}, bf16[2,512,1536]{2,1,0:T(8,128)(2,1)}, u32[]{:S(2)}) copy-start(bf16[2,512,1536]{2,1,0:T(8,128)(2,1)} %cached.3) | copy-start | bytes 9437188
  13.9 5.5 %copy-start.15 = (s32[64]{0:T(128)S(1)}, s32[64]{0:T(128)}, u32[]{:S(2)}) copy-start(s32[64]{0:T(128)} %news.3) | copy-start | bytes 772
  13.9 5.5 %copy-start.17 = (s32[64]{0:T(128)S(1)}, s32[64]{0:T(128)}, u32[]{:S(2)}) copy-start(s32[64]{0:T(128)} %order.5) | copy-start | bytes 772
  13.9 5.5 %copy-start.19 = (s32[64]{0:T(128)S(1)}, s32[64]{0:T(128)}, u32[]{:S(2)}) copy-start(s32[64]{0:T(128)} %olds.5) | copy-start | bytes 772
  14.0 26.6 %all-to-all-start.2 = ((bf16[8,2,64,768]{3,2,1,0:T(8,128)(2,1)}), bf16[8,2,64,768]{3,2,1,0:T(8,128)(2,1)}, u32[]{:S(2)}, u32[]{:S(2)}) async-start(bf16[8,2,64,768]{3,2,1,0:T(8,128)(2,1)} %copy-done.3), calls=%async_computation.2 | async-start | bytes 3145728 | tf_op jit(solution)/shard_map/all_to_all | solution.py:288
  19.4 1.1 copy-start.6
  24.4 1.2 copy-start.2
  25.5 19.0 %copy-start.25 = (s32[64]{0:T(128)S(1)}, s32[64]{0:T(128)}, u32[]{:S(2)}) copy-start(s32[64]{0:T(128)} %param.20) | copy-start | bytes 772
  40.5 24.5 %all-to-all-start = ((bf16[8,2,64,768]{3,2,1,0:T(8,128)(2,1)}), bf16[8,2,64,768]{3,2,1,0:T(8,128)(2,1)S(1)}, u32[]{:S(2)}, u32[]{:S(2)}) async-start(bf16[8,2,64,768]{3,2,1,0:T(8,128)(2,1)} %copy-done.2), calls=%async_computation | async-start | bytes 3145728 | tf_op jit(solution)/shard_map/all_to_all | solution.py:304
  44.1 113.1 %collective-permute-start = (bf16[3,1536,512]{2,1,0:T(8,128)(2,1)}, bf16[3,1536,512]{2,1,0:T(8,128)(2,1)}, u32[]{:S(2)}, u32[]{:S(2)}) collective-permute-start(bf16[3,1536,512]{2,1,0:T(8,128)(2,1)} %own.7), channel_id=1, source_target_pairs={{0,1},{1,0},{2,3},{3,2},{4,5},{5,4},{6,7},{7,6},{8,9},{9,8},{10,11... | collective-permute-start | bytes 14155784 | tf_op jit(solution)/shard_map/ppermute | solution.py:264
  47.1 1.3 copy-start.1
  65.1 39.4 %all-to-all-start.3 = ((bf16[16,64,768]{2,1,0:T(8,128)(2,1)}), bf16[16,64,768]{2,1,0:T(8,128)(2,1)S(1)}, u32[]{:S(2)}, u32[]{:S(2)}) async-start(bf16[16,64,768]{2,1,0:T(8,128)(2,1)} %copy-done.1), calls=%async_computation.3 | async-start | bytes 3145728 | tf_op jit(solution)/shard_map/all_to_all | solution.py:385
  72.3 36.0 %copy-start.13 = (f32[2,1536]{1,0:T(2,128)S(1)}, f32[2,1536]{1,0:T(2,128)}, u32[]{:S(2)}) copy-start(f32[2,1536]{1,0:T(2,128)} %gain.3) | copy-start | bytes 36868
  104.5 86.0 %all-to-all-start.1 = ((bf16[16,64,768]{2,1,0:T(8,128)(2,1)}), bf16[16,64,768]{2,1,0:T(8,128)(2,1)S(1)}, u32[]{:S(2)}, u32[]{:S(2)}) async-start(bf16[16,64,768]{2,1,0:T(8,128)(2,1)} %shard_map.129), calls=%async_computation.1 | async-start | bytes 3145728 | tf_op jit(solution)/shard_map/all_to_all | solution.py:385
  108.3 1.4 copy-start.4
  109.7 1.1 copy-start.7
  110.8 1.1 copy-start.9
  112.0 1.0 copy-start.22
  113.0 1.0 copy-start.24
  133.9 0.9 copy-start.10
  134.8 22.4 %collective-permute-start.1 = (bf16[256,1536]{1,0:T(8,128)(2,1)}, bf16[256,1536]{1,0:T(8,128)(2,1)}, u32[]{:S(2)}, u32[]{:S(2)}) collective-permute-start(bf16[256,1536]{1,0:T(8,128)(2,1)} %get-tuple-element.13.rows), channel_id=1, source_target_pairs={{0,2},{1,3},{2,0},{3,1},{4,6},{5,7},{6,4},{7,5},{8,10},{9,11},{10,... | collective-permute-start | bytes 2359304 | tf_op jit(solution)/shard_map/ppermute | solution.py:351
  138.4 36.5 %collective-permute-start.3 = (bf16[256,1536]{1,0:T(8,128)(2,1)}, bf16[256,1536]{1,0:T(8,128)(2,1)}, u32[]{:S(2)}, u32[]{:S(2)}) collective-permute-start(bf16[256,1536]{1,0:T(8,128)(2,1)} %get-tuple-element.13.rows), channel_id=1, source_target_pairs={{0,4},{1,5},{2,6},{3,7},{4,0},{5,1},{6,2},{7,3},{8,12},{9,13},{10,... | collective-permute-start | bytes 2359304 | tf_op jit(solution)/shard_map/ppermute | solution.py:351
  138.8 42.9 %collective-permute-start.5 = (bf16[256,1536]{1,0:T(8,128)(2,1)}, bf16[256,1536]{1,0:T(8,128)(2,1)}, u32[]{:S(2)}, u32[]{:S(2)}) collective-permute-start(bf16[256,1536]{1,0:T(8,128)(2,1)} %get-tuple-element.13.rows), channel_id=1, source_target_pairs={{0,6},{1,7},{2,4},{3,5},{4,2},{5,3},{6,0},{7,1},{8,14},{9,15},{10,... | collective-permute-start | bytes 2359304 | tf_op jit(solution)/shard_map/ppermute | solution.py:351
  163.9 34.3 %collective-permute-start.2 = (bf16[256,1536]{1,0:T(8,128)(2,1)}, bf16[256,1536]{1,0:T(8,128)(2,1)}, u32[]{:S(2)}, u32[]{:S(2)}) collective-permute-start(bf16[256,1536]{1,0:T(8,128)(2,1)} %shard_map.126), channel_id=1, source_target_pairs={{0,2},{1,3},{2,0},{3,1},{4,6},{5,7},{6,4},{7,5},{8,10},{9,11},{10,... | collective-permute-start | bytes 2359304 | tf_op jit(solution)/shard_map/ppermute | solution.py:354
  181.6 29.2 %collective-permute-start.4 = (bf16[256,1536]{1,0:T(8,128)(2,1)}, bf16[256,1536]{1,0:T(8,128)(2,1)}, u32[]{:S(2)}, u32[]{:S(2)}) collective-permute-start(bf16[256,1536]{1,0:T(8,128)(2,1)} %shard_map.127), channel_id=1, source_target_pairs={{0,4},{1,5},{2,6},{3,7},{4,0},{5,1},{6,2},{7,3},{8,12},{9,13},{10,... | collective-permute-start | bytes 2359304 | tf_op jit(solution)/shard_map/ppermute | solution.py:354
  188.4 22.4 %collective-permute-start.6 = (bf16[256,1536]{1,0:T(8,128)(2,1)}, bf16[256,1536]{1,0:T(8,128)(2,1)}, u32[]{:S(2)}, u32[]{:S(2)}) collective-permute-start(bf16[256,1536]{1,0:T(8,128)(2,1)} %shard_map.128), channel_id=1, source_target_pairs={{0,6},{1,7},{2,4},{3,5},{4,2},{5,3},{6,0},{7,1},{8,14},{9,15},{10,... | collective-permute-start | bytes 2359304 | tf_op jit(solution)/shard_map/ppermute | solution.py:354
  192.3 18.5 %copy-start.11 = (bf16[256,1536]{1,0:T(8,128)(2,1)S(1)}, bf16[256,1536]{1,0:T(8,128)(2,1)}, u32[]{:S(2)}) copy-start(bf16[256,1536]{1,0:T(8,128)(2,1)} %copy-done.10) | copy-start | bytes 2359300

commit v2 on v1

--- a/solution.py
+++ b/solution.py
@@ -1,4 +1,5 @@
 import functools
+import math
 
 import jax
 import jax.numpy as jnp
@@ -12,7 +13,7 @@
 KV_HEADS = 8
 HEAD_DIM = 96
 GROUP = 384
-VMEM = 48 * 1024 * 1024
+VMEM = 60 * 1024 * 1024
 
 epsilon = 1e-05
 rope_base = 100000.0
@@ -119,26 +120,30 @@
     ]
     spot = lax.broadcasted_iota(jnp.int32, (new, ctx), 1)
     token = lax.broadcasted_iota(jnp.int32, (new, ctx), 0)
+    scale = HEAD_DIM ** (-0.5) * math.log2(math.e)
     for r in range(reqs):
         old = olds[order[dev[0] * reqs + r]]
         key_rows = keys[:, r].reshape(ctx, GROUP)
         value_rows = values[:, r].reshape(ctx, GROUP)
-        allowed = spot <= old + token
+        mask = jnp.where(spot <= old + token, 0.0, -jnp.inf)
+        bias = jnp.concatenate([mask, mask], axis=0)
         pieces = []
         for k in range(4):
             key = key_rows[:, HEAD_DIM * k : HEAD_DIM * (k + 1)]
             value = value_rows[:, HEAD_DIM * k : HEAD_DIM * (k + 1)]
+            pair = []
             for h in (2 * k, 2 * k + 1):
-                place_at = HEAD_DIM * (h % 4)
-                query = queries[h // 4][r * new : (r + 1) * new, place_at : place_at + HEAD_DIM]
-                scores = lax.dot_general(
-                    query, key, (((1,), (1,)), ((), ())), preferred_element_type=f32
-                )
-                scores = jnp.where(allowed, scores * HEAD_DIM ** (-0.5), -jnp.inf)
-                highest = jnp.max(scores, axis=-1, keepdims=True)
-                exponent = jnp.exp(scores - highest)
-                weights = (exponent / jnp.sum(exponent, axis=-1, keepdims=True)).astype(bf16)
-                pieces.append(jnp.dot(weights, value, preferred_element_type=f32))
+                at = HEAD_DIM * (h % 4)
+                pair.append(queries[h // 4][r * new : (r + 1) * new, at : at + HEAD_DIM])
+            scores = lax.dot_general(
+                jnp.concatenate(pair, axis=0), key, (((1,), (1,)), ((), ())),
+                preferred_element_type=f32,
+            )
+            scores = scores * scale + bias
+            exponent = jnp.exp2(scores - jnp.max(scores, axis=-1, keepdims=True))
+            bottom = jnp.sum(exponent, axis=-1, keepdims=True)
+            mixed = jnp.dot(exponent.astype(bf16), value, preferred_element_type=f32) / bottom
+            pieces += [mixed[:new], mixed[new:]]
         attended[r * new : (r + 1) * new, :] = jnp.concatenate(pieces, axis=1).astype(bf16)
     term = jnp.dot(attended[...], w_out[...], preferred_element_type=f32)
 
@@ -157,9 +162,13 @@
         post[...] = norm_value(rounded.astype(f32), gain[1:2, :])
 
 
-def mlp_kernel(rows, own, other, out, total):
+def mlp_kernel(own, other, *refs):
+    total = refs[-1]
+    inputs = refs[: (len(refs) - 1) // 2]
+    outputs = refs[(len(refs) - 1) // 2 : -1]
     step = pl.program_id(0)
-    values = rows[...]
+    flat = inputs[0].shape[0]
+    values = jnp.concatenate([rows[...] for rows in inputs], axis=0)
     term = None
     for weights in (own, other):
         gate = jnp.dot(values, weights[0], preferred_element_type=f32)
@@ -180,50 +189,70 @@
 
     @pl.when(step == pl.num_programs(0) - 1)
     def _():
-        out[...] = total[...].astype(bf16)
-
-
-def pack_kernel(rank, source, target, sems):
-    copies = [
-        pltpu.make_async_copy(source.at[i], target.at[rank[i]], sems.at[i])
-        for i in range(source.shape[0])
-    ]
+        for i, out in enumerate(outputs):
+            out[...] = total[i * flat : (i + 1) * flat].astype(bf16)
+
+
+def run_copies(copies):
     for copy in copies:
         copy.start()
     for copy in copies:
         copy.wait()
 
 
-def unpack_kernel(columns, rows, source, *rest):
-    target, sems = rest[-2], rest[-1]
-    width = source.shape[-1]
-    copies = [
-        pltpu.make_async_copy(
-            source.at[rows[i]], target.at[i, :, pl.ds(columns, width)], sems.at[i]
-        )
-        for i in range(source.shape[0])
-    ]
-    for copy in copies:
-        copy.start()
-    for copy in copies:
-        copy.wait()
-
-
-def call(kernel, prefetched, grid, in_specs, out_specs, out_shape, scratch, operands, cost=None, aliases={}):
+def pack_kernel(picked, source, *rest):
+    targets, sems = rest[:-1], rest[-1]
+    share = targets[0].shape[0]
+    run_copies(
+        [
+            pltpu.make_async_copy(
+                source.at[picked[s * share + k]], target.at[k], sems.at[s * share + k]
+            )
+            for s, target in enumerate(targets)
+            for k in range(share)
+        ]
+    )
+
+
+def unpack_kernel(columns, count, spots, *refs):
+    sources, target, sems = refs[:count], refs[-2], refs[-1]
+    share, _, width = sources[0].shape
+    run_copies(
+        [
+            pltpu.make_async_copy(
+                source.at[k],
+                target.at[spots[s * share + k], :, pl.ds(columns, width)],
+                sems.at[s * share + k],
+            )
+            for s, source in enumerate(sources)
+            for k in range(share)
+        ]
+    )
+
+
+def call(
+    kernel, prefetched, grid, in_specs, out_specs, out_shape, scratch, operands,
+    flops=0, moved=6 << 20, aliases={}, after=(),
+):
+    begin = len(prefetched) + len(operands)
+
+    def ordered(*refs):
+        kernel(*refs[:begin], *refs[begin + len(after) :])
+
     return pl.pallas_call(
-        kernel,
+        ordered,
         out_shape=out_shape,
         grid_spec=pltpu.PrefetchScalarGridSpec(
             num_scalar_prefetch=len(prefetched),
             grid=grid,
-            in_specs=in_specs,
+            in_specs=list(in_specs) + [pl.BlockSpec(memory_space=pl.ANY)] * len(after),
             out_specs=out_specs,
             scratch_shapes=scratch,
         ),
         compiler_params=pltpu.CompilerParams(vmem_limit_bytes=VMEM),
-        cost_estimate=cost,
+        cost_estimate=pl.CostEstimate(flops=flops, bytes_accessed=moved, transcendentals=0),
         input_output_aliases=aliases,
-    )(*prefetched, *operands)
+    )(*prefetched, *operands, *after)
 
 
 def shape(dims, dtype=bf16):
@@ -283,7 +312,8 @@
         [shape(context_shape), shape(tokens.shape), shape(table, f32), shape(table, f32)],
         [],
         (tokens, norm_gains, freq, w_qkv, cached),
-        pl.CostEstimate(flops=2 * flat * width * key_width, bytes_accessed=8 << 20, transcendentals=0),
+        2 * flat * width * key_width,
+        8 << 20,
     )
     keys_moved = lax.all_to_all(keys, "tensor", split_axis=0, concat_axis=0, tiled=True)
     values = call(
@@ -299,7 +329,8 @@
         shape(context_shape),
         [],
         (normed, w_qkv, cached),
-        pl.CostEstimate(flops=2 * flat * width * key_width, bytes_accessed=8 << 20, transcendentals=0),
+        2 * flat * width * key_width,
+        8 << 20,
     )
     values_moved = lax.all_to_all(values, "tensor", split_axis=0, concat_axis=0, tiled=True)
 
@@ -322,36 +353,29 @@
         [shape((flat, width))] * 2,
         [pltpu.VMEM((flat, width), f32), pltpu.VMEM((flat, 2 * GROUP), bf16)],
         (normed, cosine, sine, w_qkv, keys, values, w_out, tokens, norm_gains),
-        pl.CostEstimate(flops=12 * flat * width * width, bytes_accessed=16 << 20, transcendentals=0),
+        12 * flat * width * width,
+        16 << 20,
     )
 
     units = mlp_weights.shape[2]
     chunk = 256 if units % 256 == 0 else units
 
-    def mlp(rows):
+    def mlp(pieces, after):
+        count = len(pieces)
+        weight_spec = pl.BlockSpec((3, width, chunk), lambda c: (0, 0, c))
         return call(
             mlp_kernel,
             (),
             (units // chunk,),
-            [
-                whole((flat, width)),
-                pl.BlockSpec((3, width, chunk), lambda c: (0, 0, c)),
-                pl.BlockSpec((3, width, chunk), lambda c: (0, 0, c)),
-            ],
-            whole((flat, width)),
-            shape((flat, width)),
-            [pltpu.VMEM((flat, width), f32)],
-            (rows, mlp_weights, other_weights),
-            pl.CostEstimate(flops=12 * flat * width * units, bytes_accessed=12 * width * units, transcendentals=0),
+            [weight_spec] * 2 + [whole((flat, width))] * count,
+            [whole((flat, width))] * count,
+            [shape((flat, width))] * count,
+            [pltpu.VMEM((count * flat, width), f32)],
+            (mlp_weights, other_weights, *pieces),
+            12 * count * flat * width * units,
+            12 * width * units,
+            after=after,
         )
-
-    partners = [
-        [(t, t ^ (2 * s)) for t in range(tensor_size)] for s in range(1, tensor_size // 2)
-    ]
-    arrivals = [lax.ppermute(post, "tensor", pairs) for pairs in partners]
-    partials = [mlp(post)]
-    for pairs, rows in zip(partners, arrivals):
-        partials.append(lax.ppermute(mlp(rows), "tensor", pairs))
 
     every = request_order.shape[0]
     indices = jnp.arange(every, dtype=jnp.int32)
@@ -361,42 +385,69 @@
     count_of = jnp.sum(
         jnp.where(request_order[:, None] == indices[None, :], new_lengths[None, :], 0), axis=1
     )
+    ordinal = jnp.arange(group_reqs, dtype=jnp.int32)
+
+    def inverse(keys_of):
+        position = jnp.sum((keys_of[None, :] < keys_of[:, None]).astype(jnp.int32), axis=1)
+        return jnp.sum(
+            jnp.where(position[None, :] == ordinal[:, None], ordinal[None, :], 0), axis=1
+        )
+
     own_slots = lax.dynamic_slice_in_dim(slot_of, group_index * group_reqs, group_reqs)
-    rank = jnp.sum((own_slots[None, :] < own_slots[:, None]).astype(jnp.int32), axis=1)
-    slot_ids = group_index * group_reqs + jnp.arange(group_reqs, dtype=jnp.int32)
+    goal = lax.rem(own_slots // group_reqs - group_index + group_total, group_total)
+    picked = inverse(goal * group_reqs + lax.rem(own_slots, group_reqs))
+    slot_ids = group_index * group_reqs + ordinal
     owners = jnp.sum(
         jnp.where(slot_of[None, :] == slot_ids[:, None], indices[None, :] // group_reqs, 0), axis=1
     )
-    per_group = group_reqs // group_total
-    ordinal = jnp.arange(group_reqs, dtype=jnp.int32)
-    same_owner = (owners[:, None] == owners[None, :]) & (ordinal[None, :] < ordinal[:, None])
-    source_rows = owners * per_group + jnp.sum(same_owner.astype(jnp.int32), axis=1)
-
-    half_shape = (group_reqs, depth, key_width)
+    origin = lax.rem(group_index - owners + group_total, group_total)
+    spots = inverse(origin * group_reqs + ordinal)
+
+    share = group_reqs // group_total
+    piece = (share, depth, key_width)
     anywhere = pl.BlockSpec(memory_space=pl.ANY)
     sems = [pltpu.SemaphoreType.DMA((group_reqs,))]
-
-    def across(moved):
-        packed = call(
-            pack_kernel, (rank,), (1,), [anywhere], anywhere, shape(half_shape), sems,
-            (moved.reshape(half_shape),),
-            pl.CostEstimate(flops=0, bytes_accessed=6 << 20, transcendentals=0),
+    shifts = [
+        [(g, (g + s) % group_total) for g in range(group_total)] for s in range(1, group_total)
+    ]
+
+    def pack(moved, after):
+        return call(
+            pack_kernel, (picked,), (1,), [anywhere], [anywhere] * group_total,
+            [shape(piece)] * group_total, sems, (moved.reshape(group_reqs, depth, key_width),),
+            after=after,
         )
-        return lax.all_to_all(packed, "dp", split_axis=0, concat_axis=0, tiled=True)
-
-    keys_arrived = across(keys_moved)
-    values_arrived = across(values_moved)
-    full_shape = shape((group_reqs, depth, 2 * key_width))
-    kv_half = call(
-        functools.partial(unpack_kernel, 0), (source_rows,), (1,), [anywhere], anywhere,
-        full_shape, sems, (keys_arrived,),
-        pl.CostEstimate(flops=0, bytes_accessed=6 << 20, transcendentals=0),
-    )
-    kv_decode = call(
-        functools.partial(unpack_kernel, key_width), (source_rows,), (1,), [anywhere, anywhere],
-        anywhere, full_shape, sems, (values_arrived, kv_half),
-        pl.CostEstimate(flops=0, bytes_accessed=6 << 20, transcendentals=0), {2: 0},
-    )
+
+    def across(packed):
+        return [packed[0]] + [
+            lax.ppermute(rows, "dp", pairs) for rows, pairs in zip(packed[1:], shifts)
+        ]
+
+    def unpack(columns, arrived, target, after):
+        return call(
+            functools.partial(unpack_kernel, columns, group_total), (spots,), (1,),
+            [anywhere] * (group_total + len(target)), anywhere,
+            shape((group_reqs, depth, 2 * key_width)), sems, (*arrived, *target),
+            aliases={1 + group_total: 0} if target else {}, after=after,
+        )
+
+    partners = [
+        [(t, t ^ (2 * s)) for t in range(tensor_size)] for s in range(1, tensor_size // 2)
+    ]
+    gathered = [lax.ppermute(post, "tensor", pairs) for pairs in partners]
+    keys_packed = pack(keys_moved, (post,))
+    keys_arrived = across(keys_packed)
+    partials = list(mlp([post], (keys_packed[0],)))
+    values_packed = pack(values_moved, (partials[0],))
+    values_arrived = across(values_packed)
+    latest = values_packed[0]
+    batches = [range(0, 2)] + [range(s, min(s + 2, len(partners))) for s in range(2, len(partners), 2)]
+    for batch in batches:
+        results = mlp([gathered[s] for s in batch], (latest,))
+        latest = results[0]
+        partials += [lax.ppermute(rows, "tensor", partners[s]) for s, rows in zip(batch, results)]
+    kv_half = unpack(0, keys_arrived, (), (latest,))
+    kv_decode = unpack(key_width, values_arrived, (kv_half,), ())
 
     own_counts = lax.dynamic_slice_in_dim(count_of, device * reqs, reqs)
     live = (jnp.arange(new, dtype=jnp.int32)[None, :] < own_counts[:, None]).reshape(flat, 1)

time: 215 us -> 302 us (1.40)
  Pallas kernels: 62.9 us -> 251 us
  waiting for transfers between devices: 102 us -> 15.9 us
  local copies, waits for them, and re-layouts: 18.2 us -> 2.5 us
    pallas_call x11 -> x10, Pallas kernels: 62.9 us -> 251 us  [call(): pl.pallas_call(ordered, out_shape=out_shape, grid_spec=pltpu.PrefetchScal...]
    ppermute x6 -> x12, waiting for transfers between devices: 38.5 us -> 0.03 us  [the longest x6 0.02 us: across(): lax.ppermute(rows, 'dp', pairs)]
    all_to_all x2 -> x0, waiting for transfers between devices: 32.2 us -> none  [across(): return lax.all_to_all(packed, 'dp', split_axis=0, concat_axis=0, tiled=True)]
    all_to_all x1, waiting for transfers between devices: 16.7 us -> 0.01 us  [local(): lax.all_to_all(values, 'tensor', split_axis=0, concat_axis=0, tiled=True)]
    unnamed x52 -> x24, local copies, waits for them, and re-layouts: 18.1 us -> 2.43 us
    ppermute x6 -> x12, starting transfers between devices: 7.09 us -> 17.2 us  [the longest x6 9.48 us: across(): lax.ppermute(rows, 'dp', pairs)]
    all_to_all x2 -> x0, starting transfers between devices: 9.09 us -> none  [across(): return lax.all_to_all(packed, 'dp', split_axis=0, concat_axis=0, tiled=True)]
  transfers between devices with their start and end apart: 11 -> 15, of which waited for: 6 -> 1; matrix products, arithmetic and copies ran while one was open for 0% -> 1% of each run, Pallas kernels for 27% -> 83%
where the time goes in v2:
time: 302 us
  Pallas kernels  251 us (83%)
  starting transfers between devices  26.2 us (9%)
  waiting for transfers between devices  15.9 us (5%)
  other arithmetic  4.81 us (2%)
    pallas_call x10, Pallas kernels, call(): pl.pallas_call(ordered, out_shape=out_shape, grid_spec=pltpu.PrefetchScal...  251 us
    all_to_all x1, waiting for transfers between devices, local(): lax.all_to_all(keys, 'tensor', split_axis=0, concat_axis=0, tiled=True)  15.8 us
    ppermute x6, starting transfers between devices, across(): lax.ppermute(rows, 'dp', pairs)  9.48 us
  transfers between devices with their start and end apart: 15, of which 1 were waited for; matrix products, arithmetic and copies ran while one was open for 1% of the time, Pallas kernels for 83%

profile of v2, /device:TPU:0, one launch (start us, length us, event | category | flops | bytes accessed | tf_op | source)
XLA Modules:
  0.0 301.6 jit_solution(2349938271018699523)
XLA Ops:
  0.6 0.5 collective-permute-start
  1.1 6.4 %shard_map.122 = (bf16[8,2,64,768]{3,2,1,0:T(8,128)(2,1)}, bf16[2,128,1536]{2,1,0:T(8,128)(2,1)}, f32[2,128,384]{2,1,0:T(8,128)}, f32[2,128,384]{2,1,0:T(8,128)}) custom-call(s32[64]{0:T(128)} %refs_0_.8, s32[64]{0:T(128)} %refs_1_.4, s32[64]{0:T(128)} %refs_1_.5, s32[1]{0:T(128)} %bitcast.1.refs_3_.refs_2_, bf16[2,128,1536]{2,1,0:T(8,128)(2,1)} %refs_10_.1, ...), custom_call_target="tpu_custom_call" | custom-call | flops 603979776 | bytes 8388608 | tf_op jit(solution)/shard_map/pallas_call | solution.py:242
  7.6 4.8 %all-to-all-start = ((bf16[8,2,64,768]{3,2,1,0:T(8,128)(2,1)}), bf16[8,2,64,768]{3,2,1,0:T(8,128)(2,1)S(1)}, u32[]{:S(2)}, u32[]{:S(2)}) async-start(bf16[8,2,64,768]{3,2,1,0:T(8,128)(2,1)} %get-tuple-element.21.refs_7_), calls=%async_computation | async-start | bytes 3145728 | tf_op jit(solution)/shard_map/all_to_all | solution.py:318
  12.4 5.2 %shard_map.123.refs_8_ = bf16[8,2,64,768]{3,2,1,0:T(8,128)(2,1)} custom-call(s32[64]{0:T(128)} %refs_0_.8, s32[64]{0:T(128)} %refs_1_.4, s32[64]{0:T(128)} %refs_1_.5, s32[1]{0:T(128)} %bitcast.1.refs_3_.refs_2_, bf16[2,128,1536]{2,1,0:T(8,128)(2,1)} %get-tuple-element.18.refs_4_.refs_3_, bf16[1536,3072]{1,0:T(8,128)(2,1)} %refs_6_.4, ...), custom_call_target="tpu_custom_call" | custom-call | flops 603979776 | bytes 8388608 | tf_op jit(solution)/shard_map/pallas_call | solution.py:242
  17.6 15.8 %all-to-all-done = bf16[8,2,64,768]{3,2,1,0:T(8,128)(2,1)S(1)} async-done(((bf16[8,2,64,768]{3,2,1,0:T(8,128)(2,1)}), bf16[8,2,64,768]{3,2,1,0:T(8,128)(2,1)S(1)}, u32[]{:S(2)}, u32[]{:S(2)}) %all-to-all-start) | async-done | bytes 1572896 | tf_op jit(solution)/shard_map/all_to_all | solution.py:318
  33.4 1.2 copy-done.2
  34.7 3.6 %all-to-all-start.1 = ((bf16[8,2,64,768]{3,2,1,0:T(8,128)(2,1)}), bf16[8,2,64,768]{3,2,1,0:T(8,128)(2,1)S(1)}, u32[]{:S(2)}, u32[]{:S(2)}) async-start(bf16[8,2,64,768]{3,2,1,0:T(8,128)(2,1)} %shard_map.123.refs_8_), calls=%async_computation.1 | async-start | bytes 3145728 | tf_op jit(solution)/shard_map/all_to_all | solution.py:335
  38.2 0.0 copy-start.7
  38.3 0.0 copy-start.8
  38.3 0.0 copy-start.9
  38.3 17.9 %shard_map.124 = (bf16[256,1536]{1,0:T(8,128)(2,1)}, bf16[256,1536]{1,0:T(8,128)(2,1)}) custom-call(s32[64]{0:T(128)} %refs_0_.8, s32[64]{0:T(128)} %refs_1_.5, s32[1]{0:T(128)} %bitcast.1.refs_3_.refs_2_, bf16[2,128,1536]{2,1,0:T(8,128)(2,1)} %get-tuple-element.18.refs_4_.refs_3_, f32[2,128,384]{2,1,0:T(8,128)} %get-tuple-element.19.refs_4_, ...), custom_call_target="tpu_custom_call" | custom-call | flops 7247757312 | bytes 16777216 | tf_op jit(solution)/shard_map/pallas_call | solution.py:242
  56.2 2.8 collective-permute-start.5
  59.0 0.5 collective-permute-start.2
  59.5 0.2 collective-permute-start.1
  59.7 0.0 copy-done.7
  59.7 0.0 copy-done.8
  59.7 0.0 copy-done.9
  59.7 0.2 select_reduce_fusion.1
  59.9 0.2 select_reduce_fusion.3
  60.1 0.1 fusion.2
  60.2 0.2 convert_reduce_fusion.1
  60.3 0.6 select_reduce_fusion.4.refs_0_
  61.0 49.6 %shard_map.125 = (bf16[4,64,768]{2,1,0:T(8,128)(2,1)}, bf16[4,64,768]{2,1,0:T(8,128)(2,1)}, bf16[4,64,768]{2,1,0:T(8,128)(2,1)}, bf16[4,64,768]{2,1,0:T(8,128)(2,1)}) custom-call(s32[16]{0:T(128)} %select_reduce_fusion.4.refs_0_, bf16[16,64,768]{2,1,0:T(8,128)(2,1)} %bitcast.7, bf16[256,1536]{1,0:T(8,128)(2,1)} %get-tuple-element.23.refs_2_), custom_call_target="tpu_custom_call" | custom-call | bytes 6291456 | tf_op jit(solution)/shard_map/pallas_call | solution.py:242
  110.5 1.6 collective-permute-start.10
  112.2 0.0 collective-permute-done.refs_1_
  112.2 2.6 collective-permute-start.11
  114.7 6.8 %shard_map.126.refs_2_ = bf16[256,1536]{1,0:T(8,128)(2,1)} custom-call(bf16[3,1536,512]{2,1,0:T(8,128)(2,1)} %refs_0_.11, bf16[3,1536,512]{2,1,0:T(8,128)(2,1)} %collective-permute-done.refs_1_, bf16[256,1536]{1,0:T(8,128)(2,1)} %get-tuple-element.23.refs_2_, bf16[4,64,768]{2,1,0:T(8,128)(2,1)} %get-tuple-element.24.refs_3_.refs_1_), custom_call_target="tpu_custom_call" | custom-call | flops 2415919104 | bytes 9437184 | tf_op jit(solution)/shard_map/pallas_call | solution.py:242
  121.6 0.0 all-to-all-done.1
  121.6 1.1 copy-done.1
  122.7 49.6 %shard_map.127 = (bf16[4,64,768]{2,1,0:T(8,128)(2,1)}, bf16[4,64,768]{2,1,0:T(8,128)(2,1)}, bf16[4,64,768]{2,1,0:T(8,128)(2,1)}, bf16[4,64,768]{2,1,0:T(8,128)(2,1)}) custom-call(s32[16]{0:T(128)} %select_reduce_fusion.4.refs_0_, bf16[16,64,768]{2,1,0:T(8,128)(2,1)} %bitcast.6, bf16[256,1536]{1,0:T(8,128)(2,1)} %shard_map.126.refs_2_), custom_call_target="tpu_custom_call" | custom-call | bytes 6291456 | tf_op jit(solution)/shard_map/pallas_call | solution.py:242
  172.3 0.0 collective-permute-done.2.refs_3_
  172.3 0.0 copy-start.10
  172.3 0.0 copy-done.11
  172.3 1.4 collective-permute-start.12
  173.7 0.0 collective-permute-done.1.refs_2_
  173.7 0.7 collective-permute-start.7
  174.4 0.0 copy-done.10
  174.4 9.9 %shard_map.128 = (bf16[256,1536]{1,0:T(8,128)(2,1)}, bf16[256,1536]{1,0:T(8,128)(2,1)}) custom-call(bf16[3,1536,512]{2,1,0:T(8,128)(2,1)} %refs_0_.11, bf16[3,1536,512]{2,1,0:T(8,128)(2,1)} %collective-permute-done.refs_1_, bf16[256,1536]{1,0:T(8,128)(2,1)} %collective-permute-done.1.refs_2_, bf16[256,1536]{1,0:T(8,128)(2,1)} %copy-done.10, ...), custom_call_target="tpu_custom_call" | custom-call | flops 4831838208 | bytes 9437184 | tf_op jit(solution)/shard_map/pallas_call | solution.py:242
  184.3 0.0 collective-permute-done.5.refs_2_
  184.3 2.0 collective-permute-start.4
  186.3 0.0 copy-done.5
  186.3 6.9 %shard_map.129.refs_5_ = bf16[256,1536]{1,0:T(8,128)(2,1)} custom-call(bf16[3,1536,512]{2,1,0:T(8,128)(2,1)} %refs_0_.11, bf16[3,1536,512]{2,1,0:T(8,128)(2,1)} %collective-permute-done.refs_1_, bf16[256,1536]{1,0:T(8,128)(2,1)} %copy-done.5, bf16[256,1536]{1,0:T(8,128)(2,1)} %get-tuple-element.26.refs_3_), custom_call_target="tpu_custom_call" | custom-call | flops 2415919104 | bytes 9437184 | tf_op jit(solution)/shard_map/pallas_call | solution.py:242
  193.1 0.0 collective-permute-done.10.refs_2_
  193.1 1.7 collective-permute-start.6
  194.8 0.0 collective-permute-done.11.refs_3_
  194.8 0.0 copy-done.4
  194.9 0.6 collective-permute-start.3
  195.4 0.0 collective-permute-done.12.refs_4_
  195.4 0.3 collective-permute-start.8
  195.8 0.0 collective-permute-done.7.refs_2_
  195.8 2.9 collective-permute-start.9
  198.6 0.2 convert_reduce_fusion
  198.8 0.1 dynamic_slice.6
  198.9 0.7 select_reduce_fusion.2.refs_0_
  199.6 0.1 compare_bitcast_fusion
  199.7 0.0 copy-done.6
  199.7 49.6 %shard_map.130.refs_5_ = bf16[16,64,1536]{2,1,0:T(8,128)(2,1)} custom-call(s32[16]{0:T(128)} %select_reduce_fusion.2.refs_0_, bf16[4,64,768]{2,1,0:T(8,128)(2,1)} %get-tuple-element.24.refs_3_.refs_1_, bf16[4,64,768]{2,1,0:T(8,128)(2,1)} %collective-permute-done.10.refs_2_, bf16[4,64,768]{2,1,0:T(8,128)(2,1)} %collective-permute-done.11.refs_3_, ...), custom_call_target="tpu_custom_call" | custom-call | bytes 6291456 | tf_op jit(solution)/shard_map/pallas_call | solution.py:242
  249.3 0.0 collective-permute-done.8.refs_3_
  249.3 0.0 collective-permute-done.9.refs_4_
  249.3 49.7 %shard_map.131 = bf16[16,64,1536]{2,1,0:T(8,128)(2,1)} custom-call(s32[16]{0:T(128)} %select_reduce_fusion.2.refs_0_, bf16[4,64,768]{2,1,0:T(8,128)(2,1)} %get-tuple-element.25.refs_4_.refs_1_, bf16[4,64,768]{2,1,0:T(8,128)(2,1)} %collective-permute-done.7.refs_2_, ...), custom_call_target="tpu_custom_call", output_to_operand_aliasing={{}: (5, {})} | custom-call | bytes 6291456 | tf_op jit(solution)/shard_map/pallas_call | solution.py:242
  299.0 0.0 collective-permute-done.4
  299.0 0.0 collective-permute-done.6
  299.0 0.0 collective-permute-done.3
  299.0 2.6 select_convert_fusion
  (12 shorter events, 0.0 us)
Async XLA Ops:
  0.6 111.6 %collective-permute-start = (bf16[3,1536,512]{2,1,0:T(8,128)(2,1)}, bf16[3,1536,512]{2,1,0:T(8,128)(2,1)}, u32[]{:S(2)}, u32[]{:S(2)}) collective-permute-start(bf16[3,1536,512]{2,1,0:T(8,128)(2,1)} %refs_0_.11), channel_id=1, source_target_pairs={{0,1},{1,0},{2,3},{3,2},{4,5},{5,4},{6,7},{7,6},{8,9},{9,8},{10,11... | collective-permute-start | bytes 14155784 | tf_op jit(solution)/shard_map/ppermute | solution.py:293
  7.6 25.9 %all-to-all-start = ((bf16[8,2,64,768]{3,2,1,0:T(8,128)(2,1)}), bf16[8,2,64,768]{3,2,1,0:T(8,128)(2,1)S(1)}, u32[]{:S(2)}, u32[]{:S(2)}) async-start(bf16[8,2,64,768]{3,2,1,0:T(8,128)(2,1)} %get-tuple-element.21.refs_7_), calls=%async_computation | async-start | bytes 3145728 | tf_op jit(solution)/shard_map/all_to_all | solution.py:318
  33.4 1.2 copy-start.2
  34.7 86.9 %all-to-all-start.1 = ((bf16[8,2,64,768]{3,2,1,0:T(8,128)(2,1)}), bf16[8,2,64,768]{3,2,1,0:T(8,128)(2,1)S(1)}, u32[]{:S(2)}, u32[]{:S(2)}) async-start(bf16[8,2,64,768]{3,2,1,0:T(8,128)(2,1)} %shard_map.123.refs_8_), calls=%async_computation.1 | async-start | bytes 3145728 | tf_op jit(solution)/shard_map/all_to_all | solution.py:335
  38.2 21.4 %copy-start.7 = (s32[64]{0:T(128)S(1)}, s32[64]{0:T(128)}, u32[]{:S(2)}) copy-start(s32[64]{0:T(128)} %refs_0_.8) | copy-start | bytes 772
  38.3 21.4 %copy-start.8 = (s32[64]{0:T(128)S(1)}, s32[64]{0:T(128)}, u32[]{:S(2)}) copy-start(s32[64]{0:T(128)} %refs_1_.4) | copy-start | bytes 772
  38.3 21.4 %copy-start.9 = (s32[64]{0:T(128)S(1)}, s32[64]{0:T(128)}, u32[]{:S(2)}) copy-start(s32[64]{0:T(128)} %param.20) | copy-start | bytes 772
  56.2 128.1 %collective-permute-start.5 = (bf16[256,1536]{1,0:T(8,128)(2,1)}, bf16[256,1536]{1,0:T(8,128)(2,1)S(1)}, u32[]{:S(2)}, u32[]{:S(2)}) collective-permute-start(bf16[256,1536]{1,0:T(8,128)(2,1)} %get-tuple-element.23.refs_2_), channel_id=1, source_target_pairs={{0,6},{1,7},{2,4},{3,5},{4,2},{5,3},{6,0},{7,1},{8,14},{9,15},{10,... | collective-permute-start | bytes 2359304 | tf_op jit(solution)/shard_map/ppermute | solution.py:437
  59.0 113.3 %collective-permute-start.2 = (bf16[256,1536]{1,0:T(8,128)(2,1)}, bf16[256,1536]{1,0:T(8,128)(2,1)S(1)}, u32[]{:S(2)}, u32[]{:S(2)}) collective-permute-start(bf16[256,1536]{1,0:T(8,128)(2,1)} %get-tuple-element.23.refs_2_), channel_id=1, source_target_pairs={{0,4},{1,5},{2,6},{3,7},{4,0},{5,1},{6,2},{7,3},{8,12},{9,13},{10,... | collective-permute-start | bytes 2359304 | tf_op jit(solution)/shard_map/ppermute | solution.py:437
  59.5 114.2 %collective-permute-start.1 = (bf16[256,1536]{1,0:T(8,128)(2,1)}, bf16[256,1536]{1,0:T(8,128)(2,1)}, u32[]{:S(2)}, u32[]{:S(2)}) collective-permute-start(bf16[256,1536]{1,0:T(8,128)(2,1)} %get-tuple-element.23.refs_2_), channel_id=1, source_target_pairs={{0,2},{1,3},{2,0},{3,1},{4,6},{5,7},{6,4},{7,5},{8,10},{9,11},{10,... | collective-permute-start | bytes 2359304 | tf_op jit(solution)/shard_map/ppermute | solution.py:437
  110.5 82.6 %collective-permute-start.10 = (bf16[4,64,768]{2,1,0:T(8,128)(2,1)}, bf16[4,64,768]{2,1,0:T(8,128)(2,1)}, u32[]{:S(2)}, u32[]{:S(2)}) collective-permute-start(bf16[4,64,768]{2,1,0:T(8,128)(2,1)} %get-tuple-element.31), channel_id=1, source_target_pairs={{0,8},{8,16},{16,24},{24,0},{1,9},{9,17},{17,25},{25,1},{2,10},{10... | collective-permute-start | bytes 1179656 | tf_op jit(solution)/shard_map/ppermute | solution.py:423
  112.2 82.7 %collective-permute-start.11 = (bf16[4,64,768]{2,1,0:T(8,128)(2,1)}, bf16[4,64,768]{2,1,0:T(8,128)(2,1)}, u32[]{:S(2)}, u32[]{:S(2)}) collective-permute-start(bf16[4,64,768]{2,1,0:T(8,128)(2,1)} %get-tuple-element.32), channel_id=1, source_target_pairs={{0,16},{8,24},{16,0},{24,8},{1,17},{9,25},{17,1},{25,9},{2,18},{10... | collective-permute-start | bytes 1179656 | tf_op jit(solution)/shard_map/ppermute | solution.py:423
  121.6 1.1 copy-start.1
  121.6 50.7 %copy-start.11 = (bf16[4,64,768]{2,1,0:T(8,128)(2,1)S(1)}, bf16[4,64,768]{2,1,0:T(8,128)(2,1)}, u32[]{:S(2)}) copy-start(bf16[4,64,768]{2,1,0:T(8,128)(2,1)} %get-tuple-element.33) | copy-start | bytes 1179652
  172.3 2.1 copy-start.10
  172.3 23.1 %collective-permute-start.12 = (bf16[4,64,768]{2,1,0:T(8,128)(2,1)S(1)}, bf16[4,64,768]{2,1,0:T(8,128)(2,1)S(1)}, u32[]{:S(2)}, u32[]{:S(2)}) collective-permute-start(bf16[4,64,768]{2,1,0:T(8,128)(2,1)S(1)} %copy-done.11), channel_id=1, source_target_pairs={{0,24},{8,0},{16,8},{24,16},{1,25},{9,1},{17,9},{25,17},{2,26},{10... | collective-permute-start | bytes 1179656 | tf_op jit(solution)/shard_map/ppermute | solution.py:423
  173.7 22.1 %collective-permute-start.7 = (bf16[4,64,768]{2,1,0:T(8,128)(2,1)}, bf16[4,64,768]{2,1,0:T(8,128)(2,1)}, u32[]{:S(2)}, u32[]{:S(2)}) collective-permute-start(bf16[4,64,768]{2,1,0:T(8,128)(2,1)} %get-tuple-element.28), channel_id=1, source_target_pairs={{0,8},{8,16},{16,24},{24,0},{1,9},{9,17},{17,25},{25,1},{2,10},{10... | collective-permute-start | bytes 1179656 | tf_op jit(solution)/shard_map/ppermute | solution.py:423
  184.3 2.0 copy-start.5
  184.3 114.7 %collective-permute-start.4 = (bf16[256,1536]{1,0:T(8,128)(2,1)}, bf16[256,1536]{1,0:T(8,128)(2,1)S(1)}, u32[]{:S(2)}, u32[]{:S(2)}) collective-permute-start(bf16[256,1536]{1,0:T(8,128)(2,1)} %get-tuple-element.27), channel_id=1, source_target_pairs={{0,4},{1,5},{2,6},{3,7},{4,0},{5,1},{6,2},{7,3},{8,12},{9,13},{10,... | collective-permute-start | bytes 2359304 | tf_op jit(solution)/shard_map/ppermute | solution.py:448
  186.3 8.6 %copy-start.4 = (bf16[256,1536]{1,0:T(8,128)(2,1)S(1)}, bf16[256,1536]{1,0:T(8,128)(2,1)}, u32[]{:S(2)}) copy-start(bf16[256,1536]{1,0:T(8,128)(2,1)} %get-tuple-element.26.refs_3_) | copy-start | bytes 2359300
  193.1 105.9 %collective-permute-start.6 = (bf16[256,1536]{1,0:T(8,128)(2,1)}, bf16[256,1536]{1,0:T(8,128)(2,1)S(1)}, u32[]{:S(2)}, u32[]{:S(2)}) collective-permute-start(bf16[256,1536]{1,0:T(8,128)(2,1)} %shard_map.129.refs_5_), channel_id=1, source_target_pairs={{0,6},{1,7},{2,4},{3,5},{4,2},{5,3},{6,0},{7,1},{8,14},{9,15},{10,... | collective-permute-start | bytes 2359304 | tf_op jit(solution)/shard_map/ppermute | solution.py:448
  194.9 104.2 %collective-permute-start.3 = (bf16[256,1536]{1,0:T(8,128)(2,1)S(1)}, bf16[256,1536]{1,0:T(8,128)(2,1)}, u32[]{:S(2)}, u32[]{:S(2)}) collective-permute-start(bf16[256,1536]{1,0:T(8,128)(2,1)S(1)} %copy-done.4), channel_id=1, source_target_pairs={{0,2},{1,3},{2,0},{3,1},{4,6},{5,7},{6,4},{7,5},{8,10},{9,11},{10,... | collective-permute-start | bytes 2359304 | tf_op jit(solution)/shard_map/ppermute | solution.py:448
  195.4 4.3 %copy-start.6 = (bf16[4,64,768]{2,1,0:T(8,128)(2,1)}, bf16[4,64,768]{2,1,0:T(8,128)(2,1)S(1)}, u32[]{:S(2)}) copy-start(bf16[4,64,768]{2,1,0:T(8,128)(2,1)S(1)} %collective-permute-done.12.refs_4_) | copy-start | bytes 1179652
  195.4 53.8 %collective-permute-start.8 = (bf16[4,64,768]{2,1,0:T(8,128)(2,1)}, bf16[4,64,768]{2,1,0:T(8,128)(2,1)}, u32[]{:S(2)}, u32[]{:S(2)}) collective-permute-start(bf16[4,64,768]{2,1,0:T(8,128)(2,1)} %get-tuple-element.29), channel_id=1, source_target_pairs={{0,16},{8,24},{16,0},{24,8},{1,17},{9,25},{17,1},{25,9},{2,18},{10... | collective-permute-start | bytes 1179656 | tf_op jit(solution)/shard_map/ppermute | solution.py:423
  195.8 53.5 %collective-permute-start.9 = (bf16[4,64,768]{2,1,0:T(8,128)(2,1)}, bf16[4,64,768]{2,1,0:T(8,128)(2,1)}, u32[]{:S(2)}, u32[]{:S(2)}) collective-permute-start(bf16[4,64,768]{2,1,0:T(8,128)(2,1)} %get-tuple-element.30), channel_id=1, source_target_pairs={{0,24},{8,0},{16,8},{24,16},{1,25},{9,1},{17,9},{25,17},{2,26},{10... | collective-permute-start | bytes 1179656 | tf_op jit(solution)/shard_map/ppermute | solution.py:423
  249.2 49.8 %copy-start = (bf16[256,1536]{1,0:T(8,128)(2,1)S(1)}, bf16[256,1536]{1,0:T(8,128)(2,1)}, u32[]{:S(2)}) copy-start(bf16[256,1536]{1,0:T(8,128)(2,1)} %shard_map.126.refs_2_) | copy-start | bytes 2359300
  249.3 49.8 %copy-start.3 = (bf16[256,1536]{1,0:T(8,128)(2,1)S(1)}, bf16[256,1536]{1,0:T(8,128)(2,1)}, u32[]{:S(2)}) copy-start(bf16[256,1536]{1,0:T(8,128)(2,1)} %get-tuple-element.22) | copy-start | bytes 2359300

commit v3 on v2

--- a/solution.py
+++ b/solution.py
@@ -90,27 +90,27 @@
         context[:, r] = merged.reshape(parts, depth, GROUP)
 
 
-def value_kernel(order, news, olds, dev, normed, weight, cached, context):
-    reqs, new, width = normed.shape
-    rows = normed[...].reshape(reqs * new, width)
-    projected = jnp.dot(rows, weight[...], preferred_element_type=f32).astype(bf16)
-    parts, _, depth, _ = context.shape
-    for r in range(reqs):
-        request = order[dev[0] * reqs + r]
-        merged = place(projected[r * new : (r + 1) * new], cached[r], news[request], olds[request])
-        context[:, r] = merged.reshape(parts, depth, GROUP)
-
-
 def attention_kernel(
-    order, olds, dev, normed, cosine, sine, weight, keys, values, w_out, tokens, gain,
-    residual, post, total, attended,
+    order, news, olds, dev, normed, cosine, sine, weight, w_value, keys, cached, tokens, gain, w_out,
+    values, residual, post, total, attended, out_weight, sems,
 ):
     step = pl.program_id(0)
     reqs, new, width = normed.shape
     parts, _, depth, _ = keys.shape
     ctx = parts * depth
     flat = reqs * new
+
+    def stream(g):
+        source = w_out.at[pl.ds(g * 2 * GROUP, 2 * GROUP)]
+        return pltpu.make_async_copy(source, out_weight.at[g], sems.at[g])
+
+    @pl.when(step == 0)
+    def _():
+        for g in range(out_weight.shape[0]):
+            stream(g).start()
+
     rows = normed[...].reshape(flat, width)
+    fresh = jnp.dot(rows, w_value[...], preferred_element_type=f32).astype(bf16)
     projected = jnp.dot(rows, weight[...], preferred_element_type=f32)
     cos_part = cosine[...].reshape(flat, GROUP)
     sin_part = sine[...].reshape(flat, GROUP)
@@ -122,9 +122,11 @@
     token = lax.broadcasted_iota(jnp.int32, (new, ctx), 0)
     scale = HEAD_DIM ** (-0.5) * math.log2(math.e)
     for r in range(reqs):
-        old = olds[order[dev[0] * reqs + r]]
+        request = order[dev[0] * reqs + r]
+        old = olds[request]
         key_rows = keys[:, r].reshape(ctx, GROUP)
-        value_rows = values[:, r].reshape(ctx, GROUP)
+        value_rows = place(fresh[r * new : (r + 1) * new], cached[r], news[request], old)
+        values[:, r] = value_rows.reshape(parts, depth, GROUP)
         mask = jnp.where(spot <= old + token, 0.0, -jnp.inf)
         bias = jnp.concatenate([mask, mask], axis=0)
         pieces = []
@@ -145,7 +147,8 @@
             mixed = jnp.dot(exponent.astype(bf16), value, preferred_element_type=f32) / bottom
             pieces += [mixed[:new], mixed[new:]]
         attended[r * new : (r + 1) * new, :] = jnp.concatenate(pieces, axis=1).astype(bf16)
-    term = jnp.dot(attended[...], w_out[...], preferred_element_type=f32)
+    stream(step).wait()
+    term = jnp.dot(attended[...], out_weight[step], preferred_element_type=f32)
 
     @pl.when(step == 0)
     def _():
@@ -316,46 +319,35 @@
         8 << 20,
     )
     keys_moved = lax.all_to_all(keys, "tensor", split_axis=0, concat_axis=0, tiled=True)
-    values = call(
-        value_kernel,
+    values, residual, post = call(
+        attention_kernel,
         scalars,
-        (groups,),
-        [
-            whole(tokens.shape),
-            pl.BlockSpec((width, GROUP), lambda g, *_: (0, (width + key_width) // GROUP + g)),
-            pl.BlockSpec((reqs, ctx, GROUP), lambda g, *_: (0, 0, groups + g)),
-        ],
-        context_spec,
-        shape(context_shape),
-        [],
-        (normed, w_qkv, cached),
-        2 * flat * width * key_width,
-        8 << 20,
-    )
-    values_moved = lax.all_to_all(values, "tensor", split_axis=0, concat_axis=0, tiled=True)
-
-    residual, post = call(
-        attention_kernel,
-        (request_order, cached_lengths, dev),
         (groups,),
         [
             whole(tokens.shape),
             whole(table),
             whole(table),
             pl.BlockSpec((width, 2 * GROUP), lambda g, *_: (0, g)),
+            pl.BlockSpec((width, GROUP), lambda g, *_: (0, (width + key_width) // GROUP + g)),
             context_spec,
-            context_spec,
-            pl.BlockSpec((2 * GROUP, width), lambda g, *_: (g, 0)),
+            pl.BlockSpec((reqs, ctx, GROUP), lambda g, *_: (0, 0, groups + g)),
             whole(tokens.shape),
             whole(norm_gains.shape),
+            pl.BlockSpec(memory_space=pl.ANY),
         ],
-        [whole((flat, width))] * 2,
-        [shape((flat, width))] * 2,
-        [pltpu.VMEM((flat, width), f32), pltpu.VMEM((flat, 2 * GROUP), bf16)],
-        (normed, cosine, sine, w_qkv, keys, values, w_out, tokens, norm_gains),
+        [context_spec, whole((flat, width)), whole((flat, width))],
+        [shape(context_shape), shape((flat, width)), shape((flat, width))],
+        [
+            pltpu.VMEM((flat, width), f32),
+            pltpu.VMEM((flat, 2 * GROUP), bf16),
+            pltpu.VMEM((groups, 2 * GROUP, width), bf16),
+            pltpu.SemaphoreType.DMA((groups,)),
+        ],
+        (normed, cosine, sine, w_qkv, w_qkv, keys, cached, tokens, norm_gains, w_out),
         12 * flat * width * width,
         16 << 20,
     )
+    values_moved = lax.all_to_all(values, "tensor", split_axis=0, concat_axis=0, tiled=True)
 
     units = mlp_weights.shape[2]
     chunk = 256 if units % 256 == 0 else units
@@ -413,7 +405,8 @@
 
     def pack(moved, after):
         return call(
-            pack_kernel, (picked,), (1,), [anywhere], [anywhere] * group_total,
+            pack_kernel, (picked,), (1,), [whole((group_reqs, depth, key_width))],
+            [anywhere] * group_total,
             [shape(piece)] * group_total, sems, (moved.reshape(group_reqs, depth, key_width),),
             after=after,
         )
@@ -426,7 +419,7 @@
     def unpack(columns, arrived, target, after):
         return call(
             functools.partial(unpack_kernel, columns, group_total), (spots,), (1,),
-            [anywhere] * (group_total + len(target)), anywhere,
+            [whole(piece)] * group_total + [anywhere] * len(target), anywhere,
             shape((group_reqs, depth, 2 * key_width)), sems, (*arrived, *target),
             aliases={1 + group_total: 0} if target else {}, after=after,
         )

time: 302 us -> 153 us (0.51)
  Pallas kernels: 251 us -> 61.6 us
  waiting for transfers between devices: 15.9 us -> 55 us
    pallas_call x10 -> x9, Pallas kernels: 251 us -> 61.6 us  [call(): pl.pallas_call(ordered, out_shape=out_shape, grid_spec=pltpu.PrefetchScal...]
    ppermute x3, waiting for transfers between devices: 0.01 us -> 27.8 us  [local(): gathered = [lax.ppermute(post, 'tensor', pairs) for pairs in partners]]
    all_to_all x1, waiting for transfers between devices: 15.8 us -> 2.67 us  [local(): lax.all_to_all(keys, 'tensor', split_axis=0, concat_axis=0, tiled=True)]
    ppermute x6, waiting for transfers between devices: 0.02 us -> 12.4 us  [across(): lax.ppermute(rows, 'dp', pairs)]
    ppermute x3, waiting for transfers between devices: 0.01 us -> 9.9 us  [local(): lax.ppermute(rows, 'tensor', partners[s])]
  transfers between devices with their start and end apart: 15 -> 15, of which waited for: 1 -> 6; matrix products, arithmetic and copies ran while one was open for 1% -> 1% of each run, Pallas kernels for 83% -> 40%
where the time goes in v3:
time: 153 us; the launch traced here: 152 us
  Pallas kernels  61.6 us (40%)
  waiting for transfers between devices  55 us (36%)
  starting transfers between devices  27.3 us (18%)
  other arithmetic  4.73 us (3%)
  local copies, waits for them, and re-layouts  2.85 us (2%)
    pallas_call x9, Pallas kernels, call(): pl.pallas_call(ordered, out_shape=out_shape, grid_spec=pltpu.PrefetchScal...  61.6 us
    ppermute x3, waiting for transfers between devices, local(): gathered = [lax.ppermute(post, 'tensor', pairs) for pairs in partners]  27.8 us
    ppermute x6, waiting for transfers between devices, across(): lax.ppermute(rows, 'dp', pairs)  12.4 us
    ppermute x6, starting transfers between devices, across(): lax.ppermute(rows, 'dp', pairs)  11.7 us
    ppermute x3, waiting for transfers between devices, local(): lax.ppermute(rows, 'tensor', partners[s])  9.9 us
    all_to_all x1, starting transfers between devices, local(): lax.all_to_all(keys, 'tensor', split_axis=0, concat_axis=0, tiled=True)  4.83 us
    all_to_all x1, starting transfers between devices, local(): lax.all_to_all(values, 'tensor', split_axis=0, concat_axis=0, tiled=True)  3.58 us
    ppermute x3, starting transfers between devices, local(): gathered = [lax.ppermute(post, 'tensor', pairs) for pairs in partners]  3.55 us
  transfers between devices with their start and end apart: 15, of which 6 were waited for; matrix products, arithmetic and copies ran while one was open for 1% of the time, Pallas kernels for 40%

profile of v3, /device:TPU:0, one launch (start us, length us, event | category | flops | bytes accessed | tf_op | source)
XLA Modules:
  0.0 152.2 jit_solution(10565206112062032539)
XLA Ops:
  0.6 0.5 collective-permute-start
  1.1 6.4 %shard_map.122 = (bf16[8,2,64,768]{3,2,1,0:T(8,128)(2,1)}, bf16[2,128,1536]{2,1,0:T(8,128)(2,1)}, f32[2,128,384]{2,1,0:T(8,128)}, f32[2,128,384]{2,1,0:T(8,128)}) custom-call(s32[64]{0:T(128)} %refs_0_.6, s32[64]{0:T(128)} %refs_1_.3, s32[64]{0:T(128)} %refs_2_.3, s32[1]{0:T(128)} %bitcast.1.refs_3_, bf16[2,128,1536]{2,1,0:T(8,128)(2,1)} %refs_11_.1, ...), custom_call_target="tpu_custom_call" | custom-call | flops 603979776 | bytes 8388608 | tf_op jit(solution)/shard_map/pallas_call | solution.py:245
  7.6 4.8 %all-to-all-start = ((bf16[8,2,64,768]{3,2,1,0:T(8,128)(2,1)}), bf16[8,2,64,768]{3,2,1,0:T(8,128)(2,1)S(1)}, u32[]{:S(2)}, u32[]{:S(2)}) async-start(bf16[8,2,64,768]{3,2,1,0:T(8,128)(2,1)} %get-tuple-element.22.refs_9_), calls=%async_computation | async-start | bytes 3145728 | tf_op jit(solution)/shard_map/all_to_all | solution.py:321
  12.4 18.3 %shard_map.123 = (bf16[8,2,64,768]{3,2,1,0:T(8,128)(2,1)}, bf16[256,1536]{1,0:T(8,128)(2,1)}, bf16[256,1536]{1,0:T(8,128)(2,1)}) custom-call(s32[64]{0:T(128)} %refs_0_.6, s32[64]{0:T(128)} %refs_1_.3, s32[64]{0:T(128)} %refs_2_.3, s32[1]{0:T(128)} %bitcast.1.refs_3_, bf16[2,128,1536]{2,1,0:T(8,128)(2,1)} %get-tuple-element.19.refs_4_, ...), custom_call_target="tpu_custom_call" | custom-call | flops 7247757312 | bytes 16777216 | tf_op jit(solution)/shard_map/pallas_call | solution.py:245
  30.7 2.7 %all-to-all-done = bf16[8,2,64,768]{3,2,1,0:T(8,128)(2,1)S(1)} async-done(((bf16[8,2,64,768]{3,2,1,0:T(8,128)(2,1)}), bf16[8,2,64,768]{3,2,1,0:T(8,128)(2,1)S(1)}, u32[]{:S(2)}, u32[]{:S(2)}) %all-to-all-start) | async-done | bytes 1572896 | tf_op jit(solution)/shard_map/all_to_all | solution.py:321
  33.4 0.0 copy-start.2
  33.4 0.0 copy-start.7
  33.4 0.0 copy-start.8
  33.4 1.1 copy-done.2
  34.6 3.6 %all-to-all-start.1 = ((bf16[8,2,64,768]{3,2,1,0:T(8,128)(2,1)}), bf16[8,2,64,768]{3,2,1,0:T(8,128)(2,1)S(1)}, u32[]{:S(2)}, u32[]{:S(2)}) async-start(bf16[8,2,64,768]{3,2,1,0:T(8,128)(2,1)} %get-tuple-element.26), calls=%async_computation.1 | async-start | bytes 3145728 | tf_op jit(solution)/shard_map/all_to_all | solution.py:350
  38.2 2.9 %collective-permute-start.5 = (bf16[256,1536]{1,0:T(8,128)(2,1)}, bf16[256,1536]{1,0:T(8,128)(2,1)S(1)}, u32[]{:S(2)}, u32[]{:S(2)}) collective-permute-start(bf16[256,1536]{1,0:T(8,128)(2,1)} %get-tuple-element.24.refs_2_), channel_id=1, source_target_pairs={{0,6},{1,7},{2,4},{3,5},{4,2},{5,3},{6,0},{7,1},{8,14},{9,15},{10,... | collective-permute-start | bytes 2359304 | tf_op jit(solution)/shard_map/ppermute | solution.py:430
  41.0 0.5 collective-permute-start.2
  41.5 0.2 collective-permute-start.1
  41.7 0.0 copy-done.7
  41.7 0.0 copy-done.8
  41.7 0.0 copy-done.9
  41.7 0.2 select_reduce_fusion.1
  41.9 0.2 select_reduce_fusion.3
  42.1 0.1 fusion.2
  42.2 0.2 convert_reduce_fusion.1
  42.4 0.6 select_reduce_fusion.4.refs_0_
  43.0 3.4 %shard_map.124 = (bf16[4,64,768]{2,1,0:T(8,128)(2,1)}, bf16[4,64,768]{2,1,0:T(8,128)(2,1)}, bf16[4,64,768]{2,1,0:T(8,128)(2,1)}, bf16[4,64,768]{2,1,0:T(8,128)(2,1)}) custom-call(s32[16]{0:T(128)} %select_reduce_fusion.4.refs_0_, bf16[16,64,768]{2,1,0:T(8,128)(2,1)} %bitcast.7, bf16[256,1536]{1,0:T(8,128)(2,1)} %get-tuple-element.24.refs_2_), custom_call_target="tpu_custom_call" | custom-call | bytes 6291456 | tf_op jit(solution)/shard_map/pallas_call | solution.py:245
  46.4 1.6 %collective-permute-start.10 = (bf16[4,64,768]{2,1,0:T(8,128)(2,1)}, bf16[4,64,768]{2,1,0:T(8,128)(2,1)}, u32[]{:S(2)}, u32[]{:S(2)}) collective-permute-start(bf16[4,64,768]{2,1,0:T(8,128)(2,1)} %get-tuple-element.33), channel_id=1, source_target_pairs={{0,8},{8,16},{16,24},{24,0},{1,9},{9,17},{17,25},{25,1},{2,10},{10... | collective-permute-start | bytes 1179656 | tf_op jit(solution)/shard_map/ppermute | solution.py:416
  48.0 0.0 collective-permute-done.refs_1_
  48.0 2.6 %collective-permute-start.11 = (bf16[4,64,768]{2,1,0:T(8,128)(2,1)}, bf16[4,64,768]{2,1,0:T(8,128)(2,1)}, u32[]{:S(2)}, u32[]{:S(2)}) collective-permute-start(bf16[4,64,768]{2,1,0:T(8,128)(2,1)} %get-tuple-element.34), channel_id=1, source_target_pairs={{0,16},{8,24},{16,0},{24,8},{1,17},{9,25},{17,1},{25,9},{2,18},{10... | collective-permute-start | bytes 1179656 | tf_op jit(solution)/shard_map/ppermute | solution.py:416
  50.6 6.8 %shard_map.125.refs_2_ = bf16[256,1536]{1,0:T(8,128)(2,1)} custom-call(bf16[3,1536,512]{2,1,0:T(8,128)(2,1)} %refs_0_.9, bf16[3,1536,512]{2,1,0:T(8,128)(2,1)} %collective-permute-done.refs_1_, bf16[256,1536]{1,0:T(8,128)(2,1)} %get-tuple-element.24.refs_2_, bf16[4,64,768]{2,1,0:T(8,128)(2,1)} %get-tuple-element.25.refs_3_.refs_1_), custom_call_target="tpu_custom_call" | custom-call | flops 2415919104 | bytes 9437184 | tf_op jit(solution)/shard_map/pallas_call | solution.py:245
  57.4 2.3 %all-to-all-done.1 = bf16[8,2,64,768]{3,2,1,0:T(8,128)(2,1)S(1)} async-done(((bf16[8,2,64,768]{3,2,1,0:T(8,128)(2,1)}), bf16[8,2,64,768]{3,2,1,0:T(8,128)(2,1)S(1)}, u32[]{:S(2)}, u32[]{:S(2)}) %all-to-all-start.1) | async-done | bytes 1572896 | tf_op jit(solution)/shard_map/all_to_all | solution.py:350
  59.7 1.1 copy-done.1
  60.8 3.4 %shard_map.126 = (bf16[4,64,768]{2,1,0:T(8,128)(2,1)}, bf16[4,64,768]{2,1,0:T(8,128)(2,1)}, bf16[4,64,768]{2,1,0:T(8,128)(2,1)}, bf16[4,64,768]{2,1,0:T(8,128)(2,1)}) custom-call(s32[16]{0:T(128)} %select_reduce_fusion.4.refs_0_, bf16[16,64,768]{2,1,0:T(8,128)(2,1)} %bitcast.6, bf16[256,1536]{1,0:T(8,128)(2,1)} %shard_map.125.refs_2_), custom_call_target="tpu_custom_call" | custom-call | bytes 6291456 | tf_op jit(solution)/shard_map/pallas_call | solution.py:245
  64.2 27.8 %collective-permute-done.2.refs_3_ = bf16[256,1536]{1,0:T(8,128)(2,1)} collective-permute-done((bf16[256,1536]{1,0:T(8,128)(2,1)}, bf16[256,1536]{1,0:T(8,128)(2,1)}, u32[]{:S(2)}, u32[]{:S(2)}) %collective-permute-start.2) | collective-permute-done | bytes 786464 | tf_op jit(solution)/shard_map/ppermute | solution.py:430
  92.0 3.6 %collective-permute-start.12 = (bf16[4,64,768]{2,1,0:T(8,128)(2,1)}, bf16[4,64,768]{2,1,0:T(8,128)(2,1)S(1)}, u32[]{:S(2)}, u32[]{:S(2)}) collective-permute-start(bf16[4,64,768]{2,1,0:T(8,128)(2,1)} %get-tuple-element.35), channel_id=1, source_target_pairs={{0,24},{8,0},{16,8},{24,16},{1,25},{9,1},{17,9},{25,17},{2,26},{10... | collective-permute-start | bytes 1179656 | tf_op jit(solution)/shard_map/ppermute | solution.py:416
  95.6 0.0 collective-permute-done.1.refs_2_
  95.6 0.0 collective-permute-start.7
  95.6 9.9 %shard_map.127 = (bf16[256,1536]{1,0:T(8,128)(2,1)}, bf16[256,1536]{1,0:T(8,128)(2,1)}) custom-call(bf16[3,1536,512]{2,1,0:T(8,128)(2,1)} %refs_0_.9, bf16[3,1536,512]{2,1,0:T(8,128)(2,1)} %collective-permute-done.refs_1_, bf16[256,1536]{1,0:T(8,128)(2,1)} %collective-permute-done.1.refs_2_, bf16[256,1536]{1,0:T(8,128)(2,1)} %collective-permute-done.2.refs_3_, ...), custom_call_target="tpu_custom_call" | custom-call | flops 4831838208 | bytes 9437184 | tf_op jit(solution)/shard_map/pallas_call | solution.py:245
  105.4 0.0 collective-permute-done.5.refs_2_
  105.4 0.4 collective-permute-start.4
  105.8 0.5 copy-done.5
  106.3 6.9 %shard_map.128.refs_5_ = bf16[256,1536]{1,0:T(8,128)(2,1)} custom-call(bf16[3,1536,512]{2,1,0:T(8,128)(2,1)} %refs_0_.9, bf16[3,1536,512]{2,1,0:T(8,128)(2,1)} %collective-permute-done.refs_1_, bf16[256,1536]{1,0:T(8,128)(2,1)} %copy-done.5, bf16[256,1536]{1,0:T(8,128)(2,1)} %get-tuple-element.28.refs_3_), custom_call_target="tpu_custom_call" | custom-call | flops 2415919104 | bytes 9437184 | tf_op jit(solution)/shard_map/pallas_call | solution.py:245
  113.2 0.0 collective-permute-done.10.refs_2_
  113.2 2.1 %collective-permute-start.6 = (bf16[256,1536]{1,0:T(8,128)(2,1)}, bf16[256,1536]{1,0:T(8,128)(2,1)S(1)}, u32[]{:S(2)}, u32[]{:S(2)}) collective-permute-start(bf16[256,1536]{1,0:T(8,128)(2,1)} %shard_map.128.refs_5_), channel_id=1, source_target_pairs={{0,6},{1,7},{2,4},{3,5},{4,2},{5,3},{6,0},{7,1},{8,14},{9,15},{10,... | collective-permute-start | bytes 2359304 | tf_op jit(solution)/shard_map/ppermute | solution.py:441
  115.3 0.0 collective-permute-done.11.refs_3_
  115.3 0.0 copy-done.4
  115.3 0.6 collective-permute-start.3
  115.9 0.0 collective-permute-done.12.refs_4_
  115.9 1.0 collective-permute-start.8
  116.9 0.0 collective-permute-done.7.refs_2_
  116.9 2.9 %collective-permute-start.9 = (bf16[4,64,768]{2,1,0:T(8,128)(2,1)}, bf16[4,64,768]{2,1,0:T(8,128)(2,1)}, u32[]{:S(2)}, u32[]{:S(2)}) collective-permute-start(bf16[4,64,768]{2,1,0:T(8,128)(2,1)} %get-tuple-element.32), channel_id=1, source_target_pairs={{0,24},{8,0},{16,8},{24,16},{1,25},{9,1},{17,9},{25,17},{2,26},{10... | collective-permute-start | bytes 1179656 | tf_op jit(solution)/shard_map/ppermute | solution.py:416
  119.8 0.2 convert_reduce_fusion
  119.9 0.1 dynamic_slice.6
  120.0 0.6 select_reduce_fusion.2.refs_0_
  120.6 0.1 compare_bitcast_fusion
  120.7 0.0 copy-done.6
  120.7 3.3 %shard_map.129.refs_5_ = bf16[16,64,1536]{2,1,0:T(8,128)(2,1)} custom-call(s32[16]{0:T(128)} %select_reduce_fusion.2.refs_0_, bf16[4,64,768]{2,1,0:T(8,128)(2,1)} %get-tuple-element.25.refs_3_.refs_1_, bf16[4,64,768]{2,1,0:T(8,128)(2,1)} %collective-permute-done.10.refs_2_, bf16[4,64,768]{2,1,0:T(8,128)(2,1)} %collective-permute-done.11.refs_3_, ...), custom_call_target="tpu_custom_call" | custom-call | bytes 6291456 | tf_op jit(solution)/shard_map/pallas_call | solution.py:245
  124.0 0.0 copy-start
  124.0 0.0 copy-start.3
  124.0 12.4 %collective-permute-done.8.refs_3_ = bf16[4,64,768]{2,1,0:T(8,128)(2,1)} collective-permute-done((bf16[4,64,768]{2,1,0:T(8,128)(2,1)}, bf16[4,64,768]{2,1,0:T(8,128)(2,1)}, u32[]{:S(2)}, u32[]{:S(2)}) %collective-permute-start.8) | collective-permute-done | bytes 393248 | tf_op jit(solution)/shard_map/ppermute | solution.py:416
  136.4 0.0 collective-permute-done.9.refs_4_
  136.4 3.3 %shard_map.130 = bf16[16,64,1536]{2,1,0:T(8,128)(2,1)} custom-call(s32[16]{0:T(128)} %select_reduce_fusion.2.refs_0_, bf16[4,64,768]{2,1,0:T(8,128)(2,1)} %get-tuple-element.27.refs_4_.refs_1_, bf16[4,64,768]{2,1,0:T(8,128)(2,1)} %collective-permute-done.7.refs_2_, ...), custom_call_target="tpu_custom_call", output_to_operand_aliasing={{}: (5, {})} | custom-call | bytes 6291456 | tf_op jit(solution)/shard_map/pallas_call | solution.py:245
  139.7 1.7 %collective-permute-done.4 = bf16[256,1536]{1,0:T(8,128)(2,1)S(1)} collective-permute-done((bf16[256,1536]{1,0:T(8,128)(2,1)}, bf16[256,1536]{1,0:T(8,128)(2,1)S(1)}, u32[]{:S(2)}, u32[]{:S(2)}) %collective-permute-start.4) | collective-permute-done | bytes 786464 | tf_op jit(solution)/shard_map/ppermute | solution.py:441
  141.4 0.0 collective-permute-done.6
  141.4 8.2 %collective-permute-done.3 = bf16[256,1536]{1,0:T(8,128)(2,1)} collective-permute-done((bf16[256,1536]{1,0:T(8,128)(2,1)S(1)}, bf16[256,1536]{1,0:T(8,128)(2,1)}, u32[]{:S(2)}, u32[]{:S(2)}) %collective-permute-start.3) | collective-permute-done | bytes 786464 | tf_op jit(solution)/shard_map/ppermute | solution.py:441
  149.6 0.0 copy-done
  149.6 0.0 copy-done.3
  149.6 2.6 %select_convert_fusion = bf16[256,1536]{1,0:T(8,128)(2,1)} fusion(bf16[256,1536]{1,0:T(8,128)(2,1)S(1)} %collective-permute-done.6, bf16[256,1536]{1,0:T(8,128)(2,1)S(1)} %collective-permute-done.4, bf16[256,1536]{1,0:T(8,128)(2,1)} %collective-permute-done.3, bf16[256,1536]{1,0:T(8,128)(2,1)S(1)} %copy-done, bf16[256,1536]{1,0:T(8,128)(2,1)S(1)} %copy-done.3, ...), kind=kLoop, calls=%fused_computation | loop fusion | flops 4325376 | bytes 4718848 | tf_op jit(solution)/shard_map/convert_element_type | solution.py:450
  (7 shorter events, 0.0 us)
Async XLA Ops:
  0.6 47.4 %collective-permute-start = (bf16[3,1536,512]{2,1,0:T(8,128)(2,1)}, bf16[3,1536,512]{2,1,0:T(8,128)(2,1)}, u32[]{:S(2)}, u32[]{:S(2)}) collective-permute-start(bf16[3,1536,512]{2,1,0:T(8,128)(2,1)} %refs_0_.9), channel_id=1, source_target_pairs={{0,1},{1,0},{2,3},{3,2},{4,5},{5,4},{6,7},{7,6},{8,9},{9,8},{10,11... | collective-permute-start | bytes 14155784 | tf_op jit(solution)/shard_map/ppermute | solution.py:296
  7.6 25.9 %all-to-all-start = ((bf16[8,2,64,768]{3,2,1,0:T(8,128)(2,1)}), bf16[8,2,64,768]{3,2,1,0:T(8,128)(2,1)S(1)}, u32[]{:S(2)}, u32[]{:S(2)}) async-start(bf16[8,2,64,768]{3,2,1,0:T(8,128)(2,1)} %get-tuple-element.22.refs_9_), calls=%async_computation | async-start | bytes 3145728 | tf_op jit(solution)/shard_map/all_to_all | solution.py:321
  33.4 1.1 copy-start.2
  33.4 8.3 %copy-start.7 = (s32[64]{0:T(128)S(1)}, s32[64]{0:T(128)}, u32[]{:S(2)}) copy-start(s32[64]{0:T(128)} %refs_0_.6) | copy-start | bytes 772
  33.4 8.3 %copy-start.8 = (s32[64]{0:T(128)S(1)}, s32[64]{0:T(128)}, u32[]{:S(2)}) copy-start(s32[64]{0:T(128)} %refs_1_.3) | copy-start | bytes 772
  33.4 8.3 %copy-start.9 = (s32[64]{0:T(128)S(1)}, s32[64]{0:T(128)}, u32[]{:S(2)}) copy-start(s32[64]{0:T(128)} %param.20) | copy-start | bytes 772
  34.6 25.1 %all-to-all-start.1 = ((bf16[8,2,64,768]{3,2,1,0:T(8,128)(2,1)}), bf16[8,2,64,768]{3,2,1,0:T(8,128)(2,1)S(1)}, u32[]{:S(2)}, u32[]{:S(2)}) async-start(bf16[8,2,64,768]{3,2,1,0:T(8,128)(2,1)} %get-tuple-element.26), calls=%async_computation.1 | async-start | bytes 3145728 | tf_op jit(solution)/shard_map/all_to_all | solution.py:350
  38.2 67.3 %collective-permute-start.5 = (bf16[256,1536]{1,0:T(8,128)(2,1)}, bf16[256,1536]{1,0:T(8,128)(2,1)S(1)}, u32[]{:S(2)}, u32[]{:S(2)}) collective-permute-start(bf16[256,1536]{1,0:T(8,128)(2,1)} %get-tuple-element.24.refs_2_), channel_id=1, source_target_pairs={{0,6},{1,7},{2,4},{3,5},{4,2},{5,3},{6,0},{7,1},{8,14},{9,15},{10,... | collective-permute-start | bytes 2359304 | tf_op jit(solution)/shard_map/ppermute | solution.py:430
  41.0 51.0 %collective-permute-start.2 = (bf16[256,1536]{1,0:T(8,128)(2,1)}, bf16[256,1536]{1,0:T(8,128)(2,1)}, u32[]{:S(2)}, u32[]{:S(2)}) collective-permute-start(bf16[256,1536]{1,0:T(8,128)(2,1)} %get-tuple-element.24.refs_2_), channel_id=1, source_target_pairs={{0,4},{1,5},{2,6},{3,7},{4,0},{5,1},{6,2},{7,3},{8,12},{9,13},{10,... | collective-permute-start | bytes 2359304 | tf_op jit(solution)/shard_map/ppermute | solution.py:430
  41.5 54.0 %collective-permute-start.1 = (bf16[256,1536]{1,0:T(8,128)(2,1)}, bf16[256,1536]{1,0:T(8,128)(2,1)}, u32[]{:S(2)}, u32[]{:S(2)}) collective-permute-start(bf16[256,1536]{1,0:T(8,128)(2,1)} %get-tuple-element.24.refs_2_), channel_id=1, source_target_pairs={{0,2},{1,3},{2,0},{3,1},{4,6},{5,7},{6,4},{7,5},{8,10},{9,11},{10,... | collective-permute-start | bytes 2359304 | tf_op jit(solution)/shard_map/ppermute | solution.py:430
  46.4 66.8 %collective-permute-start.10 = (bf16[4,64,768]{2,1,0:T(8,128)(2,1)}, bf16[4,64,768]{2,1,0:T(8,128)(2,1)}, u32[]{:S(2)}, u32[]{:S(2)}) collective-permute-start(bf16[4,64,768]{2,1,0:T(8,128)(2,1)} %get-tuple-element.33), channel_id=1, source_target_pairs={{0,8},{8,16},{16,24},{24,0},{1,9},{9,17},{17,25},{25,1},{2,10},{10... | collective-permute-start | bytes 1179656 | tf_op jit(solution)/shard_map/ppermute | solution.py:416
  48.0 67.3 %collective-permute-start.11 = (bf16[4,64,768]{2,1,0:T(8,128)(2,1)}, bf16[4,64,768]{2,1,0:T(8,128)(2,1)}, u32[]{:S(2)}, u32[]{:S(2)}) collective-permute-start(bf16[4,64,768]{2,1,0:T(8,128)(2,1)} %get-tuple-element.34), channel_id=1, source_target_pairs={{0,16},{8,24},{16,0},{24,8},{1,17},{9,25},{17,1},{25,9},{2,18},{10... | collective-permute-start | bytes 1179656 | tf_op jit(solution)/shard_map/ppermute | solution.py:416
  59.7 1.1 copy-start.1
  92.0 23.9 %collective-permute-start.12 = (bf16[4,64,768]{2,1,0:T(8,128)(2,1)}, bf16[4,64,768]{2,1,0:T(8,128)(2,1)S(1)}, u32[]{:S(2)}, u32[]{:S(2)}) collective-permute-start(bf16[4,64,768]{2,1,0:T(8,128)(2,1)} %get-tuple-element.35), channel_id=1, source_target_pairs={{0,24},{8,0},{16,8},{24,16},{1,25},{9,1},{17,9},{25,17},{2,26},{10... | collective-permute-start | bytes 1179656 | tf_op jit(solution)/shard_map/ppermute | solution.py:416
  95.6 21.3 %collective-permute-start.7 = (bf16[4,64,768]{2,1,0:T(8,128)(2,1)}, bf16[4,64,768]{2,1,0:T(8,128)(2,1)}, u32[]{:S(2)}, u32[]{:S(2)}) collective-permute-start(bf16[4,64,768]{2,1,0:T(8,128)(2,1)} %get-tuple-element.30), channel_id=1, source_target_pairs={{0,8},{8,16},{16,24},{24,0},{1,9},{9,17},{17,25},{25,1},{2,10},{10... | collective-permute-start | bytes 1179656 | tf_op jit(solution)/shard_map/ppermute | solution.py:416
  105.4 0.9 copy-start.5
  105.4 35.9 %collective-permute-start.4 = (bf16[256,1536]{1,0:T(8,128)(2,1)}, bf16[256,1536]{1,0:T(8,128)(2,1)S(1)}, u32[]{:S(2)}, u32[]{:S(2)}) collective-permute-start(bf16[256,1536]{1,0:T(8,128)(2,1)} %get-tuple-element.29), channel_id=1, source_target_pairs={{0,4},{1,5},{2,6},{3,7},{4,0},{5,1},{6,2},{7,3},{8,12},{9,13},{10,... | collective-permute-start | bytes 2359304 | tf_op jit(solution)/shard_map/ppermute | solution.py:441
  106.3 9.0 %copy-start.4 = (bf16[256,1536]{1,0:T(8,128)(2,1)S(1)}, bf16[256,1536]{1,0:T(8,128)(2,1)}, u32[]{:S(2)}) copy-start(bf16[256,1536]{1,0:T(8,128)(2,1)} %get-tuple-element.28.refs_3_) | copy-start | bytes 2359300
  113.2 28.2 %collective-permute-start.6 = (bf16[256,1536]{1,0:T(8,128)(2,1)}, bf16[256,1536]{1,0:T(8,128)(2,1)S(1)}, u32[]{:S(2)}, u32[]{:S(2)}) collective-permute-start(bf16[256,1536]{1,0:T(8,128)(2,1)} %shard_map.128.refs_5_), channel_id=1, source_target_pairs={{0,6},{1,7},{2,4},{3,5},{4,2},{5,3},{6,0},{7,1},{8,14},{9,15},{10,... | collective-permute-start | bytes 2359304 | tf_op jit(solution)/shard_map/ppermute | solution.py:441
  115.3 34.3 %collective-permute-start.3 = (bf16[256,1536]{1,0:T(8,128)(2,1)S(1)}, bf16[256,1536]{1,0:T(8,128)(2,1)}, u32[]{:S(2)}, u32[]{:S(2)}) collective-permute-start(bf16[256,1536]{1,0:T(8,128)(2,1)S(1)} %copy-done.4), channel_id=1, source_target_pairs={{0,2},{1,3},{2,0},{3,1},{4,6},{5,7},{6,4},{7,5},{8,10},{9,11},{10,... | collective-permute-start | bytes 2359304 | tf_op jit(solution)/shard_map/ppermute | solution.py:441
  115.9 4.8 %copy-start.6 = (bf16[4,64,768]{2,1,0:T(8,128)(2,1)}, bf16[4,64,768]{2,1,0:T(8,128)(2,1)S(1)}, u32[]{:S(2)}) copy-start(bf16[4,64,768]{2,1,0:T(8,128)(2,1)S(1)} %collective-permute-done.12.refs_4_) | copy-start | bytes 1179652
  115.9 20.5 %collective-permute-start.8 = (bf16[4,64,768]{2,1,0:T(8,128)(2,1)}, bf16[4,64,768]{2,1,0:T(8,128)(2,1)}, u32[]{:S(2)}, u32[]{:S(2)}) collective-permute-start(bf16[4,64,768]{2,1,0:T(8,128)(2,1)} %get-tuple-element.31), channel_id=1, source_target_pairs={{0,16},{8,24},{16,0},{24,8},{1,17},{9,25},{17,1},{25,9},{2,18},{10... | collective-permute-start | bytes 1179656 | tf_op jit(solution)/shard_map/ppermute | solution.py:416
  116.9 19.5 %collective-permute-start.9 = (bf16[4,64,768]{2,1,0:T(8,128)(2,1)}, bf16[4,64,768]{2,1,0:T(8,128)(2,1)}, u32[]{:S(2)}, u32[]{:S(2)}) collective-permute-start(bf16[4,64,768]{2,1,0:T(8,128)(2,1)} %get-tuple-element.32), channel_id=1, source_target_pairs={{0,24},{8,0},{16,8},{24,16},{1,25},{9,1},{17,9},{25,17},{2,26},{10... | collective-permute-start | bytes 1179656 | tf_op jit(solution)/shard_map/ppermute | solution.py:416
  124.0 25.6 %copy-start = (bf16[256,1536]{1,0:T(8,128)(2,1)S(1)}, bf16[256,1536]{1,0:T(8,128)(2,1)}, u32[]{:S(2)}) copy-start(bf16[256,1536]{1,0:T(8,128)(2,1)} %shard_map.125.refs_2_) | copy-start | bytes 2359300
  124.0 25.6 %copy-start.3 = (bf16[256,1536]{1,0:T(8,128)(2,1)S(1)}, bf16[256,1536]{1,0:T(8,128)(2,1)}, u32[]{:S(2)}) copy-start(bf16[256,1536]{1,0:T(8,128)(2,1)} %get-tuple-element.23) | copy-start | bytes 2359300

commit v4 on v3

--- a/solution.py
+++ b/solution.py
@@ -92,10 +92,11 @@
 
 def attention_kernel(
     order, news, olds, dev, normed, cosine, sine, weight, w_value, keys, cached, tokens, gain, w_out,
-    values, residual, post, total, attended, out_weight, sems,
+    values, residual, *rest,
 ):
     step = pl.program_id(0)
     reqs, new, width = normed.shape
+    posts, (total, attended, out_weight, sems) = rest[:reqs], rest[reqs:]
     parts, _, depth, _ = keys.shape
     ctx = parts * depth
     flat = reqs * new
@@ -162,16 +163,14 @@
     def _():
         rounded = total[...].astype(bf16)
         residual[...] = rounded
-        post[...] = norm_value(rounded.astype(f32), gain[1:2, :])
-
-
-def mlp_kernel(own, other, *refs):
-    total = refs[-1]
-    inputs = refs[: (len(refs) - 1) // 2]
-    outputs = refs[(len(refs) - 1) // 2 : -1]
+        normal = norm_value(rounded.astype(f32), gain[1:2, :])
+        for r in range(reqs):
+            posts[r][...] = normal[r * new : (r + 1) * new]
+
+
+def mlp_kernel(own, other, rows, out, total):
     step = pl.program_id(0)
-    flat = inputs[0].shape[0]
-    values = jnp.concatenate([rows[...] for rows in inputs], axis=0)
+    values = rows[...]
     term = None
     for weights in (own, other):
         gate = jnp.dot(values, weights[0], preferred_element_type=f32)
@@ -192,44 +191,48 @@
 
     @pl.when(step == pl.num_programs(0) - 1)
     def _():
-        for i, out in enumerate(outputs):
-            out[...] = total[i * flat : (i + 1) * flat].astype(bf16)
-
-
-def run_copies(copies):
-    for copy in copies:
+        out[...] = total[...].astype(bf16)
+
+
+def move_rows(pairs, held, arrive, leave):
+    inward = [
+        pltpu.make_async_copy(source, held.at[i], arrive.at[i])
+        for i, (source, _) in enumerate(pairs)
+    ]
+    outward = [
+        pltpu.make_async_copy(held.at[i], target, leave.at[i])
+        for i, (_, target) in enumerate(pairs)
+    ]
+    for copy in inward:
         copy.start()
-    for copy in copies:
+    for first, second in zip(inward, outward):
+        first.wait()
+        second.start()
+    for copy in outward:
         copy.wait()
 
 
 def pack_kernel(picked, source, *rest):
-    targets, sems = rest[:-1], rest[-1]
+    targets, (held, arrive, leave) = rest[:-3], rest[-3:]
     share = targets[0].shape[0]
-    run_copies(
+    move_rows(
+        [(source.at[picked[i]], targets[i // share].at[i % share]) for i in range(held.shape[0])],
+        held, arrive, leave,
+    )
+
+
+def unpack_kernel(columns, count, spots, *refs):
+    sources, (target, held, arrive, leave) = refs[:count], refs[-4:]
+    share, _, width = sources[0].shape
+    move_rows(
         [
-            pltpu.make_async_copy(
-                source.at[picked[s * share + k]], target.at[k], sems.at[s * share + k]
+            (
+                sources[i // share].at[i % share],
+                target.at[spots[i], :, pl.ds(columns, width)],
             )
-            for s, target in enumerate(targets)
-            for k in range(share)
-        ]
-    )
-
-
-def unpack_kernel(columns, count, spots, *refs):
-    sources, target, sems = refs[:count], refs[-2], refs[-1]
-    share, _, width = sources[0].shape
-    run_copies(
-        [
-            pltpu.make_async_copy(
-                source.at[k],
-                target.at[spots[s * share + k], :, pl.ds(columns, width)],
-                sems.at[s * share + k],
-            )
-            for s, source in enumerate(sources)
-            for k in range(share)
-        ]
+            for i in range(held.shape[0])
+        ],
+        held, arrive, leave,
     )
 
 
@@ -278,7 +281,9 @@
     cached_lengths,
     decode_slots,
 ):
-    tensor_size = lax.axis_size("tensor")
+    tensor = ("chip", "core")
+    chips, cores = lax.axis_size("chip"), lax.axis_size("core")
+    tensor_size = chips * cores
     group_total = lax.axis_size("dp")
     reqs, new, width = tokens.shape
     ctx = cached.shape[1]
@@ -286,16 +291,14 @@
     flat = reqs * new
     group_reqs = reqs * tensor_size
     group_index = lax.axis_index("dp")
-    device = group_index * tensor_size + lax.axis_index("tensor")
+    device = group_index * tensor_size + lax.axis_index(tensor)
     dev = device.astype(jnp.int32).reshape(1)
     key_width = KV_HEADS * HEAD_DIM
     groups = key_width // GROUP
     scalars = (request_order, new_lengths, cached_lengths, dev)
     freq = jnp.asarray(frequencies())
 
-    other_weights = lax.ppermute(
-        mlp_weights, "tensor", [(t, t ^ 1) for t in range(tensor_size)]
-    )
+    other_weights = lax.ppermute(mlp_weights, "core", [(0, 1), (1, 0)])
 
     context_shape = (tensor_size, reqs, depth, key_width)
     context_spec = pl.BlockSpec((tensor_size, reqs, depth, GROUP), lambda g, *_: (0, 0, 0, g))
@@ -318,8 +321,8 @@
         2 * flat * width * key_width,
         8 << 20,
     )
-    keys_moved = lax.all_to_all(keys, "tensor", split_axis=0, concat_axis=0, tiled=True)
-    values, residual, post = call(
+    keys_moved = lax.all_to_all(keys, tensor, split_axis=0, concat_axis=0, tiled=True)
+    values, residual, *posts = call(
         attention_kernel,
         scalars,
         (groups,),
@@ -335,8 +338,8 @@
             whole(norm_gains.shape),
             pl.BlockSpec(memory_space=pl.ANY),
         ],
-        [context_spec, whole((flat, width)), whole((flat, width))],
-        [shape(context_shape), shape((flat, width)), shape((flat, width))],
+        [context_spec, whole((flat, width))] + [whole((new, width))] * reqs,
+        [shape(context_shape), shape((flat, width))] + [shape((new, width))] * reqs,
         [
             pltpu.VMEM((flat, width), f32),
             pltpu.VMEM((flat, 2 * GROUP), bf16),
@@ -347,24 +350,24 @@
         12 * flat * width * width,
         16 << 20,
     )
-    values_moved = lax.all_to_all(values, "tensor", split_axis=0, concat_axis=0, tiled=True)
+    values_moved = lax.all_to_all(values, tensor, split_axis=0, concat_axis=0, tiled=True)
 
     units = mlp_weights.shape[2]
     chunk = 256 if units % 256 == 0 else units
 
-    def mlp(pieces, after):
-        count = len(pieces)
+    def mlp(rows, after):
+        count = rows.shape[0]
         weight_spec = pl.BlockSpec((3, width, chunk), lambda c: (0, 0, c))
         return call(
             mlp_kernel,
             (),
             (units // chunk,),
-            [weight_spec] * 2 + [whole((flat, width))] * count,
-            [whole((flat, width))] * count,
-            [shape((flat, width))] * count,
-            [pltpu.VMEM((count * flat, width), f32)],
-            (mlp_weights, other_weights, *pieces),
-            12 * count * flat * width * units,
+            [weight_spec] * 2 + [whole((count, width))],
+            whole((count, width)),
+            shape((count, width)),
+            [pltpu.VMEM((count, width), f32)],
+            (mlp_weights, other_weights, rows),
+            12 * count * width * units,
             12 * width * units,
             after=after,
         )
@@ -398,15 +401,16 @@
     share = group_reqs // group_total
     piece = (share, depth, key_width)
     anywhere = pl.BlockSpec(memory_space=pl.ANY)
-    sems = [pltpu.SemaphoreType.DMA((group_reqs,))]
+    sems = [pltpu.VMEM((group_reqs, depth, key_width), bf16)] + [
+        pltpu.SemaphoreType.DMA((group_reqs,))
+    ] * 2
     shifts = [
         [(g, (g + s) % group_total) for g in range(group_total)] for s in range(1, group_total)
     ]
 
     def pack(moved, after):
         return call(
-            pack_kernel, (picked,), (1,), [whole((group_reqs, depth, key_width))],
-            [anywhere] * group_total,
+            pack_kernel, (picked,), (1,), [anywhere], [anywhere] * group_total,
             [shape(piece)] * group_total, sems, (moved.reshape(group_reqs, depth, key_width),),
             after=after,
         )
@@ -419,50 +423,49 @@
     def unpack(columns, arrived, target, after):
         return call(
             functools.partial(unpack_kernel, columns, group_total), (spots,), (1,),
-            [whole(piece)] * group_total + [anywhere] * len(target), anywhere,
+            [anywhere] * (group_total + len(target)), anywhere,
             shape((group_reqs, depth, 2 * key_width)), sems, (*arrived, *target),
             aliases={1 + group_total: 0} if target else {}, after=after,
         )
 
-    partners = [
-        [(t, t ^ (2 * s)) for t in range(tensor_size)] for s in range(1, tensor_size // 2)
-    ]
-    gathered = [lax.ppermute(post, "tensor", pairs) for pairs in partners]
-    keys_packed = pack(keys_moved, (post,))
+    gathered = [lax.all_gather(rows, "chip", axis=0, tiled=True) for rows in posts]
+    keys_packed = pack(keys_moved, (residual,))
     keys_arrived = across(keys_packed)
-    partials = list(mlp([post], (keys_packed[0],)))
-    values_packed = pack(values_moved, (partials[0],))
-    values_arrived = across(values_packed)
-    latest = values_packed[0]
-    batches = [range(0, 2)] + [range(s, min(s + 2, len(partners))) for s in range(2, len(partners), 2)]
-    for batch in batches:
-        results = mlp([gathered[s] for s in batch], (latest,))
-        latest = results[0]
-        partials += [lax.ppermute(rows, "tensor", partners[s]) for s, rows in zip(batch, results)]
+    latest = keys_packed[0]
+    sums = []
+    values_arrived = None
+    for rows in gathered:
+        partial = mlp(rows, (latest,))
+        sums.append(lax.psum_scatter(partial, "chip", scatter_dimension=0, tiled=True))
+        latest = partial
+        if values_arrived is None:
+            values_packed = pack(values_moved, (latest,))
+            values_arrived = across(values_packed)
+            latest = values_packed[0]
     kv_half = unpack(0, keys_arrived, (), (latest,))
     kv_decode = unpack(key_width, values_arrived, (kv_half,), ())
 
     own_counts = lax.dynamic_slice_in_dim(count_of, device * reqs, reqs)
-    live = (jnp.arange(new, dtype=jnp.int32)[None, :] < own_counts[:, None]).reshape(flat, 1)
-    total = residual.astype(f32)
-    for partial in partials:
-        total = total + partial.astype(f32)
-    layer_out = jnp.where(live, total, 0.0).astype(bf16).reshape(reqs, new, width)
+    live = jnp.arange(new, dtype=jnp.int32)[None, :, None] < own_counts[:, None, None]
+    total = residual.reshape(reqs, new, width).astype(f32) + jnp.stack(sums).astype(f32)
+    layer_out = jnp.where(live, total, 0.0).astype(bf16)
     return (layer_out, kv_decode)
 
 
 def solution(mesh):
     in_specs = (
-        P(("dp", "tensor"), None, None),
-        P(("dp", "tensor"), None, None),
-        P(),
-        P(),
-        P(),
-        P(None, None, "tensor"),
-        P(),
-        P(),
-        P(),
-        P(),
-    )
-    out_specs = (P(("dp", "tensor"), None, None), P("dp", "tensor", None))
+        P(("dp", "chip", "core"), None, None),
+        P(("dp", "chip", "core"), None, None),
+        P(),
+        P(),
+        P(),
+        P(None, None, ("chip", "core")),
+        P(),
+        P(),
+        P(),
+        P(),
+    )
+    out_specs = (P(("dp", "chip", "core"), None, None), P("dp", ("chip", "core"), None))
+    devices = mesh.devices.reshape(mesh.devices.shape[0], -1, 2)
+    mesh = jax.sharding.Mesh(devices, ("dp", "chip", "core"))
     return jax.shard_map(local, mesh=mesh, in_specs=in_specs, out_specs=out_specs, check_vma=False)

time: 153 us -> 209 us (1.37)
  the two profiles are of different devices: /device:TPU:0 before, /device:TPU:9 now
where the time goes in v4:
time: 209 us; the launch traced here: 208 us
  waiting for transfers between devices  108 us (52%)
  Pallas kernels  57 us (27%)
  starting transfers between devices  20.5 us (10%)
  between operations  13.9 us (7%)
  other arithmetic  4.47 us (2%)
  local copies, waits for them, and re-layouts  4.29 us (2%)
    ppermute x6, waiting for transfers between devices, across(): lax.ppermute(rows, 'dp', pairs)  57.2 us
    pallas_call x8, Pallas kernels, call(): pl.pallas_call(ordered, out_shape=out_shape, grid_spec=pltpu.PrefetchScal...  57 us
    all_gather x2, waiting for transfers between devices, local(): lax.all_gather(rows, 'chip', axis=0, tiled=True)  26.9 us
    all_to_all x1, waiting for transfers between devices, local(): lax.all_to_all(keys, tensor, split_axis=0, concat_axis=0, tiled=True)  21 us
    ppermute x6, starting transfers between devices, across(): lax.ppermute(rows, 'dp', pairs)  8.87 us
    all_to_all x1, starting transfers between devices, local(): lax.all_to_all(values, tensor, split_axis=0, concat_axis=0, tiled=True)  6.94 us
    unnamed x32, local copies, waits for them, and re-layouts  4.22 us
  transfers between devices with their start and end apart: 13, of which 10 were waited for; matrix products, arithmetic and copies ran while one was open for 1% of the time, Pallas kernels for 23%

profile of v4, /device:TPU:9, one launch (start us, length us, event | category | flops | bytes accessed | tf_op | source)
XLA Modules:
  0.0 208.3 jit_solution(15686200792689535478)
XLA Ops:
  7.2 0.0 all-gather.3.cloned.1.call-start
  7.2 0.7 collective-permute-start
  7.9 6.4 %shard_map.122 = (bf16[8,2,64,768]{3,2,1,0:T(8,128)(2,1)}, bf16[2,128,1536]{2,1,0:T(8,128)(2,1)}, f32[2,128,384]{2,1,0:T(8,128)}, f32[2,128,384]{2,1,0:T(8,128)}) custom-call(s32[64]{0:T(128)} %refs_0_.5, s32[64]{0:T(128)} %refs_1_.3, s32[64]{0:T(128)} %refs_2_.3, s32[1]{0:T(128)} %bitcast.refs_3_, bf16[2,128,1536]{2,1,0:T(8,128)(2,1)} %refs_11_.1, ...), custom_call_target="tpu_custom_call" | custom-call | flops 603979776 | bytes 8388608 | tf_op jit(solution)/shard_map/pallas_call | solution.py:248
  14.4 18.4 %shard_map.123 = (bf16[8,2,64,768]{3,2,1,0:T(8,128)(2,1)}, bf16[256,1536]{1,0:T(8,128)(2,1)}, bf16[128,1536]{1,0:T(8,128)(2,1)}, bf16[128,1536]{1,0:T(8,128)(2,1)}) custom-call(s32[64]{0:T(128)} %refs_0_.5, s32[64]{0:T(128)} %refs_1_.3, s32[64]{0:T(128)} %refs_2_.3, s32[1]{0:T(128)} %bitcast.refs_3_, bf16[2,128,1536]{2,1,0:T(8,128)(2,1)} %get-tuple-element.18.refs_4_, ...), custom_call_target="tpu_custom_call" | custom-call | flops 7247757312 | bytes 16777216 | tf_op jit(solution)/shard_map/pallas_call | solution.py:248
  32.8 0.0 all-gather.3.cloned.1.call-update
  32.8 3.8 %all-to-all-start = ((bf16[8,2,64,768]{3,2,1,0:T(8,128)(2,1)}), bf16[8,2,64,768]{3,2,1,0:T(8,128)(2,1)S(1)}, u32[]{:S(2)}, u32[]{:S(2)}) async-start(bf16[8,2,64,768]{3,2,1,0:T(8,128)(2,1)} %get-tuple-element.21.refs_9_), calls=%async_computation | async-start | bytes 3145728 | tf_op jit(solution)/shard_map/all_to_all | solution.py:324
  36.6 0.0 all-gather.5.cloned.1.call-start
  36.6 0.7 all-gather.5.cloned.1.call-update
  37.4 21.0 %all-to-all-done = bf16[8,2,64,768]{3,2,1,0:T(8,128)(2,1)S(1)} async-done(((bf16[8,2,64,768]{3,2,1,0:T(8,128)(2,1)}), bf16[8,2,64,768]{3,2,1,0:T(8,128)(2,1)S(1)}, u32[]{:S(2)}, u32[]{:S(2)}) %all-to-all-start) | async-done | bytes 1572896 | tf_op jit(solution)/shard_map/all_to_all | solution.py:324
  58.4 1.1 copy-done
  59.5 6.9 %all-to-all-start.1 = ((bf16[8,2,64,768]{3,2,1,0:T(8,128)(2,1)}), bf16[8,2,64,768]{3,2,1,0:T(8,128)(2,1)S(1)}, u32[]{:S(2)}, u32[]{:S(2)}) async-start(bf16[8,2,64,768]{3,2,1,0:T(8,128)(2,1)} %get-tuple-element.26), calls=%async_computation.2 | async-start | bytes 3145728 | tf_op jit(solution)/shard_map/all_to_all | solution.py:353
  66.5 0.0 reduce-scatter.5.cloned.1.call-start
  66.5 0.0 copy-done.9
  66.5 0.0 copy-done.10
  66.5 0.0 copy-done.11
  66.5 0.2 select_reduce_fusion.1
  66.7 0.2 select_reduce_fusion.3
  66.9 0.1 fusion.4
  67.0 0.2 convert_reduce_fusion.1
  67.2 0.6 select_reduce_fusion.4.refs_0_
  67.8 3.1 %shard_map.124 = (bf16[4,64,768]{2,1,0:T(8,128)(2,1)}, bf16[4,64,768]{2,1,0:T(8,128)(2,1)}, bf16[4,64,768]{2,1,0:T(8,128)(2,1)}, bf16[4,64,768]{2,1,0:T(8,128)(2,1)}) custom-call(s32[16]{0:T(128)} %select_reduce_fusion.4.refs_0_, bf16[16,64,768]{2,1,0:T(8,128)(2,1)} %bitcast.7, bf16[256,1536]{1,0:T(8,128)(2,1)} %get-tuple-element.22.refs_2_), custom_call_target="tpu_custom_call" | custom-call | bytes 6291456 | tf_op jit(solution)/shard_map/pallas_call | solution.py:248
  70.8 5.4 %all-gather.3.cloned.1.call-done.refs_2_ = bf16[512,1536]{1,0:T(8,128)(2,1)} async-done(((bf16[128,1536]{1,0:T(8,128)(2,1)}), bf16[512,1536]{1,0:T(8,128)(2,1)}) %all-gather.3.cloned.1.call-update) | async-done | bytes 1572880 | tf_op jit(solution)/shard_map/all_gather | solution.py:431
  76.3 0.0 collective-permute-done.refs_1_
  76.3 9.9 %shard_map.125.refs_2_ = bf16[512,1536]{1,0:T(8,128)(2,1)} custom-call(bf16[3,1536,512]{2,1,0:T(8,128)(2,1)} %refs_0_.7, bf16[3,1536,512]{2,1,0:T(8,128)(2,1)} %collective-permute-done.refs_1_, bf16[512,1536]{1,0:T(8,128)(2,1)} %all-gather.3.cloned.1.call-done.refs_2_, bf16[4,64,768]{2,1,0:T(8,128)(2,1)} %get-tuple-element.24.refs_3_.refs_1_), custom_call_target="tpu_custom_call" | custom-call | flops 4831838208 | bytes 9437184 | tf_op jit(solution)/shard_map/pallas_call | solution.py:248
  86.2 1.8 all-to-all-done.1
  87.9 1.1 copy-done.1
  89.1 3.2 %shard_map.126 = (bf16[4,64,768]{2,1,0:T(8,128)(2,1)}, bf16[4,64,768]{2,1,0:T(8,128)(2,1)}, bf16[4,64,768]{2,1,0:T(8,128)(2,1)}, bf16[4,64,768]{2,1,0:T(8,128)(2,1)}) custom-call(s32[16]{0:T(128)} %select_reduce_fusion.4.refs_0_, bf16[16,64,768]{2,1,0:T(8,128)(2,1)} %bitcast.8, bf16[512,1536]{1,0:T(8,128)(2,1)} %shard_map.125.refs_2_), custom_call_target="tpu_custom_call" | custom-call | bytes 6291456 | tf_op jit(solution)/shard_map/pallas_call | solution.py:248
  92.3 21.4 %all-gather.5.cloned.1.call-done.refs_2_ = bf16[512,1536]{1,0:T(8,128)(2,1)} async-done(((bf16[128,1536]{1,0:T(8,128)(2,1)}), bf16[512,1536]{1,0:T(8,128)(2,1)}) %all-gather.5.cloned.1.call-update) | async-done | bytes 1572880 | tf_op jit(solution)/shard_map/all_gather | solution.py:431
  113.7 9.9 %shard_map.127.refs_5_ = bf16[512,1536]{1,0:T(8,128)(2,1)} custom-call(bf16[3,1536,512]{2,1,0:T(8,128)(2,1)} %refs_0_.7, bf16[3,1536,512]{2,1,0:T(8,128)(2,1)} %collective-permute-done.refs_1_, bf16[512,1536]{1,0:T(8,128)(2,1)} %all-gather.5.cloned.1.call-done.refs_2_, bf16[4,64,768]{2,1,0:T(8,128)(2,1)} %get-tuple-element.27.refs_3_.refs_1_), custom_call_target="tpu_custom_call" | custom-call | flops 4831838208 | bytes 9437184 | tf_op jit(solution)/shard_map/pallas_call | solution.py:248
  123.6 0.0 copy-start.14
  123.6 0.0 reduce-scatter.5.cloned.1.call-update
  123.7 0.0 reduce-scatter.3.cloned.1.call-start
  123.7 0.5 reduce-scatter.3.cloned.1.call-update
  124.3 0.4 copy-done.15
  124.6 1.2 collective-permute-start.4
  125.8 0.0 copy-done.13
  125.8 1.1 collective-permute-start.5
  127.0 0.0 copy-done.12
  127.0 1.3 collective-permute-start.6
  128.2 0.2 collective-permute-start.1
  128.4 3.0 %collective-permute-start.2 = (bf16[4,64,768]{2,1,0:T(8,128)(2,1)}, bf16[4,64,768]{2,1,0:T(8,128)(2,1)S(1)}, u32[]{:S(2)}, u32[]{:S(2)}) collective-permute-start(bf16[4,64,768]{2,1,0:T(8,128)(2,1)} %get-tuple-element.29), channel_id=1, source_target_pairs={{0,16},{8,24},{16,0},{24,8},{1,17},{9,25},{17,1},{25,9},{2,18},{10... | collective-permute-start | bytes 1179656 | tf_op jit(solution)/shard_map/ppermute | solution.py:420
  131.5 3.2 %collective-permute-done.4.refs_2_ = bf16[4,64,768]{2,1,0:T(8,128)(2,1)S(1)} collective-permute-done((bf16[4,64,768]{2,1,0:T(8,128)(2,1)S(1)}, bf16[4,64,768]{2,1,0:T(8,128)(2,1)S(1)}, u32[]{:S(2)}, u32[]{:S(2)}) %collective-permute-start.4) | collective-permute-done | bytes 393248 | tf_op jit(solution)/shard_map/ppermute | solution.py:420
  134.7 0.0 copy-done.14
  134.7 2.0 collective-permute-start.3
  136.8 0.2 convert_reduce_fusion
  136.9 0.1 dynamic_slice.6
  137.0 0.7 select_reduce_fusion.2.refs_0_
  137.7 0.1 iota_compare_fusion.3
  137.8 21.1 %collective-permute-done.5.refs_3_ = bf16[4,64,768]{2,1,0:T(8,128)(2,1)S(1)} collective-permute-done((bf16[4,64,768]{2,1,0:T(8,128)(2,1)S(1)}, bf16[4,64,768]{2,1,0:T(8,128)(2,1)S(1)}, u32[]{:S(2)}, u32[]{:S(2)}) %collective-permute-start.5) | collective-permute-done | bytes 393248 | tf_op jit(solution)/shard_map/ppermute | solution.py:420
  158.9 19.8 %collective-permute-done.6.refs_4_ = bf16[4,64,768]{2,1,0:T(8,128)(2,1)S(1)} collective-permute-done((bf16[4,64,768]{2,1,0:T(8,128)(2,1)S(1)}, bf16[4,64,768]{2,1,0:T(8,128)(2,1)S(1)}, u32[]{:S(2)}, u32[]{:S(2)}) %collective-permute-start.6) | collective-permute-done | bytes 393248 | tf_op jit(solution)/shard_map/ppermute | solution.py:420
  178.8 0.0 copy-done.6
  178.8 0.0 copy-done.7
  178.8 0.8 copy-done.8
  179.5 3.1 %shard_map.128.refs_5_ = bf16[16,64,1536]{2,1,0:T(8,128)(2,1)} custom-call(s32[16]{0:T(128)} %select_reduce_fusion.2.refs_0_, bf16[4,64,768]{2,1,0:T(8,128)(2,1)} %get-tuple-element.24.refs_3_.refs_1_, bf16[4,64,768]{2,1,0:T(8,128)(2,1)} %copy-done.6, bf16[4,64,768]{2,1,0:T(8,128)(2,1)} %copy-done.7, bf16[4,64,768]{2,1,0:T(8,128)(2,1)} %copy-done.8, ...), custom_call_target="tpu_custom_call" | custom-call | bytes 6291456 | tf_op jit(solution)/shard_map/pallas_call | solution.py:248
  182.6 0.0 copy-start.2
  182.6 1.7 collective-permute-done.1.refs_2_
  184.3 8.4 %collective-permute-done.2.refs_3_ = bf16[4,64,768]{2,1,0:T(8,128)(2,1)S(1)} collective-permute-done((bf16[4,64,768]{2,1,0:T(8,128)(2,1)}, bf16[4,64,768]{2,1,0:T(8,128)(2,1)S(1)}, u32[]{:S(2)}, u32[]{:S(2)}) %collective-permute-start.2) | collective-permute-done | bytes 393248 | tf_op jit(solution)/shard_map/ppermute | solution.py:420
  192.7 2.9 %collective-permute-done.3.refs_4_ = bf16[4,64,768]{2,1,0:T(8,128)(2,1)S(1)} collective-permute-done((bf16[4,64,768]{2,1,0:T(8,128)(2,1)S(1)}, bf16[4,64,768]{2,1,0:T(8,128)(2,1)S(1)}, u32[]{:S(2)}, u32[]{:S(2)}) %collective-permute-start.3) | collective-permute-done | bytes 393248 | tf_op jit(solution)/shard_map/ppermute | solution.py:420
  195.6 0.0 copy-done.3
  195.6 0.8 copy-done.5
  196.4 3.1 %shard_map.129 = bf16[16,64,1536]{2,1,0:T(8,128)(2,1)} custom-call(s32[16]{0:T(128)} %select_reduce_fusion.2.refs_0_, bf16[4,64,768]{2,1,0:T(8,128)(2,1)} %get-tuple-element.27.refs_3_.refs_1_, bf16[4,64,768]{2,1,0:T(8,128)(2,1)} %copy-done.3, bf16[4,64,768]{2,1,0:T(8,128)(2,1)} %copy-done.4, ...), custom_call_target="tpu_custom_call", output_to_operand_aliasing={{}: (5, {})} | custom-call | bytes 6291456 | tf_op jit(solution)/shard_map/pallas_call | solution.py:248
  199.5 0.0 reduce-scatter.5.cloned.1.call-done
  199.5 0.0 reduce-scatter.3.cloned.1.call-done
  199.5 2.3 %fusion.1 = bf16[2,128,1536]{2,1,0:T(8,128)(2,1)} fusion(bf16[2,128,1536]{2,1,0:T(8,128)(2,1)S(1)} %bitcast.9, bf16[1,128,1536]{2,1,0:T(8,128)(2,1)} %bitcast.10, bf16[1,128,1536]{2,1,0:T(8,128)(2,1)} %bitcast.11, pred[2,128]{1,0:T(4,128)(4,1)S(1)} %iota_compare_fusion.3), kind=kLoop, calls=%fused_computation.2 | loop fusion | flops 2359296 | bytes 2359552 | tf_op jit(solution)/shard_map/convert_element_type | solution.py:451
  (18 shorter events, 0.0 us)
Async XLA Ops:
  7.2 69.1 %all-gather.3.cloned.1.call-start = ((), (), s32[]{:S(2)}) async-start(), calls=%async_computation.4 | async-start | bytes 1966080 | tf_op jit(solution)/shard_map/all_gather | solution.py:431
  7.2 69.1 %collective-permute-start = (bf16[3,1536,512]{2,1,0:T(8,128)(2,1)}, bf16[3,1536,512]{2,1,0:T(8,128)(2,1)}, u32[]{:S(2)}, u32[]{:S(2)}) collective-permute-start(bf16[3,1536,512]{2,1,0:T(8,128)(2,1)} %refs_0_.7), channel_id=1, source_target_pairs={{0,1},{1,0},{2,3},{3,2},{4,5},{5,4},{6,7},{7,6},{8,9},{9,8},{10,11... | collective-permute-start | bytes 14155784 | tf_op jit(solution)/shard_map/ppermute | solution.py:301
  32.8 25.6 %all-to-all-start = ((bf16[8,2,64,768]{3,2,1,0:T(8,128)(2,1)}), bf16[8,2,64,768]{3,2,1,0:T(8,128)(2,1)S(1)}, u32[]{:S(2)}, u32[]{:S(2)}) async-start(bf16[8,2,64,768]{3,2,1,0:T(8,128)(2,1)} %get-tuple-element.21.refs_9_), calls=%async_computation | async-start | bytes 3145728 | tf_op jit(solution)/shard_map/all_to_all | solution.py:324
  36.6 77.1 %all-gather.5.cloned.1.call-start = ((), (), s32[]{:S(2)}) async-start(), calls=%async_computation.6 | async-start | bytes 1966080 | tf_op jit(solution)/shard_map/all_gather | solution.py:431
  58.4 1.1 copy-start
  58.4 8.1 %copy-start.9 = (s32[64]{0:T(128)S(1)}, s32[64]{0:T(128)}, u32[]{:S(2)}) copy-start(s32[64]{0:T(128)} %refs_0_.5) | copy-start | bytes 772
  58.4 8.1 %copy-start.10 = (s32[64]{0:T(128)S(1)}, s32[64]{0:T(128)}, u32[]{:S(2)}) copy-start(s32[64]{0:T(128)} %refs_1_.3) | copy-start | bytes 772
  58.4 8.1 %copy-start.11 = (s32[64]{0:T(128)S(1)}, s32[64]{0:T(128)}, u32[]{:S(2)}) copy-start(s32[64]{0:T(128)} %param.20) | copy-start | bytes 772
  59.5 28.4 %all-to-all-start.1 = ((bf16[8,2,64,768]{3,2,1,0:T(8,128)(2,1)}), bf16[8,2,64,768]{3,2,1,0:T(8,128)(2,1)S(1)}, u32[]{:S(2)}, u32[]{:S(2)}) async-start(bf16[8,2,64,768]{3,2,1,0:T(8,128)(2,1)} %get-tuple-element.26), calls=%async_computation.2 | async-start | bytes 3145728 | tf_op jit(solution)/shard_map/all_to_all | solution.py:353
  66.5 133.0 %reduce-scatter.5.cloned.1.call-start = ((), (), s32[]{:S(2)}) async-start(), calls=%async_computation.7 | async-start | bytes 1966080 | tf_op jit(solution)/shard_map/reduce_scatter | solution.py:439
  87.9 1.1 copy-start.1
  123.6 1.0 copy-start.15
  123.6 2.2 %copy-start.13 = (bf16[4,64,768]{2,1,0:T(8,128)(2,1)S(1)}, bf16[4,64,768]{2,1,0:T(8,128)(2,1)}, u32[]{:S(2)}) copy-start(bf16[4,64,768]{2,1,0:T(8,128)(2,1)} %get-tuple-element.32) | copy-start | bytes 1179652
  123.6 3.3 %copy-start.12 = (bf16[4,64,768]{2,1,0:T(8,128)(2,1)S(1)}, bf16[4,64,768]{2,1,0:T(8,128)(2,1)}, u32[]{:S(2)}) copy-start(bf16[4,64,768]{2,1,0:T(8,128)(2,1)} %get-tuple-element.33) | copy-start | bytes 1179652
  123.6 11.1 %copy-start.14 = (bf16[4,64,768]{2,1,0:T(8,128)(2,1)S(1)}, bf16[4,64,768]{2,1,0:T(8,128)(2,1)}, u32[]{:S(2)}) copy-start(bf16[4,64,768]{2,1,0:T(8,128)(2,1)} %get-tuple-element.30) | copy-start | bytes 1179652
  123.7 75.8 %reduce-scatter.3.cloned.1.call-start = ((), (), s32[]{:S(2)}) async-start(), calls=%async_computation.5 | async-start | bytes 1966080 | tf_op jit(solution)/shard_map/reduce_scatter | solution.py:439
  124.6 10.1 %collective-permute-start.4 = (bf16[4,64,768]{2,1,0:T(8,128)(2,1)S(1)}, bf16[4,64,768]{2,1,0:T(8,128)(2,1)S(1)}, u32[]{:S(2)}, u32[]{:S(2)}) collective-permute-start(bf16[4,64,768]{2,1,0:T(8,128)(2,1)S(1)} %copy-done.15), channel_id=1, source_target_pairs={{0,8},{8,16},{16,24},{24,0},{1,9},{9,17},{17,25},{25,1},{2,10},{10... | collective-permute-start | bytes 1179656 | tf_op jit(solution)/shard_map/ppermute | solution.py:420
  125.8 33.1 %collective-permute-start.5 = (bf16[4,64,768]{2,1,0:T(8,128)(2,1)S(1)}, bf16[4,64,768]{2,1,0:T(8,128)(2,1)S(1)}, u32[]{:S(2)}, u32[]{:S(2)}) collective-permute-start(bf16[4,64,768]{2,1,0:T(8,128)(2,1)S(1)} %copy-done.13), channel_id=1, source_target_pairs={{0,16},{8,24},{16,0},{24,8},{1,17},{9,25},{17,1},{25,9},{2,18},{10... | collective-permute-start | bytes 1179656 | tf_op jit(solution)/shard_map/ppermute | solution.py:420
  127.0 51.8 %collective-permute-start.6 = (bf16[4,64,768]{2,1,0:T(8,128)(2,1)S(1)}, bf16[4,64,768]{2,1,0:T(8,128)(2,1)S(1)}, u32[]{:S(2)}, u32[]{:S(2)}) collective-permute-start(bf16[4,64,768]{2,1,0:T(8,128)(2,1)S(1)} %copy-done.12), channel_id=1, source_target_pairs={{0,24},{8,0},{16,8},{24,16},{1,25},{9,1},{17,9},{25,17},{2,26},{10... | collective-permute-start | bytes 1179656 | tf_op jit(solution)/shard_map/ppermute | solution.py:420
  128.2 56.1 %collective-permute-start.1 = (bf16[4,64,768]{2,1,0:T(8,128)(2,1)}, bf16[4,64,768]{2,1,0:T(8,128)(2,1)S(1)}, u32[]{:S(2)}, u32[]{:S(2)}) collective-permute-start(bf16[4,64,768]{2,1,0:T(8,128)(2,1)} %get-tuple-element.28), channel_id=1, source_target_pairs={{0,8},{8,16},{16,24},{24,0},{1,9},{9,17},{17,25},{25,1},{2,10},{10... | collective-permute-start | bytes 1179656 | tf_op jit(solution)/shard_map/ppermute | solution.py:420
  128.4 64.3 %collective-permute-start.2 = (bf16[4,64,768]{2,1,0:T(8,128)(2,1)}, bf16[4,64,768]{2,1,0:T(8,128)(2,1)S(1)}, u32[]{:S(2)}, u32[]{:S(2)}) collective-permute-start(bf16[4,64,768]{2,1,0:T(8,128)(2,1)} %get-tuple-element.29), channel_id=1, source_target_pairs={{0,16},{8,24},{16,0},{24,8},{1,17},{9,25},{17,1},{25,9},{2,18},{10... | collective-permute-start | bytes 1179656 | tf_op jit(solution)/shard_map/ppermute | solution.py:420
  134.7 44.0 %copy-start.6 = (bf16[4,64,768]{2,1,0:T(8,128)(2,1)}, bf16[4,64,768]{2,1,0:T(8,128)(2,1)S(1)}, u32[]{:S(2)}) copy-start(bf16[4,64,768]{2,1,0:T(8,128)(2,1)S(1)} %collective-permute-done.4.refs_2_) | copy-start | bytes 1179652
  134.7 60.9 %collective-permute-start.3 = (bf16[4,64,768]{2,1,0:T(8,128)(2,1)S(1)}, bf16[4,64,768]{2,1,0:T(8,128)(2,1)S(1)}, u32[]{:S(2)}, u32[]{:S(2)}) collective-permute-start(bf16[4,64,768]{2,1,0:T(8,128)(2,1)S(1)} %copy-done.14), channel_id=1, source_target_pairs={{0,24},{8,0},{16,8},{24,16},{1,25},{9,1},{17,9},{25,17},{2,26},{10... | collective-permute-start | bytes 1179656 | tf_op jit(solution)/shard_map/ppermute | solution.py:420
  158.9 19.8 %copy-start.7 = (bf16[4,64,768]{2,1,0:T(8,128)(2,1)}, bf16[4,64,768]{2,1,0:T(8,128)(2,1)S(1)}, u32[]{:S(2)}) copy-start(bf16[4,64,768]{2,1,0:T(8,128)(2,1)S(1)} %collective-permute-done.5.refs_3_) | copy-start | bytes 1179652
  178.8 0.8 copy-start.8
  182.6 16.9 %copy-start.2 = (bf16[256,1536]{1,0:T(8,128)(2,1)S(1)}, bf16[256,1536]{1,0:T(8,128)(2,1)}, u32[]{:S(2)}) copy-start(bf16[256,1536]{1,0:T(8,128)(2,1)} %get-tuple-element.22.refs_2_) | copy-start | bytes 2359300
  184.3 11.3 %copy-start.3 = (bf16[4,64,768]{2,1,0:T(8,128)(2,1)}, bf16[4,64,768]{2,1,0:T(8,128)(2,1)S(1)}, u32[]{:S(2)}) copy-start(bf16[4,64,768]{2,1,0:T(8,128)(2,1)S(1)} %collective-permute-done.1.refs_2_) | copy-start | bytes 1179652
  192.7 2.9 %copy-start.4 = (bf16[4,64,768]{2,1,0:T(8,128)(2,1)}, bf16[4,64,768]{2,1,0:T(8,128)(2,1)S(1)}, u32[]{:S(2)}) copy-start(bf16[4,64,768]{2,1,0:T(8,128)(2,1)S(1)} %collective-permute-done.2.refs_3_) | copy-start | bytes 1179652
  195.6 0.8 copy-start.5
Sparse Core Ops, SparseCore 0:
  32.9 43.2 all-gather.2
  78.1 35.5 all-gather.4
  123.8 30.9 reduce-scatter.4
  157.6 30.9 reduce-scatter.2

commit v5 on v4

--- a/solution.py
+++ b/solution.py
@@ -92,11 +92,10 @@
 
 def attention_kernel(
     order, news, olds, dev, normed, cosine, sine, weight, w_value, keys, cached, tokens, gain, w_out,
-    values, residual, *rest,
+    values, residual, post, total, attended, out_weight, sems,
 ):
     step = pl.program_id(0)
     reqs, new, width = normed.shape
-    posts, (total, attended, out_weight, sems) = rest[:reqs], rest[reqs:]
     parts, _, depth, _ = keys.shape
     ctx = parts * depth
     flat = reqs * new
@@ -163,14 +162,13 @@
     def _():
         rounded = total[...].astype(bf16)
         residual[...] = rounded
-        normal = norm_value(rounded.astype(f32), gain[1:2, :])
-        for r in range(reqs):
-            posts[r][...] = normal[r * new : (r + 1) * new]
-
-
-def mlp_kernel(own, other, rows, out, total):
+        post[...] = norm_value(rounded.astype(f32), gain[1:2, :])
+
+
+def mlp_kernel(count, own, other, *refs):
+    inputs, outputs, total = refs[:count], refs[count:-1], refs[-1]
     step = pl.program_id(0)
-    values = rows[...]
+    values = jnp.concatenate([rows[...] for rows in inputs], axis=0)
     term = None
     for weights in (own, other):
         gate = jnp.dot(values, weights[0], preferred_element_type=f32)
@@ -191,7 +189,9 @@
 
     @pl.when(step == pl.num_programs(0) - 1)
     def _():
-        out[...] = total[...].astype(bf16)
+        flat = outputs[0].shape[0]
+        for i, out in enumerate(outputs):
+            out[...] = total[i * flat : (i + 1) * flat].astype(bf16)
 
 
 def move_rows(pairs, held, arrive, leave):
@@ -212,28 +212,38 @@
         copy.wait()
 
 
-def pack_kernel(picked, source, *rest):
-    targets, (held, arrive, leave) = rest[:-3], rest[-3:]
-    share = targets[0].shape[0]
-    move_rows(
-        [(source.at[picked[i]], targets[i // share].at[i % share]) for i in range(held.shape[0])],
-        held, arrive, leave,
-    )
-
-
-def unpack_kernel(columns, count, spots, *refs):
+def pack_kernel(groups, share, count, passed, picked, group, source, *rest):
+    held, arrive, leave = rest[-3:]
+    targets = rest[passed : passed + count]
+    pairs = []
+    for i in range(groups * share):
+        if count > 1:
+            target = targets[i // share].at[i % share]
+        else:
+            goal = lax.rem(group[0] + i // share, groups)
+            target = targets[0].at[goal * share + i % share]
+        pairs.append((source.at[picked[i]], target))
+    move_rows(pairs, held, arrive, leave)
+
+
+def unpack_kernel(columns, groups, share, count, spots, group, *refs):
     sources, (target, held, arrive, leave) = refs[:count], refs[-4:]
-    share, _, width = sources[0].shape
-    move_rows(
-        [
-            (
-                sources[i // share].at[i % share],
-                target.at[spots[i], :, pl.ds(columns, width)],
-            )
-            for i in range(held.shape[0])
-        ],
-        held, arrive, leave,
-    )
+    width = sources[0].shape[-1]
+    pairs = []
+    for i in range(groups * share):
+        if count > 1:
+            source = sources[i // share].at[i % share]
+        else:
+            origin = lax.rem(group[0] + groups - i // share, groups)
+            source = sources[0].at[origin * share + i % share]
+        pairs.append((source, target.at[spots[i], :, pl.ds(columns, width)]))
+    move_rows(pairs, held, arrive, leave)
+
+
+def cut_kernel(first, second, *halves):
+    middle = first.shape[0] // 2
+    halves[0][...] = second[:middle]
+    halves[1][...] = first[middle:]
 
 
 def call(
@@ -322,7 +332,7 @@
         8 << 20,
     )
     keys_moved = lax.all_to_all(keys, tensor, split_axis=0, concat_axis=0, tiled=True)
-    values, residual, *posts = call(
+    values, residual, post = call(
         attention_kernel,
         scalars,
         (groups,),
@@ -338,8 +348,8 @@
             whole(norm_gains.shape),
             pl.BlockSpec(memory_space=pl.ANY),
         ],
-        [context_spec, whole((flat, width))] + [whole((new, width))] * reqs,
-        [shape(context_shape), shape((flat, width))] + [shape((new, width))] * reqs,
+        [context_spec, whole((flat, width)), whole((flat, width))],
+        [shape(context_shape), shape((flat, width)), shape((flat, width))],
         [
             pltpu.VMEM((flat, width), f32),
             pltpu.VMEM((flat, 2 * GROUP), bf16),
@@ -350,24 +360,22 @@
         12 * flat * width * width,
         16 << 20,
     )
-    values_moved = lax.all_to_all(values, tensor, split_axis=0, concat_axis=0, tiled=True)
-
     units = mlp_weights.shape[2]
     chunk = 256 if units % 256 == 0 else units
 
-    def mlp(rows, after):
-        count = rows.shape[0]
+    def mlp(pieces, after):
+        total_rows = sum(rows.shape[0] for rows in pieces)
         weight_spec = pl.BlockSpec((3, width, chunk), lambda c: (0, 0, c))
         return call(
-            mlp_kernel,
+            functools.partial(mlp_kernel, len(pieces)),
             (),
             (units // chunk,),
-            [weight_spec] * 2 + [whole((count, width))],
-            whole((count, width)),
-            shape((count, width)),
-            [pltpu.VMEM((count, width), f32)],
-            (mlp_weights, other_weights, rows),
-            12 * count * width * units,
+            [weight_spec] * 2 + [whole(rows.shape) for rows in pieces],
+            [whole((flat, width))] * (total_rows // flat),
+            [shape((flat, width))] * (total_rows // flat),
+            [pltpu.VMEM((total_rows, width), f32)],
+            (mlp_weights, other_weights, *pieces),
+            12 * total_rows * width * units,
             12 * width * units,
             after=after,
         )
@@ -408,47 +416,72 @@
         [(g, (g + s) % group_total) for g in range(group_total)] for s in range(1, group_total)
     ]
 
-    def pack(moved, after):
+    group = group_index.astype(jnp.int32).reshape(1)
+
+    def pack(moved, targets, passed, after):
         return call(
-            pack_kernel, (picked,), (1,), [anywhere], [anywhere] * group_total,
-            [shape(piece)] * group_total, sems, (moved.reshape(group_reqs, depth, key_width),),
-            after=after,
+            functools.partial(pack_kernel, group_total, share, len(targets), len(passed)),
+            (picked, group), (1,),
+            [anywhere] * (1 + len(passed)), [anywhere] * (len(targets) + len(passed)),
+            [shape(dims) for dims in targets] + [shape(rows.shape) for rows in passed], sems,
+            (moved.reshape(group_reqs, depth, key_width), *passed),
+            aliases={3 + i: len(targets) + i for i in range(len(passed))}, after=after,
         )
-
-    def across(packed):
-        return [packed[0]] + [
-            lax.ppermute(rows, "dp", pairs) for rows, pairs in zip(packed[1:], shifts)
-        ]
 
     def unpack(columns, arrived, target, after):
         return call(
-            functools.partial(unpack_kernel, columns, group_total), (spots,), (1,),
-            [anywhere] * (group_total + len(target)), anywhere,
+            functools.partial(unpack_kernel, columns, group_total, share, len(arrived)),
+            (spots, group), (1,), [anywhere] * (len(arrived) + len(target)), anywhere,
             shape((group_reqs, depth, 2 * key_width)), sems, (*arrived, *target),
-            aliases={1 + group_total: 0} if target else {}, after=after,
+            aliases={2 + len(arrived): 0} if target else {}, after=after,
         )
 
-    gathered = [lax.all_gather(rows, "chip", axis=0, tiled=True) for rows in posts]
-    keys_packed = pack(keys_moved, (residual,))
-    keys_arrived = across(keys_packed)
-    latest = keys_packed[0]
-    sums = []
-    values_arrived = None
-    for rows in gathered:
-        partial = mlp(rows, (latest,))
-        sums.append(lax.psum_scatter(partial, "chip", scatter_dimension=0, tiled=True))
-        latest = partial
-        if values_arrived is None:
-            values_packed = pack(values_moved, (latest,))
-            values_arrived = across(values_packed)
-            latest = values_packed[0]
-    kv_half = unpack(0, keys_arrived, (), (latest,))
-    kv_decode = unpack(key_width, values_arrived, (kv_half,), ())
+    def swap(rows, mask):
+        return lax.ppermute(rows, "chip", [(c, c ^ mask) for c in range(chips)])
+
+    masks = [1, 2] if chips == 4 else range(1, chips)
+    gathered = [swap(post, mask) for mask in masks]
+    *keys_packed, values = pack(
+        keys_moved, [piece] * group_total, (values,), (post, other_weights)
+    )
+    values_moved = lax.all_to_all(values, tensor, split_axis=0, concat_axis=0, tiled=True)
+    keys_arrived = [keys_packed[0]] + [
+        lax.ppermute(rows, "dp", pairs) for rows, pairs in zip(keys_packed[1:], shifts)
+    ]
+    partials = list(mlp([post], (keys_packed[0],)))
+    latest = partials[0]
+    if chips == 4:
+        half = (flat // 2, width)
+        halves = call(
+            cut_kernel, (), (1,), [whole((flat, width))] * 2, [whole(half)] * 2, [shape(half)] * 2,
+            [], tuple(gathered), after=(latest,),
+        )
+        latest = halves[0]
+        batches = [([1, 2], gathered), ([3], [swap(halves[0], 1), swap(halves[1], 2)])]
+    else:
+        batches = [([mask], [rows]) for mask, rows in zip(masks, gathered)]
+    values_packed = None
+    for batch_masks, pieces in batches:
+        results = mlp(pieces, (latest,))
+        latest = results[0]
+        partials += [swap(rows, mask) for mask, rows in zip(batch_masks, results)]
+        if values_packed is None:
+            values_packed = pack(
+                values_moved, [(group_reqs, depth, key_width)], (), (latest,)
+            )[0]
+            values_arrived = lax.all_to_all(
+                values_packed, "dp", split_axis=0, concat_axis=0, tiled=True
+            )
+            kv_half = unpack(0, keys_arrived, (), (values_packed,))
+            latest = kv_half
+    kv_decode = unpack(key_width, [values_arrived], (kv_half,), ())
 
     own_counts = lax.dynamic_slice_in_dim(count_of, device * reqs, reqs)
-    live = jnp.arange(new, dtype=jnp.int32)[None, :, None] < own_counts[:, None, None]
-    total = residual.reshape(reqs, new, width).astype(f32) + jnp.stack(sums).astype(f32)
-    layer_out = jnp.where(live, total, 0.0).astype(bf16)
+    live = (jnp.arange(new, dtype=jnp.int32)[None, :] < own_counts[:, None]).reshape(flat, 1)
+    total = residual.astype(f32)
+    for partial in partials:
+        total = total + partial.astype(f32)
+    layer_out = jnp.where(live, total, 0.0).astype(bf16).reshape(reqs, new, width)
     return (layer_out, kv_decode)
 
 

time: 209 us -> 211 us (level)
  the two profiles are of different devices: /device:TPU:9 before, /device:TPU:24 now
where the time goes in v5:
time: 211 us; the launch traced here: 210 us
  waiting for transfers between devices  111 us (53%)
  Pallas kernels  62.8 us (30%)
  starting transfers between devices  24 us (11%)
  local copies, waits for them, and re-layouts  6.65 us (3%)
  other arithmetic  5.36 us (3%)
    pallas_call x10, Pallas kernels, call(): pl.pallas_call(ordered, out_shape=out_shape, grid_spec=pltpu.PrefetchScal...  62.8 us
    ppermute x3, waiting for transfers between devices, local(): lax.ppermute(rows, 'dp', pairs)  62.1 us
    ppermute x7, waiting for transfers between devices, swap(): return lax.ppermute(rows, 'chip', [(c, c ^ mask) for c in range(chips)])  47.3 us
    ppermute x7, starting transfers between devices, swap(): return lax.ppermute(rows, 'chip', [(c, c ^ mask) for c in range(chips)])  8.23 us
    unnamed x32, local copies, waits for them, and re-layouts  6.58 us
    all_to_all x1, starting transfers between devices, local(): lax.all_to_all(values_packed, 'dp', split_axis=0, concat_axis=0, tiled=True)  5.23 us
  transfers between devices with their start and end apart: 14, of which 5 were waited for; matrix products, arithmetic and copies ran while one was open for 3% of the time, Pallas kernels for 25%

profile of v5, /device:TPU:24, one launch (start us, length us, event | category | flops | bytes accessed | tf_op | source)
XLA Modules:
  0.0 210.5 jit_solution(7600188242676024283)
XLA Ops:
  0.6 0.1 collective-permute-start
  0.7 6.4 %shard_map.122 = (bf16[8,2,64,768]{3,2,1,0:T(8,128)(2,1)}, bf16[2,128,1536]{2,1,0:T(8,128)(2,1)}, f32[2,128,384]{2,1,0:T(8,128)}, f32[2,128,384]{2,1,0:T(8,128)}) custom-call(s32[64]{0:T(128)} %refs_0_.6, s32[64]{0:T(128)} %refs_1_.3, s32[64]{0:T(128)} %refs_2_.3, s32[1]{0:T(128)} %bitcast.1.refs_3_, bf16[2,128,1536]{2,1,0:T(8,128)(2,1)} %refs_11_.1, ...), custom_call_target="tpu_custom_call" | custom-call | flops 603979776 | bytes 8388608 | tf_op jit(solution)/shard_map/pallas_call | solution.py:258
  7.1 0.0 copy-start.14
  7.2 3.9 %all-to-all-start = ((bf16[8,2,64,768]{3,2,1,0:T(8,128)(2,1)}), bf16[8,2,64,768]{3,2,1,0:T(8,128)(2,1)S(1)}, u32[]{:S(2)}, u32[]{:S(2)}) async-start(bf16[8,2,64,768]{3,2,1,0:T(8,128)(2,1)} %get-tuple-element.21.refs_9_), calls=%async_computation | async-start | bytes 3145728 | tf_op jit(solution)/shard_map/all_to_all | solution.py:334
  11.1 0.0 copy-done.12
  11.1 0.0 copy-done.13
  11.1 0.0 copy-done.14
  11.2 0.2 select_reduce_fusion.1
  11.3 0.2 select_reduce_fusion.3
  11.5 0.1 fusion.2
  11.6 0.2 convert_reduce_fusion.1
  11.8 0.7 select_reduce_fusion.4.refs_0_
  12.5 18.4 %shard_map.123 = (bf16[8,2,64,768]{3,2,1,0:T(8,128)(2,1)}, bf16[256,1536]{1,0:T(8,128)(2,1)}, bf16[256,1536]{1,0:T(8,128)(2,1)}) custom-call(s32[64]{0:T(128)} %refs_0_.6, s32[64]{0:T(128)} %refs_1_.3, s32[64]{0:T(128)} %refs_2_.3, s32[1]{0:T(128)} %bitcast.1.refs_3_, bf16[2,128,1536]{2,1,0:T(8,128)(2,1)} %get-tuple-element.18.refs_4_, ...), custom_call_target="tpu_custom_call" | custom-call | flops 7247757312 | bytes 16777216 | tf_op jit(solution)/shard_map/pallas_call | solution.py:258
  30.9 1.2 all-to-all-done
  32.1 0.0 collective-permute-done.refs_5_.refs_1_
  32.1 1.1 copy-done.1
  33.3 3.1 %shard_map.124 = (bf16[4,64,768]{2,1,0:T(8,128)(2,1)}, bf16[4,64,768]{2,1,0:T(8,128)(2,1)}, bf16[4,64,768]{2,1,0:T(8,128)(2,1)}, bf16[4,64,768]{2,1,0:T(8,128)(2,1)}, bf16[8,2,64,768]{3,2,1,0:T(8,128)(2,1)}) custom-call(s32[16]{0:T(128)} %select_reduce_fusion.4.refs_0_, s32[1]{0:T(128)} %bitcast.2.refs_1_, ...), custom_call_target="tpu_custom_call", output_to_operand_aliasing={{4}: (3, {})} | custom-call | bytes 6291456 | tf_op jit(solution)/shard_map/pallas_call | solution.py:258
  36.4 0.0 copy-start.4
  36.4 3.9 %all-to-all-start.1 = ((bf16[8,2,64,768]{3,2,1,0:T(8,128)(2,1)}), bf16[8,2,64,768]{3,2,1,0:T(8,128)(2,1)S(1)}, u32[]{:S(2)}, u32[]{:S(2)}) async-start(bf16[8,2,64,768]{3,2,1,0:T(8,128)(2,1)} %get-tuple-element.33), calls=%async_computation.1 | async-start | bytes 3145728 | tf_op jit(solution)/shard_map/all_to_all | solution.py:447
  40.3 0.0 copy-done.4
  40.3 1.7 collective-permute-start.1
  42.0 1.5 collective-permute-start.2
  43.5 6.7 %shard_map.125.refs_2_ = bf16[256,1536]{1,0:T(8,128)(2,1)} custom-call(bf16[3,1536,512]{2,1,0:T(8,128)(2,1)} %refs_0_.9, bf16[3,1536,512]{2,1,0:T(8,128)(2,1)} %collective-permute-done.refs_5_.refs_1_, bf16[256,1536]{1,0:T(8,128)(2,1)} %get-tuple-element.23.refs_4_.refs_2_, bf16[4,64,768]{2,1,0:T(8,128)(2,1)} %get-tuple-element.25.refs_3_.refs_2_), custom_call_target="tpu_custom_call" | custom-call | flops 2415919104 | bytes 9437184 | tf_op jit(solution)/shard_map/pallas_call | solution.py:258
  50.3 26.8 %collective-permute-done.1.refs_0_.refs_2_ = bf16[256,1536]{1,0:T(8,128)(2,1)S(1)} collective-permute-done((bf16[256,1536]{1,0:T(8,128)(2,1)S(1)}, bf16[256,1536]{1,0:T(8,128)(2,1)S(1)}, u32[]{:S(2)}, u32[]{:S(2)}) %collective-permute-start.1) | collective-permute-done | bytes 786464 | tf_op jit(solution)/shard_map/ppermute | solution.py:440
  77.0 0.0 collective-permute-done.2.refs_1_.refs_3_
  77.1 0.9 copy-done.6
  77.9 2.3 %shard_map.126 = (bf16[128,1536]{1,0:T(8,128)(2,1)}, bf16[128,1536]{1,0:T(8,128)(2,1)}) custom-call(bf16[256,1536]{1,0:T(8,128)(2,1)} %copy-done.6, bf16[256,1536]{1,0:T(8,128)(2,1)} %collective-permute-done.2.refs_1_.refs_3_, bf16[256,1536]{1,0:T(8,128)(2,1)} %shard_map.125.refs_2_), custom_call_target="tpu_custom_call" | custom-call | bytes 6291456 | tf_op jit(solution)/shard_map/pallas_call | solution.py:258
  80.2 9.9 %shard_map.127 = (bf16[256,1536]{1,0:T(8,128)(2,1)}, bf16[256,1536]{1,0:T(8,128)(2,1)}) custom-call(bf16[3,1536,512]{2,1,0:T(8,128)(2,1)} %refs_0_.9, bf16[3,1536,512]{2,1,0:T(8,128)(2,1)} %collective-permute-done.refs_5_.refs_1_, bf16[256,1536]{1,0:T(8,128)(2,1)} %copy-done.6, bf16[256,1536]{1,0:T(8,128)(2,1)} %collective-permute-done.2.refs_1_.refs_3_, ...), custom_call_target="tpu_custom_call" | custom-call | flops 4831838208 | bytes 9437184 | tf_op jit(solution)/shard_map/pallas_call | solution.py:258
  90.1 0.0 all-to-all-done.1
  90.1 1.1 copy-done.2
  91.3 3.1 %shard_map.128.refs_6_ = bf16[16,64,768]{2,1,0:T(8,128)(2,1)} custom-call(s32[16]{0:T(128)} %select_reduce_fusion.4.refs_0_, s32[1]{0:T(128)} %bitcast.2.refs_1_, bf16[16,64,768]{2,1,0:T(8,128)(2,1)} %bitcast.8, bf16[256,1536]{1,0:T(8,128)(2,1)} %get-tuple-element.27.refs_3_), custom_call_target="tpu_custom_call" | custom-call | bytes 6291456 | tf_op jit(solution)/shard_map/pallas_call | solution.py:258
  94.4 5.2 %all-to-all-start.2 = ((bf16[16,64,768]{2,1,0:T(8,128)(2,1)}), bf16[16,64,768]{2,1,0:T(8,128)(2,1)S(1)}, u32[]{:S(2)}, u32[]{:S(2)}) async-start(bf16[16,64,768]{2,1,0:T(8,128)(2,1)} %shard_map.128.refs_6_), calls=%async_computation.2 | async-start | bytes 3145728 | tf_op jit(solution)/shard_map/all_to_all | solution.py:472
  99.6 0.0 collective-permute-start.7
  99.7 2.0 collective-permute-start.8
  101.7 0.6 collective-permute-start.9
  102.2 0.6 collective-permute-start.5
  102.8 1.4 collective-permute-start.6
  104.3 0.2 convert_reduce_fusion
  104.4 0.7 select_reduce_fusion.2.refs_0_
  105.1 29.7 %collective-permute-done.7.refs_3_ = bf16[4,64,768]{2,1,0:T(8,128)(2,1)S(1)} collective-permute-done((bf16[4,64,768]{2,1,0:T(8,128)(2,1)}, bf16[4,64,768]{2,1,0:T(8,128)(2,1)S(1)}, u32[]{:S(2)}, u32[]{:S(2)}) %collective-permute-start.7) | collective-permute-done | bytes 393248 | tf_op jit(solution)/shard_map/ppermute | solution.py:449
  134.9 0.6 collective-permute-start.3
  135.4 32.4 %collective-permute-done.8.refs_4_ = bf16[4,64,768]{2,1,0:T(8,128)(2,1)S(1)} collective-permute-done((bf16[4,64,768]{2,1,0:T(8,128)(2,1)}, bf16[4,64,768]{2,1,0:T(8,128)(2,1)S(1)}, u32[]{:S(2)}, u32[]{:S(2)}) %collective-permute-start.8) | collective-permute-done | bytes 393248 | tf_op jit(solution)/shard_map/ppermute | solution.py:449
  167.9 1.4 collective-permute-start.4
  169.2 0.0 collective-permute-done.9.refs_5_
  169.3 0.8 copy-done.11
  170.0 3.1 %shard_map.129.refs_4_.refs_3_ = bf16[16,64,1536]{2,1,0:T(8,128)(2,1)} custom-call(s32[16]{0:T(128)} %select_reduce_fusion.2.refs_0_, s32[1]{0:T(128)} %bitcast.2.refs_1_, bf16[4,64,768]{2,1,0:T(8,128)(2,1)} %get-tuple-element.25.refs_3_.refs_2_, bf16[4,64,768]{2,1,0:T(8,128)(2,1)} %copy-done.9, bf16[4,64,768]{2,1,0:T(8,128)(2,1)} %copy-done.10, ...), custom_call_target="tpu_custom_call" | custom-call | bytes 6291456 | tf_op jit(solution)/shard_map/pallas_call | solution.py:258
  173.1 0.0 copy-start
  173.1 0.0 copy-start.5
  173.1 0.0 collective-permute-done.5.refs_2_
  173.1 0.0 collective-permute-done.6.refs_3_
  173.1 0.7 copy-done.7
  173.9 0.7 copy-done.8
  174.6 6.7 %shard_map.130 = bf16[256,1536]{1,0:T(8,128)(2,1)} custom-call(bf16[3,1536,512]{2,1,0:T(8,128)(2,1)} %refs_0_.9, bf16[3,1536,512]{2,1,0:T(8,128)(2,1)} %collective-permute-done.refs_5_.refs_1_, bf16[128,1536]{1,0:T(8,128)(2,1)} %copy-done.7, bf16[128,1536]{1,0:T(8,128)(2,1)} %copy-done.8, bf16[16,64,1536]{2,1,0:T(8,128)(2,1)} %shard_map.129.refs_4_.refs_3_), custom_call_target="tpu_custom_call" | custom-call | flops 2415919104 | bytes 9437184 | tf_op jit(solution)/shard_map/pallas_call | solution.py:258
  181.3 1.0 collective-permute-start.10
  182.3 0.1 dynamic_slice.6
  182.4 0.1 compare_bitcast_fusion
  182.5 20.5 %collective-permute-done.4 = bf16[256,1536]{1,0:T(8,128)(2,1)} collective-permute-done((bf16[256,1536]{1,0:T(8,128)(2,1)}, bf16[256,1536]{1,0:T(8,128)(2,1)}, u32[]{:S(2)}, u32[]{:S(2)}) %collective-permute-start.4) | collective-permute-done | bytes 786464 | tf_op jit(solution)/shard_map/ppermute | solution.py:440
  203.0 0.0 collective-permute-done.3
  203.0 0.0 collective-permute-done.10
  203.0 0.0 copy-done.5
  203.0 3.1 %select_convert_fusion = bf16[256,1536]{1,0:T(8,128)(2,1)} fusion(bf16[256,1536]{1,0:T(8,128)(2,1)} %collective-permute-done.10, bf16[256,1536]{1,0:T(8,128)(2,1)} %collective-permute-done.4, bf16[256,1536]{1,0:T(8,128)(2,1)} %collective-permute-done.3, bf16[256,1536]{1,0:T(8,128)(2,1)S(1)} %copy-done, bf16[256,1536]{1,0:T(8,128)(2,1)S(1)} %copy-done.5, ...), kind=kLoop, calls=%fused_computation | loop fusion | flops 4325376 | bytes 4718848 | tf_op jit(solution)/shard_map/convert_element_type | solution.py:484
  206.1 0.0 all-to-all-done.2.refs_2_
  206.1 1.2 copy-done.3
  207.3 3.1 %shard_map.131 = bf16[16,64,1536]{2,1,0:T(8,128)(2,1)} custom-call(s32[16]{0:T(128)} %select_reduce_fusion.2.refs_0_, s32[1]{0:T(128)} %bitcast.2.refs_1_, bf16[16,64,768]{2,1,0:T(8,128)(2,1)} %copy-done.3, bf16[16,64,1536]{2,1,0:T(8,128)(2,1)} %shard_map.129.refs_4_.refs_3_), custom_call_target="tpu_custom_call", output_to_operand_aliasing={{}: (3, {})} | custom-call | bytes 6291456 | tf_op jit(solution)/shard_map/pallas_call | solution.py:258
  (18 shorter events, 0.0 us)
Async XLA Ops:
  0.6 31.5 %collective-permute-start = (bf16[3,1536,512]{2,1,0:T(8,128)(2,1)}, bf16[3,1536,512]{2,1,0:T(8,128)(2,1)}, u32[]{:S(2)}, u32[]{:S(2)}) collective-permute-start(bf16[3,1536,512]{2,1,0:T(8,128)(2,1)} %refs_0_.9), channel_id=1, source_target_pairs={{0,1},{1,0},{2,3},{3,2},{4,5},{5,4},{6,7},{7,6},{8,9},{9,8},{10,11... | collective-permute-start | bytes 14155784 | tf_op jit(solution)/shard_map/ppermute | solution.py:311
  7.1 4.0 %copy-start.12 = (s32[64]{0:T(128)S(1)}, s32[64]{0:T(128)}, u32[]{:S(2)}) copy-start(s32[64]{0:T(128)} %refs_0_.6) | copy-start | bytes 772
  7.1 4.0 %copy-start.13 = (s32[64]{0:T(128)S(1)}, s32[64]{0:T(128)}, u32[]{:S(2)}) copy-start(s32[64]{0:T(128)} %refs_1_.3) | copy-start | bytes 772
  7.1 4.0 %copy-start.14 = (s32[64]{0:T(128)S(1)}, s32[64]{0:T(128)}, u32[]{:S(2)}) copy-start(s32[64]{0:T(128)} %param.20) | copy-start | bytes 772
  7.2 25.0 %all-to-all-start = ((bf16[8,2,64,768]{3,2,1,0:T(8,128)(2,1)}), bf16[8,2,64,768]{3,2,1,0:T(8,128)(2,1)S(1)}, u32[]{:S(2)}, u32[]{:S(2)}) async-start(bf16[8,2,64,768]{3,2,1,0:T(8,128)(2,1)} %get-tuple-element.21.refs_9_), calls=%async_computation | async-start | bytes 3145728 | tf_op jit(solution)/shard_map/all_to_all | solution.py:334
  32.1 1.1 copy-start.1
  36.4 3.9 %copy-start.4 = (bf16[256,1536]{1,0:T(8,128)(2,1)S(1)}, bf16[256,1536]{1,0:T(8,128)(2,1)}, u32[]{:S(2)}) copy-start(bf16[256,1536]{1,0:T(8,128)(2,1)} %get-tuple-element.23.refs_4_.refs_2_) | copy-start | bytes 2359300
  36.4 53.8 %all-to-all-start.1 = ((bf16[8,2,64,768]{3,2,1,0:T(8,128)(2,1)}), bf16[8,2,64,768]{3,2,1,0:T(8,128)(2,1)S(1)}, u32[]{:S(2)}, u32[]{:S(2)}) async-start(bf16[8,2,64,768]{3,2,1,0:T(8,128)(2,1)} %get-tuple-element.33), calls=%async_computation.1 | async-start | bytes 3145728 | tf_op jit(solution)/shard_map/all_to_all | solution.py:447
  40.3 36.7 %collective-permute-start.1 = (bf16[256,1536]{1,0:T(8,128)(2,1)S(1)}, bf16[256,1536]{1,0:T(8,128)(2,1)S(1)}, u32[]{:S(2)}, u32[]{:S(2)}) collective-permute-start(bf16[256,1536]{1,0:T(8,128)(2,1)S(1)} %copy-done.4), channel_id=1, source_target_pairs={{0,2},{2,0},{4,6},{6,4},{1,3},{3,1},{5,7},{7,5},{8,10},{10,8},{12,... | collective-permute-start | bytes 2359304 | tf_op jit(solution)/shard_map/ppermute | solution.py:440
  42.0 35.0 %collective-permute-start.2 = (bf16[256,1536]{1,0:T(8,128)(2,1)S(1)}, bf16[256,1536]{1,0:T(8,128)(2,1)}, u32[]{:S(2)}, u32[]{:S(2)}) collective-permute-start(bf16[256,1536]{1,0:T(8,128)(2,1)S(1)} %copy-done.4), channel_id=1, source_target_pairs={{0,4},{2,6},{4,0},{6,2},{1,5},{3,7},{5,1},{7,3},{8,12},{10,14},{12... | collective-permute-start | bytes 2359304 | tf_op jit(solution)/shard_map/ppermute | solution.py:440
  77.0 0.9 copy-start.6
  90.1 1.1 copy-start.2
  94.4 7.3 %copy-start.15 = (bf16[4,64,768]{2,1,0:T(8,128)(2,1)S(1)}, bf16[4,64,768]{2,1,0:T(8,128)(2,1)}, u32[]{:S(2)}) copy-start(bf16[4,64,768]{2,1,0:T(8,128)(2,1)} %get-tuple-element.32) | copy-start | bytes 1179652
  94.4 111.7 %all-to-all-start.2 = ((bf16[16,64,768]{2,1,0:T(8,128)(2,1)}), bf16[16,64,768]{2,1,0:T(8,128)(2,1)S(1)}, u32[]{:S(2)}, u32[]{:S(2)}) async-start(bf16[16,64,768]{2,1,0:T(8,128)(2,1)} %shard_map.128.refs_6_), calls=%async_computation.2 | async-start | bytes 3145728 | tf_op jit(solution)/shard_map/all_to_all | solution.py:472
  99.6 35.2 %collective-permute-start.7 = (bf16[4,64,768]{2,1,0:T(8,128)(2,1)}, bf16[4,64,768]{2,1,0:T(8,128)(2,1)S(1)}, u32[]{:S(2)}, u32[]{:S(2)}) collective-permute-start(bf16[4,64,768]{2,1,0:T(8,128)(2,1)} %get-tuple-element.30), channel_id=1, source_target_pairs={{0,8},{8,16},{16,24},{24,0},{1,9},{9,17},{17,25},{25,1},{2,10},{10... | collective-permute-start | bytes 1179656 | tf_op jit(solution)/shard_map/ppermute | solution.py:449
  99.7 68.2 %collective-permute-start.8 = (bf16[4,64,768]{2,1,0:T(8,128)(2,1)}, bf16[4,64,768]{2,1,0:T(8,128)(2,1)S(1)}, u32[]{:S(2)}, u32[]{:S(2)}) collective-permute-start(bf16[4,64,768]{2,1,0:T(8,128)(2,1)} %get-tuple-element.31), channel_id=1, source_target_pairs={{0,16},{8,24},{16,0},{24,8},{1,17},{9,25},{17,1},{25,9},{2,18},{10... | collective-permute-start | bytes 1179656 | tf_op jit(solution)/shard_map/ppermute | solution.py:449
  101.7 67.6 %collective-permute-start.9 = (bf16[4,64,768]{2,1,0:T(8,128)(2,1)S(1)}, bf16[4,64,768]{2,1,0:T(8,128)(2,1)S(1)}, u32[]{:S(2)}, u32[]{:S(2)}) collective-permute-start(bf16[4,64,768]{2,1,0:T(8,128)(2,1)S(1)} %copy-done.15), channel_id=1, source_target_pairs={{0,24},{8,0},{16,8},{24,16},{1,25},{9,1},{17,9},{25,17},{2,26},{10... | collective-permute-start | bytes 1179656 | tf_op jit(solution)/shard_map/ppermute | solution.py:449
  102.2 70.9 %collective-permute-start.5 = (bf16[128,1536]{1,0:T(8,128)(2,1)}, bf16[128,1536]{1,0:T(8,128)(2,1)S(1)}, u32[]{:S(2)}, u32[]{:S(2)}) collective-permute-start(bf16[128,1536]{1,0:T(8,128)(2,1)} %get-tuple-element.26.refs_4_), channel_id=1, source_target_pairs={{0,2},{2,0},{4,6},{6,4},{1,3},{3,1},{5,7},{7,5},{8,10},{10,8},{12,... | collective-permute-start | bytes 1179656 | tf_op jit(solution)/shard_map/ppermute | solution.py:440
  102.8 70.3 %collective-permute-start.6 = (bf16[128,1536]{1,0:T(8,128)(2,1)}, bf16[128,1536]{1,0:T(8,128)(2,1)S(1)}, u32[]{:S(2)}, u32[]{:S(2)}) collective-permute-start(bf16[128,1536]{1,0:T(8,128)(2,1)} %get-tuple-element.29), channel_id=1, source_target_pairs={{0,4},{2,6},{4,0},{6,2},{1,5},{3,7},{5,1},{7,3},{8,12},{10,14},{12... | collective-permute-start | bytes 1179656 | tf_op jit(solution)/shard_map/ppermute | solution.py:440
  134.9 34.4 %copy-start.9 = (bf16[4,64,768]{2,1,0:T(8,128)(2,1)}, bf16[4,64,768]{2,1,0:T(8,128)(2,1)S(1)}, u32[]{:S(2)}) copy-start(bf16[4,64,768]{2,1,0:T(8,128)(2,1)S(1)} %collective-permute-done.7.refs_3_) | copy-start | bytes 1179652
  134.9 68.2 %collective-permute-start.3 = (bf16[256,1536]{1,0:T(8,128)(2,1)}, bf16[256,1536]{1,0:T(8,128)(2,1)}, u32[]{:S(2)}, u32[]{:S(2)}) collective-permute-start(bf16[256,1536]{1,0:T(8,128)(2,1)} %get-tuple-element.27.refs_3_), channel_id=1, source_target_pairs={{0,2},{2,0},{4,6},{6,4},{1,3},{3,1},{5,7},{7,5},{8,10},{10,8},{12,... | collective-permute-start | bytes 2359304 | tf_op jit(solution)/shard_map/ppermute | solution.py:440
  167.9 1.4 copy-start.10
  167.9 35.2 %collective-permute-start.4 = (bf16[256,1536]{1,0:T(8,128)(2,1)}, bf16[256,1536]{1,0:T(8,128)(2,1)}, u32[]{:S(2)}, u32[]{:S(2)}) collective-permute-start(bf16[256,1536]{1,0:T(8,128)(2,1)} %get-tuple-element.28), channel_id=1, source_target_pairs={{0,4},{2,6},{4,0},{6,2},{1,5},{3,7},{5,1},{7,3},{8,12},{10,14},{12... | collective-permute-start | bytes 2359304 | tf_op jit(solution)/shard_map/ppermute | solution.py:440
  169.3 0.8 copy-start.11
  173.1 29.9 %copy-start = (bf16[256,1536]{1,0:T(8,128)(2,1)S(1)}, bf16[256,1536]{1,0:T(8,128)(2,1)}, u32[]{:S(2)}) copy-start(bf16[256,1536]{1,0:T(8,128)(2,1)} %shard_map.125.refs_2_) | copy-start | bytes 2359300
  173.1 29.9 %copy-start.5 = (bf16[256,1536]{1,0:T(8,128)(2,1)S(1)}, bf16[256,1536]{1,0:T(8,128)(2,1)}, u32[]{:S(2)}) copy-start(bf16[256,1536]{1,0:T(8,128)(2,1)} %get-tuple-element.22) | copy-start | bytes 2359300
  173.1 0.7 copy-start.7
  173.9 0.7 copy-start.8
  181.3 21.7 %collective-permute-start.10 = (bf16[256,1536]{1,0:T(8,128)(2,1)}, bf16[256,1536]{1,0:T(8,128)(2,1)}, u32[]{:S(2)}, u32[]{:S(2)}) collective-permute-start(bf16[256,1536]{1,0:T(8,128)(2,1)} %shard_map.130), channel_id=1, source_target_pairs={{0,6},{2,4},{4,2},{6,0},{1,7},{3,5},{5,3},{7,1},{8,14},{10,12},{12... | collective-permute-start | bytes 2359304 | tf_op jit(solution)/shard_map/ppermute | solution.py:440
  206.1 1.2 copy-start.3

commit v6 on v5

--- a/solution.py
+++ b/solution.py
@@ -449,30 +449,29 @@
         lax.ppermute(rows, "dp", pairs) for rows, pairs in zip(keys_packed[1:], shifts)
     ]
     partials = list(mlp([post], (keys_packed[0],)))
-    latest = partials[0]
+    values_packed = pack(
+        values_moved, [(group_reqs, depth, key_width)], (),
+        (partials[0], *keys_arrived[1:], *gathered),
+    )[0]
+    values_arrived = lax.all_to_all(values_packed, "dp", split_axis=0, concat_axis=0, tiled=True)
+    latest = values_packed
     if chips == 4:
         half = (flat // 2, width)
-        halves = call(
-            cut_kernel, (), (1,), [whole((flat, width))] * 2, [whole(half)] * 2, [shape(half)] * 2,
-            [], tuple(gathered), after=(latest,),
+        first, second = call(
+            cut_kernel, (), (1,), [whole((flat, width))] * 2, [whole(half)] * 2,
+            [shape(half)] * 2, [], tuple(gathered), after=(latest,),
         )
-        latest = halves[0]
-        batches = [([1, 2], gathered), ([3], [swap(halves[0], 1), swap(halves[1], 2)])]
+        latest = first
+        batches = [([1, 2], gathered), ([3], [swap(first, 1), swap(second, 2)])]
     else:
         batches = [([mask], [rows]) for mask, rows in zip(masks, gathered)]
-    values_packed = None
+    kv_half = None
     for batch_masks, pieces in batches:
         results = mlp(pieces, (latest,))
         latest = results[0]
         partials += [swap(rows, mask) for mask, rows in zip(batch_masks, results)]
-        if values_packed is None:
-            values_packed = pack(
-                values_moved, [(group_reqs, depth, key_width)], (), (latest,)
-            )[0]
-            values_arrived = lax.all_to_all(
-                values_packed, "dp", split_axis=0, concat_axis=0, tiled=True
-            )
-            kv_half = unpack(0, keys_arrived, (), (values_packed,))
+        if kv_half is None:
+            kv_half = unpack(0, keys_arrived, (), (latest,))
             latest = kv_half
     kv_decode = unpack(key_width, [values_arrived], (kv_half,), ())
 

time: 211 us -> 149 us (0.71)
  the two profiles are of different devices: /device:TPU:24 before, /device:TPU:0 now
where the time goes in v6:
time: 149 us; the launch traced here: 148 us
  Pallas kernels  62.8 us (42%)
  waiting for transfers between devices  43.4 us (29%)
  starting transfers between devices  29.8 us (20%)
  local copies, waits for them, and re-layouts  5.81 us (4%)
  other arithmetic  5.27 us (4%)
    pallas_call x10, Pallas kernels, call(): pl.pallas_call(ordered, out_shape=out_shape, grid_spec=pltpu.PrefetchScal...  62.8 us
    ppermute x7, waiting for transfers between devices, swap(): return lax.ppermute(rows, 'chip', [(c, c ^ mask) for c in range(chips)])  42.1 us
    ppermute x7, starting transfers between devices, swap(): return lax.ppermute(rows, 'chip', [(c, c ^ mask) for c in range(chips)])  7.79 us
    all_to_all x1, starting transfers between devices, local(): lax.all_to_all(values_packed, 'dp', split_axis=0, concat_axis=0, tiled=True)  7.28 us
    unnamed x28, local copies, waits for them, and re-layouts  5.73 us
    ppermute x3, starting transfers between devices, local(): lax.ppermute(rows, 'dp', pairs)  5.51 us
    all_to_all x1, starting transfers between devices, local(): lax.all_to_all(keys, tensor, split_axis=0, concat_axis=0, tiled=True)  4.98 us
    all_to_all x1, starting transfers between devices, local(): lax.all_to_all(values, tensor, split_axis=0, concat_axis=0, tiled=True)  3.72 us
  transfers between devices with their start and end apart: 14, of which 5 were waited for; matrix products, arithmetic and copies ran while one was open for 4% of the time, Pallas kernels for 36%

profile of v6, /device:TPU:0, one launch (start us, length us, event | category | flops | bytes accessed | tf_op | source)
XLA Modules:
  0.0 148.0 jit_solution(8211732104923770361)
XLA Ops:
  0.6 0.5 collective-permute-start
  1.1 6.4 %shard_map.122 = (bf16[8,2,64,768]{3,2,1,0:T(8,128)(2,1)}, bf16[2,128,1536]{2,1,0:T(8,128)(2,1)}, f32[2,128,384]{2,1,0:T(8,128)}, f32[2,128,384]{2,1,0:T(8,128)}) custom-call(s32[64]{0:T(128)} %refs_0_.6, s32[64]{0:T(128)} %refs_1_.3, s32[64]{0:T(128)} %refs_2_.3, s32[1]{0:T(128)} %bitcast.1.refs_3_, bf16[2,128,1536]{2,1,0:T(8,128)(2,1)} %refs_11_.1, ...), custom_call_target="tpu_custom_call" | custom-call | flops 603979776 | bytes 8388608 | tf_op jit(solution)/shard_map/pallas_call | solution.py:258
  7.6 0.0 copy-start.13
  7.6 5.0 %all-to-all-start = ((bf16[8,2,64,768]{3,2,1,0:T(8,128)(2,1)}), bf16[8,2,64,768]{3,2,1,0:T(8,128)(2,1)S(1)}, u32[]{:S(2)}, u32[]{:S(2)}) async-start(bf16[8,2,64,768]{3,2,1,0:T(8,128)(2,1)} %get-tuple-element.21.refs_9_), calls=%async_computation | async-start | bytes 3145728 | tf_op jit(solution)/shard_map/all_to_all | solution.py:334
  12.6 0.0 copy-done.11
  12.6 0.0 copy-done.12
  12.6 0.0 copy-done.13
  12.6 0.2 select_reduce_fusion.1
  12.8 0.2 select_reduce_fusion.3
  13.0 0.1 fusion.2
  13.1 0.2 convert_reduce_fusion.1
  13.2 0.7 select_reduce_fusion.4.refs_0_
  14.0 18.4 %shard_map.123 = (bf16[8,2,64,768]{3,2,1,0:T(8,128)(2,1)}, bf16[256,1536]{1,0:T(8,128)(2,1)}, bf16[256,1536]{1,0:T(8,128)(2,1)}) custom-call(s32[64]{0:T(128)} %refs_0_.6, s32[64]{0:T(128)} %refs_1_.3, s32[64]{0:T(128)} %refs_2_.3, s32[1]{0:T(128)} %bitcast.1.refs_3_, bf16[2,128,1536]{2,1,0:T(8,128)(2,1)} %get-tuple-element.18.refs_4_, ...), custom_call_target="tpu_custom_call" | custom-call | flops 7247757312 | bytes 16777216 | tf_op jit(solution)/shard_map/pallas_call | solution.py:258
  32.4 1.2 all-to-all-done
  33.6 0.0 collective-permute-done.refs_5_.refs_1_
  33.6 1.1 copy-done.1
  34.7 3.1 %shard_map.124 = (bf16[4,64,768]{2,1,0:T(8,128)(2,1)}, bf16[4,64,768]{2,1,0:T(8,128)(2,1)}, bf16[4,64,768]{2,1,0:T(8,128)(2,1)}, bf16[4,64,768]{2,1,0:T(8,128)(2,1)}, bf16[8,2,64,768]{3,2,1,0:T(8,128)(2,1)}) custom-call(s32[16]{0:T(128)} %select_reduce_fusion.4.refs_0_, s32[1]{0:T(128)} %bitcast.2.refs_1_, ...), custom_call_target="tpu_custom_call", output_to_operand_aliasing={{4}: (3, {})} | custom-call | bytes 6291456 | tf_op jit(solution)/shard_map/pallas_call | solution.py:258
  37.8 0.0 copy-start.4
  37.9 3.7 %all-to-all-start.1 = ((bf16[8,2,64,768]{3,2,1,0:T(8,128)(2,1)}), bf16[8,2,64,768]{3,2,1,0:T(8,128)(2,1)S(1)}, u32[]{:S(2)}, u32[]{:S(2)}) async-start(bf16[8,2,64,768]{3,2,1,0:T(8,128)(2,1)} %get-tuple-element.26), calls=%async_computation.1 | async-start | bytes 3145728 | tf_op jit(solution)/shard_map/all_to_all | solution.py:447
  41.6 1.9 %collective-permute-start.1 = (bf16[256,1536]{1,0:T(8,128)(2,1)S(1)}, bf16[256,1536]{1,0:T(8,128)(2,1)S(1)}, u32[]{:S(2)}, u32[]{:S(2)}) collective-permute-start(bf16[256,1536]{1,0:T(8,128)(2,1)S(1)} %copy-done.4), channel_id=1, source_target_pairs={{0,2},{2,0},{4,6},{6,4},{1,3},{3,1},{5,7},{7,5},{8,10},{10,8},{12,... | collective-permute-start | bytes 2359304 | tf_op jit(solution)/shard_map/ppermute | solution.py:440
  43.5 1.5 %collective-permute-start.2 = (bf16[256,1536]{1,0:T(8,128)(2,1)S(1)}, bf16[256,1536]{1,0:T(8,128)(2,1)}, u32[]{:S(2)}, u32[]{:S(2)}) collective-permute-start(bf16[256,1536]{1,0:T(8,128)(2,1)S(1)} %copy-done.4), channel_id=1, source_target_pairs={{0,4},{2,6},{4,0},{6,2},{1,5},{3,7},{5,1},{7,3},{8,12},{10,14},{12... | collective-permute-start | bytes 2359304 | tf_op jit(solution)/shard_map/ppermute | solution.py:440
  45.0 1.6 %collective-permute-start.3 = (bf16[4,64,768]{2,1,0:T(8,128)(2,1)}, bf16[4,64,768]{2,1,0:T(8,128)(2,1)S(1)}, u32[]{:S(2)}, u32[]{:S(2)}) collective-permute-start(bf16[4,64,768]{2,1,0:T(8,128)(2,1)} %get-tuple-element.27), channel_id=1, source_target_pairs={{0,8},{8,16},{16,24},{24,0},{1,9},{9,17},{17,25},{25,1},{2,10},{10... | collective-permute-start | bytes 1179656 | tf_op jit(solution)/shard_map/ppermute | solution.py:449
  46.6 2.6 %collective-permute-start.4 = (bf16[4,64,768]{2,1,0:T(8,128)(2,1)}, bf16[4,64,768]{2,1,0:T(8,128)(2,1)S(1)}, u32[]{:S(2)}, u32[]{:S(2)}) collective-permute-start(bf16[4,64,768]{2,1,0:T(8,128)(2,1)} %get-tuple-element.28), channel_id=1, source_target_pairs={{0,16},{8,24},{16,0},{24,8},{1,17},{9,25},{17,1},{25,9},{2,18},{10... | collective-permute-start | bytes 1179656 | tf_op jit(solution)/shard_map/ppermute | solution.py:449
  49.2 1.3 collective-permute-start.5
  50.5 6.8 %shard_map.125.refs_3_ = bf16[256,1536]{1,0:T(8,128)(2,1)} custom-call(bf16[3,1536,512]{2,1,0:T(8,128)(2,1)} %refs_0_.9, bf16[3,1536,512]{2,1,0:T(8,128)(2,1)} %collective-permute-done.refs_5_.refs_1_, bf16[256,1536]{1,0:T(8,128)(2,1)} %get-tuple-element.23.refs_4_.refs_2_, bf16[4,64,768]{2,1,0:T(8,128)(2,1)} %get-tuple-element.25.refs_3_.refs_2_), custom_call_target="tpu_custom_call" | custom-call | flops 2415919104 | bytes 9437184 | tf_op jit(solution)/shard_map/pallas_call | solution.py:258
  57.3 21.2 %collective-permute-done.1.refs_7_.refs_0_.refs_2_ = bf16[256,1536]{1,0:T(8,128)(2,1)S(1)} collective-permute-done((bf16[256,1536]{1,0:T(8,128)(2,1)S(1)}, bf16[256,1536]{1,0:T(8,128)(2,1)S(1)}, u32[]{:S(2)}, u32[]{:S(2)}) %collective-permute-start.1) | collective-permute-done | bytes 786464 | tf_op jit(solution)/shard_map/ppermute | solution.py:440
  78.5 0.0 collective-permute-done.2.refs_8_.refs_1_.refs_3_
  78.5 0.0 collective-permute-done.3.refs_4_.refs_3_
  78.5 0.0 collective-permute-done.4.refs_5_.refs_4_
  78.6 0.0 copy-start.7
  78.6 0.8 copy-done.7
  79.4 0.0 collective-permute-done.5.refs_6_.refs_5_
  79.4 0.0 all-to-all-done.1
  79.4 0.2 copy-done.5
  79.5 0.1 copy-done.6
  79.6 0.9 copy-done.3
  80.5 3.1 %shard_map.126.refs_2_ = bf16[16,64,768]{2,1,0:T(8,128)(2,1)} custom-call(s32[16]{0:T(128)} %select_reduce_fusion.4.refs_0_, s32[1]{0:T(128)} %bitcast.2.refs_1_, bf16[16,64,768]{2,1,0:T(8,128)(2,1)} %bitcast.8, bf16[256,1536]{1,0:T(8,128)(2,1)} %shard_map.125.refs_3_, bf16[4,64,768]{2,1,0:T(8,128)(2,1)} %copy-done.6, bf16[4,64,768]{2,1,0:T(8,128)(2,1)} %copy-done.7, ...), custom_call_target="tpu_custom_call" | custom-call | bytes 6291456 | tf_op jit(solution)/shard_map/pallas_call | solution.py:258
  83.6 7.3 %all-to-all-start.2 = ((bf16[16,64,768]{2,1,0:T(8,128)(2,1)}), bf16[16,64,768]{2,1,0:T(8,128)(2,1)S(1)}, u32[]{:S(2)}, u32[]{:S(2)}) async-start(bf16[16,64,768]{2,1,0:T(8,128)(2,1)} %shard_map.126.refs_2_), calls=%async_computation.2 | async-start | bytes 3145728 | tf_op jit(solution)/shard_map/all_to_all | solution.py:456
  90.9 0.2 convert_reduce_fusion
  91.1 0.6 select_reduce_fusion.2.refs_0_
  91.7 2.3 %shard_map.127 = (bf16[128,1536]{1,0:T(8,128)(2,1)}, bf16[128,1536]{1,0:T(8,128)(2,1)}) custom-call(bf16[256,1536]{1,0:T(8,128)(2,1)} %copy-done.5, bf16[256,1536]{1,0:T(8,128)(2,1)} %collective-permute-done.2.refs_8_.refs_1_.refs_3_, bf16[16,64,768]{2,1,0:T(8,128)(2,1)} %shard_map.126.refs_2_), custom_call_target="tpu_custom_call" | custom-call | bytes 6291456 | tf_op jit(solution)/shard_map/pallas_call | solution.py:258
  94.0 0.5 collective-permute-start.8
  94.6 0.3 collective-permute-start.9
  94.9 9.8 %shard_map.128 = (bf16[256,1536]{1,0:T(8,128)(2,1)}, bf16[256,1536]{1,0:T(8,128)(2,1)}) custom-call(bf16[3,1536,512]{2,1,0:T(8,128)(2,1)} %refs_0_.9, bf16[3,1536,512]{2,1,0:T(8,128)(2,1)} %collective-permute-done.refs_5_.refs_1_, bf16[256,1536]{1,0:T(8,128)(2,1)} %copy-done.5, bf16[256,1536]{1,0:T(8,128)(2,1)} %collective-permute-done.2.refs_8_.refs_1_.refs_3_, ...), custom_call_target="tpu_custom_call" | custom-call | flops 4831838208 | bytes 9437184 | tf_op jit(solution)/shard_map/pallas_call | solution.py:258
  104.7 1.7 %collective-permute-start.7 = (bf16[256,1536]{1,0:T(8,128)(2,1)}, bf16[256,1536]{1,0:T(8,128)(2,1)}, u32[]{:S(2)}, u32[]{:S(2)}) collective-permute-start(bf16[256,1536]{1,0:T(8,128)(2,1)} %get-tuple-element.32), channel_id=1, source_target_pairs={{0,4},{2,6},{4,0},{6,2},{1,5},{3,7},{5,1},{7,3},{8,12},{10,14},{12... | collective-permute-start | bytes 2359304 | tf_op jit(solution)/shard_map/ppermute | solution.py:440
  106.4 1.5 collective-permute-start.6
  107.9 3.1 %shard_map.129.refs_4_.refs_3_ = bf16[16,64,1536]{2,1,0:T(8,128)(2,1)} custom-call(s32[16]{0:T(128)} %select_reduce_fusion.2.refs_0_, s32[1]{0:T(128)} %bitcast.2.refs_1_, bf16[4,64,768]{2,1,0:T(8,128)(2,1)} %get-tuple-element.25.refs_3_.refs_2_, bf16[4,64,768]{2,1,0:T(8,128)(2,1)} %copy-done.6, bf16[4,64,768]{2,1,0:T(8,128)(2,1)} %copy-done.7, ...), custom_call_target="tpu_custom_call" | custom-call | bytes 6291456 | tf_op jit(solution)/shard_map/pallas_call | solution.py:258
  111.0 0.0 copy-start
  111.0 0.0 copy-start.8
  111.0 0.0 collective-permute-done.8.refs_2_
  111.0 0.0 collective-permute-done.9.refs_3_
  111.0 0.7 copy-done.9
  111.7 0.7 copy-done.10
  112.5 6.7 %shard_map.130 = bf16[256,1536]{1,0:T(8,128)(2,1)} custom-call(bf16[3,1536,512]{2,1,0:T(8,128)(2,1)} %refs_0_.9, bf16[3,1536,512]{2,1,0:T(8,128)(2,1)} %collective-permute-done.refs_5_.refs_1_, bf16[128,1536]{1,0:T(8,128)(2,1)} %copy-done.9, bf16[128,1536]{1,0:T(8,128)(2,1)} %copy-done.10, bf16[16,64,1536]{2,1,0:T(8,128)(2,1)} %shard_map.129.refs_4_.refs_3_), custom_call_target="tpu_custom_call" | custom-call | flops 2415919104 | bytes 9437184 | tf_op jit(solution)/shard_map/pallas_call | solution.py:258
  119.2 0.3 collective-permute-start.10
  119.5 0.1 dynamic_slice.6
  119.6 0.1 compare_bitcast_fusion
  119.7 5.0 %collective-permute-done.7 = bf16[256,1536]{1,0:T(8,128)(2,1)} collective-permute-done((bf16[256,1536]{1,0:T(8,128)(2,1)}, bf16[256,1536]{1,0:T(8,128)(2,1)}, u32[]{:S(2)}, u32[]{:S(2)}) %collective-permute-start.7) | collective-permute-done | bytes 786464 | tf_op jit(solution)/shard_map/ppermute | solution.py:440
  124.6 2.6 %collective-permute-done.6 = bf16[256,1536]{1,0:T(8,128)(2,1)} collective-permute-done((bf16[256,1536]{1,0:T(8,128)(2,1)}, bf16[256,1536]{1,0:T(8,128)(2,1)}, u32[]{:S(2)}, u32[]{:S(2)}) %collective-permute-start.6) | collective-permute-done | bytes 786464 | tf_op jit(solution)/shard_map/ppermute | solution.py:440
  127.2 13.4 %collective-permute-done.10 = bf16[256,1536]{1,0:T(8,128)(2,1)} collective-permute-done((bf16[256,1536]{1,0:T(8,128)(2,1)}, bf16[256,1536]{1,0:T(8,128)(2,1)}, u32[]{:S(2)}, u32[]{:S(2)}) %collective-permute-start.10) | collective-permute-done | bytes 786464 | tf_op jit(solution)/shard_map/ppermute | solution.py:440
  140.6 3.1 %select_convert_fusion = bf16[256,1536]{1,0:T(8,128)(2,1)} fusion(bf16[256,1536]{1,0:T(8,128)(2,1)} %collective-permute-done.10, bf16[256,1536]{1,0:T(8,128)(2,1)} %collective-permute-done.7, bf16[256,1536]{1,0:T(8,128)(2,1)} %collective-permute-done.6, bf16[256,1536]{1,0:T(8,128)(2,1)S(1)} %copy-done, bf16[256,1536]{1,0:T(8,128)(2,1)S(1)} %copy-done.8, ...), kind=kLoop, calls=%fused_computation | loop fusion | flops 4325376 | bytes 4718848 | tf_op jit(solution)/shard_map/convert_element_type | solution.py:483
  143.6 0.0 all-to-all-done.2.refs_2_
  143.6 1.2 copy-done.2
  144.8 3.1 %shard_map.131 = bf16[16,64,1536]{2,1,0:T(8,128)(2,1)} custom-call(s32[16]{0:T(128)} %select_reduce_fusion.2.refs_0_, s32[1]{0:T(128)} %bitcast.2.refs_1_, bf16[16,64,768]{2,1,0:T(8,128)(2,1)} %copy-done.2, bf16[16,64,1536]{2,1,0:T(8,128)(2,1)} %shard_map.129.refs_4_.refs_3_), custom_call_target="tpu_custom_call", output_to_operand_aliasing={{}: (3, {})} | custom-call | bytes 6291456 | tf_op jit(solution)/shard_map/pallas_call | solution.py:258
  (14 shorter events, 0.0 us)
Async XLA Ops:
  0.6 33.0 %collective-permute-start = (bf16[3,1536,512]{2,1,0:T(8,128)(2,1)}, bf16[3,1536,512]{2,1,0:T(8,128)(2,1)}, u32[]{:S(2)}, u32[]{:S(2)}) collective-permute-start(bf16[3,1536,512]{2,1,0:T(8,128)(2,1)} %refs_0_.9), channel_id=1, source_target_pairs={{0,1},{1,0},{2,3},{3,2},{4,5},{5,4},{6,7},{7,6},{8,9},{9,8},{10,11... | collective-permute-start | bytes 14155784 | tf_op jit(solution)/shard_map/ppermute | solution.py:311
  7.6 5.0 %copy-start.11 = (s32[64]{0:T(128)S(1)}, s32[64]{0:T(128)}, u32[]{:S(2)}) copy-start(s32[64]{0:T(128)} %refs_0_.6) | copy-start | bytes 772
  7.6 5.0 %copy-start.12 = (s32[64]{0:T(128)S(1)}, s32[64]{0:T(128)}, u32[]{:S(2)}) copy-start(s32[64]{0:T(128)} %refs_1_.3) | copy-start | bytes 772
  7.6 5.0 %copy-start.13 = (s32[64]{0:T(128)S(1)}, s32[64]{0:T(128)}, u32[]{:S(2)}) copy-start(s32[64]{0:T(128)} %param.20) | copy-start | bytes 772
  7.6 26.0 %all-to-all-start = ((bf16[8,2,64,768]{3,2,1,0:T(8,128)(2,1)}), bf16[8,2,64,768]{3,2,1,0:T(8,128)(2,1)S(1)}, u32[]{:S(2)}, u32[]{:S(2)}) async-start(bf16[8,2,64,768]{3,2,1,0:T(8,128)(2,1)} %get-tuple-element.21.refs_9_), calls=%async_computation | async-start | bytes 3145728 | tf_op jit(solution)/shard_map/all_to_all | solution.py:334
  33.6 1.1 copy-start.1
  37.8 3.7 %copy-start.4 = (bf16[256,1536]{1,0:T(8,128)(2,1)S(1)}, bf16[256,1536]{1,0:T(8,128)(2,1)}, u32[]{:S(2)}) copy-start(bf16[256,1536]{1,0:T(8,128)(2,1)} %get-tuple-element.23.refs_4_.refs_2_) | copy-start | bytes 2359300
  37.9 41.5 %all-to-all-start.1 = ((bf16[8,2,64,768]{3,2,1,0:T(8,128)(2,1)}), bf16[8,2,64,768]{3,2,1,0:T(8,128)(2,1)S(1)}, u32[]{:S(2)}, u32[]{:S(2)}) async-start(bf16[8,2,64,768]{3,2,1,0:T(8,128)(2,1)} %get-tuple-element.26), calls=%async_computation.1 | async-start | bytes 3145728 | tf_op jit(solution)/shard_map/all_to_all | solution.py:447
  41.6 36.9 %collective-permute-start.1 = (bf16[256,1536]{1,0:T(8,128)(2,1)S(1)}, bf16[256,1536]{1,0:T(8,128)(2,1)S(1)}, u32[]{:S(2)}, u32[]{:S(2)}) collective-permute-start(bf16[256,1536]{1,0:T(8,128)(2,1)S(1)} %copy-done.4), channel_id=1, source_target_pairs={{0,2},{2,0},{4,6},{6,4},{1,3},{3,1},{5,7},{7,5},{8,10},{10,8},{12,... | collective-permute-start | bytes 2359304 | tf_op jit(solution)/shard_map/ppermute | solution.py:440
  43.5 35.0 %collective-permute-start.2 = (bf16[256,1536]{1,0:T(8,128)(2,1)S(1)}, bf16[256,1536]{1,0:T(8,128)(2,1)}, u32[]{:S(2)}, u32[]{:S(2)}) collective-permute-start(bf16[256,1536]{1,0:T(8,128)(2,1)S(1)} %copy-done.4), channel_id=1, source_target_pairs={{0,4},{2,6},{4,0},{6,2},{1,5},{3,7},{5,1},{7,3},{8,12},{10,14},{12... | collective-permute-start | bytes 2359304 | tf_op jit(solution)/shard_map/ppermute | solution.py:440
  45.0 33.5 %collective-permute-start.3 = (bf16[4,64,768]{2,1,0:T(8,128)(2,1)}, bf16[4,64,768]{2,1,0:T(8,128)(2,1)S(1)}, u32[]{:S(2)}, u32[]{:S(2)}) collective-permute-start(bf16[4,64,768]{2,1,0:T(8,128)(2,1)} %get-tuple-element.27), channel_id=1, source_target_pairs={{0,8},{8,16},{16,24},{24,0},{1,9},{9,17},{17,25},{25,1},{2,10},{10... | collective-permute-start | bytes 1179656 | tf_op jit(solution)/shard_map/ppermute | solution.py:449
  46.6 32.0 %collective-permute-start.4 = (bf16[4,64,768]{2,1,0:T(8,128)(2,1)}, bf16[4,64,768]{2,1,0:T(8,128)(2,1)S(1)}, u32[]{:S(2)}, u32[]{:S(2)}) collective-permute-start(bf16[4,64,768]{2,1,0:T(8,128)(2,1)} %get-tuple-element.28), channel_id=1, source_target_pairs={{0,16},{8,24},{16,0},{24,8},{1,17},{9,25},{17,1},{25,9},{2,18},{10... | collective-permute-start | bytes 1179656 | tf_op jit(solution)/shard_map/ppermute | solution.py:449
  49.2 30.2 %collective-permute-start.5 = (bf16[4,64,768]{2,1,0:T(8,128)(2,1)}, bf16[4,64,768]{2,1,0:T(8,128)(2,1)}, u32[]{:S(2)}, u32[]{:S(2)}) collective-permute-start(bf16[4,64,768]{2,1,0:T(8,128)(2,1)} %get-tuple-element.29), channel_id=1, source_target_pairs={{0,24},{8,0},{16,8},{24,16},{1,25},{9,1},{17,9},{25,17},{2,26},{10... | collective-permute-start | bytes 1179656 | tf_op jit(solution)/shard_map/ppermute | solution.py:449
  78.5 1.0 copy-start.5
  78.5 1.1 copy-start.6
  78.6 0.8 copy-start.7
  79.4 1.1 copy-start.3
  83.6 60.0 %all-to-all-start.2 = ((bf16[16,64,768]{2,1,0:T(8,128)(2,1)}), bf16[16,64,768]{2,1,0:T(8,128)(2,1)S(1)}, u32[]{:S(2)}, u32[]{:S(2)}) async-start(bf16[16,64,768]{2,1,0:T(8,128)(2,1)} %shard_map.126.refs_2_), calls=%async_computation.2 | async-start | bytes 3145728 | tf_op jit(solution)/shard_map/all_to_all | solution.py:456
  94.0 17.0 %collective-permute-start.8 = (bf16[128,1536]{1,0:T(8,128)(2,1)}, bf16[128,1536]{1,0:T(8,128)(2,1)S(1)}, u32[]{:S(2)}, u32[]{:S(2)}) collective-permute-start(bf16[128,1536]{1,0:T(8,128)(2,1)} %get-tuple-element.30.refs_4_), channel_id=1, source_target_pairs={{0,2},{2,0},{4,6},{6,4},{1,3},{3,1},{5,7},{7,5},{8,10},{10,8},{12,... | collective-permute-start | bytes 1179656 | tf_op jit(solution)/shard_map/ppermute | solution.py:440
  94.6 16.5 %collective-permute-start.9 = (bf16[128,1536]{1,0:T(8,128)(2,1)}, bf16[128,1536]{1,0:T(8,128)(2,1)S(1)}, u32[]{:S(2)}, u32[]{:S(2)}) collective-permute-start(bf16[128,1536]{1,0:T(8,128)(2,1)} %get-tuple-element.33), channel_id=1, source_target_pairs={{0,4},{2,6},{4,0},{6,2},{1,5},{3,7},{5,1},{7,3},{8,12},{10,14},{12... | collective-permute-start | bytes 1179656 | tf_op jit(solution)/shard_map/ppermute | solution.py:440
  104.7 19.9 %collective-permute-start.7 = (bf16[256,1536]{1,0:T(8,128)(2,1)}, bf16[256,1536]{1,0:T(8,128)(2,1)}, u32[]{:S(2)}, u32[]{:S(2)}) collective-permute-start(bf16[256,1536]{1,0:T(8,128)(2,1)} %get-tuple-element.32), channel_id=1, source_target_pairs={{0,4},{2,6},{4,0},{6,2},{1,5},{3,7},{5,1},{7,3},{8,12},{10,14},{12... | collective-permute-start | bytes 2359304 | tf_op jit(solution)/shard_map/ppermute | solution.py:440
  106.4 20.8 %collective-permute-start.6 = (bf16[256,1536]{1,0:T(8,128)(2,1)}, bf16[256,1536]{1,0:T(8,128)(2,1)}, u32[]{:S(2)}, u32[]{:S(2)}) collective-permute-start(bf16[256,1536]{1,0:T(8,128)(2,1)} %get-tuple-element.31.refs_6_), channel_id=1, source_target_pairs={{0,2},{2,0},{4,6},{6,4},{1,3},{3,1},{5,7},{7,5},{8,10},{10,8},{12,... | collective-permute-start | bytes 2359304 | tf_op jit(solution)/shard_map/ppermute | solution.py:440
  111.0 29.6 %copy-start = (bf16[256,1536]{1,0:T(8,128)(2,1)S(1)}, bf16[256,1536]{1,0:T(8,128)(2,1)}, u32[]{:S(2)}) copy-start(bf16[256,1536]{1,0:T(8,128)(2,1)} %shard_map.125.refs_3_) | copy-start | bytes 2359300
  111.0 29.6 %copy-start.8 = (bf16[256,1536]{1,0:T(8,128)(2,1)S(1)}, bf16[256,1536]{1,0:T(8,128)(2,1)}, u32[]{:S(2)}) copy-start(bf16[256,1536]{1,0:T(8,128)(2,1)} %get-tuple-element.22) | copy-start | bytes 2359300
  111.0 0.7 copy-start.9
  111.7 0.7 copy-start.10
  119.2 21.4 %collective-permute-start.10 = (bf16[256,1536]{1,0:T(8,128)(2,1)}, bf16[256,1536]{1,0:T(8,128)(2,1)}, u32[]{:S(2)}, u32[]{:S(2)}) collective-permute-start(bf16[256,1536]{1,0:T(8,128)(2,1)} %shard_map.130), channel_id=1, source_target_pairs={{0,6},{2,4},{4,2},{6,0},{1,7},{3,5},{5,3},{7,1},{8,14},{10,12},{12... | collective-permute-start | bytes 2359304 | tf_op jit(solution)/shard_map/ppermute | solution.py:440
  143.6 1.2 copy-start.2

commit v7 on v6

--- a/solution.py
+++ b/solution.py
@@ -14,6 +14,7 @@
 HEAD_DIM = 96
 GROUP = 384
 VMEM = 60 * 1024 * 1024
+SMALL = 60 * 1024 * 1024
 
 epsilon = 1e-05
 rope_base = 100000.0
@@ -240,6 +241,20 @@
     move_rows(pairs, held, arrive, leave)
 
 
+def gate_kernel(passed, out):
+    pass
+
+
+def sum_kernel(order, news, dev, residual, *refs):
+    partials, out = refs[:-1], refs[-1]
+    request = order[dev[0] * pl.num_programs(0) + pl.program_id(0)]
+    total = residual[...].astype(f32)
+    for partial in partials:
+        total = total + partial[...].astype(f32)
+    live = lax.broadcasted_iota(jnp.int32, total.shape, 0) < news[request]
+    out[0] = jnp.where(live, total, 0.0).astype(bf16)
+
+
 def cut_kernel(first, second, *halves):
     middle = first.shape[0] // 2
     halves[0][...] = second[:middle]
@@ -248,7 +263,7 @@
 
 def call(
     kernel, prefetched, grid, in_specs, out_specs, out_shape, scratch, operands,
-    flops=0, moved=6 << 20, aliases={}, after=(),
+    flops=0, moved=6 << 20, aliases={}, after=(), vmem=VMEM,
 ):
     begin = len(prefetched) + len(operands)
 
@@ -265,7 +280,7 @@
             out_specs=out_specs,
             scratch_shapes=scratch,
         ),
-        compiler_params=pltpu.CompilerParams(vmem_limit_bytes=VMEM),
+        compiler_params=pltpu.CompilerParams(vmem_limit_bytes=vmem),
         cost_estimate=pl.CostEstimate(flops=flops, bytes_accessed=moved, transcendentals=0),
         input_output_aliases=aliases,
     )(*prefetched, *operands, *after)
@@ -385,9 +400,6 @@
     slot_of = jnp.sum(
         jnp.where(request_order[:, None] == indices[None, :], decode_slots[None, :], 0), axis=1
     )
-    count_of = jnp.sum(
-        jnp.where(request_order[:, None] == indices[None, :], new_lengths[None, :], 0), axis=1
-    )
     ordinal = jnp.arange(group_reqs, dtype=jnp.int32)
 
     def inverse(keys_of):
@@ -425,7 +437,7 @@
             [anywhere] * (1 + len(passed)), [anywhere] * (len(targets) + len(passed)),
             [shape(dims) for dims in targets] + [shape(rows.shape) for rows in passed], sems,
             (moved.reshape(group_reqs, depth, key_width), *passed),
-            aliases={3 + i: len(targets) + i for i in range(len(passed))}, after=after,
+            aliases={3 + i: len(targets) + i for i in range(len(passed))}, after=after, vmem=SMALL,
         )
 
     def unpack(columns, arrived, target, after):
@@ -433,7 +445,7 @@
             functools.partial(unpack_kernel, columns, group_total, share, len(arrived)),
             (spots, group), (1,), [anywhere] * (len(arrived) + len(target)), anywhere,
             shape((group_reqs, depth, 2 * key_width)), sems, (*arrived, *target),
-            aliases={2 + len(arrived): 0} if target else {}, after=after,
+            aliases={2 + len(arrived): 0} if target else {}, after=after, vmem=SMALL,
         )
 
     def swap(rows, mask):
@@ -448,12 +460,10 @@
     keys_arrived = [keys_packed[0]] + [
         lax.ppermute(rows, "dp", pairs) for rows, pairs in zip(keys_packed[1:], shifts)
     ]
-    partials = list(mlp([post], (keys_packed[0],)))
+    partials = list(mlp([post], (keys_packed[0], spots)))
     values_packed = pack(
-        values_moved, [(group_reqs, depth, key_width)], (),
-        (partials[0], *keys_arrived[1:], *gathered),
+        values_moved, [(group_reqs, depth, key_width)], (), (partials[0],)
     )[0]
-    values_arrived = lax.all_to_all(values_packed, "dp", split_axis=0, concat_axis=0, tiled=True)
     latest = values_packed
     if chips == 4:
         half = (flat // 2, width)
@@ -465,22 +475,25 @@
         batches = [([1, 2], gathered), ([3], [swap(first, 1), swap(second, 2)])]
     else:
         batches = [([mask], [rows]) for mask, rows in zip(masks, gathered)]
-    kv_half = None
+    values_ready = call(
+        gate_kernel, (), (1,), [anywhere], anywhere, shape(values_packed.shape), [],
+        (values_packed,), moved=1 << 10, aliases={0: 0}, after=(latest, *keys_arrived[1:]),
+    )
+    values_arrived = lax.all_to_all(values_ready, "dp", split_axis=0, concat_axis=0, tiled=True)
+    latest = values_ready
     for batch_masks, pieces in batches:
         results = mlp(pieces, (latest,))
         latest = results[0]
         partials += [swap(rows, mask) for mask, rows in zip(batch_masks, results)]
-        if kv_half is None:
-            kv_half = unpack(0, keys_arrived, (), (latest,))
-            latest = kv_half
+    kv_half = unpack(0, keys_arrived, (), (latest,))
     kv_decode = unpack(key_width, [values_arrived], (kv_half,), ())
 
-    own_counts = lax.dynamic_slice_in_dim(count_of, device * reqs, reqs)
-    live = (jnp.arange(new, dtype=jnp.int32)[None, :] < own_counts[:, None]).reshape(flat, 1)
-    total = residual.astype(f32)
-    for partial in partials:
-        total = total + partial.astype(f32)
-    layer_out = jnp.where(live, total, 0.0).astype(bf16).reshape(reqs, new, width)
+    layer_out = call(
+        sum_kernel, (request_order, new_lengths, dev), (reqs,),
+        [pl.BlockSpec((new, width), lambda r, *_: (r, 0))] * (1 + len(partials)),
+        pl.BlockSpec((1, new, width), lambda r, *_: (r, 0, 0)),
+        shape(tokens.shape), [], (residual, *partials), after=(kv_decode,), vmem=SMALL,
+    )
     return (layer_out, kv_decode)
 
 

time: 149 us -> 140 us (0.940)
  waiting for transfers between devices: 43.4 us -> 35 us
  Pallas kernels: 62.8 us -> 66.6 us
  other arithmetic: 5.27 us -> 2.18 us
    ppermute x7, waiting for transfers between devices: 42.1 us -> 18.9 us  [swap(): return lax.ppermute(rows, 'chip', [(c, c ^ mask) for c in range(chips)])]
    all_to_all x1, waiting for transfers between devices: 0.01 us -> 9.93 us  [local(): lax.all_to_all(values_ready, 'dp', split_axis=0, concat_axis=0, tiled=True)]
    all_to_all x1, waiting for transfers between devices: 0.01 us -> 4.73 us  [local(): lax.all_to_all(values, tensor, split_axis=0, concat_axis=0, tiled=True)]
    pallas_call x10 -> x12, Pallas kernels: 62.8 us -> 66.6 us  [call(): pl.pallas_call(ordered, out_shape=out_shape, grid_spec=pltpu.PrefetchScal...]
    convert_element_type x1 -> x0, other arithmetic: 3.05 us -> none  [local(): jnp.where(live, total, 0.0).astype(bf16).reshape(reqs, new, width)]
    all_to_all x1, starting transfers between devices: 7.28 us -> 5.07 us  [local(): lax.all_to_all(values_ready, 'dp', split_axis=0, concat_axis=0, tiled=True)]
    unnamed x28 -> x26, local copies, waits for them, and re-layouts: 5.73 us -> 5.96 us
  transfers between devices with their start and end apart: 14 -> 14, of which waited for: 5 -> 5; matrix products, arithmetic and copies ran while one was open for 4% -> 2% of each run, Pallas kernels for 36% -> 43%
where the time goes in v7:
time: 140 us; the launch traced here: 139 us
  Pallas kernels  66.6 us (48%)
  waiting for transfers between devices  35 us (25%)
  starting transfers between devices  28.6 us (20%)
  local copies, waits for them, and re-layouts  5.96 us (4%)
  other arithmetic  2.18 us (2%)
    pallas_call x12, Pallas kernels, call(): pl.pallas_call(ordered, out_shape=out_shape, grid_spec=pltpu.PrefetchScal...  66.6 us
    ppermute x7, waiting for transfers between devices, swap(): return lax.ppermute(rows, 'chip', [(c, c ^ mask) for c in range(chips)])  18.9 us
    all_to_all x1, waiting for transfers between devices, local(): lax.all_to_all(values_ready, 'dp', split_axis=0, concat_axis=0, tiled=True)  9.93 us
    ppermute x7, starting transfers between devices, swap(): return lax.ppermute(rows, 'chip', [(c, c ^ mask) for c in range(chips)])  8.74 us
    unnamed x26, local copies, waits for them, and re-layouts  5.96 us
    ppermute x3, starting transfers between devices, local(): lax.ppermute(rows, 'dp', pairs)  5.56 us
    all_to_all x1, starting transfers between devices, local(): lax.all_to_all(values_ready, 'dp', split_axis=0, concat_axis=0, tiled=True)  5.07 us
    all_to_all x1, starting transfers between devices, local(): lax.all_to_all(keys, tensor, split_axis=0, concat_axis=0, tiled=True)  4.98 us
  transfers between devices with their start and end apart: 14, of which 5 were waited for; matrix products, arithmetic and copies ran while one was open for 2% of the time, Pallas kernels for 43%

profile of v7, /device:TPU:0, one launch (start us, length us, event | category | flops | bytes accessed | tf_op | source)
XLA Modules:
  0.0 139.1 jit_solution(142857650603026506)
XLA Ops:
  0.6 0.5 collective-permute-start
  1.1 6.4 %shard_map.122 = (bf16[8,2,64,768]{3,2,1,0:T(8,128)(2,1)}, bf16[2,128,1536]{2,1,0:T(8,128)(2,1)}, f32[2,128,384]{2,1,0:T(8,128)}, f32[2,128,384]{2,1,0:T(8,128)}) custom-call(s32[64]{0:T(128)} %refs_0_.11, s32[64]{0:T(128)} %refs_1_.5, s32[64]{0:T(128)} %refs_2_.3, s32[1]{0:T(128)} %bitcast.refs_3_.refs_2_, bf16[2,128,1536]{2,1,0:T(8,128)(2,1)} %refs_11_.1, ...), custom_call_target="tpu_custom_call" | custom-call | flops 603979776 | bytes 8388608 | tf_op jit(solution)/shard_map/pallas_call | solution.py:273
  7.6 5.0 %all-to-all-start = ((bf16[8,2,64,768]{3,2,1,0:T(8,128)(2,1)}), bf16[8,2,64,768]{3,2,1,0:T(8,128)(2,1)S(1)}, u32[]{:S(2)}, u32[]{:S(2)}) async-start(bf16[8,2,64,768]{3,2,1,0:T(8,128)(2,1)} %get-tuple-element.21.refs_9_), calls=%async_computation | async-start | bytes 3145728 | tf_op jit(solution)/shard_map/all_to_all | solution.py:349
  12.5 0.0 copy-done.11
  12.5 0.0 copy-done.12
  12.6 0.2 select_reduce_fusion
  12.7 0.1 fusion.2
  12.8 0.2 convert_reduce_fusion.1
  13.0 0.7 select_reduce_fusion.3.refs_0_
  13.7 18.4 %shard_map.123 = (bf16[8,2,64,768]{3,2,1,0:T(8,128)(2,1)}, bf16[256,1536]{1,0:T(8,128)(2,1)}, bf16[256,1536]{1,0:T(8,128)(2,1)}) custom-call(s32[64]{0:T(128)} %refs_0_.11, s32[64]{0:T(128)} %refs_1_.5, s32[64]{0:T(128)} %refs_2_.3, s32[1]{0:T(128)} %bitcast.refs_3_.refs_2_, bf16[2,128,1536]{2,1,0:T(8,128)(2,1)} %get-tuple-element.18.refs_4_, ...), custom_call_target="tpu_custom_call" | custom-call | flops 7247757312 | bytes 16777216 | tf_op jit(solution)/shard_map/pallas_call | solution.py:273
  32.2 1.4 %all-to-all-done = bf16[8,2,64,768]{3,2,1,0:T(8,128)(2,1)S(1)} async-done(((bf16[8,2,64,768]{3,2,1,0:T(8,128)(2,1)}), bf16[8,2,64,768]{3,2,1,0:T(8,128)(2,1)S(1)}, u32[]{:S(2)}, u32[]{:S(2)}) %all-to-all-start) | async-done | bytes 1572896 | tf_op jit(solution)/shard_map/all_to_all | solution.py:349
  33.6 0.0 collective-permute-done.refs_5_.refs_1_
  33.6 1.1 copy-done.1
  34.7 3.0 %shard_map.124 = (bf16[4,64,768]{2,1,0:T(8,128)(2,1)}, bf16[4,64,768]{2,1,0:T(8,128)(2,1)}, bf16[4,64,768]{2,1,0:T(8,128)(2,1)}, bf16[4,64,768]{2,1,0:T(8,128)(2,1)}, bf16[8,2,64,768]{3,2,1,0:T(8,128)(2,1)}) custom-call(s32[16]{0:T(128)} %select_reduce_fusion.3.refs_0_, s32[1]{0:T(128)} %bitcast.1.refs_1_, ...), custom_call_target="tpu_custom_call", output_to_operand_aliasing={{4}: (3, {})} | custom-call | bytes 6291456 | tf_op jit(solution)/shard_map/pallas_call | solution.py:273
  37.8 0.0 copy-start.3
  37.8 3.7 %all-to-all-start.1 = ((bf16[8,2,64,768]{3,2,1,0:T(8,128)(2,1)}), bf16[8,2,64,768]{3,2,1,0:T(8,128)(2,1)S(1)}, u32[]{:S(2)}, u32[]{:S(2)}) async-start(bf16[8,2,64,768]{3,2,1,0:T(8,128)(2,1)} %get-tuple-element.26), calls=%async_computation.1 | async-start | bytes 3145728 | tf_op jit(solution)/shard_map/all_to_all | solution.py:459
  41.5 0.0 copy-done.3
  41.5 1.9 %collective-permute-start.1 = (bf16[256,1536]{1,0:T(8,128)(2,1)S(1)}, bf16[256,1536]{1,0:T(8,128)(2,1)}, u32[]{:S(2)}, u32[]{:S(2)}) collective-permute-start(bf16[256,1536]{1,0:T(8,128)(2,1)S(1)} %copy-done.3), channel_id=1, source_target_pairs={{0,2},{2,0},{4,6},{6,4},{1,3},{3,1},{5,7},{7,5},{8,10},{10,8},{12,... | collective-permute-start | bytes 2359304 | tf_op jit(solution)/shard_map/ppermute | solution.py:452
  43.4 1.5 %collective-permute-start.2 = (bf16[256,1536]{1,0:T(8,128)(2,1)S(1)}, bf16[256,1536]{1,0:T(8,128)(2,1)}, u32[]{:S(2)}, u32[]{:S(2)}) collective-permute-start(bf16[256,1536]{1,0:T(8,128)(2,1)S(1)} %copy-done.3), channel_id=1, source_target_pairs={{0,4},{2,6},{4,0},{6,2},{1,5},{3,7},{5,1},{7,3},{8,12},{10,14},{12... | collective-permute-start | bytes 2359304 | tf_op jit(solution)/shard_map/ppermute | solution.py:452
  44.9 0.2 select_reduce_fusion.2
  45.1 1.6 %collective-permute-start.3 = (bf16[4,64,768]{2,1,0:T(8,128)(2,1)}, bf16[4,64,768]{2,1,0:T(8,128)(2,1)S(1)}, u32[]{:S(2)}, u32[]{:S(2)}) collective-permute-start(bf16[4,64,768]{2,1,0:T(8,128)(2,1)} %get-tuple-element.28), channel_id=1, source_target_pairs={{0,8},{8,16},{16,24},{24,0},{1,9},{9,17},{17,25},{25,1},{2,10},{10... | collective-permute-start | bytes 1179656 | tf_op jit(solution)/shard_map/ppermute | solution.py:461
  46.8 2.6 %collective-permute-start.4 = (bf16[4,64,768]{2,1,0:T(8,128)(2,1)}, bf16[4,64,768]{2,1,0:T(8,128)(2,1)S(1)}, u32[]{:S(2)}, u32[]{:S(2)}) collective-permute-start(bf16[4,64,768]{2,1,0:T(8,128)(2,1)} %get-tuple-element.29), channel_id=1, source_target_pairs={{0,16},{8,24},{16,0},{24,8},{1,17},{9,25},{17,1},{25,9},{2,18},{10... | collective-permute-start | bytes 1179656 | tf_op jit(solution)/shard_map/ppermute | solution.py:461
  49.3 1.3 collective-permute-start.5
  50.7 0.2 convert_reduce_fusion
  50.9 0.6 select_reduce_fusion.1.refs_4_.refs_0_
  51.5 6.7 %shard_map.125.refs_3_.refs_4_ = bf16[256,1536]{1,0:T(8,128)(2,1)} custom-call(bf16[3,1536,512]{2,1,0:T(8,128)(2,1)} %refs_0_.10, bf16[3,1536,512]{2,1,0:T(8,128)(2,1)} %collective-permute-done.refs_5_.refs_1_, bf16[256,1536]{1,0:T(8,128)(2,1)} %get-tuple-element.23.refs_4_.refs_2_, bf16[4,64,768]{2,1,0:T(8,128)(2,1)} %get-tuple-element.25.refs_3_.refs_2_, ...), custom_call_target="tpu_custom_call" | custom-call | flops 2415919104 | bytes 9437184 | tf_op jit(solution)/shard_map/pallas_call | solution.py:273
  58.3 4.7 %all-to-all-done.1 = bf16[8,2,64,768]{3,2,1,0:T(8,128)(2,1)S(1)} async-done(((bf16[8,2,64,768]{3,2,1,0:T(8,128)(2,1)}), bf16[8,2,64,768]{3,2,1,0:T(8,128)(2,1)S(1)}, u32[]{:S(2)}, u32[]{:S(2)}) %all-to-all-start.1) | async-done | bytes 1572896 | tf_op jit(solution)/shard_map/all_to_all | solution.py:459
  63.0 1.1 copy-done
  64.1 3.1 %shard_map.126.refs_2_.refs_0_ = bf16[16,64,768]{2,1,0:T(8,128)(2,1)} custom-call(s32[16]{0:T(128)} %select_reduce_fusion.3.refs_0_, s32[1]{0:T(128)} %bitcast.1.refs_1_, bf16[16,64,768]{2,1,0:T(8,128)(2,1)} %bitcast.4, bf16[256,1536]{1,0:T(8,128)(2,1)} %shard_map.125.refs_3_.refs_4_), custom_call_target="tpu_custom_call" | custom-call | bytes 6291456 | tf_op jit(solution)/shard_map/pallas_call | solution.py:273
  67.2 11.3 %collective-permute-done.1.refs_0_.refs_2_ = bf16[256,1536]{1,0:T(8,128)(2,1)} collective-permute-done((bf16[256,1536]{1,0:T(8,128)(2,1)S(1)}, bf16[256,1536]{1,0:T(8,128)(2,1)}, u32[]{:S(2)}, u32[]{:S(2)}) %collective-permute-start.1) | collective-permute-done | bytes 786464 | tf_op jit(solution)/shard_map/ppermute | solution.py:452
  78.5 0.0 collective-permute-done.2.refs_1_.refs_3_
  78.5 2.3 %shard_map.127 = (bf16[128,1536]{1,0:T(8,128)(2,1)}, bf16[128,1536]{1,0:T(8,128)(2,1)}) custom-call(bf16[256,1536]{1,0:T(8,128)(2,1)} %collective-permute-done.1.refs_0_.refs_2_, bf16[256,1536]{1,0:T(8,128)(2,1)} %collective-permute-done.2.refs_1_.refs_3_, bf16[16,64,768]{2,1,0:T(8,128)(2,1)} %shard_map.126.refs_2_.refs_0_), custom_call_target="tpu_custom_call" | custom-call | bytes 6291456 | tf_op jit(solution)/shard_map/pallas_call | solution.py:273
  80.8 0.0 collective-permute-done.3.refs_2_.refs_3_
  80.8 0.0 collective-permute-done.4.refs_3_.refs_4_
  80.8 0.0 copy-start.5
  80.8 0.0 collective-permute-done.5.refs_4_.refs_5_
  80.8 0.0 copy-start.6
  80.8 0.7 copy-done.4
  81.6 0.1 copy-done.5
  81.7 0.1 copy-done.6
  81.8 5.1 %all-to-all-start.2 = ((bf16[16,64,768]{2,1,0:T(8,128)(2,1)}), bf16[16,64,768]{2,1,0:T(8,128)(2,1)S(1)}, u32[]{:S(2)}, u32[]{:S(2)}) async-start(bf16[16,64,768]{2,1,0:T(8,128)(2,1)} %shard_map.128.refs_4_), calls=%async_computation.2 | async-start | bytes 3145728 | tf_op jit(solution)/shard_map/all_to_all | solution.py:482
  86.9 1.2 collective-permute-start.8
  88.1 0.7 collective-permute-start.9
  88.7 10.0 %shard_map.129 = (bf16[256,1536]{1,0:T(8,128)(2,1)}, bf16[256,1536]{1,0:T(8,128)(2,1)}) custom-call(bf16[3,1536,512]{2,1,0:T(8,128)(2,1)} %refs_0_.10, bf16[3,1536,512]{2,1,0:T(8,128)(2,1)} %collective-permute-done.refs_5_.refs_1_, bf16[256,1536]{1,0:T(8,128)(2,1)} %collective-permute-done.1.refs_0_.refs_2_, ...), custom_call_target="tpu_custom_call" | custom-call | flops 4831838208 | bytes 9437184 | tf_op jit(solution)/shard_map/pallas_call | solution.py:273
  98.7 1.5 %collective-permute-start.6 = (bf16[256,1536]{1,0:T(8,128)(2,1)}, bf16[256,1536]{1,0:T(8,128)(2,1)S(1)}, u32[]{:S(2)}, u32[]{:S(2)}) collective-permute-start(bf16[256,1536]{1,0:T(8,128)(2,1)} %get-tuple-element.31.refs_4_), channel_id=1, source_target_pairs={{0,2},{2,0},{4,6},{6,4},{1,3},{3,1},{5,7},{7,5},{8,10},{10,8},{12,... | collective-permute-start | bytes 2359304 | tf_op jit(solution)/shard_map/ppermute | solution.py:452
  100.2 0.7 collective-permute-start.7
  100.9 0.0 collective-permute-done.8.refs_2_
  100.9 0.0 collective-permute-done.9.refs_3_
  100.9 0.7 copy-done.9
  101.7 0.8 copy-done.10
  102.4 6.8 %shard_map.130.refs_6_ = bf16[256,1536]{1,0:T(8,128)(2,1)} custom-call(bf16[3,1536,512]{2,1,0:T(8,128)(2,1)} %refs_0_.10, bf16[3,1536,512]{2,1,0:T(8,128)(2,1)} %collective-permute-done.refs_5_.refs_1_, bf16[128,1536]{1,0:T(8,128)(2,1)} %copy-done.9, bf16[128,1536]{1,0:T(8,128)(2,1)} %copy-done.10, bf16[256,1536]{1,0:T(8,128)(2,1)} %get-tuple-element.31.refs_4_), custom_call_target="tpu_custom_call" | custom-call | flops 2415919104 | bytes 9437184 | tf_op jit(solution)/shard_map/pallas_call | solution.py:273
  109.2 1.3 collective-permute-start.10
  110.5 3.1 %shard_map.131.refs_3_ = bf16[16,64,1536]{2,1,0:T(8,128)(2,1)} custom-call(s32[16]{0:T(128)} %select_reduce_fusion.1.refs_4_.refs_0_, s32[1]{0:T(128)} %bitcast.1.refs_1_, bf16[4,64,768]{2,1,0:T(8,128)(2,1)} %get-tuple-element.25.refs_3_.refs_2_, bf16[4,64,768]{2,1,0:T(8,128)(2,1)} %copy-done.4, bf16[4,64,768]{2,1,0:T(8,128)(2,1)} %copy-done.5, ...), custom_call_target="tpu_custom_call" | custom-call | bytes 6291456 | tf_op jit(solution)/shard_map/pallas_call | solution.py:273
  113.5 9.9 %all-to-all-done.2.refs_2_ = bf16[16,64,768]{2,1,0:T(8,128)(2,1)S(1)} async-done(((bf16[16,64,768]{2,1,0:T(8,128)(2,1)}), bf16[16,64,768]{2,1,0:T(8,128)(2,1)S(1)}, u32[]{:S(2)}, u32[]{:S(2)}) %all-to-all-start.2) | async-done | bytes 1572896 | tf_op jit(solution)/shard_map/all_to_all | solution.py:482
  123.5 1.2 copy-done.2
  124.6 3.1 %shard_map.132.refs_8_ = bf16[16,64,1536]{2,1,0:T(8,128)(2,1)} custom-call(s32[16]{0:T(128)} %select_reduce_fusion.1.refs_4_.refs_0_, s32[1]{0:T(128)} %bitcast.1.refs_1_, bf16[16,64,768]{2,1,0:T(8,128)(2,1)} %copy-done.2, bf16[16,64,1536]{2,1,0:T(8,128)(2,1)} %shard_map.131.refs_3_), custom_call_target="tpu_custom_call", output_to_operand_aliasing={{}: (3, {})} | custom-call | bytes 6291456 | tf_op jit(solution)/shard_map/pallas_call | solution.py:273
  127.7 0.0 collective-permute-done.6.refs_5_
  127.7 0.0 copy-start.7
  127.7 0.0 collective-permute-done.7.refs_6_
  127.7 0.0 copy-start.8
  127.8 7.6 %collective-permute-done.10.refs_7_ = bf16[256,1536]{1,0:T(8,128)(2,1)} collective-permute-done((bf16[256,1536]{1,0:T(8,128)(2,1)}, bf16[256,1536]{1,0:T(8,128)(2,1)}, u32[]{:S(2)}, u32[]{:S(2)}) %collective-permute-start.10) | collective-permute-done | bytes 786464 | tf_op jit(solution)/shard_map/ppermute | solution.py:452
  135.4 0.0 copy-done.7
  135.4 0.0 copy-done.8
  135.4 3.8 %shard_map.133 = bf16[2,128,1536]{2,1,0:T(8,128)(2,1)} custom-call(s32[64]{0:T(128)} %refs_0_.11, s32[64]{0:T(128)} %refs_1_.5, s32[1]{0:T(128)} %bitcast.refs_3_.refs_2_, bf16[256,1536]{1,0:T(8,128)(2,1)} %get-tuple-element.22.refs_3_, bf16[256,1536]{1,0:T(8,128)(2,1)} %shard_map.125.refs_3_.refs_4_, bf16[256,1536]{1,0:T(8,128)(2,1)} %copy-done.7, ...), custom_call_target="tpu_custom_call" | custom-call | bytes 6291456 | tf_op jit(solution)/shard_map/pallas_call | solution.py:273
  (12 shorter events, 0.0 us)
Async XLA Ops:
  0.6 32.9 %collective-permute-start = (bf16[3,1536,512]{2,1,0:T(8,128)(2,1)}, bf16[3,1536,512]{2,1,0:T(8,128)(2,1)}, u32[]{:S(2)}, u32[]{:S(2)}) collective-permute-start(bf16[3,1536,512]{2,1,0:T(8,128)(2,1)} %refs_0_.10), channel_id=1, source_target_pairs={{0,1},{1,0},{2,3},{3,2},{4,5},{5,4},{6,7},{7,6},{8,9},{9,8},{10,11... | collective-permute-start | bytes 14155784 | tf_op jit(solution)/shard_map/ppermute | solution.py:326
  7.6 5.0 %copy-start.11 = (s32[64]{0:T(128)S(1)}, s32[64]{0:T(128)}, u32[]{:S(2)}) copy-start(s32[64]{0:T(128)} %refs_0_.11) | copy-start | bytes 772
  7.6 5.0 %copy-start.12 = (s32[64]{0:T(128)S(1)}, s32[64]{0:T(128)}, u32[]{:S(2)}) copy-start(s32[64]{0:T(128)} %param.20) | copy-start | bytes 772
  7.6 26.0 %all-to-all-start = ((bf16[8,2,64,768]{3,2,1,0:T(8,128)(2,1)}), bf16[8,2,64,768]{3,2,1,0:T(8,128)(2,1)S(1)}, u32[]{:S(2)}, u32[]{:S(2)}) async-start(bf16[8,2,64,768]{3,2,1,0:T(8,128)(2,1)} %get-tuple-element.21.refs_9_), calls=%async_computation | async-start | bytes 3145728 | tf_op jit(solution)/shard_map/all_to_all | solution.py:349
  33.6 1.1 copy-start.1
  37.8 3.7 %copy-start.3 = (bf16[256,1536]{1,0:T(8,128)(2,1)S(1)}, bf16[256,1536]{1,0:T(8,128)(2,1)}, u32[]{:S(2)}) copy-start(bf16[256,1536]{1,0:T(8,128)(2,1)} %get-tuple-element.23.refs_4_.refs_2_) | copy-start | bytes 2359300
  37.8 25.2 %all-to-all-start.1 = ((bf16[8,2,64,768]{3,2,1,0:T(8,128)(2,1)}), bf16[8,2,64,768]{3,2,1,0:T(8,128)(2,1)S(1)}, u32[]{:S(2)}, u32[]{:S(2)}) async-start(bf16[8,2,64,768]{3,2,1,0:T(8,128)(2,1)} %get-tuple-element.26), calls=%async_computation.1 | async-start | bytes 3145728 | tf_op jit(solution)/shard_map/all_to_all | solution.py:459
  41.5 37.0 %collective-permute-start.1 = (bf16[256,1536]{1,0:T(8,128)(2,1)S(1)}, bf16[256,1536]{1,0:T(8,128)(2,1)}, u32[]{:S(2)}, u32[]{:S(2)}) collective-permute-start(bf16[256,1536]{1,0:T(8,128)(2,1)S(1)} %copy-done.3), channel_id=1, source_target_pairs={{0,2},{2,0},{4,6},{6,4},{1,3},{3,1},{5,7},{7,5},{8,10},{10,8},{12,... | collective-permute-start | bytes 2359304 | tf_op jit(solution)/shard_map/ppermute | solution.py:452
  43.4 35.1 %collective-permute-start.2 = (bf16[256,1536]{1,0:T(8,128)(2,1)S(1)}, bf16[256,1536]{1,0:T(8,128)(2,1)}, u32[]{:S(2)}, u32[]{:S(2)}) collective-permute-start(bf16[256,1536]{1,0:T(8,128)(2,1)S(1)} %copy-done.3), channel_id=1, source_target_pairs={{0,4},{2,6},{4,0},{6,2},{1,5},{3,7},{5,1},{7,3},{8,12},{10,14},{12... | collective-permute-start | bytes 2359304 | tf_op jit(solution)/shard_map/ppermute | solution.py:452
  45.1 35.7 %collective-permute-start.3 = (bf16[4,64,768]{2,1,0:T(8,128)(2,1)}, bf16[4,64,768]{2,1,0:T(8,128)(2,1)S(1)}, u32[]{:S(2)}, u32[]{:S(2)}) collective-permute-start(bf16[4,64,768]{2,1,0:T(8,128)(2,1)} %get-tuple-element.28), channel_id=1, source_target_pairs={{0,8},{8,16},{16,24},{24,0},{1,9},{9,17},{17,25},{25,1},{2,10},{10... | collective-permute-start | bytes 1179656 | tf_op jit(solution)/shard_map/ppermute | solution.py:461
  46.8 34.1 %collective-permute-start.4 = (bf16[4,64,768]{2,1,0:T(8,128)(2,1)}, bf16[4,64,768]{2,1,0:T(8,128)(2,1)S(1)}, u32[]{:S(2)}, u32[]{:S(2)}) collective-permute-start(bf16[4,64,768]{2,1,0:T(8,128)(2,1)} %get-tuple-element.29), channel_id=1, source_target_pairs={{0,16},{8,24},{16,0},{24,8},{1,17},{9,25},{17,1},{25,9},{2,18},{10... | collective-permute-start | bytes 1179656 | tf_op jit(solution)/shard_map/ppermute | solution.py:461
  49.3 31.5 %collective-permute-start.5 = (bf16[4,64,768]{2,1,0:T(8,128)(2,1)}, bf16[4,64,768]{2,1,0:T(8,128)(2,1)S(1)}, u32[]{:S(2)}, u32[]{:S(2)}) collective-permute-start(bf16[4,64,768]{2,1,0:T(8,128)(2,1)} %get-tuple-element.30), channel_id=1, source_target_pairs={{0,24},{8,0},{16,8},{24,16},{1,25},{9,1},{17,9},{25,17},{2,26},{10... | collective-permute-start | bytes 1179656 | tf_op jit(solution)/shard_map/ppermute | solution.py:461
  63.0 1.1 copy-start
  80.8 0.8 copy-start.4
  80.8 0.9 copy-start.5
  80.8 1.0 copy-start.6
  81.8 41.6 %all-to-all-start.2 = ((bf16[16,64,768]{2,1,0:T(8,128)(2,1)}), bf16[16,64,768]{2,1,0:T(8,128)(2,1)S(1)}, u32[]{:S(2)}, u32[]{:S(2)}) async-start(bf16[16,64,768]{2,1,0:T(8,128)(2,1)} %shard_map.128.refs_4_), calls=%async_computation.2 | async-start | bytes 3145728 | tf_op jit(solution)/shard_map/all_to_all | solution.py:482
  86.9 14.0 %collective-permute-start.8 = (bf16[128,1536]{1,0:T(8,128)(2,1)}, bf16[128,1536]{1,0:T(8,128)(2,1)S(1)}, u32[]{:S(2)}, u32[]{:S(2)}) collective-permute-start(bf16[128,1536]{1,0:T(8,128)(2,1)} %get-tuple-element.27.refs_1_), channel_id=1, source_target_pairs={{0,2},{2,0},{4,6},{6,4},{1,3},{3,1},{5,7},{7,5},{8,10},{10,8},{12,... | collective-permute-start | bytes 1179656 | tf_op jit(solution)/shard_map/ppermute | solution.py:452
  88.1 12.8 %collective-permute-start.9 = (bf16[128,1536]{1,0:T(8,128)(2,1)}, bf16[128,1536]{1,0:T(8,128)(2,1)S(1)}, u32[]{:S(2)}, u32[]{:S(2)}) collective-permute-start(bf16[128,1536]{1,0:T(8,128)(2,1)} %get-tuple-element.33), channel_id=1, source_target_pairs={{0,4},{2,6},{4,0},{6,2},{1,5},{3,7},{5,1},{7,3},{8,12},{10,14},{12... | collective-permute-start | bytes 1179656 | tf_op jit(solution)/shard_map/ppermute | solution.py:452
  98.7 29.0 %collective-permute-start.6 = (bf16[256,1536]{1,0:T(8,128)(2,1)}, bf16[256,1536]{1,0:T(8,128)(2,1)S(1)}, u32[]{:S(2)}, u32[]{:S(2)}) collective-permute-start(bf16[256,1536]{1,0:T(8,128)(2,1)} %get-tuple-element.31.refs_4_), channel_id=1, source_target_pairs={{0,2},{2,0},{4,6},{6,4},{1,3},{3,1},{5,7},{7,5},{8,10},{10,8},{12,... | collective-permute-start | bytes 2359304 | tf_op jit(solution)/shard_map/ppermute | solution.py:452
  100.2 27.6 %collective-permute-start.7 = (bf16[256,1536]{1,0:T(8,128)(2,1)}, bf16[256,1536]{1,0:T(8,128)(2,1)S(1)}, u32[]{:S(2)}, u32[]{:S(2)}) collective-permute-start(bf16[256,1536]{1,0:T(8,128)(2,1)} %get-tuple-element.32), channel_id=1, source_target_pairs={{0,4},{2,6},{4,0},{6,2},{1,5},{3,7},{5,1},{7,3},{8,12},{10,14},{12... | collective-permute-start | bytes 2359304 | tf_op jit(solution)/shard_map/ppermute | solution.py:452
  100.9 0.7 copy-start.9
  101.7 0.8 copy-start.10
  109.2 26.2 %collective-permute-start.10 = (bf16[256,1536]{1,0:T(8,128)(2,1)}, bf16[256,1536]{1,0:T(8,128)(2,1)}, u32[]{:S(2)}, u32[]{:S(2)}) collective-permute-start(bf16[256,1536]{1,0:T(8,128)(2,1)} %shard_map.130.refs_6_), channel_id=1, source_target_pairs={{0,6},{2,4},{4,2},{6,0},{1,7},{3,5},{5,3},{7,1},{8,14},{10,12},{12... | collective-permute-start | bytes 2359304 | tf_op jit(solution)/shard_map/ppermute | solution.py:452
  123.5 1.2 copy-start.2
  127.7 7.6 %copy-start.7 = (bf16[256,1536]{1,0:T(8,128)(2,1)}, bf16[256,1536]{1,0:T(8,128)(2,1)S(1)}, u32[]{:S(2)}) copy-start(bf16[256,1536]{1,0:T(8,128)(2,1)S(1)} %collective-permute-done.6.refs_5_) | copy-start | bytes 2359300
  127.7 7.6 %copy-start.8 = (bf16[256,1536]{1,0:T(8,128)(2,1)}, bf16[256,1536]{1,0:T(8,128)(2,1)S(1)}, u32[]{:S(2)}) copy-start(bf16[256,1536]{1,0:T(8,128)(2,1)S(1)} %collective-permute-done.7.refs_6_) | copy-start | bytes 2359300

commit v8 on v6

--- a/solution.py
+++ b/solution.py
@@ -14,6 +14,7 @@
 HEAD_DIM = 96
 GROUP = 384
 VMEM = 60 * 1024 * 1024
+LONG = 40
 
 epsilon = 1e-05
 rope_base = 100000.0
@@ -240,10 +241,24 @@
     move_rows(pairs, held, arrive, leave)
 
 
+def gate_kernel(*passed):
+    pass
+
+
 def cut_kernel(first, second, *halves):
     middle = first.shape[0] // 2
     halves[0][...] = second[:middle]
     halves[1][...] = first[middle:]
+
+
+def sum_kernel(order, news, dev, *refs):
+    terms, out = refs[:-1], refs[-1]
+    request = order[dev[0] * pl.num_programs(0) + pl.program_id(0)]
+    total = terms[0][...].astype(f32)
+    for term in terms[1:]:
+        total = total + term[...].astype(f32)
+    live = lax.broadcasted_iota(jnp.int32, total.shape, 0) < news[request]
+    out[0] = jnp.where(live, total, 0.0).astype(out.dtype)
 
 
 def call(
@@ -363,7 +378,7 @@
     units = mlp_weights.shape[2]
     chunk = 256 if units % 256 == 0 else units
 
-    def mlp(pieces, after):
+    def mlp(pieces, after, weight=1):
         total_rows = sum(rows.shape[0] for rows in pieces)
         weight_spec = pl.BlockSpec((3, width, chunk), lambda c: (0, 0, c))
         return call(
@@ -375,7 +390,7 @@
             [shape((flat, width))] * (total_rows // flat),
             [pltpu.VMEM((total_rows, width), f32)],
             (mlp_weights, other_weights, *pieces),
-            12 * total_rows * width * units,
+            weight * 12 * total_rows * width * units,
             12 * width * units,
             after=after,
         )
@@ -384,9 +399,6 @@
     indices = jnp.arange(every, dtype=jnp.int32)
     slot_of = jnp.sum(
         jnp.where(request_order[:, None] == indices[None, :], decode_slots[None, :], 0), axis=1
-    )
-    count_of = jnp.sum(
-        jnp.where(request_order[:, None] == indices[None, :], new_lengths[None, :], 0), axis=1
     )
     ordinal = jnp.arange(group_reqs, dtype=jnp.int32)
 
@@ -448,13 +460,7 @@
     keys_arrived = [keys_packed[0]] + [
         lax.ppermute(rows, "dp", pairs) for rows, pairs in zip(keys_packed[1:], shifts)
     ]
-    partials = list(mlp([post], (keys_packed[0],)))
-    values_packed = pack(
-        values_moved, [(group_reqs, depth, key_width)], (),
-        (partials[0], *keys_arrived[1:], *gathered),
-    )[0]
-    values_arrived = lax.all_to_all(values_packed, "dp", split_axis=0, concat_axis=0, tiled=True)
-    latest = values_packed
+    latest = keys_packed[0]
     if chips == 4:
         half = (flat // 2, width)
         first, second = call(
@@ -465,22 +471,39 @@
         batches = [([1, 2], gathered), ([3], [swap(first, 1), swap(second, 2)])]
     else:
         batches = [([mask], [rows]) for mask, rows in zip(masks, gathered)]
-    kv_half = None
-    for batch_masks, pieces in batches:
-        results = mlp(pieces, (latest,))
-        latest = results[0]
+    partials = list(mlp([post], (latest, spots), LONG))
+    values_packed = pack(
+        values_moved, [(group_reqs, depth, key_width)], (), (partials[0],)
+    )[0]
+    latest = values_packed
+    pair = mlp(batches[0][1], (latest, *(rows for batch in batches[1:2] for rows in batch[1])))
+    latest = pair[0]
+    values_ready, *pair = call(
+        gate_kernel, (), (1,), [anywhere] * (1 + len(pair)), [anywhere] * (1 + len(pair)),
+        [shape(rows.shape) for rows in (values_packed, *pair)], [], (values_packed, *pair),
+        moved=1 << 10, aliases={i: i for i in range(1 + len(pair))}, after=tuple(keys_arrived[1:]),
+    )
+    values_arrived = lax.all_to_all(values_ready, "dp", split_axis=0, concat_axis=0, tiled=True)
+    latest = values_ready
+    for i, (batch_masks, pieces) in enumerate(batches):
+        results = mlp(pieces, (latest,)) if i else pair
+        latest = results[0] if i else latest
         partials += [swap(rows, mask) for mask, rows in zip(batch_masks, results)]
-        if kv_half is None:
-            kv_half = unpack(0, keys_arrived, (), (latest,))
-            latest = kv_half
+
+    def add(terms, out_shape, after, flops):
+        return call(
+            sum_kernel, (request_order, new_lengths, dev), (reqs,),
+            [pl.BlockSpec((new, width), lambda r, *_: (r, 0))] * len(terms),
+            pl.BlockSpec((1, new, width), lambda r, *_: (r, 0, 0)),
+            out_shape, [], tuple(terms), flops, after=after,
+        )
+
+    most = add(
+        [residual, *partials[:-1]], shape(tokens.shape, f32), (values_ready,), LONG * flat * width * width * 8
+    )
+    layer_out = add([most.reshape(flat, width), partials[-1]], shape(tokens.shape), (), 0)
+    kv_half = unpack(0, keys_arrived, (), (layer_out,))
     kv_decode = unpack(key_width, [values_arrived], (kv_half,), ())
-
-    own_counts = lax.dynamic_slice_in_dim(count_of, device * reqs, reqs)
-    live = (jnp.arange(new, dtype=jnp.int32)[None, :] < own_counts[:, None]).reshape(flat, 1)
-    total = residual.astype(f32)
-    for partial in partials:
-        total = total + partial.astype(f32)
-    layer_out = jnp.where(live, total, 0.0).astype(bf16).reshape(reqs, new, width)
     return (layer_out, kv_decode)
 
 

time: 149 us -> 141 us (0.946)
  waiting for transfers between devices: 43.4 us -> 33.2 us
  Pallas kernels: 62.8 us -> 69.5 us
  other arithmetic: 5.27 us -> 2.15 us
    ppermute x7, waiting for transfers between devices: 42.1 us -> 28.9 us  [swap(): return lax.ppermute(rows, 'chip', [(c, c ^ mask) for c in range(chips)])]
    pallas_call x10 -> x13, Pallas kernels: 62.8 us -> 69.5 us  [call(): pl.pallas_call(ordered, out_shape=out_shape, grid_spec=pltpu.PrefetchScal...]
    all_to_all x1, waiting for transfers between devices: 0.01 us -> 4.34 us  [local(): lax.all_to_all(values, tensor, split_axis=0, concat_axis=0, tiled=True)]
    convert_element_type x1 -> x0, other arithmetic: 3.05 us -> none  [local(): jnp.where(live, total, 0.0).astype(bf16).reshape(reqs, new, width)]
    all_to_all x1, starting transfers between devices: 7.28 us -> 4.87 us  [local(): lax.all_to_all(values_ready, 'dp', split_axis=0, concat_axis=0, tiled=True)]
    ppermute x7, starting transfers between devices: 7.79 us -> 10 us  [swap(): return lax.ppermute(rows, 'chip', [(c, c ^ mask) for c in range(chips)])]
    unnamed x28 -> x24, local copies, waits for them, and re-layouts: 5.73 us -> 4.98 us
  transfers between devices with their start and end apart: 14 -> 14, of which waited for: 5 -> 7; matrix products, arithmetic and copies ran while one was open for 4% -> 2% of each run, Pallas kernels for 36% -> 47%
where the time goes in v8:
time: 141 us; the launch traced here: 140 us
  Pallas kernels  69.5 us (49%)
  waiting for transfers between devices  33.2 us (24%)
  starting transfers between devices  29.4 us (21%)
  local copies, waits for them, and re-layouts  4.98 us (4%)
  other arithmetic  2.15 us (2%)
    pallas_call x13, Pallas kernels, call(): pl.pallas_call(ordered, out_shape=out_shape, grid_spec=pltpu.PrefetchScal...  69.5 us
    ppermute x7, waiting for transfers between devices, swap(): return lax.ppermute(rows, 'chip', [(c, c ^ mask) for c in range(chips)])  28.9 us
    ppermute x7, starting transfers between devices, swap(): return lax.ppermute(rows, 'chip', [(c, c ^ mask) for c in range(chips)])  10 us
    ppermute x3, starting transfers between devices, local(): lax.ppermute(rows, 'dp', pairs)  5.57 us
    unnamed x24, local copies, waits for them, and re-layouts  4.98 us
    all_to_all x1, starting transfers between devices, local(): lax.all_to_all(values_ready, 'dp', split_axis=0, concat_axis=0, tiled=True)  4.87 us
    all_to_all x1, starting transfers between devices, local(): lax.all_to_all(keys, tensor, split_axis=0, concat_axis=0, tiled=True)  4.83 us
    all_to_all x1, waiting for transfers between devices, local(): lax.all_to_all(values, tensor, split_axis=0, concat_axis=0, tiled=True)  4.34 us
  transfers between devices with their start and end apart: 14, of which 7 were waited for; matrix products, arithmetic and copies ran while one was open for 2% of the time, Pallas kernels for 47%

profile of v8, /device:TPU:0, one launch (start us, length us, event | category | flops | bytes accessed | tf_op | source)
XLA Modules:
  0.0 140.2 jit_solution(8522997342870804335)
XLA Ops:
  0.6 0.5 collective-permute-start
  1.1 6.4 %shard_map.122 = (bf16[8,2,64,768]{3,2,1,0:T(8,128)(2,1)}, bf16[2,128,1536]{2,1,0:T(8,128)(2,1)}, f32[2,128,384]{2,1,0:T(8,128)}, f32[2,128,384]{2,1,0:T(8,128)}) custom-call(s32[64]{0:T(128)} %refs_0_.13, s32[64]{0:T(128)} %refs_1_.7, s32[64]{0:T(128)} %refs_2_.3, s32[1]{0:T(128)} %bitcast.refs_3_.refs_2_, bf16[2,128,1536]{2,1,0:T(8,128)(2,1)} %refs_11_.1, ...), custom_call_target="tpu_custom_call" | custom-call | flops 603979776 | bytes 8388608 | tf_op jit(solution)/shard_map/pallas_call | solution.py:273
  7.6 4.8 %all-to-all-start = ((bf16[8,2,64,768]{3,2,1,0:T(8,128)(2,1)}), bf16[8,2,64,768]{3,2,1,0:T(8,128)(2,1)S(1)}, u32[]{:S(2)}, u32[]{:S(2)}) async-start(bf16[8,2,64,768]{3,2,1,0:T(8,128)(2,1)} %get-tuple-element.24.refs_9_), calls=%async_computation | async-start | bytes 3145728 | tf_op jit(solution)/shard_map/all_to_all | solution.py:349
  12.4 0.0 copy-start.8
  12.4 0.0 copy-start.11
  12.4 18.5 %shard_map.123 = (bf16[8,2,64,768]{3,2,1,0:T(8,128)(2,1)}, bf16[256,1536]{1,0:T(8,128)(2,1)}, bf16[256,1536]{1,0:T(8,128)(2,1)}) custom-call(s32[64]{0:T(128)} %refs_0_.13, s32[64]{0:T(128)} %refs_1_.7, s32[64]{0:T(128)} %refs_2_.3, s32[1]{0:T(128)} %bitcast.refs_3_.refs_2_, bf16[2,128,1536]{2,1,0:T(8,128)(2,1)} %get-tuple-element.21.refs_4_, ...), custom_call_target="tpu_custom_call" | custom-call | flops 7247757312 | bytes 16777216 | tf_op jit(solution)/shard_map/pallas_call | solution.py:273
  30.9 2.2 %collective-permute-start.2 = (bf16[256,1536]{1,0:T(8,128)(2,1)}, bf16[256,1536]{1,0:T(8,128)(2,1)S(1)}, u32[]{:S(2)}, u32[]{:S(2)}) collective-permute-start(bf16[256,1536]{1,0:T(8,128)(2,1)} %get-tuple-element.26.refs_4_.refs_2_), channel_id=1, source_target_pairs={{0,4},{2,6},{4,0},{6,2},{1,5},{3,7},{5,1},{7,3},{8,12},{10,14},{12... | collective-permute-start | bytes 2359304 | tf_op jit(solution)/shard_map/ppermute | solution.py:452
  33.0 1.5 %collective-permute-start.1 = (bf16[256,1536]{1,0:T(8,128)(2,1)}, bf16[256,1536]{1,0:T(8,128)(2,1)}, u32[]{:S(2)}, u32[]{:S(2)}) collective-permute-start(bf16[256,1536]{1,0:T(8,128)(2,1)} %get-tuple-element.26.refs_4_.refs_2_), channel_id=1, source_target_pairs={{0,2},{2,0},{4,6},{6,4},{1,3},{3,1},{5,7},{7,5},{8,10},{10,8},{12,... | collective-permute-start | bytes 2359304 | tf_op jit(solution)/shard_map/ppermute | solution.py:452
  34.5 0.0 copy-done.8
  34.5 0.0 copy-done.11
  34.5 0.2 select_reduce_fusion
  34.7 0.1 fusion.2
  34.8 0.2 convert_reduce_fusion.1
  35.0 0.7 select_reduce_fusion.3.refs_0_
  35.7 0.2 select_reduce_fusion.2
  35.9 0.2 convert_reduce_fusion
  36.1 0.6 select_reduce_fusion.1.refs_4_.refs_0_
  36.7 0.0 all-to-all-done
  36.7 0.0 collective-permute-done.refs_5_.refs_1_
  36.7 1.1 copy-done
  37.8 3.1 %shard_map.124 = (bf16[4,64,768]{2,1,0:T(8,128)(2,1)}, bf16[4,64,768]{2,1,0:T(8,128)(2,1)}, bf16[4,64,768]{2,1,0:T(8,128)(2,1)}, bf16[4,64,768]{2,1,0:T(8,128)(2,1)}, bf16[8,2,64,768]{3,2,1,0:T(8,128)(2,1)}) custom-call(s32[16]{0:T(128)} %select_reduce_fusion.3.refs_0_, s32[1]{0:T(128)} %bitcast.1.refs_1_, ...), custom_call_target="tpu_custom_call", output_to_operand_aliasing={{4}: (3, {})} | custom-call | bytes 6291456 | tf_op jit(solution)/shard_map/pallas_call | solution.py:273
  40.9 3.6 %all-to-all-start.1 = ((bf16[8,2,64,768]{3,2,1,0:T(8,128)(2,1)}), bf16[8,2,64,768]{3,2,1,0:T(8,128)(2,1)S(1)}, u32[]{:S(2)}, u32[]{:S(2)}) async-start(bf16[8,2,64,768]{3,2,1,0:T(8,128)(2,1)} %get-tuple-element.30), calls=%async_computation.1 | async-start | bytes 3145728 | tf_op jit(solution)/shard_map/all_to_all | solution.py:459
  44.5 1.6 %collective-permute-start.5 = (bf16[4,64,768]{2,1,0:T(8,128)(2,1)}, bf16[4,64,768]{2,1,0:T(8,128)(2,1)S(1)}, u32[]{:S(2)}, u32[]{:S(2)}) collective-permute-start(bf16[4,64,768]{2,1,0:T(8,128)(2,1)} %get-tuple-element.34), channel_id=1, source_target_pairs={{0,8},{8,16},{16,24},{24,0},{1,9},{9,17},{17,25},{25,1},{2,10},{10... | collective-permute-start | bytes 1179656 | tf_op jit(solution)/shard_map/ppermute | solution.py:461
  46.2 2.6 %collective-permute-start.6 = (bf16[4,64,768]{2,1,0:T(8,128)(2,1)}, bf16[4,64,768]{2,1,0:T(8,128)(2,1)S(1)}, u32[]{:S(2)}, u32[]{:S(2)}) collective-permute-start(bf16[4,64,768]{2,1,0:T(8,128)(2,1)} %get-tuple-element.35), channel_id=1, source_target_pairs={{0,16},{8,24},{16,0},{24,8},{1,17},{9,25},{17,1},{25,9},{2,18},{10... | collective-permute-start | bytes 1179656 | tf_op jit(solution)/shard_map/ppermute | solution.py:461
  48.8 1.3 collective-permute-start.7
  50.1 1.5 %collective-permute-done.2.refs_1_.refs_3_ = bf16[256,1536]{1,0:T(8,128)(2,1)S(1)} collective-permute-done((bf16[256,1536]{1,0:T(8,128)(2,1)}, bf16[256,1536]{1,0:T(8,128)(2,1)S(1)}, u32[]{:S(2)}, u32[]{:S(2)}) %collective-permute-start.2) | collective-permute-done | bytes 786464 | tf_op jit(solution)/shard_map/ppermute | solution.py:452
  51.6 0.0 copy-start.5
  51.6 2.2 %collective-permute-done.1.refs_0_.refs_2_ = bf16[256,1536]{1,0:T(8,128)(2,1)} collective-permute-done((bf16[256,1536]{1,0:T(8,128)(2,1)}, bf16[256,1536]{1,0:T(8,128)(2,1)}, u32[]{:S(2)}, u32[]{:S(2)}) %collective-permute-start.1) | collective-permute-done | bytes 786464 | tf_op jit(solution)/shard_map/ppermute | solution.py:452
  53.8 0.0 copy-done.5
  53.8 2.3 %shard_map.125 = (bf16[128,1536]{1,0:T(8,128)(2,1)}, bf16[128,1536]{1,0:T(8,128)(2,1)}) custom-call(bf16[256,1536]{1,0:T(8,128)(2,1)} %collective-permute-done.1.refs_0_.refs_2_, bf16[256,1536]{1,0:T(8,128)(2,1)} %copy-done.5, bf16[4,64,768]{2,1,0:T(8,128)(2,1)} %get-tuple-element.28.refs_2_), custom_call_target="tpu_custom_call" | custom-call | bytes 6291456 | tf_op jit(solution)/shard_map/pallas_call | solution.py:273
  56.1 0.7 collective-permute-start.4
  56.8 2.2 %collective-permute-start.3 = (bf16[128,1536]{1,0:T(8,128)(2,1)}, bf16[128,1536]{1,0:T(8,128)(2,1)S(1)}, u32[]{:S(2)}, u32[]{:S(2)}) collective-permute-start(bf16[128,1536]{1,0:T(8,128)(2,1)} %get-tuple-element.29.refs_3_), channel_id=1, source_target_pairs={{0,2},{2,0},{4,6},{6,4},{1,3},{3,1},{5,7},{7,5},{8,10},{10,8},{12,... | collective-permute-start | bytes 1179656 | tf_op jit(solution)/shard_map/ppermute | solution.py:452
  59.0 6.8 %shard_map.126.refs_3_.refs_4_ = bf16[256,1536]{1,0:T(8,128)(2,1)} custom-call(bf16[3,1536,512]{2,1,0:T(8,128)(2,1)} %refs_0_.12, bf16[3,1536,512]{2,1,0:T(8,128)(2,1)} %collective-permute-done.refs_5_.refs_1_, bf16[256,1536]{1,0:T(8,128)(2,1)} %get-tuple-element.26.refs_4_.refs_2_, bf16[128,1536]{1,0:T(8,128)(2,1)} %get-tuple-element.29.refs_3_, ...), custom_call_target="tpu_custom_call" | custom-call | flops 96636764160 | bytes 9437184 | tf_op jit(solution)/shard_map/pallas_call | solution.py:273
  65.8 4.3 %all-to-all-done.1 = bf16[8,2,64,768]{3,2,1,0:T(8,128)(2,1)S(1)} async-done(((bf16[8,2,64,768]{3,2,1,0:T(8,128)(2,1)}), bf16[8,2,64,768]{3,2,1,0:T(8,128)(2,1)S(1)}, u32[]{:S(2)}, u32[]{:S(2)}) %all-to-all-start.1) | async-done | bytes 1572896 | tf_op jit(solution)/shard_map/all_to_all | solution.py:459
  70.1 1.1 copy-done.1
  71.2 3.1 %shard_map.127.refs_4_.refs_0_ = bf16[16,64,768]{2,1,0:T(8,128)(2,1)} custom-call(s32[16]{0:T(128)} %select_reduce_fusion.3.refs_0_, s32[1]{0:T(128)} %bitcast.1.refs_1_, bf16[16,64,768]{2,1,0:T(8,128)(2,1)} %bitcast.6, bf16[256,1536]{1,0:T(8,128)(2,1)} %shard_map.126.refs_3_.refs_4_), custom_call_target="tpu_custom_call" | custom-call | bytes 6291456 | tf_op jit(solution)/shard_map/pallas_call | solution.py:273
  74.3 2.1 %collective-permute-done.4.refs_6_.refs_3_ = bf16[128,1536]{1,0:T(8,128)(2,1)S(1)} collective-permute-done((bf16[128,1536]{1,0:T(8,128)(2,1)}, bf16[128,1536]{1,0:T(8,128)(2,1)S(1)}, u32[]{:S(2)}, u32[]{:S(2)}) %collective-permute-start.4) | collective-permute-done | bytes 393248 | tf_op jit(solution)/shard_map/ppermute | solution.py:452
  76.5 1.5 %collective-permute-done.3.refs_5_.refs_2_ = bf16[128,1536]{1,0:T(8,128)(2,1)S(1)} collective-permute-done((bf16[128,1536]{1,0:T(8,128)(2,1)}, bf16[128,1536]{1,0:T(8,128)(2,1)S(1)}, u32[]{:S(2)}, u32[]{:S(2)}) %collective-permute-start.3) | collective-permute-done | bytes 393248 | tf_op jit(solution)/shard_map/ppermute | solution.py:452
  77.9 0.0 copy-done.6
  77.9 0.8 copy-done.7
  78.7 9.8 %shard_map.128 = (bf16[256,1536]{1,0:T(8,128)(2,1)}, bf16[256,1536]{1,0:T(8,128)(2,1)}) custom-call(bf16[3,1536,512]{2,1,0:T(8,128)(2,1)} %refs_0_.12, bf16[3,1536,512]{2,1,0:T(8,128)(2,1)} %collective-permute-done.refs_5_.refs_1_, bf16[256,1536]{1,0:T(8,128)(2,1)} %collective-permute-done.1.refs_0_.refs_2_, bf16[256,1536]{1,0:T(8,128)(2,1)} %copy-done.5, ...), custom_call_target="tpu_custom_call" | custom-call | flops 4831838208 | bytes 9437184 | tf_op jit(solution)/shard_map/pallas_call | solution.py:273
  88.5 0.0 collective-permute-done.5.refs_3_
  88.5 0.0 collective-permute-done.6.refs_4_
  88.5 0.0 copy-start.3
  88.5 0.0 collective-permute-done.7.refs_5_
  88.6 0.0 copy-start.4
  88.6 0.7 copy-done.2
  89.3 0.1 copy-done.3
  89.4 0.2 copy-done.4
  89.6 1.5 %collective-permute-start.8 = (bf16[256,1536]{1,0:T(8,128)(2,1)}, bf16[256,1536]{1,0:T(8,128)(2,1)S(1)}, u32[]{:S(2)}, u32[]{:S(2)}) collective-permute-start(bf16[256,1536]{1,0:T(8,128)(2,1)} %get-tuple-element.37), channel_id=1, source_target_pairs={{0,2},{2,0},{4,6},{6,4},{1,3},{3,1},{5,7},{7,5},{8,10},{10,8},{12,... | collective-permute-start | bytes 2359304 | tf_op jit(solution)/shard_map/ppermute | solution.py:452
  91.0 1.0 collective-permute-start.9
  92.0 4.9 %all-to-all-start.2 = ((bf16[16,64,768]{2,1,0:T(8,128)(2,1)}), bf16[16,64,768]{2,1,0:T(8,128)(2,1)}, u32[]{:S(2)}, u32[]{:S(2)}) async-start(bf16[16,64,768]{2,1,0:T(8,128)(2,1)} %get-tuple-element.39.refs_7_.refs_4_), calls=%async_computation.2 | async-start | bytes 3145728 | tf_op jit(solution)/shard_map/all_to_all | solution.py:486
  96.9 6.7 %shard_map.131 = bf16[256,1536]{1,0:T(8,128)(2,1)} custom-call(bf16[3,1536,512]{2,1,0:T(8,128)(2,1)} %refs_0_.12, bf16[3,1536,512]{2,1,0:T(8,128)(2,1)} %collective-permute-done.refs_5_.refs_1_, bf16[128,1536]{1,0:T(8,128)(2,1)} %copy-done.7, bf16[128,1536]{1,0:T(8,128)(2,1)} %copy-done.6, bf16[16,64,768]{2,1,0:T(8,128)(2,1)} %get-tuple-element.39.refs_7_.refs_4_), custom_call_target="tpu_custom_call" | custom-call | flops 2415919104 | bytes 9437184 | tf_op jit(solution)/shard_map/pallas_call | solution.py:273
  103.6 1.1 collective-permute-start.10
  104.7 5.6 %collective-permute-done.8.refs_5_ = bf16[256,1536]{1,0:T(8,128)(2,1)S(1)} collective-permute-done((bf16[256,1536]{1,0:T(8,128)(2,1)}, bf16[256,1536]{1,0:T(8,128)(2,1)S(1)}, u32[]{:S(2)}, u32[]{:S(2)}) %collective-permute-start.8) | collective-permute-done | bytes 786464 | tf_op jit(solution)/shard_map/ppermute | solution.py:452
  110.3 16.0 %collective-permute-done.9.refs_6_ = bf16[256,1536]{1,0:T(8,128)(2,1)S(1)} collective-permute-done((bf16[256,1536]{1,0:T(8,128)(2,1)}, bf16[256,1536]{1,0:T(8,128)(2,1)S(1)}, u32[]{:S(2)}, u32[]{:S(2)}) %collective-permute-start.9) | collective-permute-done | bytes 786464 | tf_op jit(solution)/shard_map/ppermute | solution.py:452
  126.3 0.0 copy-done.9
  126.3 0.9 copy-done.10
  127.2 3.6 %shard_map.130 = f32[2,128,1536]{2,1,0:T(8,128)} custom-call(s32[64]{0:T(128)} %refs_0_.13, s32[64]{0:T(128)} %refs_1_.7, s32[1]{0:T(128)} %bitcast.refs_3_.refs_2_, bf16[256,1536]{1,0:T(8,128)(2,1)} %get-tuple-element.25.refs_3_, bf16[256,1536]{1,0:T(8,128)(2,1)} %shard_map.126.refs_3_.refs_4_, bf16[256,1536]{1,0:T(8,128)(2,1)} %copy-done.9, ...), custom_call_target="tpu_custom_call" | custom-call | flops 193273528320 | bytes 6291456 | tf_op jit(solution)/shard_map/pallas_call | solution.py:273
  130.8 0.0 collective-permute-done.10.refs_4_
  130.8 3.1 %shard_map.132.refs_6_ = bf16[2,128,1536]{2,1,0:T(8,128)(2,1)} custom-call(s32[64]{0:T(128)} %refs_0_.13, s32[64]{0:T(128)} %refs_1_.7, s32[1]{0:T(128)} %bitcast.refs_3_.refs_2_, f32[256,1536]{1,0:T(8,128)} %bitcast.7, bf16[256,1536]{1,0:T(8,128)(2,1)} %collective-permute-done.10.refs_4_), custom_call_target="tpu_custom_call" | custom-call | bytes 6291456 | tf_op jit(solution)/shard_map/pallas_call | solution.py:273
  133.9 3.1 %shard_map.133.refs_3_ = bf16[16,64,1536]{2,1,0:T(8,128)(2,1)} custom-call(s32[16]{0:T(128)} %select_reduce_fusion.1.refs_4_.refs_0_, s32[1]{0:T(128)} %bitcast.1.refs_1_, bf16[4,64,768]{2,1,0:T(8,128)(2,1)} %get-tuple-element.28.refs_2_, bf16[4,64,768]{2,1,0:T(8,128)(2,1)} %copy-done.2, bf16[4,64,768]{2,1,0:T(8,128)(2,1)} %copy-done.3, ...), custom_call_target="tpu_custom_call" | custom-call | bytes 6291456 | tf_op jit(solution)/shard_map/pallas_call | solution.py:273
  137.0 0.0 all-to-all-done.2.refs_2_
  137.0 3.1 %shard_map.134 = bf16[16,64,1536]{2,1,0:T(8,128)(2,1)} custom-call(s32[16]{0:T(128)} %select_reduce_fusion.1.refs_4_.refs_0_, s32[1]{0:T(128)} %bitcast.1.refs_1_, bf16[16,64,768]{2,1,0:T(8,128)(2,1)} %all-to-all-done.2.refs_2_, bf16[16,64,1536]{2,1,0:T(8,128)(2,1)} %shard_map.133.refs_3_), custom_call_target="tpu_custom_call", output_to_operand_aliasing={{}: (3, {})} | custom-call | bytes 6291456 | tf_op jit(solution)/shard_map/pallas_call | solution.py:273
  (11 shorter events, 0.0 us)
Async XLA Ops:
  0.6 36.1 %collective-permute-start = (bf16[3,1536,512]{2,1,0:T(8,128)(2,1)}, bf16[3,1536,512]{2,1,0:T(8,128)(2,1)}, u32[]{:S(2)}, u32[]{:S(2)}) collective-permute-start(bf16[3,1536,512]{2,1,0:T(8,128)(2,1)} %refs_0_.12), channel_id=1, source_target_pairs={{0,1},{1,0},{2,3},{3,2},{4,5},{5,4},{6,7},{7,6},{8,9},{9,8},{10,11... | collective-permute-start | bytes 14155784 | tf_op jit(solution)/shard_map/ppermute | solution.py:326
  7.6 29.1 %all-to-all-start = ((bf16[8,2,64,768]{3,2,1,0:T(8,128)(2,1)}), bf16[8,2,64,768]{3,2,1,0:T(8,128)(2,1)S(1)}, u32[]{:S(2)}, u32[]{:S(2)}) async-start(bf16[8,2,64,768]{3,2,1,0:T(8,128)(2,1)} %get-tuple-element.24.refs_9_), calls=%async_computation | async-start | bytes 3145728 | tf_op jit(solution)/shard_map/all_to_all | solution.py:349
  12.4 22.1 %copy-start.8 = (s32[64]{0:T(128)S(1)}, s32[64]{0:T(128)}, u32[]{:S(2)}) copy-start(s32[64]{0:T(128)} %refs_0_.13) | copy-start | bytes 772
  12.4 22.1 %copy-start.11 = (s32[64]{0:T(128)S(1)}, s32[64]{0:T(128)}, u32[]{:S(2)}) copy-start(s32[64]{0:T(128)} %param.20) | copy-start | bytes 772
  30.9 20.7 %collective-permute-start.2 = (bf16[256,1536]{1,0:T(8,128)(2,1)}, bf16[256,1536]{1,0:T(8,128)(2,1)S(1)}, u32[]{:S(2)}, u32[]{:S(2)}) collective-permute-start(bf16[256,1536]{1,0:T(8,128)(2,1)} %get-tuple-element.26.refs_4_.refs_2_), channel_id=1, source_target_pairs={{0,4},{2,6},{4,0},{6,2},{1,5},{3,7},{5,1},{7,3},{8,12},{10,14},{12... | collective-permute-start | bytes 2359304 | tf_op jit(solution)/shard_map/ppermute | solution.py:452
  33.0 20.7 %collective-permute-start.1 = (bf16[256,1536]{1,0:T(8,128)(2,1)}, bf16[256,1536]{1,0:T(8,128)(2,1)}, u32[]{:S(2)}, u32[]{:S(2)}) collective-permute-start(bf16[256,1536]{1,0:T(8,128)(2,1)} %get-tuple-element.26.refs_4_.refs_2_), channel_id=1, source_target_pairs={{0,2},{2,0},{4,6},{6,4},{1,3},{3,1},{5,7},{7,5},{8,10},{10,8},{12,... | collective-permute-start | bytes 2359304 | tf_op jit(solution)/shard_map/ppermute | solution.py:452
  36.7 1.1 copy-start
  40.9 29.2 %all-to-all-start.1 = ((bf16[8,2,64,768]{3,2,1,0:T(8,128)(2,1)}), bf16[8,2,64,768]{3,2,1,0:T(8,128)(2,1)S(1)}, u32[]{:S(2)}, u32[]{:S(2)}) async-start(bf16[8,2,64,768]{3,2,1,0:T(8,128)(2,1)} %get-tuple-element.30), calls=%async_computation.1 | async-start | bytes 3145728 | tf_op jit(solution)/shard_map/all_to_all | solution.py:459
  44.5 44.0 %collective-permute-start.5 = (bf16[4,64,768]{2,1,0:T(8,128)(2,1)}, bf16[4,64,768]{2,1,0:T(8,128)(2,1)S(1)}, u32[]{:S(2)}, u32[]{:S(2)}) collective-permute-start(bf16[4,64,768]{2,1,0:T(8,128)(2,1)} %get-tuple-element.34), channel_id=1, source_target_pairs={{0,8},{8,16},{16,24},{24,0},{1,9},{9,17},{17,25},{25,1},{2,10},{10... | collective-permute-start | bytes 1179656 | tf_op jit(solution)/shard_map/ppermute | solution.py:461
  46.2 42.4 %collective-permute-start.6 = (bf16[4,64,768]{2,1,0:T(8,128)(2,1)}, bf16[4,64,768]{2,1,0:T(8,128)(2,1)S(1)}, u32[]{:S(2)}, u32[]{:S(2)}) collective-permute-start(bf16[4,64,768]{2,1,0:T(8,128)(2,1)} %get-tuple-element.35), channel_id=1, source_target_pairs={{0,16},{8,24},{16,0},{24,8},{1,17},{9,25},{17,1},{25,9},{2,18},{10... | collective-permute-start | bytes 1179656 | tf_op jit(solution)/shard_map/ppermute | solution.py:461
  48.8 39.8 %collective-permute-start.7 = (bf16[4,64,768]{2,1,0:T(8,128)(2,1)}, bf16[4,64,768]{2,1,0:T(8,128)(2,1)S(1)}, u32[]{:S(2)}, u32[]{:S(2)}) collective-permute-start(bf16[4,64,768]{2,1,0:T(8,128)(2,1)} %get-tuple-element.36), channel_id=1, source_target_pairs={{0,24},{8,0},{16,8},{24,16},{1,25},{9,1},{17,9},{25,17},{2,26},{10... | collective-permute-start | bytes 1179656 | tf_op jit(solution)/shard_map/ppermute | solution.py:461
  51.6 2.2 %copy-start.5 = (bf16[256,1536]{1,0:T(8,128)(2,1)}, bf16[256,1536]{1,0:T(8,128)(2,1)S(1)}, u32[]{:S(2)}) copy-start(bf16[256,1536]{1,0:T(8,128)(2,1)S(1)} %collective-permute-done.2.refs_1_.refs_3_) | copy-start | bytes 2359300
  56.1 20.4 %collective-permute-start.4 = (bf16[128,1536]{1,0:T(8,128)(2,1)}, bf16[128,1536]{1,0:T(8,128)(2,1)S(1)}, u32[]{:S(2)}, u32[]{:S(2)}) collective-permute-start(bf16[128,1536]{1,0:T(8,128)(2,1)} %get-tuple-element.31), channel_id=1, source_target_pairs={{0,4},{2,6},{4,0},{6,2},{1,5},{3,7},{5,1},{7,3},{8,12},{10,14},{12... | collective-permute-start | bytes 1179656 | tf_op jit(solution)/shard_map/ppermute | solution.py:452
  56.8 21.1 %collective-permute-start.3 = (bf16[128,1536]{1,0:T(8,128)(2,1)}, bf16[128,1536]{1,0:T(8,128)(2,1)S(1)}, u32[]{:S(2)}, u32[]{:S(2)}) collective-permute-start(bf16[128,1536]{1,0:T(8,128)(2,1)} %get-tuple-element.29.refs_3_), channel_id=1, source_target_pairs={{0,2},{2,0},{4,6},{6,4},{1,3},{3,1},{5,7},{7,5},{8,10},{10,8},{12,... | collective-permute-start | bytes 1179656 | tf_op jit(solution)/shard_map/ppermute | solution.py:452
  70.1 1.1 copy-start.1
  76.5 1.5 %copy-start.6 = (bf16[128,1536]{1,0:T(8,128)(2,1)}, bf16[128,1536]{1,0:T(8,128)(2,1)S(1)}, u32[]{:S(2)}) copy-start(bf16[128,1536]{1,0:T(8,128)(2,1)S(1)} %collective-permute-done.4.refs_6_.refs_3_) | copy-start | bytes 1179652
  77.9 0.8 copy-start.7
  88.5 0.7 copy-start.2
  88.5 0.9 copy-start.3
  88.6 1.0 copy-start.4
  89.6 20.7 %collective-permute-start.8 = (bf16[256,1536]{1,0:T(8,128)(2,1)}, bf16[256,1536]{1,0:T(8,128)(2,1)S(1)}, u32[]{:S(2)}, u32[]{:S(2)}) collective-permute-start(bf16[256,1536]{1,0:T(8,128)(2,1)} %get-tuple-element.37), channel_id=1, source_target_pairs={{0,2},{2,0},{4,6},{6,4},{1,3},{3,1},{5,7},{7,5},{8,10},{10,8},{12,... | collective-permute-start | bytes 2359304 | tf_op jit(solution)/shard_map/ppermute | solution.py:452
  91.0 35.2 %collective-permute-start.9 = (bf16[256,1536]{1,0:T(8,128)(2,1)}, bf16[256,1536]{1,0:T(8,128)(2,1)S(1)}, u32[]{:S(2)}, u32[]{:S(2)}) collective-permute-start(bf16[256,1536]{1,0:T(8,128)(2,1)} %get-tuple-element.38), channel_id=1, source_target_pairs={{0,4},{2,6},{4,0},{6,2},{1,5},{3,7},{5,1},{7,3},{8,12},{10,14},{12... | collective-permute-start | bytes 2359304 | tf_op jit(solution)/shard_map/ppermute | solution.py:452
  92.0 45.0 %all-to-all-start.2 = ((bf16[16,64,768]{2,1,0:T(8,128)(2,1)}), bf16[16,64,768]{2,1,0:T(8,128)(2,1)}, u32[]{:S(2)}, u32[]{:S(2)}) async-start(bf16[16,64,768]{2,1,0:T(8,128)(2,1)} %get-tuple-element.39.refs_7_.refs_4_), calls=%async_computation.2 | async-start | bytes 3145728 | tf_op jit(solution)/shard_map/all_to_all | solution.py:486
  103.6 27.2 %collective-permute-start.10 = (bf16[256,1536]{1,0:T(8,128)(2,1)}, bf16[256,1536]{1,0:T(8,128)(2,1)}, u32[]{:S(2)}, u32[]{:S(2)}) collective-permute-start(bf16[256,1536]{1,0:T(8,128)(2,1)} %shard_map.131), channel_id=1, source_target_pairs={{0,6},{2,4},{4,2},{6,0},{1,7},{3,5},{5,3},{7,1},{8,14},{10,12},{12... | collective-permute-start | bytes 2359304 | tf_op jit(solution)/shard_map/ppermute | solution.py:452
  110.3 16.0 %copy-start.9 = (bf16[256,1536]{1,0:T(8,128)(2,1)}, bf16[256,1536]{1,0:T(8,128)(2,1)S(1)}, u32[]{:S(2)}) copy-start(bf16[256,1536]{1,0:T(8,128)(2,1)S(1)} %collective-permute-done.8.refs_5_) | copy-start | bytes 2359300
  126.3 0.9 copy-start.10

commit v9 on v8

--- a/solution.py
+++ b/solution.py
@@ -440,11 +440,11 @@
             aliases={3 + i: len(targets) + i for i in range(len(passed))}, after=after,
         )
 
-    def unpack(columns, arrived, target, after):
+    def unpack(columns, arrived, target, after, flops=0):
         return call(
             functools.partial(unpack_kernel, columns, group_total, share, len(arrived)),
             (spots, group), (1,), [anywhere] * (len(arrived) + len(target)), anywhere,
-            shape((group_reqs, depth, 2 * key_width)), sems, (*arrived, *target),
+            shape((group_reqs, depth, 2 * key_width)), sems, (*arrived, *target), flops,
             aliases={2 + len(arrived): 0} if target else {}, after=after,
         )
 
@@ -490,6 +490,8 @@
         latest = results[0] if i else latest
         partials += [swap(rows, mask) for mask, rows in zip(batch_masks, results)]
 
+    kv_half = unpack(0, keys_arrived, (), (latest,))
+
     def add(terms, out_shape, after, flops):
         return call(
             sum_kernel, (request_order, new_lengths, dev), (reqs,),
@@ -498,12 +500,10 @@
             out_shape, [], tuple(terms), flops, after=after,
         )
 
-    most = add(
-        [residual, *partials[:-1]], shape(tokens.shape, f32), (values_ready,), LONG * flat * width * width * 8
-    )
-    layer_out = add([most.reshape(flat, width), partials[-1]], shape(tokens.shape), (), 0)
-    kv_half = unpack(0, keys_arrived, (), (layer_out,))
-    kv_decode = unpack(key_width, [values_arrived], (kv_half,), ())
+    kv_decode = unpack(
+        key_width, [values_arrived], (kv_half,), tuple(partials[1:-1]), LONG * flat * width * width * 8
+    )
+    layer_out = add([residual, *partials], shape(tokens.shape), (kv_decode,), 0)
     return (layer_out, kv_decode)
 
 

time: 141 us -> 140 us (level)
  Pallas kernels: 69.5 us -> 66.6 us
  waiting for transfers between devices: 33.2 us -> 34.8 us
    pallas_call x13 -> x12, Pallas kernels: 69.5 us -> 66.6 us  [call(): pl.pallas_call(ordered, out_shape=out_shape, grid_spec=pltpu.PrefetchScal...]
    ppermute x7, waiting for transfers between devices: 28.9 us -> 30.4 us  [swap(): return lax.ppermute(rows, 'chip', [(c, c ^ mask) for c in range(chips)])]
    unnamed x24 -> x26, local copies, waits for them, and re-layouts: 4.98 us -> 6.08 us
  transfers between devices with their start and end apart: 14 -> 14, of which waited for: 7 -> 7; matrix products, arithmetic and copies ran while one was open for 2% -> 2% of each run, Pallas kernels for 47% -> 45%
where the time goes in v9:
time: 140 us
  Pallas kernels  66.6 us (48%)
  waiting for transfers between devices  34.8 us (25%)
  starting transfers between devices  29.4 us (21%)
  local copies, waits for them, and re-layouts  6.08 us (4%)
  other arithmetic  2.12 us (2%)
    pallas_call x12, Pallas kernels, call(): pl.pallas_call(ordered, out_shape=out_shape, grid_spec=pltpu.PrefetchScal...  66.6 us
    ppermute x7, waiting for transfers between devices, swap(): return lax.ppermute(rows, 'chip', [(c, c ^ mask) for c in range(chips)])  30.4 us
    ppermute x7, starting transfers between devices, swap(): return lax.ppermute(rows, 'chip', [(c, c ^ mask) for c in range(chips)])  10 us
    unnamed x26, local copies, waits for them, and re-layouts  6.08 us
    ppermute x3, starting transfers between devices, local(): lax.ppermute(rows, 'dp', pairs)  5.57 us
    all_to_all x1, starting transfers between devices, local(): lax.all_to_all(values_ready, 'dp', split_axis=0, concat_axis=0, tiled=True)  4.87 us
    all_to_all x1, starting transfers between devices, local(): lax.all_to_all(keys, tensor, split_axis=0, concat_axis=0, tiled=True)  4.83 us
    all_to_all x1, waiting for transfers between devices, local(): lax.all_to_all(values, tensor, split_axis=0, concat_axis=0, tiled=True)  4.33 us
  transfers between devices with their start and end apart: 14, of which 7 were waited for; matrix products, arithmetic and copies ran while one was open for 2% of the time, Pallas kernels for 45%

profile of v9, /device:TPU:0, one launch (start us, length us, event | category | flops | bytes accessed | tf_op | source)
XLA Modules:
  0.0 139.8 jit_solution(822354760000006112)
XLA Ops:
  0.6 0.5 collective-permute-start
  1.1 6.4 %shard_map.122 = (bf16[8,2,64,768]{3,2,1,0:T(8,128)(2,1)}, bf16[2,128,1536]{2,1,0:T(8,128)(2,1)}, f32[2,128,384]{2,1,0:T(8,128)}, f32[2,128,384]{2,1,0:T(8,128)}) custom-call(s32[64]{0:T(128)} %refs_0_.11, s32[64]{0:T(128)} %refs_1_.5, s32[64]{0:T(128)} %refs_2_.3, s32[1]{0:T(128)} %bitcast.refs_3_.refs_2_, bf16[2,128,1536]{2,1,0:T(8,128)(2,1)} %refs_11_.1, ...), custom_call_target="tpu_custom_call" | custom-call | flops 603979776 | bytes 8388608 | tf_op jit(solution)/shard_map/pallas_call | solution.py:273
  7.6 4.8 %all-to-all-start = ((bf16[8,2,64,768]{3,2,1,0:T(8,128)(2,1)}), bf16[8,2,64,768]{3,2,1,0:T(8,128)(2,1)S(1)}, u32[]{:S(2)}, u32[]{:S(2)}) async-start(bf16[8,2,64,768]{3,2,1,0:T(8,128)(2,1)} %get-tuple-element.24.refs_9_), calls=%async_computation | async-start | bytes 3145728 | tf_op jit(solution)/shard_map/all_to_all | solution.py:349
  12.4 0.0 copy-start.11
  12.4 0.0 copy-start.12
  12.4 18.4 %shard_map.123 = (bf16[8,2,64,768]{3,2,1,0:T(8,128)(2,1)}, bf16[256,1536]{1,0:T(8,128)(2,1)}, bf16[256,1536]{1,0:T(8,128)(2,1)}) custom-call(s32[64]{0:T(128)} %refs_0_.11, s32[64]{0:T(128)} %refs_1_.5, s32[64]{0:T(128)} %refs_2_.3, s32[1]{0:T(128)} %bitcast.refs_3_.refs_2_, bf16[2,128,1536]{2,1,0:T(8,128)(2,1)} %get-tuple-element.21.refs_4_, ...), custom_call_target="tpu_custom_call" | custom-call | flops 7247757312 | bytes 16777216 | tf_op jit(solution)/shard_map/pallas_call | solution.py:273
  30.8 2.2 %collective-permute-start.2 = (bf16[256,1536]{1,0:T(8,128)(2,1)}, bf16[256,1536]{1,0:T(8,128)(2,1)S(1)}, u32[]{:S(2)}, u32[]{:S(2)}) collective-permute-start(bf16[256,1536]{1,0:T(8,128)(2,1)} %get-tuple-element.26.refs_4_.refs_2_), channel_id=1, source_target_pairs={{0,4},{2,6},{4,0},{6,2},{1,5},{3,7},{5,1},{7,3},{8,12},{10,14},{12... | collective-permute-start | bytes 2359304 | tf_op jit(solution)/shard_map/ppermute | solution.py:452
  33.0 1.5 %collective-permute-start.1 = (bf16[256,1536]{1,0:T(8,128)(2,1)}, bf16[256,1536]{1,0:T(8,128)(2,1)}, u32[]{:S(2)}, u32[]{:S(2)}) collective-permute-start(bf16[256,1536]{1,0:T(8,128)(2,1)} %get-tuple-element.26.refs_4_.refs_2_), channel_id=1, source_target_pairs={{0,2},{2,0},{4,6},{6,4},{1,3},{3,1},{5,7},{7,5},{8,10},{10,8},{12,... | collective-permute-start | bytes 2359304 | tf_op jit(solution)/shard_map/ppermute | solution.py:452
  34.5 0.0 copy-done.11
  34.5 0.0 copy-done.12
  34.5 0.2 select_reduce_fusion
  34.6 0.1 fusion.2
  34.7 0.2 convert_reduce_fusion.1
  34.9 0.7 select_reduce_fusion.3.refs_0_
  35.6 0.2 select_reduce_fusion.2
  35.8 0.2 convert_reduce_fusion
  36.0 0.6 select_reduce_fusion.1.refs_4_.refs_0_
  36.6 0.0 all-to-all-done
  36.6 0.0 copy-start
  36.6 0.0 collective-permute-done.refs_5_.refs_1_
  36.6 1.1 copy-done
  37.7 3.1 %shard_map.124 = (bf16[4,64,768]{2,1,0:T(8,128)(2,1)}, bf16[4,64,768]{2,1,0:T(8,128)(2,1)}, bf16[4,64,768]{2,1,0:T(8,128)(2,1)}, bf16[4,64,768]{2,1,0:T(8,128)(2,1)}, bf16[8,2,64,768]{3,2,1,0:T(8,128)(2,1)}) custom-call(s32[16]{0:T(128)} %select_reduce_fusion.3.refs_0_, s32[1]{0:T(128)} %bitcast.1.refs_1_, ...), custom_call_target="tpu_custom_call", output_to_operand_aliasing={{4}: (3, {})} | custom-call | bytes 6291456 | tf_op jit(solution)/shard_map/pallas_call | solution.py:273
  40.9 3.6 %all-to-all-start.1 = ((bf16[8,2,64,768]{3,2,1,0:T(8,128)(2,1)}), bf16[8,2,64,768]{3,2,1,0:T(8,128)(2,1)S(1)}, u32[]{:S(2)}, u32[]{:S(2)}) async-start(bf16[8,2,64,768]{3,2,1,0:T(8,128)(2,1)} %get-tuple-element.30), calls=%async_computation.1 | async-start | bytes 3145728 | tf_op jit(solution)/shard_map/all_to_all | solution.py:459
  44.5 1.6 %collective-permute-start.5 = (bf16[4,64,768]{2,1,0:T(8,128)(2,1)}, bf16[4,64,768]{2,1,0:T(8,128)(2,1)S(1)}, u32[]{:S(2)}, u32[]{:S(2)}) collective-permute-start(bf16[4,64,768]{2,1,0:T(8,128)(2,1)} %get-tuple-element.34), channel_id=1, source_target_pairs={{0,8},{8,16},{16,24},{24,0},{1,9},{9,17},{17,25},{25,1},{2,10},{10... | collective-permute-start | bytes 1179656 | tf_op jit(solution)/shard_map/ppermute | solution.py:461
  46.1 2.6 %collective-permute-start.6 = (bf16[4,64,768]{2,1,0:T(8,128)(2,1)}, bf16[4,64,768]{2,1,0:T(8,128)(2,1)S(1)}, u32[]{:S(2)}, u32[]{:S(2)}) collective-permute-start(bf16[4,64,768]{2,1,0:T(8,128)(2,1)} %get-tuple-element.35), channel_id=1, source_target_pairs={{0,16},{8,24},{16,0},{24,8},{1,17},{9,25},{17,1},{25,9},{2,18},{10... | collective-permute-start | bytes 1179656 | tf_op jit(solution)/shard_map/ppermute | solution.py:461
  48.7 1.3 collective-permute-start.7
  50.0 1.5 %collective-permute-done.2.refs_1_.refs_3_ = bf16[256,1536]{1,0:T(8,128)(2,1)S(1)} collective-permute-done((bf16[256,1536]{1,0:T(8,128)(2,1)}, bf16[256,1536]{1,0:T(8,128)(2,1)S(1)}, u32[]{:S(2)}, u32[]{:S(2)}) %collective-permute-start.2) | collective-permute-done | bytes 786464 | tf_op jit(solution)/shard_map/ppermute | solution.py:452
  51.5 2.2 %collective-permute-done.1.refs_0_.refs_2_ = bf16[256,1536]{1,0:T(8,128)(2,1)} collective-permute-done((bf16[256,1536]{1,0:T(8,128)(2,1)}, bf16[256,1536]{1,0:T(8,128)(2,1)}, u32[]{:S(2)}, u32[]{:S(2)}) %collective-permute-start.1) | collective-permute-done | bytes 786464 | tf_op jit(solution)/shard_map/ppermute | solution.py:452
  53.7 0.0 copy-done.8
  53.7 2.3 %shard_map.125 = (bf16[128,1536]{1,0:T(8,128)(2,1)}, bf16[128,1536]{1,0:T(8,128)(2,1)}) custom-call(bf16[256,1536]{1,0:T(8,128)(2,1)} %collective-permute-done.1.refs_0_.refs_2_, bf16[256,1536]{1,0:T(8,128)(2,1)} %copy-done.8, bf16[4,64,768]{2,1,0:T(8,128)(2,1)} %get-tuple-element.28.refs_2_), custom_call_target="tpu_custom_call" | custom-call | bytes 6291456 | tf_op jit(solution)/shard_map/pallas_call | solution.py:273
  56.0 0.7 collective-permute-start.4
  56.7 2.2 %collective-permute-start.3 = (bf16[128,1536]{1,0:T(8,128)(2,1)}, bf16[128,1536]{1,0:T(8,128)(2,1)S(1)}, u32[]{:S(2)}, u32[]{:S(2)}) collective-permute-start(bf16[128,1536]{1,0:T(8,128)(2,1)} %get-tuple-element.29.refs_3_), channel_id=1, source_target_pairs={{0,2},{2,0},{4,6},{6,4},{1,3},{3,1},{5,7},{7,5},{8,10},{10,8},{12,... | collective-permute-start | bytes 1179656 | tf_op jit(solution)/shard_map/ppermute | solution.py:452
  58.9 6.8 %shard_map.126.refs_3_.refs_4_ = bf16[256,1536]{1,0:T(8,128)(2,1)} custom-call(bf16[3,1536,512]{2,1,0:T(8,128)(2,1)} %refs_0_.10, bf16[3,1536,512]{2,1,0:T(8,128)(2,1)} %collective-permute-done.refs_5_.refs_1_, bf16[256,1536]{1,0:T(8,128)(2,1)} %get-tuple-element.26.refs_4_.refs_2_, bf16[128,1536]{1,0:T(8,128)(2,1)} %get-tuple-element.29.refs_3_, ...), custom_call_target="tpu_custom_call" | custom-call | flops 96636764160 | bytes 9437184 | tf_op jit(solution)/shard_map/pallas_call | solution.py:273
  65.7 4.3 %all-to-all-done.1 = bf16[8,2,64,768]{3,2,1,0:T(8,128)(2,1)S(1)} async-done(((bf16[8,2,64,768]{3,2,1,0:T(8,128)(2,1)}), bf16[8,2,64,768]{3,2,1,0:T(8,128)(2,1)S(1)}, u32[]{:S(2)}, u32[]{:S(2)}) %all-to-all-start.1) | async-done | bytes 1572896 | tf_op jit(solution)/shard_map/all_to_all | solution.py:459
  70.0 1.1 copy-done.1
  71.2 3.1 %shard_map.127.refs_4_.refs_0_ = bf16[16,64,768]{2,1,0:T(8,128)(2,1)} custom-call(s32[16]{0:T(128)} %select_reduce_fusion.3.refs_0_, s32[1]{0:T(128)} %bitcast.1.refs_1_, bf16[16,64,768]{2,1,0:T(8,128)(2,1)} %bitcast.5, bf16[256,1536]{1,0:T(8,128)(2,1)} %shard_map.126.refs_3_.refs_4_), custom_call_target="tpu_custom_call" | custom-call | bytes 6291456 | tf_op jit(solution)/shard_map/pallas_call | solution.py:273
  74.3 2.1 %collective-permute-done.4.refs_6_.refs_3_ = bf16[128,1536]{1,0:T(8,128)(2,1)S(1)} collective-permute-done((bf16[128,1536]{1,0:T(8,128)(2,1)}, bf16[128,1536]{1,0:T(8,128)(2,1)S(1)}, u32[]{:S(2)}, u32[]{:S(2)}) %collective-permute-start.4) | collective-permute-done | bytes 393248 | tf_op jit(solution)/shard_map/ppermute | solution.py:452
  76.4 1.5 %collective-permute-done.3.refs_5_.refs_2_ = bf16[128,1536]{1,0:T(8,128)(2,1)S(1)} collective-permute-done((bf16[128,1536]{1,0:T(8,128)(2,1)}, bf16[128,1536]{1,0:T(8,128)(2,1)S(1)}, u32[]{:S(2)}, u32[]{:S(2)}) %collective-permute-start.3) | collective-permute-done | bytes 393248 | tf_op jit(solution)/shard_map/ppermute | solution.py:452
  77.9 0.0 copy-done.9
  77.9 0.7 copy-done.10
  78.6 9.9 %shard_map.128 = (bf16[256,1536]{1,0:T(8,128)(2,1)}, bf16[256,1536]{1,0:T(8,128)(2,1)}) custom-call(bf16[3,1536,512]{2,1,0:T(8,128)(2,1)} %refs_0_.10, bf16[3,1536,512]{2,1,0:T(8,128)(2,1)} %collective-permute-done.refs_5_.refs_1_, bf16[256,1536]{1,0:T(8,128)(2,1)} %collective-permute-done.1.refs_0_.refs_2_, bf16[256,1536]{1,0:T(8,128)(2,1)} %copy-done.8, ...), custom_call_target="tpu_custom_call" | custom-call | flops 4831838208 | bytes 9437184 | tf_op jit(solution)/shard_map/pallas_call | solution.py:273
  88.5 0.0 collective-permute-done.5.refs_3_
  88.5 0.0 collective-permute-done.6.refs_4_
  88.5 0.0 copy-start.3
  88.5 0.0 collective-permute-done.7.refs_5_
  88.6 0.0 copy-start.4
  88.6 0.7 copy-done.2
  89.3 0.1 copy-done.3
  89.4 0.2 copy-done.4
  89.6 4.9 %all-to-all-start.2 = ((bf16[16,64,768]{2,1,0:T(8,128)(2,1)}), bf16[16,64,768]{2,1,0:T(8,128)(2,1)S(1)}, u32[]{:S(2)}, u32[]{:S(2)}) async-start(bf16[16,64,768]{2,1,0:T(8,128)(2,1)} %get-tuple-element.39.refs_4_), calls=%async_computation.2 | async-start | bytes 3145728 | tf_op jit(solution)/shard_map/all_to_all | solution.py:486
  94.4 1.5 %collective-permute-start.8 = (bf16[256,1536]{1,0:T(8,128)(2,1)}, bf16[256,1536]{1,0:T(8,128)(2,1)S(1)}, u32[]{:S(2)}, u32[]{:S(2)}) collective-permute-start(bf16[256,1536]{1,0:T(8,128)(2,1)} %get-tuple-element.37), channel_id=1, source_target_pairs={{0,2},{2,0},{4,6},{6,4},{1,3},{3,1},{5,7},{7,5},{8,10},{10,8},{12,... | collective-permute-start | bytes 2359304 | tf_op jit(solution)/shard_map/ppermute | solution.py:452
  95.9 0.9 collective-permute-start.9
  96.8 6.7 %shard_map.130.refs_6_ = bf16[256,1536]{1,0:T(8,128)(2,1)} custom-call(bf16[3,1536,512]{2,1,0:T(8,128)(2,1)} %refs_0_.10, bf16[3,1536,512]{2,1,0:T(8,128)(2,1)} %collective-permute-done.refs_5_.refs_1_, bf16[128,1536]{1,0:T(8,128)(2,1)} %copy-done.10, bf16[128,1536]{1,0:T(8,128)(2,1)} %copy-done.9, bf16[16,64,768]{2,1,0:T(8,128)(2,1)} %get-tuple-element.39.refs_4_), custom_call_target="tpu_custom_call" | custom-call | flops 2415919104 | bytes 9437184 | tf_op jit(solution)/shard_map/pallas_call | solution.py:273
  103.5 1.1 collective-permute-start.10
  104.6 3.1 %shard_map.131.refs_3_ = bf16[16,64,1536]{2,1,0:T(8,128)(2,1)} custom-call(s32[16]{0:T(128)} %select_reduce_fusion.1.refs_4_.refs_0_, s32[1]{0:T(128)} %bitcast.1.refs_1_, bf16[4,64,768]{2,1,0:T(8,128)(2,1)} %get-tuple-element.28.refs_2_, bf16[4,64,768]{2,1,0:T(8,128)(2,1)} %copy-done.2, bf16[4,64,768]{2,1,0:T(8,128)(2,1)} %copy-done.3, ...), custom_call_target="tpu_custom_call" | custom-call | bytes 6291456 | tf_op jit(solution)/shard_map/pallas_call | solution.py:273
  107.7 7.4 %collective-permute-done.8.refs_4_.refs_5_ = bf16[256,1536]{1,0:T(8,128)(2,1)S(1)} collective-permute-done((bf16[256,1536]{1,0:T(8,128)(2,1)}, bf16[256,1536]{1,0:T(8,128)(2,1)S(1)}, u32[]{:S(2)}, u32[]{:S(2)}) %collective-permute-start.8) | collective-permute-done | bytes 786464 | tf_op jit(solution)/shard_map/ppermute | solution.py:452
  115.1 15.7 %collective-permute-done.9.refs_5_.refs_6_ = bf16[256,1536]{1,0:T(8,128)(2,1)S(1)} collective-permute-done((bf16[256,1536]{1,0:T(8,128)(2,1)}, bf16[256,1536]{1,0:T(8,128)(2,1)S(1)}, u32[]{:S(2)}, u32[]{:S(2)}) %collective-permute-start.9) | collective-permute-done | bytes 786464 | tf_op jit(solution)/shard_map/ppermute | solution.py:452
  130.8 0.0 all-to-all-done.2.refs_2_
  130.8 0.0 copy-done.6
  130.9 0.9 copy-done.7
  131.7 1.2 copy-done.5
  132.9 3.1 %shard_map.132.refs_8_ = bf16[16,64,1536]{2,1,0:T(8,128)(2,1)} custom-call(s32[16]{0:T(128)} %select_reduce_fusion.1.refs_4_.refs_0_, s32[1]{0:T(128)} %bitcast.1.refs_1_, bf16[16,64,768]{2,1,0:T(8,128)(2,1)} %copy-done.5, bf16[16,64,1536]{2,1,0:T(8,128)(2,1)} %shard_map.131.refs_3_, bf16[256,1536]{1,0:T(8,128)(2,1)} %copy-done.6, ...), custom_call_target="tpu_custom_call", output_to_operand_aliasing={{}: (3, {})} | custom-call | flops 193273528320 | bytes 6291456 | tf_op jit(solution)/shard_map/pallas_call | solution.py:273
  136.0 0.0 collective-permute-done.10.refs_7_
  136.0 3.8 %shard_map.133 = bf16[2,128,1536]{2,1,0:T(8,128)(2,1)} custom-call(s32[64]{0:T(128)} %refs_0_.11, s32[64]{0:T(128)} %refs_1_.5, s32[1]{0:T(128)} %bitcast.refs_3_.refs_2_, bf16[256,1536]{1,0:T(8,128)(2,1)} %get-tuple-element.25.refs_3_, bf16[256,1536]{1,0:T(8,128)(2,1)} %shard_map.126.refs_3_.refs_4_, bf16[256,1536]{1,0:T(8,128)(2,1)} %copy-done.6, ...), custom_call_target="tpu_custom_call" | custom-call | bytes 6291456 | tf_op jit(solution)/shard_map/pallas_call | solution.py:273
  (12 shorter events, 0.0 us)
Async XLA Ops:
  0.6 36.0 %collective-permute-start = (bf16[3,1536,512]{2,1,0:T(8,128)(2,1)}, bf16[3,1536,512]{2,1,0:T(8,128)(2,1)}, u32[]{:S(2)}, u32[]{:S(2)}) collective-permute-start(bf16[3,1536,512]{2,1,0:T(8,128)(2,1)} %refs_0_.10), channel_id=1, source_target_pairs={{0,1},{1,0},{2,3},{3,2},{4,5},{5,4},{6,7},{7,6},{8,9},{9,8},{10,11... | collective-permute-start | bytes 14155784 | tf_op jit(solution)/shard_map/ppermute | solution.py:326
  7.6 29.0 %all-to-all-start = ((bf16[8,2,64,768]{3,2,1,0:T(8,128)(2,1)}), bf16[8,2,64,768]{3,2,1,0:T(8,128)(2,1)S(1)}, u32[]{:S(2)}, u32[]{:S(2)}) async-start(bf16[8,2,64,768]{3,2,1,0:T(8,128)(2,1)} %get-tuple-element.24.refs_9_), calls=%async_computation | async-start | bytes 3145728 | tf_op jit(solution)/shard_map/all_to_all | solution.py:349
  12.4 22.1 %copy-start.11 = (s32[64]{0:T(128)S(1)}, s32[64]{0:T(128)}, u32[]{:S(2)}) copy-start(s32[64]{0:T(128)} %refs_0_.11) | copy-start | bytes 772
  12.4 22.1 %copy-start.12 = (s32[64]{0:T(128)S(1)}, s32[64]{0:T(128)}, u32[]{:S(2)}) copy-start(s32[64]{0:T(128)} %param.20) | copy-start | bytes 772
  30.8 20.7 %collective-permute-start.2 = (bf16[256,1536]{1,0:T(8,128)(2,1)}, bf16[256,1536]{1,0:T(8,128)(2,1)S(1)}, u32[]{:S(2)}, u32[]{:S(2)}) collective-permute-start(bf16[256,1536]{1,0:T(8,128)(2,1)} %get-tuple-element.26.refs_4_.refs_2_), channel_id=1, source_target_pairs={{0,4},{2,6},{4,0},{6,2},{1,5},{3,7},{5,1},{7,3},{8,12},{10,14},{12... | collective-permute-start | bytes 2359304 | tf_op jit(solution)/shard_map/ppermute | solution.py:452
  33.0 20.7 %collective-permute-start.1 = (bf16[256,1536]{1,0:T(8,128)(2,1)}, bf16[256,1536]{1,0:T(8,128)(2,1)}, u32[]{:S(2)}, u32[]{:S(2)}) collective-permute-start(bf16[256,1536]{1,0:T(8,128)(2,1)} %get-tuple-element.26.refs_4_.refs_2_), channel_id=1, source_target_pairs={{0,2},{2,0},{4,6},{6,4},{1,3},{3,1},{5,7},{7,5},{8,10},{10,8},{12,... | collective-permute-start | bytes 2359304 | tf_op jit(solution)/shard_map/ppermute | solution.py:452
  36.6 1.1 copy-start
  40.9 29.2 %all-to-all-start.1 = ((bf16[8,2,64,768]{3,2,1,0:T(8,128)(2,1)}), bf16[8,2,64,768]{3,2,1,0:T(8,128)(2,1)S(1)}, u32[]{:S(2)}, u32[]{:S(2)}) async-start(bf16[8,2,64,768]{3,2,1,0:T(8,128)(2,1)} %get-tuple-element.30), calls=%async_computation.1 | async-start | bytes 3145728 | tf_op jit(solution)/shard_map/all_to_all | solution.py:459
  44.5 44.1 %collective-permute-start.5 = (bf16[4,64,768]{2,1,0:T(8,128)(2,1)}, bf16[4,64,768]{2,1,0:T(8,128)(2,1)S(1)}, u32[]{:S(2)}, u32[]{:S(2)}) collective-permute-start(bf16[4,64,768]{2,1,0:T(8,128)(2,1)} %get-tuple-element.34), channel_id=1, source_target_pairs={{0,8},{8,16},{16,24},{24,0},{1,9},{9,17},{17,25},{25,1},{2,10},{10... | collective-permute-start | bytes 1179656 | tf_op jit(solution)/shard_map/ppermute | solution.py:461
  46.1 42.4 %collective-permute-start.6 = (bf16[4,64,768]{2,1,0:T(8,128)(2,1)}, bf16[4,64,768]{2,1,0:T(8,128)(2,1)S(1)}, u32[]{:S(2)}, u32[]{:S(2)}) collective-permute-start(bf16[4,64,768]{2,1,0:T(8,128)(2,1)} %get-tuple-element.35), channel_id=1, source_target_pairs={{0,16},{8,24},{16,0},{24,8},{1,17},{9,25},{17,1},{25,9},{2,18},{10... | collective-permute-start | bytes 1179656 | tf_op jit(solution)/shard_map/ppermute | solution.py:461
  48.7 39.9 %collective-permute-start.7 = (bf16[4,64,768]{2,1,0:T(8,128)(2,1)}, bf16[4,64,768]{2,1,0:T(8,128)(2,1)S(1)}, u32[]{:S(2)}, u32[]{:S(2)}) collective-permute-start(bf16[4,64,768]{2,1,0:T(8,128)(2,1)} %get-tuple-element.36), channel_id=1, source_target_pairs={{0,24},{8,0},{16,8},{24,16},{1,25},{9,1},{17,9},{25,17},{2,26},{10... | collective-permute-start | bytes 1179656 | tf_op jit(solution)/shard_map/ppermute | solution.py:461
  51.5 2.2 %copy-start.8 = (bf16[256,1536]{1,0:T(8,128)(2,1)}, bf16[256,1536]{1,0:T(8,128)(2,1)S(1)}, u32[]{:S(2)}) copy-start(bf16[256,1536]{1,0:T(8,128)(2,1)S(1)} %collective-permute-done.2.refs_1_.refs_3_) | copy-start | bytes 2359300
  56.0 20.4 %collective-permute-start.4 = (bf16[128,1536]{1,0:T(8,128)(2,1)}, bf16[128,1536]{1,0:T(8,128)(2,1)S(1)}, u32[]{:S(2)}, u32[]{:S(2)}) collective-permute-start(bf16[128,1536]{1,0:T(8,128)(2,1)} %get-tuple-element.31), channel_id=1, source_target_pairs={{0,4},{2,6},{4,0},{6,2},{1,5},{3,7},{5,1},{7,3},{8,12},{10,14},{12... | collective-permute-start | bytes 1179656 | tf_op jit(solution)/shard_map/ppermute | solution.py:452
  56.7 21.1 %collective-permute-start.3 = (bf16[128,1536]{1,0:T(8,128)(2,1)}, bf16[128,1536]{1,0:T(8,128)(2,1)S(1)}, u32[]{:S(2)}, u32[]{:S(2)}) collective-permute-start(bf16[128,1536]{1,0:T(8,128)(2,1)} %get-tuple-element.29.refs_3_), channel_id=1, source_target_pairs={{0,2},{2,0},{4,6},{6,4},{1,3},{3,1},{5,7},{7,5},{8,10},{10,8},{12,... | collective-permute-start | bytes 1179656 | tf_op jit(solution)/shard_map/ppermute | solution.py:452
  70.0 1.1 copy-start.1
  76.4 1.5 %copy-start.9 = (bf16[128,1536]{1,0:T(8,128)(2,1)}, bf16[128,1536]{1,0:T(8,128)(2,1)S(1)}, u32[]{:S(2)}) copy-start(bf16[128,1536]{1,0:T(8,128)(2,1)S(1)} %collective-permute-done.4.refs_6_.refs_3_) | copy-start | bytes 1179652
  77.9 0.7 copy-start.10
  88.5 0.7 copy-start.2
  88.5 0.9 copy-start.3
  88.6 1.0 copy-start.4
  89.6 41.3 %all-to-all-start.2 = ((bf16[16,64,768]{2,1,0:T(8,128)(2,1)}), bf16[16,64,768]{2,1,0:T(8,128)(2,1)S(1)}, u32[]{:S(2)}, u32[]{:S(2)}) async-start(bf16[16,64,768]{2,1,0:T(8,128)(2,1)} %get-tuple-element.39.refs_4_), calls=%async_computation.2 | async-start | bytes 3145728 | tf_op jit(solution)/shard_map/all_to_all | solution.py:486
  94.4 20.7 %collective-permute-start.8 = (bf16[256,1536]{1,0:T(8,128)(2,1)}, bf16[256,1536]{1,0:T(8,128)(2,1)S(1)}, u32[]{:S(2)}, u32[]{:S(2)}) collective-permute-start(bf16[256,1536]{1,0:T(8,128)(2,1)} %get-tuple-element.37), channel_id=1, source_target_pairs={{0,2},{2,0},{4,6},{6,4},{1,3},{3,1},{5,7},{7,5},{8,10},{10,8},{12,... | collective-permute-start | bytes 2359304 | tf_op jit(solution)/shard_map/ppermute | solution.py:452
  95.9 35.0 %collective-permute-start.9 = (bf16[256,1536]{1,0:T(8,128)(2,1)}, bf16[256,1536]{1,0:T(8,128)(2,1)S(1)}, u32[]{:S(2)}, u32[]{:S(2)}) collective-permute-start(bf16[256,1536]{1,0:T(8,128)(2,1)} %get-tuple-element.38), channel_id=1, source_target_pairs={{0,4},{2,6},{4,0},{6,2},{1,5},{3,7},{5,1},{7,3},{8,12},{10,14},{12... | collective-permute-start | bytes 2359304 | tf_op jit(solution)/shard_map/ppermute | solution.py:452
  103.5 32.4 %collective-permute-start.10 = (bf16[256,1536]{1,0:T(8,128)(2,1)}, bf16[256,1536]{1,0:T(8,128)(2,1)}, u32[]{:S(2)}, u32[]{:S(2)}) collective-permute-start(bf16[256,1536]{1,0:T(8,128)(2,1)} %shard_map.130.refs_6_), channel_id=1, source_target_pairs={{0,6},{2,4},{4,2},{6,0},{1,7},{3,5},{5,3},{7,1},{8,14},{10,12},{12... | collective-permute-start | bytes 2359304 | tf_op jit(solution)/shard_map/ppermute | solution.py:452
  115.1 15.7 %copy-start.6 = (bf16[256,1536]{1,0:T(8,128)(2,1)}, bf16[256,1536]{1,0:T(8,128)(2,1)S(1)}, u32[]{:S(2)}) copy-start(bf16[256,1536]{1,0:T(8,128)(2,1)S(1)} %collective-permute-done.8.refs_4_.refs_5_) | copy-start | bytes 2359300
  130.8 0.9 copy-start.7
  131.7 1.2 copy-start.5

commit v10 on v9

--- a/solution.py
+++ b/solution.py
@@ -257,7 +257,8 @@
     total = terms[0][...].astype(f32)
     for term in terms[1:]:
         total = total + term[...].astype(f32)
-    live = lax.broadcasted_iota(jnp.int32, total.shape, 0) < news[request]
+    token = lax.broadcasted_iota(jnp.int32, total.shape, 0)
+    live = token + pl.program_id(1) * total.shape[0] < news[request]
     out[0] = jnp.where(live, total, 0.0).astype(out.dtype)
 
 
@@ -494,14 +495,14 @@
 
     def add(terms, out_shape, after, flops):
         return call(
-            sum_kernel, (request_order, new_lengths, dev), (reqs,),
-            [pl.BlockSpec((new, width), lambda r, *_: (r, 0))] * len(terms),
-            pl.BlockSpec((1, new, width), lambda r, *_: (r, 0, 0)),
+            sum_kernel, (request_order, new_lengths, dev), (reqs, 2),
+            [pl.BlockSpec((new // 2, width), lambda r, h, *_: (2 * r + h, 0))] * len(terms),
+            pl.BlockSpec((1, new // 2, width), lambda r, h, *_: (r, h, 0)),
             out_shape, [], tuple(terms), flops, after=after,
         )
 
     kv_decode = unpack(
-        key_width, [values_arrived], (kv_half,), tuple(partials[1:-1]), LONG * flat * width * width * 8
+        key_width, [values_arrived], (kv_half,), tuple(partials[1:2]), LONG * flat * width * width * 8
     )
     layer_out = add([residual, *partials], shape(tokens.shape), (kv_decode,), 0)
     return (layer_out, kv_decode)

time: 140 us -> 141 us (level)
    ppermute x7, waiting for transfers between devices: 30.4 us -> 14.4 us  [swap(): return lax.ppermute(rows, 'chip', [(c, c ^ mask) for c in range(chips)])]
    all_to_all x1, waiting for transfers between devices: 0.01 us -> 15.6 us  [local(): lax.all_to_all(values_ready, 'dp', split_axis=0, concat_axis=0, tiled=True)]
where the time goes in v10:
time: 141 us; the launch traced here: 140 us
  Pallas kernels  67.7 us (48%)
  waiting for transfers between devices  34.4 us (24%)
  starting transfers between devices  29.5 us (21%)
  local copies, waits for them, and re-layouts  5.22 us (4%)
  other arithmetic  2.21 us (2%)
    pallas_call x12, Pallas kernels, call(): pl.pallas_call(ordered, out_shape=out_shape, grid_spec=pltpu.PrefetchScal...  67.7 us
    all_to_all x1, waiting for transfers between devices, local(): lax.all_to_all(values_ready, 'dp', split_axis=0, concat_axis=0, tiled=True)  15.6 us
    ppermute x7, waiting for transfers between devices, swap(): return lax.ppermute(rows, 'chip', [(c, c ^ mask) for c in range(chips)])  14.4 us
    ppermute x7, starting transfers between devices, swap(): return lax.ppermute(rows, 'chip', [(c, c ^ mask) for c in range(chips)])  10 us
    ppermute x3, starting transfers between devices, local(): lax.ppermute(rows, 'dp', pairs)  5.57 us
    unnamed x26, local copies, waits for them, and re-layouts  5.22 us
    all_to_all x1, starting transfers between devices, local(): lax.all_to_all(values_ready, 'dp', split_axis=0, concat_axis=0, tiled=True)  5.01 us
    all_to_all x1, starting transfers between devices, local(): lax.all_to_all(keys, tensor, split_axis=0, concat_axis=0, tiled=True)  4.83 us
  transfers between devices with their start and end apart: 14, of which 7 were waited for; matrix products, arithmetic and copies ran while one was open for 2% of the time, Pallas kernels for 45%

profile of v10, /device:TPU:0, one launch (start us, length us, event | category | flops | bytes accessed | tf_op | source)
XLA Modules:
  0.0 139.8 jit_solution(11515965946339014899)
XLA Ops:
  0.6 0.5 collective-permute-start
  1.1 6.4 %shard_map.122 = (bf16[8,2,64,768]{3,2,1,0:T(8,128)(2,1)}, bf16[2,128,1536]{2,1,0:T(8,128)(2,1)}, f32[2,128,384]{2,1,0:T(8,128)}, f32[2,128,384]{2,1,0:T(8,128)}) custom-call(s32[64]{0:T(128)} %refs_0_.11, s32[64]{0:T(128)} %refs_1_.5, s32[64]{0:T(128)} %refs_2_.3, s32[1]{0:T(128)} %bitcast.refs_3_.refs_2_, bf16[2,128,1536]{2,1,0:T(8,128)(2,1)} %refs_11_.1, ...), custom_call_target="tpu_custom_call" | custom-call | flops 603979776 | bytes 8388608 | tf_op jit(solution)/shard_map/pallas_call | solution.py:274
  7.6 4.8 %all-to-all-start = ((bf16[8,2,64,768]{3,2,1,0:T(8,128)(2,1)}), bf16[8,2,64,768]{3,2,1,0:T(8,128)(2,1)S(1)}, u32[]{:S(2)}, u32[]{:S(2)}) async-start(bf16[8,2,64,768]{3,2,1,0:T(8,128)(2,1)} %get-tuple-element.24.refs_9_), calls=%async_computation | async-start | bytes 3145728 | tf_op jit(solution)/shard_map/all_to_all | solution.py:350
  12.4 0.0 copy-start.11
  12.4 0.0 copy-start.12
  12.4 18.4 %shard_map.123 = (bf16[8,2,64,768]{3,2,1,0:T(8,128)(2,1)}, bf16[256,1536]{1,0:T(8,128)(2,1)}, bf16[256,1536]{1,0:T(8,128)(2,1)}) custom-call(s32[64]{0:T(128)} %refs_0_.11, s32[64]{0:T(128)} %refs_1_.5, s32[64]{0:T(128)} %refs_2_.3, s32[1]{0:T(128)} %bitcast.refs_3_.refs_2_, bf16[2,128,1536]{2,1,0:T(8,128)(2,1)} %get-tuple-element.21.refs_4_, ...), custom_call_target="tpu_custom_call" | custom-call | flops 7247757312 | bytes 16777216 | tf_op jit(solution)/shard_map/pallas_call | solution.py:274
  30.8 2.2 %collective-permute-start.2 = (bf16[256,1536]{1,0:T(8,128)(2,1)}, bf16[256,1536]{1,0:T(8,128)(2,1)S(1)}, u32[]{:S(2)}, u32[]{:S(2)}) collective-permute-start(bf16[256,1536]{1,0:T(8,128)(2,1)} %get-tuple-element.26.refs_4_.refs_2_), channel_id=1, source_target_pairs={{0,4},{2,6},{4,0},{6,2},{1,5},{3,7},{5,1},{7,3},{8,12},{10,14},{12... | collective-permute-start | bytes 2359304 | tf_op jit(solution)/shard_map/ppermute | solution.py:453
  33.0 1.5 %collective-permute-start.1 = (bf16[256,1536]{1,0:T(8,128)(2,1)}, bf16[256,1536]{1,0:T(8,128)(2,1)}, u32[]{:S(2)}, u32[]{:S(2)}) collective-permute-start(bf16[256,1536]{1,0:T(8,128)(2,1)} %get-tuple-element.26.refs_4_.refs_2_), channel_id=1, source_target_pairs={{0,2},{2,0},{4,6},{6,4},{1,3},{3,1},{5,7},{7,5},{8,10},{10,8},{12,... | collective-permute-start | bytes 2359304 | tf_op jit(solution)/shard_map/ppermute | solution.py:453
  34.5 0.0 copy-done.11
  34.5 0.0 copy-done.12
  34.5 0.2 select_reduce_fusion
  34.6 0.1 fusion.2
  34.7 0.2 convert_reduce_fusion.1
  34.9 0.7 select_reduce_fusion.3.refs_0_
  35.6 0.2 select_reduce_fusion.2
  35.8 0.2 convert_reduce_fusion
  36.0 0.7 select_reduce_fusion.1.refs_4_.refs_0_
  36.7 0.0 all-to-all-done
  36.7 0.0 copy-start
  36.7 0.0 collective-permute-done.refs_5_.refs_1_
  36.7 1.1 copy-done
  37.8 3.1 %shard_map.124 = (bf16[4,64,768]{2,1,0:T(8,128)(2,1)}, bf16[4,64,768]{2,1,0:T(8,128)(2,1)}, bf16[4,64,768]{2,1,0:T(8,128)(2,1)}, bf16[4,64,768]{2,1,0:T(8,128)(2,1)}, bf16[8,2,64,768]{3,2,1,0:T(8,128)(2,1)}) custom-call(s32[16]{0:T(128)} %select_reduce_fusion.3.refs_0_, s32[1]{0:T(128)} %bitcast.1.refs_1_, ...), custom_call_target="tpu_custom_call", output_to_operand_aliasing={{4}: (3, {})} | custom-call | bytes 6291456 | tf_op jit(solution)/shard_map/pallas_call | solution.py:274
  40.9 3.6 %all-to-all-start.1 = ((bf16[8,2,64,768]{3,2,1,0:T(8,128)(2,1)}), bf16[8,2,64,768]{3,2,1,0:T(8,128)(2,1)S(1)}, u32[]{:S(2)}, u32[]{:S(2)}) async-start(bf16[8,2,64,768]{3,2,1,0:T(8,128)(2,1)} %get-tuple-element.30), calls=%async_computation.1 | async-start | bytes 3145728 | tf_op jit(solution)/shard_map/all_to_all | solution.py:460
  44.5 1.6 %collective-permute-start.5 = (bf16[4,64,768]{2,1,0:T(8,128)(2,1)}, bf16[4,64,768]{2,1,0:T(8,128)(2,1)S(1)}, u32[]{:S(2)}, u32[]{:S(2)}) collective-permute-start(bf16[4,64,768]{2,1,0:T(8,128)(2,1)} %get-tuple-element.34), channel_id=1, source_target_pairs={{0,8},{8,16},{16,24},{24,0},{1,9},{9,17},{17,25},{25,1},{2,10},{10... | collective-permute-start | bytes 1179656 | tf_op jit(solution)/shard_map/ppermute | solution.py:462
  46.2 2.6 %collective-permute-start.6 = (bf16[4,64,768]{2,1,0:T(8,128)(2,1)}, bf16[4,64,768]{2,1,0:T(8,128)(2,1)S(1)}, u32[]{:S(2)}, u32[]{:S(2)}) collective-permute-start(bf16[4,64,768]{2,1,0:T(8,128)(2,1)} %get-tuple-element.35), channel_id=1, source_target_pairs={{0,16},{8,24},{16,0},{24,8},{1,17},{9,25},{17,1},{25,9},{2,18},{10... | collective-permute-start | bytes 1179656 | tf_op jit(solution)/shard_map/ppermute | solution.py:462
  48.8 1.3 collective-permute-start.7
  50.1 1.4 %collective-permute-done.2.refs_1_.refs_3_ = bf16[256,1536]{1,0:T(8,128)(2,1)S(1)} collective-permute-done((bf16[256,1536]{1,0:T(8,128)(2,1)}, bf16[256,1536]{1,0:T(8,128)(2,1)S(1)}, u32[]{:S(2)}, u32[]{:S(2)}) %collective-permute-start.2) | collective-permute-done | bytes 786464 | tf_op jit(solution)/shard_map/ppermute | solution.py:453
  51.5 2.2 %collective-permute-done.1.refs_0_.refs_2_ = bf16[256,1536]{1,0:T(8,128)(2,1)} collective-permute-done((bf16[256,1536]{1,0:T(8,128)(2,1)}, bf16[256,1536]{1,0:T(8,128)(2,1)}, u32[]{:S(2)}, u32[]{:S(2)}) %collective-permute-start.1) | collective-permute-done | bytes 786464 | tf_op jit(solution)/shard_map/ppermute | solution.py:453
  53.7 0.0 copy-done.7
  53.7 2.3 %shard_map.125 = (bf16[128,1536]{1,0:T(8,128)(2,1)}, bf16[128,1536]{1,0:T(8,128)(2,1)}) custom-call(bf16[256,1536]{1,0:T(8,128)(2,1)} %collective-permute-done.1.refs_0_.refs_2_, bf16[256,1536]{1,0:T(8,128)(2,1)} %copy-done.7, bf16[4,64,768]{2,1,0:T(8,128)(2,1)} %get-tuple-element.28.refs_2_), custom_call_target="tpu_custom_call" | custom-call | bytes 6291456 | tf_op jit(solution)/shard_map/pallas_call | solution.py:274
  56.0 0.7 collective-permute-start.4
  56.7 2.2 %collective-permute-start.3 = (bf16[128,1536]{1,0:T(8,128)(2,1)}, bf16[128,1536]{1,0:T(8,128)(2,1)S(1)}, u32[]{:S(2)}, u32[]{:S(2)}) collective-permute-start(bf16[128,1536]{1,0:T(8,128)(2,1)} %get-tuple-element.29.refs_3_), channel_id=1, source_target_pairs={{0,2},{2,0},{4,6},{6,4},{1,3},{3,1},{5,7},{7,5},{8,10},{10,8},{12,... | collective-permute-start | bytes 1179656 | tf_op jit(solution)/shard_map/ppermute | solution.py:453
  58.9 6.8 %shard_map.126.refs_3_.refs_4_ = bf16[256,1536]{1,0:T(8,128)(2,1)} custom-call(bf16[3,1536,512]{2,1,0:T(8,128)(2,1)} %refs_0_.10, bf16[3,1536,512]{2,1,0:T(8,128)(2,1)} %collective-permute-done.refs_5_.refs_1_, bf16[256,1536]{1,0:T(8,128)(2,1)} %get-tuple-element.26.refs_4_.refs_2_, bf16[128,1536]{1,0:T(8,128)(2,1)} %get-tuple-element.29.refs_3_, ...), custom_call_target="tpu_custom_call" | custom-call | flops 96636764160 | bytes 9437184 | tf_op jit(solution)/shard_map/pallas_call | solution.py:274
  65.7 4.3 %all-to-all-done.1 = bf16[8,2,64,768]{3,2,1,0:T(8,128)(2,1)S(1)} async-done(((bf16[8,2,64,768]{3,2,1,0:T(8,128)(2,1)}), bf16[8,2,64,768]{3,2,1,0:T(8,128)(2,1)S(1)}, u32[]{:S(2)}, u32[]{:S(2)}) %all-to-all-start.1) | async-done | bytes 1572896 | tf_op jit(solution)/shard_map/all_to_all | solution.py:460
  70.0 1.1 copy-done.1
  71.2 3.1 %shard_map.127.refs_4_.refs_0_ = bf16[16,64,768]{2,1,0:T(8,128)(2,1)} custom-call(s32[16]{0:T(128)} %select_reduce_fusion.3.refs_0_, s32[1]{0:T(128)} %bitcast.1.refs_1_, bf16[16,64,768]{2,1,0:T(8,128)(2,1)} %bitcast.5, bf16[256,1536]{1,0:T(8,128)(2,1)} %shard_map.126.refs_3_.refs_4_), custom_call_target="tpu_custom_call" | custom-call | bytes 6291456 | tf_op jit(solution)/shard_map/pallas_call | solution.py:274
  74.3 2.1 %collective-permute-done.4.refs_6_.refs_3_ = bf16[128,1536]{1,0:T(8,128)(2,1)S(1)} collective-permute-done((bf16[128,1536]{1,0:T(8,128)(2,1)}, bf16[128,1536]{1,0:T(8,128)(2,1)S(1)}, u32[]{:S(2)}, u32[]{:S(2)}) %collective-permute-start.4) | collective-permute-done | bytes 393248 | tf_op jit(solution)/shard_map/ppermute | solution.py:453
  76.4 1.5 %collective-permute-done.3.refs_5_.refs_2_ = bf16[128,1536]{1,0:T(8,128)(2,1)S(1)} collective-permute-done((bf16[128,1536]{1,0:T(8,128)(2,1)}, bf16[128,1536]{1,0:T(8,128)(2,1)S(1)}, u32[]{:S(2)}, u32[]{:S(2)}) %collective-permute-start.3) | collective-permute-done | bytes 393248 | tf_op jit(solution)/shard_map/ppermute | solution.py:453
  77.9 0.0 copy-done.9
  77.9 0.7 copy-done.10
  78.6 9.9 %shard_map.128 = (bf16[256,1536]{1,0:T(8,128)(2,1)}, bf16[256,1536]{1,0:T(8,128)(2,1)}) custom-call(bf16[3,1536,512]{2,1,0:T(8,128)(2,1)} %refs_0_.10, bf16[3,1536,512]{2,1,0:T(8,128)(2,1)} %collective-permute-done.refs_5_.refs_1_, bf16[256,1536]{1,0:T(8,128)(2,1)} %collective-permute-done.1.refs_0_.refs_2_, bf16[256,1536]{1,0:T(8,128)(2,1)} %copy-done.7, ...), custom_call_target="tpu_custom_call" | custom-call | flops 4831838208 | bytes 9437184 | tf_op jit(solution)/shard_map/pallas_call | solution.py:274
  88.5 0.0 collective-permute-done.5.refs_3_
  88.5 0.0 collective-permute-done.6.refs_4_
  88.5 0.0 copy-start.3
  88.6 0.0 collective-permute-done.7.refs_5_
  88.6 0.0 copy-start.4
  88.6 0.7 copy-done.2
  89.3 0.1 copy-done.3
  89.4 0.1 copy-done.4
  89.6 5.0 %all-to-all-start.2 = ((bf16[16,64,768]{2,1,0:T(8,128)(2,1)}), bf16[16,64,768]{2,1,0:T(8,128)(2,1)S(1)}, u32[]{:S(2)}, u32[]{:S(2)}) async-start(bf16[16,64,768]{2,1,0:T(8,128)(2,1)} %get-tuple-element.39.refs_4_), calls=%async_computation.2 | async-start | bytes 3145728 | tf_op jit(solution)/shard_map/all_to_all | solution.py:487
  94.6 0.0 copy-done.8
  94.6 1.5 %collective-permute-start.8 = (bf16[256,1536]{1,0:T(8,128)(2,1)S(1)}, bf16[256,1536]{1,0:T(8,128)(2,1)S(1)}, u32[]{:S(2)}, u32[]{:S(2)}) collective-permute-start(bf16[256,1536]{1,0:T(8,128)(2,1)S(1)} %copy-done.8), channel_id=1, source_target_pairs={{0,2},{2,0},{4,6},{6,4},{1,3},{3,1},{5,7},{7,5},{8,10},{10,8},{12,... | collective-permute-start | bytes 2359304 | tf_op jit(solution)/shard_map/ppermute | solution.py:453
  96.0 0.9 collective-permute-start.9
  97.0 6.7 %shard_map.130.refs_6_ = bf16[256,1536]{1,0:T(8,128)(2,1)} custom-call(bf16[3,1536,512]{2,1,0:T(8,128)(2,1)} %refs_0_.10, bf16[3,1536,512]{2,1,0:T(8,128)(2,1)} %collective-permute-done.refs_5_.refs_1_, bf16[128,1536]{1,0:T(8,128)(2,1)} %copy-done.10, bf16[128,1536]{1,0:T(8,128)(2,1)} %copy-done.9, bf16[16,64,768]{2,1,0:T(8,128)(2,1)} %get-tuple-element.39.refs_4_), custom_call_target="tpu_custom_call" | custom-call | flops 2415919104 | bytes 9437184 | tf_op jit(solution)/shard_map/pallas_call | solution.py:274
  103.7 1.1 collective-permute-start.10
  104.8 3.1 %shard_map.131.refs_3_ = bf16[16,64,1536]{2,1,0:T(8,128)(2,1)} custom-call(s32[16]{0:T(128)} %select_reduce_fusion.1.refs_4_.refs_0_, s32[1]{0:T(128)} %bitcast.1.refs_1_, bf16[4,64,768]{2,1,0:T(8,128)(2,1)} %get-tuple-element.28.refs_2_, bf16[4,64,768]{2,1,0:T(8,128)(2,1)} %copy-done.2, bf16[4,64,768]{2,1,0:T(8,128)(2,1)} %copy-done.3, ...), custom_call_target="tpu_custom_call" | custom-call | bytes 6291456 | tf_op jit(solution)/shard_map/pallas_call | solution.py:274
  107.8 7.2 %collective-permute-done.8.refs_4_.refs_5_ = bf16[256,1536]{1,0:T(8,128)(2,1)S(1)} collective-permute-done((bf16[256,1536]{1,0:T(8,128)(2,1)S(1)}, bf16[256,1536]{1,0:T(8,128)(2,1)S(1)}, u32[]{:S(2)}, u32[]{:S(2)}) %collective-permute-start.8) | collective-permute-done | bytes 786464 | tf_op jit(solution)/shard_map/ppermute | solution.py:453
  115.1 15.6 %all-to-all-done.2.refs_2_ = bf16[16,64,768]{2,1,0:T(8,128)(2,1)S(1)} async-done(((bf16[16,64,768]{2,1,0:T(8,128)(2,1)}), bf16[16,64,768]{2,1,0:T(8,128)(2,1)S(1)}, u32[]{:S(2)}, u32[]{:S(2)}) %all-to-all-start.2) | async-done | bytes 1572896 | tf_op jit(solution)/shard_map/all_to_all | solution.py:487
  130.7 0.0 copy-done.6
  130.7 1.2 copy-done.5
  131.9 3.1 %shard_map.132.refs_8_ = bf16[16,64,1536]{2,1,0:T(8,128)(2,1)} custom-call(s32[16]{0:T(128)} %select_reduce_fusion.1.refs_4_.refs_0_, s32[1]{0:T(128)} %bitcast.1.refs_1_, bf16[16,64,768]{2,1,0:T(8,128)(2,1)} %copy-done.5, bf16[16,64,1536]{2,1,0:T(8,128)(2,1)} %shard_map.131.refs_3_, bf16[256,1536]{1,0:T(8,128)(2,1)} %copy-done.6), custom_call_target="tpu_custom_call", output_to_operand_aliasing={{}: (3, {})} | custom-call | flops 193273528320 | bytes 6291456 | tf_op jit(solution)/shard_map/pallas_call | solution.py:274
  135.0 0.0 collective-permute-done.9.refs_6_
  135.0 0.0 collective-permute-done.10.refs_7_
  135.0 4.8 %shard_map.133 = bf16[2,128,1536]{2,1,0:T(8,128)(2,1)} custom-call(s32[64]{0:T(128)} %refs_0_.11, s32[64]{0:T(128)} %refs_1_.5, s32[1]{0:T(128)} %bitcast.refs_3_.refs_2_, bf16[256,1536]{1,0:T(8,128)(2,1)} %get-tuple-element.25.refs_3_, bf16[256,1536]{1,0:T(8,128)(2,1)} %shard_map.126.refs_3_.refs_4_, bf16[256,1536]{1,0:T(8,128)(2,1)} %copy-done.6, ...), custom_call_target="tpu_custom_call" | custom-call | bytes 6291456 | tf_op jit(solution)/shard_map/pallas_call | solution.py:274
  (12 shorter events, 0.0 us)
Async XLA Ops:
  0.6 36.1 %collective-permute-start = (bf16[3,1536,512]{2,1,0:T(8,128)(2,1)}, bf16[3,1536,512]{2,1,0:T(8,128)(2,1)}, u32[]{:S(2)}, u32[]{:S(2)}) collective-permute-start(bf16[3,1536,512]{2,1,0:T(8,128)(2,1)} %refs_0_.10), channel_id=1, source_target_pairs={{0,1},{1,0},{2,3},{3,2},{4,5},{5,4},{6,7},{7,6},{8,9},{9,8},{10,11... | collective-permute-start | bytes 14155784 | tf_op jit(solution)/shard_map/ppermute | solution.py:327
  7.6 29.1 %all-to-all-start = ((bf16[8,2,64,768]{3,2,1,0:T(8,128)(2,1)}), bf16[8,2,64,768]{3,2,1,0:T(8,128)(2,1)S(1)}, u32[]{:S(2)}, u32[]{:S(2)}) async-start(bf16[8,2,64,768]{3,2,1,0:T(8,128)(2,1)} %get-tuple-element.24.refs_9_), calls=%async_computation | async-start | bytes 3145728 | tf_op jit(solution)/shard_map/all_to_all | solution.py:350
  12.4 22.1 %copy-start.11 = (s32[64]{0:T(128)S(1)}, s32[64]{0:T(128)}, u32[]{:S(2)}) copy-start(s32[64]{0:T(128)} %refs_0_.11) | copy-start | bytes 772
  12.4 22.1 %copy-start.12 = (s32[64]{0:T(128)S(1)}, s32[64]{0:T(128)}, u32[]{:S(2)}) copy-start(s32[64]{0:T(128)} %param.20) | copy-start | bytes 772
  30.8 20.7 %collective-permute-start.2 = (bf16[256,1536]{1,0:T(8,128)(2,1)}, bf16[256,1536]{1,0:T(8,128)(2,1)S(1)}, u32[]{:S(2)}, u32[]{:S(2)}) collective-permute-start(bf16[256,1536]{1,0:T(8,128)(2,1)} %get-tuple-element.26.refs_4_.refs_2_), channel_id=1, source_target_pairs={{0,4},{2,6},{4,0},{6,2},{1,5},{3,7},{5,1},{7,3},{8,12},{10,14},{12... | collective-permute-start | bytes 2359304 | tf_op jit(solution)/shard_map/ppermute | solution.py:453
  33.0 20.7 %collective-permute-start.1 = (bf16[256,1536]{1,0:T(8,128)(2,1)}, bf16[256,1536]{1,0:T(8,128)(2,1)}, u32[]{:S(2)}, u32[]{:S(2)}) collective-permute-start(bf16[256,1536]{1,0:T(8,128)(2,1)} %get-tuple-element.26.refs_4_.refs_2_), channel_id=1, source_target_pairs={{0,2},{2,0},{4,6},{6,4},{1,3},{3,1},{5,7},{7,5},{8,10},{10,8},{12,... | collective-permute-start | bytes 2359304 | tf_op jit(solution)/shard_map/ppermute | solution.py:453
  36.7 1.1 copy-start
  40.9 29.1 %all-to-all-start.1 = ((bf16[8,2,64,768]{3,2,1,0:T(8,128)(2,1)}), bf16[8,2,64,768]{3,2,1,0:T(8,128)(2,1)S(1)}, u32[]{:S(2)}, u32[]{:S(2)}) async-start(bf16[8,2,64,768]{3,2,1,0:T(8,128)(2,1)} %get-tuple-element.30), calls=%async_computation.1 | async-start | bytes 3145728 | tf_op jit(solution)/shard_map/all_to_all | solution.py:460
  44.5 44.0 %collective-permute-start.5 = (bf16[4,64,768]{2,1,0:T(8,128)(2,1)}, bf16[4,64,768]{2,1,0:T(8,128)(2,1)S(1)}, u32[]{:S(2)}, u32[]{:S(2)}) collective-permute-start(bf16[4,64,768]{2,1,0:T(8,128)(2,1)} %get-tuple-element.34), channel_id=1, source_target_pairs={{0,8},{8,16},{16,24},{24,0},{1,9},{9,17},{17,25},{25,1},{2,10},{10... | collective-permute-start | bytes 1179656 | tf_op jit(solution)/shard_map/ppermute | solution.py:462
  46.2 42.4 %collective-permute-start.6 = (bf16[4,64,768]{2,1,0:T(8,128)(2,1)}, bf16[4,64,768]{2,1,0:T(8,128)(2,1)S(1)}, u32[]{:S(2)}, u32[]{:S(2)}) collective-permute-start(bf16[4,64,768]{2,1,0:T(8,128)(2,1)} %get-tuple-element.35), channel_id=1, source_target_pairs={{0,16},{8,24},{16,0},{24,8},{1,17},{9,25},{17,1},{25,9},{2,18},{10... | collective-permute-start | bytes 1179656 | tf_op jit(solution)/shard_map/ppermute | solution.py:462
  48.8 39.8 %collective-permute-start.7 = (bf16[4,64,768]{2,1,0:T(8,128)(2,1)}, bf16[4,64,768]{2,1,0:T(8,128)(2,1)S(1)}, u32[]{:S(2)}, u32[]{:S(2)}) collective-permute-start(bf16[4,64,768]{2,1,0:T(8,128)(2,1)} %get-tuple-element.36), channel_id=1, source_target_pairs={{0,24},{8,0},{16,8},{24,16},{1,25},{9,1},{17,9},{25,17},{2,26},{10... | collective-permute-start | bytes 1179656 | tf_op jit(solution)/shard_map/ppermute | solution.py:462
  51.5 2.2 %copy-start.7 = (bf16[256,1536]{1,0:T(8,128)(2,1)}, bf16[256,1536]{1,0:T(8,128)(2,1)S(1)}, u32[]{:S(2)}) copy-start(bf16[256,1536]{1,0:T(8,128)(2,1)S(1)} %collective-permute-done.2.refs_1_.refs_3_) | copy-start | bytes 2359300
  56.0 20.4 %collective-permute-start.4 = (bf16[128,1536]{1,0:T(8,128)(2,1)}, bf16[128,1536]{1,0:T(8,128)(2,1)S(1)}, u32[]{:S(2)}, u32[]{:S(2)}) collective-permute-start(bf16[128,1536]{1,0:T(8,128)(2,1)} %get-tuple-element.31), channel_id=1, source_target_pairs={{0,4},{2,6},{4,0},{6,2},{1,5},{3,7},{5,1},{7,3},{8,12},{10,14},{12... | collective-permute-start | bytes 1179656 | tf_op jit(solution)/shard_map/ppermute | solution.py:453
  56.7 21.1 %collective-permute-start.3 = (bf16[128,1536]{1,0:T(8,128)(2,1)}, bf16[128,1536]{1,0:T(8,128)(2,1)S(1)}, u32[]{:S(2)}, u32[]{:S(2)}) collective-permute-start(bf16[128,1536]{1,0:T(8,128)(2,1)} %get-tuple-element.29.refs_3_), channel_id=1, source_target_pairs={{0,2},{2,0},{4,6},{6,4},{1,3},{3,1},{5,7},{7,5},{8,10},{10,8},{12,... | collective-permute-start | bytes 1179656 | tf_op jit(solution)/shard_map/ppermute | solution.py:453
  70.0 1.1 copy-start.1
  76.4 1.5 %copy-start.9 = (bf16[128,1536]{1,0:T(8,128)(2,1)}, bf16[128,1536]{1,0:T(8,128)(2,1)S(1)}, u32[]{:S(2)}) copy-start(bf16[128,1536]{1,0:T(8,128)(2,1)S(1)} %collective-permute-done.4.refs_6_.refs_3_) | copy-start | bytes 1179652
  77.9 0.7 copy-start.10
  88.5 0.8 copy-start.2
  88.5 0.9 copy-start.3
  88.6 1.0 copy-start.4
  89.6 5.0 %copy-start.8 = (bf16[256,1536]{1,0:T(8,128)(2,1)S(1)}, bf16[256,1536]{1,0:T(8,128)(2,1)}, u32[]{:S(2)}) copy-start(bf16[256,1536]{1,0:T(8,128)(2,1)} %get-tuple-element.37) | copy-start | bytes 2359300
  89.6 41.1 %all-to-all-start.2 = ((bf16[16,64,768]{2,1,0:T(8,128)(2,1)}), bf16[16,64,768]{2,1,0:T(8,128)(2,1)S(1)}, u32[]{:S(2)}, u32[]{:S(2)}) async-start(bf16[16,64,768]{2,1,0:T(8,128)(2,1)} %get-tuple-element.39.refs_4_), calls=%async_computation.2 | async-start | bytes 3145728 | tf_op jit(solution)/shard_map/all_to_all | solution.py:487
  94.6 20.5 %collective-permute-start.8 = (bf16[256,1536]{1,0:T(8,128)(2,1)S(1)}, bf16[256,1536]{1,0:T(8,128)(2,1)S(1)}, u32[]{:S(2)}, u32[]{:S(2)}) collective-permute-start(bf16[256,1536]{1,0:T(8,128)(2,1)S(1)} %copy-done.8), channel_id=1, source_target_pairs={{0,2},{2,0},{4,6},{6,4},{1,3},{3,1},{5,7},{7,5},{8,10},{10,8},{12,... | collective-permute-start | bytes 2359304 | tf_op jit(solution)/shard_map/ppermute | solution.py:453
  96.0 38.9 %collective-permute-start.9 = (bf16[256,1536]{1,0:T(8,128)(2,1)}, bf16[256,1536]{1,0:T(8,128)(2,1)}, u32[]{:S(2)}, u32[]{:S(2)}) collective-permute-start(bf16[256,1536]{1,0:T(8,128)(2,1)} %get-tuple-element.38), channel_id=1, source_target_pairs={{0,4},{2,6},{4,0},{6,2},{1,5},{3,7},{5,1},{7,3},{8,12},{10,14},{12... | collective-permute-start | bytes 2359304 | tf_op jit(solution)/shard_map/ppermute | solution.py:453
  103.7 31.3 %collective-permute-start.10 = (bf16[256,1536]{1,0:T(8,128)(2,1)}, bf16[256,1536]{1,0:T(8,128)(2,1)}, u32[]{:S(2)}, u32[]{:S(2)}) collective-permute-start(bf16[256,1536]{1,0:T(8,128)(2,1)} %shard_map.130.refs_6_), channel_id=1, source_target_pairs={{0,6},{2,4},{4,2},{6,0},{1,7},{3,5},{5,3},{7,1},{8,14},{10,12},{12... | collective-permute-start | bytes 2359304 | tf_op jit(solution)/shard_map/ppermute | solution.py:453
  115.1 15.6 %copy-start.6 = (bf16[256,1536]{1,0:T(8,128)(2,1)}, bf16[256,1536]{1,0:T(8,128)(2,1)S(1)}, u32[]{:S(2)}) copy-start(bf16[256,1536]{1,0:T(8,128)(2,1)S(1)} %collective-permute-done.8.refs_4_.refs_5_) | copy-start | bytes 2359300
  130.7 1.2 copy-start.5

commit v11 on v9

--- a/solution.py
+++ b/solution.py
@@ -263,7 +263,7 @@
 
 def call(
     kernel, prefetched, grid, in_specs, out_specs, out_shape, scratch, operands,
-    flops=0, moved=6 << 20, aliases={}, after=(),
+    flops=0, moved=6 << 20, aliases={}, after=(), vmem=VMEM,
 ):
     begin = len(prefetched) + len(operands)
 
@@ -280,7 +280,7 @@
             out_specs=out_specs,
             scratch_shapes=scratch,
         ),
-        compiler_params=pltpu.CompilerParams(vmem_limit_bytes=VMEM),
+        compiler_params=pltpu.CompilerParams(vmem_limit_bytes=vmem),
         cost_estimate=pl.CostEstimate(flops=flops, bytes_accessed=moved, transcendentals=0),
         input_output_aliases=aliases,
     )(*prefetched, *operands, *after)
@@ -446,6 +446,7 @@
             (spots, group), (1,), [anywhere] * (len(arrived) + len(target)), anywhere,
             shape((group_reqs, depth, 2 * key_width)), sems, (*arrived, *target), flops,
             aliases={2 + len(arrived): 0} if target else {}, after=after,
+            vmem=VMEM // 8 if target else VMEM,
         )
 
     def swap(rows, mask):
@@ -501,7 +502,7 @@
         )
 
     kv_decode = unpack(
-        key_width, [values_arrived], (kv_half,), tuple(partials[1:-1]), LONG * flat * width * width * 8
+        key_width, [values_arrived], (kv_half,), tuple(partials[1:2]), LONG * flat * width * width * 8
     )
     layer_out = add([residual, *partials], shape(tokens.shape), (kv_decode,), 0)
     return (layer_out, kv_decode)

time: 140 us -> 139 us (level)
  local copies, waits for them, and re-layouts: 6.08 us -> 4.05 us
    ppermute x7, waiting for transfers between devices: 30.4 us -> 14.4 us  [swap(): return lax.ppermute(rows, 'chip', [(c, c ^ mask) for c in range(chips)])]
    all_to_all x1, waiting for transfers between devices: 0.01 us -> 15.6 us  [local(): lax.all_to_all(values_ready, 'dp', split_axis=0, concat_axis=0, tiled=True)]
    unnamed x26, local copies, waits for them, and re-layouts: 6.08 us -> 4.05 us
  transfers between devices with their start and end apart: 14 -> 14, of which waited for: 7 -> 7; matrix products, arithmetic and copies ran while one was open for 2% -> 2% of each run, Pallas kernels for 45% -> 46%
where the time goes in v11:
time: 139 us
  Pallas kernels  67.5 us (49%)
  waiting for transfers between devices  34.4 us (25%)
  starting transfers between devices  29.5 us (21%)
  local copies, waits for them, and re-layouts  4.05 us (3%)
  other arithmetic  2.21 us (2%)
    pallas_call x12, Pallas kernels, call(): pl.pallas_call(ordered, out_shape=out_shape, grid_spec=pltpu.PrefetchScal...  67.5 us
    all_to_all x1, waiting for transfers between devices, local(): lax.all_to_all(values_ready, 'dp', split_axis=0, concat_axis=0, tiled=True)  15.6 us
    ppermute x7, waiting for transfers between devices, swap(): return lax.ppermute(rows, 'chip', [(c, c ^ mask) for c in range(chips)])  14.4 us
    ppermute x7, starting transfers between devices, swap(): return lax.ppermute(rows, 'chip', [(c, c ^ mask) for c in range(chips)])  10 us
    ppermute x3, starting transfers between devices, local(): lax.ppermute(rows, 'dp', pairs)  5.57 us
    all_to_all x1, starting transfers between devices, local(): lax.all_to_all(values_ready, 'dp', split_axis=0, concat_axis=0, tiled=True)  5.01 us
    all_to_all x1, starting transfers between devices, local(): lax.all_to_all(keys, tensor, split_axis=0, concat_axis=0, tiled=True)  4.83 us
    all_to_all x1, waiting for transfers between devices, local(): lax.all_to_all(values, tensor, split_axis=0, concat_axis=0, tiled=True)  4.33 us
  transfers between devices with their start and end apart: 14, of which 7 were waited for; matrix products, arithmetic and copies ran while one was open for 2% of the time, Pallas kernels for 46%

profile of v11, /device:TPU:0, one launch (start us, length us, event | category | flops | bytes accessed | tf_op | source)
XLA Modules:
  0.0 138.5 jit_solution(15182783927936413132)
XLA Ops:
  0.6 0.5 collective-permute-start
  1.1 6.4 %shard_map.122 = (bf16[8,2,64,768]{3,2,1,0:T(8,128)(2,1)}, bf16[2,128,1536]{2,1,0:T(8,128)(2,1)}, f32[2,128,384]{2,1,0:T(8,128)}, f32[2,128,384]{2,1,0:T(8,128)}) custom-call(s32[64]{0:T(128)} %refs_0_.11, s32[64]{0:T(128)} %refs_1_.5, s32[64]{0:T(128)} %refs_2_.3, s32[1]{0:T(128)} %bitcast.refs_3_.refs_2_, bf16[2,128,1536]{2,1,0:T(8,128)(2,1)} %refs_11_.1, ...), custom_call_target="tpu_custom_call" | custom-call | flops 603979776 | bytes 8388608 | tf_op jit(solution)/shard_map/pallas_call | solution.py:273
  7.6 4.8 %all-to-all-start = ((bf16[8,2,64,768]{3,2,1,0:T(8,128)(2,1)}), bf16[8,2,64,768]{3,2,1,0:T(8,128)(2,1)S(1)}, u32[]{:S(2)}, u32[]{:S(2)}) async-start(bf16[8,2,64,768]{3,2,1,0:T(8,128)(2,1)} %get-tuple-element.24.refs_9_), calls=%async_computation | async-start | bytes 3145728 | tf_op jit(solution)/shard_map/all_to_all | solution.py:349
  12.4 0.0 copy-start.11
  12.4 0.0 copy-start.12
  12.4 18.4 %shard_map.123 = (bf16[8,2,64,768]{3,2,1,0:T(8,128)(2,1)}, bf16[256,1536]{1,0:T(8,128)(2,1)}, bf16[256,1536]{1,0:T(8,128)(2,1)}) custom-call(s32[64]{0:T(128)} %refs_0_.11, s32[64]{0:T(128)} %refs_1_.5, s32[64]{0:T(128)} %refs_2_.3, s32[1]{0:T(128)} %bitcast.refs_3_.refs_2_, bf16[2,128,1536]{2,1,0:T(8,128)(2,1)} %get-tuple-element.21.refs_4_, ...), custom_call_target="tpu_custom_call" | custom-call | flops 7247757312 | bytes 16777216 | tf_op jit(solution)/shard_map/pallas_call | solution.py:273
  30.8 2.2 %collective-permute-start.2 = (bf16[256,1536]{1,0:T(8,128)(2,1)}, bf16[256,1536]{1,0:T(8,128)(2,1)S(1)}, u32[]{:S(2)}, u32[]{:S(2)}) collective-permute-start(bf16[256,1536]{1,0:T(8,128)(2,1)} %get-tuple-element.26.refs_4_.refs_2_), channel_id=1, source_target_pairs={{0,4},{2,6},{4,0},{6,2},{1,5},{3,7},{5,1},{7,3},{8,12},{10,14},{12... | collective-permute-start | bytes 2359304 | tf_op jit(solution)/shard_map/ppermute | solution.py:453
  33.0 1.5 %collective-permute-start.1 = (bf16[256,1536]{1,0:T(8,128)(2,1)}, bf16[256,1536]{1,0:T(8,128)(2,1)}, u32[]{:S(2)}, u32[]{:S(2)}) collective-permute-start(bf16[256,1536]{1,0:T(8,128)(2,1)} %get-tuple-element.26.refs_4_.refs_2_), channel_id=1, source_target_pairs={{0,2},{2,0},{4,6},{6,4},{1,3},{3,1},{5,7},{7,5},{8,10},{10,8},{12,... | collective-permute-start | bytes 2359304 | tf_op jit(solution)/shard_map/ppermute | solution.py:453
  34.5 0.0 copy-done.11
  34.5 0.0 copy-done.12
  34.5 0.2 select_reduce_fusion
  34.6 0.1 fusion.2
  34.7 0.2 convert_reduce_fusion.1
  34.9 0.7 select_reduce_fusion.3.refs_0_
  35.6 0.2 select_reduce_fusion.2
  35.8 0.2 convert_reduce_fusion
  36.0 0.7 select_reduce_fusion.1.refs_4_.refs_0_
  36.7 0.0 all-to-all-done
  36.7 0.0 copy-start.2
  36.7 0.0 collective-permute-done.refs_5_.refs_1_
  36.7 1.1 copy-done.2
  37.8 3.1 %shard_map.124 = (bf16[4,64,768]{2,1,0:T(8,128)(2,1)}, bf16[4,64,768]{2,1,0:T(8,128)(2,1)}, bf16[4,64,768]{2,1,0:T(8,128)(2,1)}, bf16[4,64,768]{2,1,0:T(8,128)(2,1)}, bf16[8,2,64,768]{3,2,1,0:T(8,128)(2,1)}) custom-call(s32[16]{0:T(128)} %select_reduce_fusion.3.refs_0_, s32[1]{0:T(128)} %bitcast.1.refs_1_, ...), custom_call_target="tpu_custom_call", output_to_operand_aliasing={{4}: (3, {})} | custom-call | bytes 6291456 | tf_op jit(solution)/shard_map/pallas_call | solution.py:273
  40.9 3.6 %all-to-all-start.1 = ((bf16[8,2,64,768]{3,2,1,0:T(8,128)(2,1)}), bf16[8,2,64,768]{3,2,1,0:T(8,128)(2,1)S(1)}, u32[]{:S(2)}, u32[]{:S(2)}) async-start(bf16[8,2,64,768]{3,2,1,0:T(8,128)(2,1)} %get-tuple-element.30), calls=%async_computation.1 | async-start | bytes 3145728 | tf_op jit(solution)/shard_map/all_to_all | solution.py:460
  44.5 1.6 %collective-permute-start.5 = (bf16[4,64,768]{2,1,0:T(8,128)(2,1)}, bf16[4,64,768]{2,1,0:T(8,128)(2,1)S(1)}, u32[]{:S(2)}, u32[]{:S(2)}) collective-permute-start(bf16[4,64,768]{2,1,0:T(8,128)(2,1)} %get-tuple-element.34), channel_id=1, source_target_pairs={{0,8},{8,16},{16,24},{24,0},{1,9},{9,17},{17,25},{25,1},{2,10},{10... | collective-permute-start | bytes 1179656 | tf_op jit(solution)/shard_map/ppermute | solution.py:462
  46.2 2.6 %collective-permute-start.6 = (bf16[4,64,768]{2,1,0:T(8,128)(2,1)}, bf16[4,64,768]{2,1,0:T(8,128)(2,1)S(1)}, u32[]{:S(2)}, u32[]{:S(2)}) collective-permute-start(bf16[4,64,768]{2,1,0:T(8,128)(2,1)} %get-tuple-element.35), channel_id=1, source_target_pairs={{0,16},{8,24},{16,0},{24,8},{1,17},{9,25},{17,1},{25,9},{2,18},{10... | collective-permute-start | bytes 1179656 | tf_op jit(solution)/shard_map/ppermute | solution.py:462
  48.8 1.3 collective-permute-start.7
  50.1 1.4 %collective-permute-done.2.refs_1_.refs_3_ = bf16[256,1536]{1,0:T(8,128)(2,1)S(1)} collective-permute-done((bf16[256,1536]{1,0:T(8,128)(2,1)}, bf16[256,1536]{1,0:T(8,128)(2,1)S(1)}, u32[]{:S(2)}, u32[]{:S(2)}) %collective-permute-start.2) | collective-permute-done | bytes 786464 | tf_op jit(solution)/shard_map/ppermute | solution.py:453
  51.5 2.2 %collective-permute-done.1.refs_0_.refs_2_ = bf16[256,1536]{1,0:T(8,128)(2,1)} collective-permute-done((bf16[256,1536]{1,0:T(8,128)(2,1)}, bf16[256,1536]{1,0:T(8,128)(2,1)}, u32[]{:S(2)}, u32[]{:S(2)}) %collective-permute-start.1) | collective-permute-done | bytes 786464 | tf_op jit(solution)/shard_map/ppermute | solution.py:453
  53.7 0.0 copy-done.7
  53.7 2.3 %shard_map.125 = (bf16[128,1536]{1,0:T(8,128)(2,1)}, bf16[128,1536]{1,0:T(8,128)(2,1)}) custom-call(bf16[256,1536]{1,0:T(8,128)(2,1)} %collective-permute-done.1.refs_0_.refs_2_, bf16[256,1536]{1,0:T(8,128)(2,1)} %copy-done.7, bf16[4,64,768]{2,1,0:T(8,128)(2,1)} %get-tuple-element.28.refs_2_), custom_call_target="tpu_custom_call" | custom-call | bytes 6291456 | tf_op jit(solution)/shard_map/pallas_call | solution.py:273
  56.0 0.7 collective-permute-start.4
  56.7 2.2 %collective-permute-start.3 = (bf16[128,1536]{1,0:T(8,128)(2,1)}, bf16[128,1536]{1,0:T(8,128)(2,1)S(1)}, u32[]{:S(2)}, u32[]{:S(2)}) collective-permute-start(bf16[128,1536]{1,0:T(8,128)(2,1)} %get-tuple-element.29.refs_3_), channel_id=1, source_target_pairs={{0,2},{2,0},{4,6},{6,4},{1,3},{3,1},{5,7},{7,5},{8,10},{10,8},{12,... | collective-permute-start | bytes 1179656 | tf_op jit(solution)/shard_map/ppermute | solution.py:453
  58.9 6.8 %shard_map.126.refs_3_.refs_4_ = bf16[256,1536]{1,0:T(8,128)(2,1)} custom-call(bf16[3,1536,512]{2,1,0:T(8,128)(2,1)} %refs_0_.10, bf16[3,1536,512]{2,1,0:T(8,128)(2,1)} %collective-permute-done.refs_5_.refs_1_, bf16[256,1536]{1,0:T(8,128)(2,1)} %get-tuple-element.26.refs_4_.refs_2_, bf16[128,1536]{1,0:T(8,128)(2,1)} %get-tuple-element.29.refs_3_, ...), custom_call_target="tpu_custom_call" | custom-call | flops 96636764160 | bytes 9437184 | tf_op jit(solution)/shard_map/pallas_call | solution.py:273
  65.7 4.3 %all-to-all-done.1 = bf16[8,2,64,768]{3,2,1,0:T(8,128)(2,1)S(1)} async-done(((bf16[8,2,64,768]{3,2,1,0:T(8,128)(2,1)}), bf16[8,2,64,768]{3,2,1,0:T(8,128)(2,1)S(1)}, u32[]{:S(2)}, u32[]{:S(2)}) %all-to-all-start.1) | async-done | bytes 1572896 | tf_op jit(solution)/shard_map/all_to_all | solution.py:460
  70.0 1.1 copy-done.3
  71.2 3.1 %shard_map.127.refs_4_.refs_0_ = bf16[16,64,768]{2,1,0:T(8,128)(2,1)} custom-call(s32[16]{0:T(128)} %select_reduce_fusion.3.refs_0_, s32[1]{0:T(128)} %bitcast.1.refs_1_, bf16[16,64,768]{2,1,0:T(8,128)(2,1)} %bitcast.5, bf16[256,1536]{1,0:T(8,128)(2,1)} %shard_map.126.refs_3_.refs_4_), custom_call_target="tpu_custom_call" | custom-call | bytes 6291456 | tf_op jit(solution)/shard_map/pallas_call | solution.py:273
  74.3 2.1 %collective-permute-done.4.refs_6_.refs_3_ = bf16[128,1536]{1,0:T(8,128)(2,1)S(1)} collective-permute-done((bf16[128,1536]{1,0:T(8,128)(2,1)}, bf16[128,1536]{1,0:T(8,128)(2,1)S(1)}, u32[]{:S(2)}, u32[]{:S(2)}) %collective-permute-start.4) | collective-permute-done | bytes 393248 | tf_op jit(solution)/shard_map/ppermute | solution.py:453
  76.4 1.5 %collective-permute-done.3.refs_5_.refs_2_ = bf16[128,1536]{1,0:T(8,128)(2,1)S(1)} collective-permute-done((bf16[128,1536]{1,0:T(8,128)(2,1)}, bf16[128,1536]{1,0:T(8,128)(2,1)S(1)}, u32[]{:S(2)}, u32[]{:S(2)}) %collective-permute-start.3) | collective-permute-done | bytes 393248 | tf_op jit(solution)/shard_map/ppermute | solution.py:453
  77.9 0.0 copy-done.9
  77.9 0.7 copy-done.10
  78.6 9.9 %shard_map.128 = (bf16[256,1536]{1,0:T(8,128)(2,1)}, bf16[256,1536]{1,0:T(8,128)(2,1)}) custom-call(bf16[3,1536,512]{2,1,0:T(8,128)(2,1)} %refs_0_.10, bf16[3,1536,512]{2,1,0:T(8,128)(2,1)} %collective-permute-done.refs_5_.refs_1_, bf16[256,1536]{1,0:T(8,128)(2,1)} %collective-permute-done.1.refs_0_.refs_2_, bf16[256,1536]{1,0:T(8,128)(2,1)} %copy-done.7, ...), custom_call_target="tpu_custom_call" | custom-call | flops 4831838208 | bytes 9437184 | tf_op jit(solution)/shard_map/pallas_call | solution.py:273
  88.5 0.0 collective-permute-done.5.refs_3_
  88.5 0.0 collective-permute-done.6.refs_4_
  88.5 0.0 copy-start.5
  88.6 0.0 collective-permute-done.7.refs_5_
  88.6 0.0 copy-start.6
  88.6 0.7 copy-done.4
  89.3 0.1 copy-done.5
  89.4 0.1 copy-done.6
  89.6 5.0 %all-to-all-start.2 = ((bf16[16,64,768]{2,1,0:T(8,128)(2,1)}), bf16[16,64,768]{2,1,0:T(8,128)(2,1)S(1)}, u32[]{:S(2)}, u32[]{:S(2)}) async-start(bf16[16,64,768]{2,1,0:T(8,128)(2,1)} %get-tuple-element.39.refs_4_), calls=%async_computation.2 | async-start | bytes 3145728 | tf_op jit(solution)/shard_map/all_to_all | solution.py:487
  94.6 0.0 copy-done.8
  94.6 1.5 %collective-permute-start.8 = (bf16[256,1536]{1,0:T(8,128)(2,1)S(1)}, bf16[256,1536]{1,0:T(8,128)(2,1)S(1)}, u32[]{:S(2)}, u32[]{:S(2)}) collective-permute-start(bf16[256,1536]{1,0:T(8,128)(2,1)S(1)} %copy-done.8), channel_id=1, source_target_pairs={{0,2},{2,0},{4,6},{6,4},{1,3},{3,1},{5,7},{7,5},{8,10},{10,8},{12,... | collective-permute-start | bytes 2359304 | tf_op jit(solution)/shard_map/ppermute | solution.py:453
  96.0 0.9 collective-permute-start.9
  97.0 6.7 %shard_map.130.refs_6_ = bf16[256,1536]{1,0:T(8,128)(2,1)} custom-call(bf16[3,1536,512]{2,1,0:T(8,128)(2,1)} %refs_0_.10, bf16[3,1536,512]{2,1,0:T(8,128)(2,1)} %collective-permute-done.refs_5_.refs_1_, bf16[128,1536]{1,0:T(8,128)(2,1)} %copy-done.10, bf16[128,1536]{1,0:T(8,128)(2,1)} %copy-done.9, bf16[16,64,768]{2,1,0:T(8,128)(2,1)} %get-tuple-element.39.refs_4_), custom_call_target="tpu_custom_call" | custom-call | flops 2415919104 | bytes 9437184 | tf_op jit(solution)/shard_map/pallas_call | solution.py:273
  103.7 1.1 collective-permute-start.10
  104.8 3.1 %shard_map.131.refs_3_ = bf16[16,64,1536]{2,1,0:T(8,128)(2,1)} custom-call(s32[16]{0:T(128)} %select_reduce_fusion.1.refs_4_.refs_0_, s32[1]{0:T(128)} %bitcast.1.refs_1_, bf16[4,64,768]{2,1,0:T(8,128)(2,1)} %get-tuple-element.28.refs_2_, bf16[4,64,768]{2,1,0:T(8,128)(2,1)} %copy-done.4, bf16[4,64,768]{2,1,0:T(8,128)(2,1)} %copy-done.5, ...), custom_call_target="tpu_custom_call" | custom-call | bytes 6291456 | tf_op jit(solution)/shard_map/pallas_call | solution.py:273
  107.8 7.2 %collective-permute-done.8.refs_4_.refs_5_ = bf16[256,1536]{1,0:T(8,128)(2,1)S(1)} collective-permute-done((bf16[256,1536]{1,0:T(8,128)(2,1)S(1)}, bf16[256,1536]{1,0:T(8,128)(2,1)S(1)}, u32[]{:S(2)}, u32[]{:S(2)}) %collective-permute-start.8) | collective-permute-done | bytes 786464 | tf_op jit(solution)/shard_map/ppermute | solution.py:453
  115.1 15.6 %all-to-all-done.2.refs_2_ = bf16[16,64,768]{2,1,0:T(8,128)(2,1)S(1)} async-done(((bf16[16,64,768]{2,1,0:T(8,128)(2,1)}), bf16[16,64,768]{2,1,0:T(8,128)(2,1)S(1)}, u32[]{:S(2)}, u32[]{:S(2)}) %all-to-all-start.2) | async-done | bytes 1572896 | tf_op jit(solution)/shard_map/all_to_all | solution.py:487
  130.7 0.0 copy-done.1
  130.7 4.0 %shard_map.132.refs_8_ = bf16[16,64,1536]{2,1,0:T(8,128)(2,1)} custom-call(s32[16]{0:T(128)S(1)} %copy-done.1, s32[1]{0:T(128)} %bitcast.1.refs_1_, bf16[16,64,768]{2,1,0:T(8,128)(2,1)S(1)} %all-to-all-done.2.refs_2_, bf16[16,64,1536]{2,1,0:T(8,128)(2,1)} %shard_map.131.refs_3_, ...), custom_call_target="tpu_custom_call", output_to_operand_aliasing={{}: (3, {})} | custom-call | flops 193273528320 | bytes 6291456 | tf_op jit(solution)/shard_map/pallas_call | solution.py:273
  134.7 0.0 copy-done
  134.7 0.0 collective-permute-done.9.refs_6_
  134.7 0.0 collective-permute-done.10.refs_7_
  134.7 3.8 %shard_map.133 = bf16[2,128,1536]{2,1,0:T(8,128)(2,1)} custom-call(s32[64]{0:T(128)} %refs_0_.11, s32[64]{0:T(128)} %refs_1_.5, s32[1]{0:T(128)} %bitcast.refs_3_.refs_2_, bf16[256,1536]{1,0:T(8,128)(2,1)} %get-tuple-element.25.refs_3_, bf16[256,1536]{1,0:T(8,128)(2,1)} %shard_map.126.refs_3_.refs_4_, bf16[256,1536]{1,0:T(8,128)(2,1)} %copy-done, ...), custom_call_target="tpu_custom_call" | custom-call | bytes 6291456 | tf_op jit(solution)/shard_map/pallas_call | solution.py:273
  (12 shorter events, 0.0 us)
Async XLA Ops:
  0.6 36.1 %collective-permute-start = (bf16[3,1536,512]{2,1,0:T(8,128)(2,1)}, bf16[3,1536,512]{2,1,0:T(8,128)(2,1)}, u32[]{:S(2)}, u32[]{:S(2)}) collective-permute-start(bf16[3,1536,512]{2,1,0:T(8,128)(2,1)} %refs_0_.10), channel_id=1, source_target_pairs={{0,1},{1,0},{2,3},{3,2},{4,5},{5,4},{6,7},{7,6},{8,9},{9,8},{10,11... | collective-permute-start | bytes 14155784 | tf_op jit(solution)/shard_map/ppermute | solution.py:326
  7.6 29.1 %all-to-all-start = ((bf16[8,2,64,768]{3,2,1,0:T(8,128)(2,1)}), bf16[8,2,64,768]{3,2,1,0:T(8,128)(2,1)S(1)}, u32[]{:S(2)}, u32[]{:S(2)}) async-start(bf16[8,2,64,768]{3,2,1,0:T(8,128)(2,1)} %get-tuple-element.24.refs_9_), calls=%async_computation | async-start | bytes 3145728 | tf_op jit(solution)/shard_map/all_to_all | solution.py:349
  12.4 22.1 %copy-start.11 = (s32[64]{0:T(128)S(1)}, s32[64]{0:T(128)}, u32[]{:S(2)}) copy-start(s32[64]{0:T(128)} %refs_0_.11) | copy-start | bytes 772
  12.4 22.1 %copy-start.12 = (s32[64]{0:T(128)S(1)}, s32[64]{0:T(128)}, u32[]{:S(2)}) copy-start(s32[64]{0:T(128)} %param.20) | copy-start | bytes 772
  30.8 20.7 %collective-permute-start.2 = (bf16[256,1536]{1,0:T(8,128)(2,1)}, bf16[256,1536]{1,0:T(8,128)(2,1)S(1)}, u32[]{:S(2)}, u32[]{:S(2)}) collective-permute-start(bf16[256,1536]{1,0:T(8,128)(2,1)} %get-tuple-element.26.refs_4_.refs_2_), channel_id=1, source_target_pairs={{0,4},{2,6},{4,0},{6,2},{1,5},{3,7},{5,1},{7,3},{8,12},{10,14},{12... | collective-permute-start | bytes 2359304 | tf_op jit(solution)/shard_map/ppermute | solution.py:453
  33.0 20.7 %collective-permute-start.1 = (bf16[256,1536]{1,0:T(8,128)(2,1)}, bf16[256,1536]{1,0:T(8,128)(2,1)}, u32[]{:S(2)}, u32[]{:S(2)}) collective-permute-start(bf16[256,1536]{1,0:T(8,128)(2,1)} %get-tuple-element.26.refs_4_.refs_2_), channel_id=1, source_target_pairs={{0,2},{2,0},{4,6},{6,4},{1,3},{3,1},{5,7},{7,5},{8,10},{10,8},{12,... | collective-permute-start | bytes 2359304 | tf_op jit(solution)/shard_map/ppermute | solution.py:453
  36.7 1.1 copy-start.2
  40.9 29.1 %all-to-all-start.1 = ((bf16[8,2,64,768]{3,2,1,0:T(8,128)(2,1)}), bf16[8,2,64,768]{3,2,1,0:T(8,128)(2,1)S(1)}, u32[]{:S(2)}, u32[]{:S(2)}) async-start(bf16[8,2,64,768]{3,2,1,0:T(8,128)(2,1)} %get-tuple-element.30), calls=%async_computation.1 | async-start | bytes 3145728 | tf_op jit(solution)/shard_map/all_to_all | solution.py:460
  44.5 44.0 %collective-permute-start.5 = (bf16[4,64,768]{2,1,0:T(8,128)(2,1)}, bf16[4,64,768]{2,1,0:T(8,128)(2,1)S(1)}, u32[]{:S(2)}, u32[]{:S(2)}) collective-permute-start(bf16[4,64,768]{2,1,0:T(8,128)(2,1)} %get-tuple-element.34), channel_id=1, source_target_pairs={{0,8},{8,16},{16,24},{24,0},{1,9},{9,17},{17,25},{25,1},{2,10},{10... | collective-permute-start | bytes 1179656 | tf_op jit(solution)/shard_map/ppermute | solution.py:462
  46.2 42.4 %collective-permute-start.6 = (bf16[4,64,768]{2,1,0:T(8,128)(2,1)}, bf16[4,64,768]{2,1,0:T(8,128)(2,1)S(1)}, u32[]{:S(2)}, u32[]{:S(2)}) collective-permute-start(bf16[4,64,768]{2,1,0:T(8,128)(2,1)} %get-tuple-element.35), channel_id=1, source_target_pairs={{0,16},{8,24},{16,0},{24,8},{1,17},{9,25},{17,1},{25,9},{2,18},{10... | collective-permute-start | bytes 1179656 | tf_op jit(solution)/shard_map/ppermute | solution.py:462
  48.8 39.8 %collective-permute-start.7 = (bf16[4,64,768]{2,1,0:T(8,128)(2,1)}, bf16[4,64,768]{2,1,0:T(8,128)(2,1)S(1)}, u32[]{:S(2)}, u32[]{:S(2)}) collective-permute-start(bf16[4,64,768]{2,1,0:T(8,128)(2,1)} %get-tuple-element.36), channel_id=1, source_target_pairs={{0,24},{8,0},{16,8},{24,16},{1,25},{9,1},{17,9},{25,17},{2,26},{10... | collective-permute-start | bytes 1179656 | tf_op jit(solution)/shard_map/ppermute | solution.py:462
  51.5 2.2 %copy-start.7 = (bf16[256,1536]{1,0:T(8,128)(2,1)}, bf16[256,1536]{1,0:T(8,128)(2,1)S(1)}, u32[]{:S(2)}) copy-start(bf16[256,1536]{1,0:T(8,128)(2,1)S(1)} %collective-permute-done.2.refs_1_.refs_3_) | copy-start | bytes 2359300
  56.0 20.4 %collective-permute-start.4 = (bf16[128,1536]{1,0:T(8,128)(2,1)}, bf16[128,1536]{1,0:T(8,128)(2,1)S(1)}, u32[]{:S(2)}, u32[]{:S(2)}) collective-permute-start(bf16[128,1536]{1,0:T(8,128)(2,1)} %get-tuple-element.31), channel_id=1, source_target_pairs={{0,4},{2,6},{4,0},{6,2},{1,5},{3,7},{5,1},{7,3},{8,12},{10,14},{12... | collective-permute-start | bytes 1179656 | tf_op jit(solution)/shard_map/ppermute | solution.py:453
  56.7 21.1 %collective-permute-start.3 = (bf16[128,1536]{1,0:T(8,128)(2,1)}, bf16[128,1536]{1,0:T(8,128)(2,1)S(1)}, u32[]{:S(2)}, u32[]{:S(2)}) collective-permute-start(bf16[128,1536]{1,0:T(8,128)(2,1)} %get-tuple-element.29.refs_3_), channel_id=1, source_target_pairs={{0,2},{2,0},{4,6},{6,4},{1,3},{3,1},{5,7},{7,5},{8,10},{10,8},{12,... | collective-permute-start | bytes 1179656 | tf_op jit(solution)/shard_map/ppermute | solution.py:453
  70.0 1.1 copy-start.3
  76.4 1.5 %copy-start.9 = (bf16[128,1536]{1,0:T(8,128)(2,1)}, bf16[128,1536]{1,0:T(8,128)(2,1)S(1)}, u32[]{:S(2)}) copy-start(bf16[128,1536]{1,0:T(8,128)(2,1)S(1)} %collective-permute-done.4.refs_6_.refs_3_) | copy-start | bytes 1179652
  77.9 0.7 copy-start.10
  88.5 0.8 copy-start.4
  88.5 0.9 copy-start.5
  88.6 1.0 copy-start.6
  89.6 5.0 %copy-start.8 = (bf16[256,1536]{1,0:T(8,128)(2,1)S(1)}, bf16[256,1536]{1,0:T(8,128)(2,1)}, u32[]{:S(2)}) copy-start(bf16[256,1536]{1,0:T(8,128)(2,1)} %get-tuple-element.37) | copy-start | bytes 2359300
  89.6 41.1 %all-to-all-start.2 = ((bf16[16,64,768]{2,1,0:T(8,128)(2,1)}), bf16[16,64,768]{2,1,0:T(8,128)(2,1)S(1)}, u32[]{:S(2)}, u32[]{:S(2)}) async-start(bf16[16,64,768]{2,1,0:T(8,128)(2,1)} %get-tuple-element.39.refs_4_), calls=%async_computation.2 | async-start | bytes 3145728 | tf_op jit(solution)/shard_map/all_to_all | solution.py:487
  94.6 20.5 %collective-permute-start.8 = (bf16[256,1536]{1,0:T(8,128)(2,1)S(1)}, bf16[256,1536]{1,0:T(8,128)(2,1)S(1)}, u32[]{:S(2)}, u32[]{:S(2)}) collective-permute-start(bf16[256,1536]{1,0:T(8,128)(2,1)S(1)} %copy-done.8), channel_id=1, source_target_pairs={{0,2},{2,0},{4,6},{6,4},{1,3},{3,1},{5,7},{7,5},{8,10},{10,8},{12,... | collective-permute-start | bytes 2359304 | tf_op jit(solution)/shard_map/ppermute | solution.py:453
  96.0 38.7 %collective-permute-start.9 = (bf16[256,1536]{1,0:T(8,128)(2,1)}, bf16[256,1536]{1,0:T(8,128)(2,1)}, u32[]{:S(2)}, u32[]{:S(2)}) collective-permute-start(bf16[256,1536]{1,0:T(8,128)(2,1)} %get-tuple-element.38), channel_id=1, source_target_pairs={{0,4},{2,6},{4,0},{6,2},{1,5},{3,7},{5,1},{7,3},{8,12},{10,14},{12... | collective-permute-start | bytes 2359304 | tf_op jit(solution)/shard_map/ppermute | solution.py:453
  103.7 27.0 %copy-start.1 = (s32[16]{0:T(128)S(1)}, s32[16]{0:T(128)}, u32[]{:S(2)}) copy-start(s32[16]{0:T(128)} %select_reduce_fusion.1.refs_4_.refs_0_) | copy-start | bytes 196
  103.7 31.1 %collective-permute-start.10 = (bf16[256,1536]{1,0:T(8,128)(2,1)}, bf16[256,1536]{1,0:T(8,128)(2,1)}, u32[]{:S(2)}, u32[]{:S(2)}) collective-permute-start(bf16[256,1536]{1,0:T(8,128)(2,1)} %shard_map.130.refs_6_), channel_id=1, source_target_pairs={{0,6},{2,4},{4,2},{6,0},{1,7},{3,5},{5,3},{7,1},{8,14},{10,12},{12... | collective-permute-start | bytes 2359304 | tf_op jit(solution)/shard_map/ppermute | solution.py:453
  115.1 19.7 %copy-start = (bf16[256,1536]{1,0:T(8,128)(2,1)}, bf16[256,1536]{1,0:T(8,128)(2,1)S(1)}, u32[]{:S(2)}) copy-start(bf16[256,1536]{1,0:T(8,128)(2,1)S(1)} %collective-permute-done.8.refs_4_.refs_5_) | copy-start | bytes 2359300

commit v12 on v11

--- a/solution.py
+++ b/solution.py
@@ -501,10 +501,13 @@
             out_shape, [], tuple(terms), flops, after=after,
         )
 
+    most = add([residual, *partials[:2]], shape(tokens.shape, f32), (kv_half,), 0)
     kv_decode = unpack(
-        key_width, [values_arrived], (kv_half,), tuple(partials[1:2]), LONG * flat * width * width * 8
-    )
-    layer_out = add([residual, *partials], shape(tokens.shape), (kv_decode,), 0)
+        key_width, [values_arrived], (kv_half,), (most,), LONG * flat * width * width * 8
+    )
+    layer_out = add(
+        [most.reshape(flat, width), *partials[2:]], shape(tokens.shape), (kv_decode,), 0
+    )
     return (layer_out, kv_decode)
 
 

time: 139 us -> 140 us (level)
  waiting for transfers between devices: 34.4 us -> 30 us
  Pallas kernels: 67.5 us -> 70.7 us
  local copies, waits for them, and re-layouts: 4.05 us -> 6.32 us
    all_to_all x1, waiting for transfers between devices: 15.6 us -> 11.3 us  [local(): lax.all_to_all(values_ready, 'dp', split_axis=0, concat_axis=0, tiled=True)]
    pallas_call x12 -> x13, Pallas kernels: 67.5 us -> 70.7 us  [call(): pl.pallas_call(ordered, out_shape=out_shape, grid_spec=pltpu.PrefetchScal...]
    unnamed x26 -> x28, local copies, waits for them, and re-layouts: 4.05 us -> 6.32 us
  transfers between devices with their start and end apart: 14 -> 14, of which waited for: 7 -> 7; matrix products, arithmetic and copies ran while one was open for 2% -> 2% of each run, Pallas kernels for 46% -> 48%
where the time goes in v12:
time: 140 us
  Pallas kernels  70.7 us (50%)
  waiting for transfers between devices  30 us (21%)
  starting transfers between devices  29.5 us (21%)
  local copies, waits for them, and re-layouts  6.32 us (5%)
  other arithmetic  2.23 us (2%)
    pallas_call x13, Pallas kernels, call(): pl.pallas_call(ordered, out_shape=out_shape, grid_spec=pltpu.PrefetchScal...  70.7 us
    ppermute x7, waiting for transfers between devices, swap(): return lax.ppermute(rows, 'chip', [(c, c ^ mask) for c in range(chips)])  14.4 us
    all_to_all x1, waiting for transfers between devices, local(): lax.all_to_all(values_ready, 'dp', split_axis=0, concat_axis=0, tiled=True)  11.3 us
    ppermute x7, starting transfers between devices, swap(): return lax.ppermute(rows, 'chip', [(c, c ^ mask) for c in range(chips)])  10 us
    unnamed x28, local copies, waits for them, and re-layouts  6.32 us
    ppermute x3, starting transfers between devices, local(): lax.ppermute(rows, 'dp', pairs)  5.57 us
    all_to_all x1, starting transfers between devices, local(): lax.all_to_all(values_ready, 'dp', split_axis=0, concat_axis=0, tiled=True)  5.01 us
    all_to_all x1, starting transfers between devices, local(): lax.all_to_all(keys, tensor, split_axis=0, concat_axis=0, tiled=True)  4.83 us
  transfers between devices with their start and end apart: 14, of which 7 were waited for; matrix products, arithmetic and copies ran while one was open for 2% of the time, Pallas kernels for 48%

profile of v12, /device:TPU:0, one launch (start us, length us, event | category | flops | bytes accessed | tf_op | source)
XLA Modules:
  0.0 139.6 jit_solution(3903702680630452419)
XLA Ops:
  0.6 0.5 collective-permute-start
  1.1 6.4 %shard_map.122 = (bf16[8,2,64,768]{3,2,1,0:T(8,128)(2,1)}, bf16[2,128,1536]{2,1,0:T(8,128)(2,1)}, f32[2,128,384]{2,1,0:T(8,128)}, f32[2,128,384]{2,1,0:T(8,128)}) custom-call(s32[64]{0:T(128)} %refs_0_.13, s32[64]{0:T(128)} %refs_1_.7, s32[64]{0:T(128)} %refs_2_.3, s32[1]{0:T(128)} %bitcast.refs_3_.refs_2_, bf16[2,128,1536]{2,1,0:T(8,128)(2,1)} %refs_11_.1, ...), custom_call_target="tpu_custom_call" | custom-call | flops 603979776 | bytes 8388608 | tf_op jit(solution)/shard_map/pallas_call | solution.py:273
  7.6 4.8 %all-to-all-start = ((bf16[8,2,64,768]{3,2,1,0:T(8,128)(2,1)}), bf16[8,2,64,768]{3,2,1,0:T(8,128)(2,1)S(1)}, u32[]{:S(2)}, u32[]{:S(2)}) async-start(bf16[8,2,64,768]{3,2,1,0:T(8,128)(2,1)} %get-tuple-element.24.refs_9_), calls=%async_computation | async-start | bytes 3145728 | tf_op jit(solution)/shard_map/all_to_all | solution.py:349
  12.4 0.0 copy-start.13
  12.4 18.4 %shard_map.123 = (bf16[8,2,64,768]{3,2,1,0:T(8,128)(2,1)}, bf16[256,1536]{1,0:T(8,128)(2,1)}, bf16[256,1536]{1,0:T(8,128)(2,1)}) custom-call(s32[64]{0:T(128)} %refs_0_.13, s32[64]{0:T(128)} %refs_1_.7, s32[64]{0:T(128)} %refs_2_.3, s32[1]{0:T(128)} %bitcast.refs_3_.refs_2_, bf16[2,128,1536]{2,1,0:T(8,128)(2,1)} %get-tuple-element.21.refs_4_, ...), custom_call_target="tpu_custom_call" | custom-call | flops 7247757312 | bytes 16777216 | tf_op jit(solution)/shard_map/pallas_call | solution.py:273
  30.8 2.2 %collective-permute-start.2 = (bf16[256,1536]{1,0:T(8,128)(2,1)}, bf16[256,1536]{1,0:T(8,128)(2,1)S(1)}, u32[]{:S(2)}, u32[]{:S(2)}) collective-permute-start(bf16[256,1536]{1,0:T(8,128)(2,1)} %get-tuple-element.26.refs_4_.refs_2_), channel_id=1, source_target_pairs={{0,4},{2,6},{4,0},{6,2},{1,5},{3,7},{5,1},{7,3},{8,12},{10,14},{12... | collective-permute-start | bytes 2359304 | tf_op jit(solution)/shard_map/ppermute | solution.py:453
  33.0 1.5 %collective-permute-start.1 = (bf16[256,1536]{1,0:T(8,128)(2,1)}, bf16[256,1536]{1,0:T(8,128)(2,1)}, u32[]{:S(2)}, u32[]{:S(2)}) collective-permute-start(bf16[256,1536]{1,0:T(8,128)(2,1)} %get-tuple-element.26.refs_4_.refs_2_), channel_id=1, source_target_pairs={{0,2},{2,0},{4,6},{6,4},{1,3},{3,1},{5,7},{7,5},{8,10},{10,8},{12,... | collective-permute-start | bytes 2359304 | tf_op jit(solution)/shard_map/ppermute | solution.py:453
  34.5 0.0 copy-done.12
  34.5 0.0 copy-done.13
  34.5 0.2 select_reduce_fusion
  34.6 0.1 fusion.2
  34.8 0.2 convert_reduce_fusion.1
  34.9 0.7 select_reduce_fusion.3.refs_0_
  35.6 0.2 select_reduce_fusion.2
  35.8 0.2 convert_reduce_fusion
  36.0 0.7 select_reduce_fusion.1.refs_4_.refs_0_
  36.7 0.0 all-to-all-done
  36.7 0.0 collective-permute-done.refs_5_.refs_1_
  36.7 1.1 copy-done.2
  37.9 3.1 %shard_map.124 = (bf16[4,64,768]{2,1,0:T(8,128)(2,1)}, bf16[4,64,768]{2,1,0:T(8,128)(2,1)}, bf16[4,64,768]{2,1,0:T(8,128)(2,1)}, bf16[4,64,768]{2,1,0:T(8,128)(2,1)}, bf16[8,2,64,768]{3,2,1,0:T(8,128)(2,1)}) custom-call(s32[16]{0:T(128)} %select_reduce_fusion.3.refs_0_, s32[1]{0:T(128)} %bitcast.1.refs_1_, ...), custom_call_target="tpu_custom_call", output_to_operand_aliasing={{4}: (3, {})} | custom-call | bytes 6291456 | tf_op jit(solution)/shard_map/pallas_call | solution.py:273
  41.0 3.6 %all-to-all-start.1 = ((bf16[8,2,64,768]{3,2,1,0:T(8,128)(2,1)}), bf16[8,2,64,768]{3,2,1,0:T(8,128)(2,1)S(1)}, u32[]{:S(2)}, u32[]{:S(2)}) async-start(bf16[8,2,64,768]{3,2,1,0:T(8,128)(2,1)} %get-tuple-element.30), calls=%async_computation.1 | async-start | bytes 3145728 | tf_op jit(solution)/shard_map/all_to_all | solution.py:460
  44.6 1.6 %collective-permute-start.5 = (bf16[4,64,768]{2,1,0:T(8,128)(2,1)}, bf16[4,64,768]{2,1,0:T(8,128)(2,1)S(1)}, u32[]{:S(2)}, u32[]{:S(2)}) collective-permute-start(bf16[4,64,768]{2,1,0:T(8,128)(2,1)} %get-tuple-element.34), channel_id=1, source_target_pairs={{0,8},{8,16},{16,24},{24,0},{1,9},{9,17},{17,25},{25,1},{2,10},{10... | collective-permute-start | bytes 1179656 | tf_op jit(solution)/shard_map/ppermute | solution.py:462
  46.2 2.6 %collective-permute-start.6 = (bf16[4,64,768]{2,1,0:T(8,128)(2,1)}, bf16[4,64,768]{2,1,0:T(8,128)(2,1)S(1)}, u32[]{:S(2)}, u32[]{:S(2)}) collective-permute-start(bf16[4,64,768]{2,1,0:T(8,128)(2,1)} %get-tuple-element.35), channel_id=1, source_target_pairs={{0,16},{8,24},{16,0},{24,8},{1,17},{9,25},{17,1},{25,9},{2,18},{10... | collective-permute-start | bytes 1179656 | tf_op jit(solution)/shard_map/ppermute | solution.py:462
  48.8 1.3 collective-permute-start.7
  50.1 1.4 %collective-permute-done.2.refs_1_.refs_3_ = bf16[256,1536]{1,0:T(8,128)(2,1)S(1)} collective-permute-done((bf16[256,1536]{1,0:T(8,128)(2,1)}, bf16[256,1536]{1,0:T(8,128)(2,1)S(1)}, u32[]{:S(2)}, u32[]{:S(2)}) %collective-permute-start.2) | collective-permute-done | bytes 786464 | tf_op jit(solution)/shard_map/ppermute | solution.py:453
  51.5 2.2 %collective-permute-done.1.refs_0_.refs_2_ = bf16[256,1536]{1,0:T(8,128)(2,1)} collective-permute-done((bf16[256,1536]{1,0:T(8,128)(2,1)}, bf16[256,1536]{1,0:T(8,128)(2,1)}, u32[]{:S(2)}, u32[]{:S(2)}) %collective-permute-start.1) | collective-permute-done | bytes 786464 | tf_op jit(solution)/shard_map/ppermute | solution.py:453
  53.7 0.0 copy-done.7
  53.7 2.3 %shard_map.125 = (bf16[128,1536]{1,0:T(8,128)(2,1)}, bf16[128,1536]{1,0:T(8,128)(2,1)}) custom-call(bf16[256,1536]{1,0:T(8,128)(2,1)} %collective-permute-done.1.refs_0_.refs_2_, bf16[256,1536]{1,0:T(8,128)(2,1)} %copy-done.7, bf16[4,64,768]{2,1,0:T(8,128)(2,1)} %get-tuple-element.28.refs_2_), custom_call_target="tpu_custom_call" | custom-call | bytes 6291456 | tf_op jit(solution)/shard_map/pallas_call | solution.py:273
  56.0 0.7 collective-permute-start.4
  56.8 2.2 %collective-permute-start.3 = (bf16[128,1536]{1,0:T(8,128)(2,1)}, bf16[128,1536]{1,0:T(8,128)(2,1)S(1)}, u32[]{:S(2)}, u32[]{:S(2)}) collective-permute-start(bf16[128,1536]{1,0:T(8,128)(2,1)} %get-tuple-element.29.refs_3_), channel_id=1, source_target_pairs={{0,2},{2,0},{4,6},{6,4},{1,3},{3,1},{5,7},{7,5},{8,10},{10,8},{12,... | collective-permute-start | bytes 1179656 | tf_op jit(solution)/shard_map/ppermute | solution.py:453
  58.9 6.8 %shard_map.126.refs_3_.refs_4_ = bf16[256,1536]{1,0:T(8,128)(2,1)} custom-call(bf16[3,1536,512]{2,1,0:T(8,128)(2,1)} %refs_0_.11, bf16[3,1536,512]{2,1,0:T(8,128)(2,1)} %collective-permute-done.refs_5_.refs_1_, bf16[256,1536]{1,0:T(8,128)(2,1)} %get-tuple-element.26.refs_4_.refs_2_, bf16[128,1536]{1,0:T(8,128)(2,1)} %get-tuple-element.29.refs_3_, ...), custom_call_target="tpu_custom_call" | custom-call | flops 96636764160 | bytes 9437184 | tf_op jit(solution)/shard_map/pallas_call | solution.py:273
  65.8 4.3 %all-to-all-done.1 = bf16[8,2,64,768]{3,2,1,0:T(8,128)(2,1)S(1)} async-done(((bf16[8,2,64,768]{3,2,1,0:T(8,128)(2,1)}), bf16[8,2,64,768]{3,2,1,0:T(8,128)(2,1)S(1)}, u32[]{:S(2)}, u32[]{:S(2)}) %all-to-all-start.1) | async-done | bytes 1572896 | tf_op jit(solution)/shard_map/all_to_all | solution.py:460
  70.1 1.1 copy-done.3
  71.2 3.1 %shard_map.127.refs_4_.refs_0_ = bf16[16,64,768]{2,1,0:T(8,128)(2,1)} custom-call(s32[16]{0:T(128)} %select_reduce_fusion.3.refs_0_, s32[1]{0:T(128)} %bitcast.1.refs_1_, bf16[16,64,768]{2,1,0:T(8,128)(2,1)} %bitcast.7, bf16[256,1536]{1,0:T(8,128)(2,1)} %shard_map.126.refs_3_.refs_4_), custom_call_target="tpu_custom_call" | custom-call | bytes 6291456 | tf_op jit(solution)/shard_map/pallas_call | solution.py:273
  74.3 2.1 %collective-permute-done.4.refs_6_.refs_3_ = bf16[128,1536]{1,0:T(8,128)(2,1)S(1)} collective-permute-done((bf16[128,1536]{1,0:T(8,128)(2,1)}, bf16[128,1536]{1,0:T(8,128)(2,1)S(1)}, u32[]{:S(2)}, u32[]{:S(2)}) %collective-permute-start.4) | collective-permute-done | bytes 393248 | tf_op jit(solution)/shard_map/ppermute | solution.py:453
  76.4 1.5 %collective-permute-done.3.refs_5_.refs_2_ = bf16[128,1536]{1,0:T(8,128)(2,1)S(1)} collective-permute-done((bf16[128,1536]{1,0:T(8,128)(2,1)}, bf16[128,1536]{1,0:T(8,128)(2,1)S(1)}, u32[]{:S(2)}, u32[]{:S(2)}) %collective-permute-start.3) | collective-permute-done | bytes 393248 | tf_op jit(solution)/shard_map/ppermute | solution.py:453
  77.9 0.0 copy-done.10
  77.9 0.7 copy-done.11
  78.6 9.9 %shard_map.128 = (bf16[256,1536]{1,0:T(8,128)(2,1)}, bf16[256,1536]{1,0:T(8,128)(2,1)}) custom-call(bf16[3,1536,512]{2,1,0:T(8,128)(2,1)} %refs_0_.11, bf16[3,1536,512]{2,1,0:T(8,128)(2,1)} %collective-permute-done.refs_5_.refs_1_, bf16[256,1536]{1,0:T(8,128)(2,1)} %collective-permute-done.1.refs_0_.refs_2_, bf16[256,1536]{1,0:T(8,128)(2,1)} %copy-done.7, ...), custom_call_target="tpu_custom_call" | custom-call | flops 4831838208 | bytes 9437184 | tf_op jit(solution)/shard_map/pallas_call | solution.py:273
  88.6 0.0 collective-permute-done.5.refs_3_
  88.6 0.0 collective-permute-done.6.refs_4_
  88.6 0.0 copy-start.5
  88.6 0.0 collective-permute-done.7.refs_5_
  88.6 0.0 copy-start.6
  88.6 0.7 copy-done.4
  89.3 0.1 copy-done.5
  89.4 0.1 copy-done.6
  89.6 5.0 %all-to-all-start.2 = ((bf16[16,64,768]{2,1,0:T(8,128)(2,1)}), bf16[16,64,768]{2,1,0:T(8,128)(2,1)S(1)}, u32[]{:S(2)}, u32[]{:S(2)}) async-start(bf16[16,64,768]{2,1,0:T(8,128)(2,1)} %get-tuple-element.38.refs_4_), calls=%async_computation.2 | async-start | bytes 3145728 | tf_op jit(solution)/shard_map/all_to_all | solution.py:487
  94.6 0.0 copy-done.9
  94.6 1.5 %collective-permute-start.8 = (bf16[256,1536]{1,0:T(8,128)(2,1)S(1)}, bf16[256,1536]{1,0:T(8,128)(2,1)S(1)}, u32[]{:S(2)}, u32[]{:S(2)}) collective-permute-start(bf16[256,1536]{1,0:T(8,128)(2,1)S(1)} %copy-done.9), channel_id=1, source_target_pairs={{0,2},{2,0},{4,6},{6,4},{1,3},{3,1},{5,7},{7,5},{8,10},{10,8},{12,... | collective-permute-start | bytes 2359304 | tf_op jit(solution)/shard_map/ppermute | solution.py:453
  96.1 0.9 collective-permute-start.9
  97.0 6.7 %shard_map.130.refs_6_ = bf16[256,1536]{1,0:T(8,128)(2,1)} custom-call(bf16[3,1536,512]{2,1,0:T(8,128)(2,1)} %refs_0_.11, bf16[3,1536,512]{2,1,0:T(8,128)(2,1)} %collective-permute-done.refs_5_.refs_1_, bf16[128,1536]{1,0:T(8,128)(2,1)} %copy-done.11, bf16[128,1536]{1,0:T(8,128)(2,1)} %copy-done.10, bf16[16,64,768]{2,1,0:T(8,128)(2,1)} %get-tuple-element.38.refs_4_), custom_call_target="tpu_custom_call" | custom-call | flops 2415919104 | bytes 9437184 | tf_op jit(solution)/shard_map/pallas_call | solution.py:273
  103.7 1.1 collective-permute-start.10
  104.8 3.1 %shard_map.131.refs_6_.refs_3_ = bf16[16,64,1536]{2,1,0:T(8,128)(2,1)} custom-call(s32[16]{0:T(128)} %select_reduce_fusion.1.refs_4_.refs_0_, s32[1]{0:T(128)} %bitcast.1.refs_1_, bf16[4,64,768]{2,1,0:T(8,128)(2,1)} %get-tuple-element.28.refs_2_, bf16[4,64,768]{2,1,0:T(8,128)(2,1)} %copy-done.4, bf16[4,64,768]{2,1,0:T(8,128)(2,1)} %copy-done.5, ...), custom_call_target="tpu_custom_call" | custom-call | bytes 6291456 | tf_op jit(solution)/shard_map/pallas_call | solution.py:273
  107.9 7.2 %collective-permute-done.8.refs_5_ = bf16[256,1536]{1,0:T(8,128)(2,1)S(1)} collective-permute-done((bf16[256,1536]{1,0:T(8,128)(2,1)S(1)}, bf16[256,1536]{1,0:T(8,128)(2,1)S(1)}, u32[]{:S(2)}, u32[]{:S(2)}) %collective-permute-start.8) | collective-permute-done | bytes 786464 | tf_op jit(solution)/shard_map/ppermute | solution.py:453
  115.1 0.9 copy-done.8
  116.0 3.5 %shard_map.132.refs_4_ = f32[2,128,1536]{2,1,0:T(8,128)} custom-call(s32[64]{0:T(128)} %refs_0_.13, s32[64]{0:T(128)} %refs_1_.7, s32[1]{0:T(128)} %bitcast.refs_3_.refs_2_, bf16[256,1536]{1,0:T(8,128)(2,1)} %get-tuple-element.25.refs_3_, bf16[256,1536]{1,0:T(8,128)(2,1)} %shard_map.126.refs_3_.refs_4_, bf16[256,1536]{1,0:T(8,128)(2,1)} %copy-done.8, ...), custom_call_target="tpu_custom_call" | custom-call | bytes 6291456 | tf_op jit(solution)/shard_map/pallas_call | solution.py:273
  119.4 11.3 %all-to-all-done.2.refs_2_ = bf16[16,64,768]{2,1,0:T(8,128)(2,1)S(1)} async-done(((bf16[16,64,768]{2,1,0:T(8,128)(2,1)}), bf16[16,64,768]{2,1,0:T(8,128)(2,1)S(1)}, u32[]{:S(2)}, u32[]{:S(2)}) %all-to-all-start.2) | async-done | bytes 1572896 | tf_op jit(solution)/shard_map/all_to_all | solution.py:487
  130.7 0.0 copy-done.1
  130.7 1.4 %copy-done = f32[2,128,1536]{2,1,0:T(8,128)S(1)} copy-done((f32[2,128,1536]{2,1,0:T(8,128)S(1)}, f32[2,128,1536]{2,1,0:T(8,128)}, u32[]{:S(2)}) %copy-start) | copy-done | bytes 1572888
  132.1 4.0 %shard_map.133.refs_6_ = bf16[16,64,1536]{2,1,0:T(8,128)(2,1)} custom-call(s32[16]{0:T(128)S(1)} %copy-done.1, s32[1]{0:T(128)} %bitcast.1.refs_1_, bf16[16,64,768]{2,1,0:T(8,128)(2,1)S(1)} %all-to-all-done.2.refs_2_, bf16[16,64,1536]{2,1,0:T(8,128)(2,1)} %shard_map.131.refs_6_.refs_3_, f32[2,128,1536]{2,1,0:T(8,128)S(1)} %copy-done), custom_call_target="tpu_custom_call", output_to_operand_aliasing={{}: (3, {})} | custom-call | flops 193273528320 | bytes 6291456 | tf_op jit(solution)/shard_map/pallas_call | solution.py:273
  136.1 0.0 collective-permute-done.9.refs_4_
  136.1 0.0 collective-permute-done.10.refs_5_
  136.2 3.4 %shard_map.134 = bf16[2,128,1536]{2,1,0:T(8,128)(2,1)} custom-call(s32[64]{0:T(128)} %refs_0_.13, s32[64]{0:T(128)} %refs_1_.7, s32[1]{0:T(128)} %bitcast.refs_3_.refs_2_, f32[256,1536]{1,0:T(8,128)} %bitcast.5, bf16[256,1536]{1,0:T(8,128)(2,1)} %collective-permute-done.9.refs_4_, bf16[256,1536]{1,0:T(8,128)(2,1)} %collective-permute-done.10.refs_5_, ...), custom_call_target="tpu_custom_call" | custom-call | bytes 6291456 | tf_op jit(solution)/shard_map/pallas_call | solution.py:273
  (15 shorter events, 0.0 us)
Async XLA Ops:
  0.6 36.1 %collective-permute-start = (bf16[3,1536,512]{2,1,0:T(8,128)(2,1)}, bf16[3,1536,512]{2,1,0:T(8,128)(2,1)}, u32[]{:S(2)}, u32[]{:S(2)}) collective-permute-start(bf16[3,1536,512]{2,1,0:T(8,128)(2,1)} %refs_0_.11), channel_id=1, source_target_pairs={{0,1},{1,0},{2,3},{3,2},{4,5},{5,4},{6,7},{7,6},{8,9},{9,8},{10,11... | collective-permute-start | bytes 14155784 | tf_op jit(solution)/shard_map/ppermute | solution.py:326
  7.6 29.2 %all-to-all-start = ((bf16[8,2,64,768]{3,2,1,0:T(8,128)(2,1)}), bf16[8,2,64,768]{3,2,1,0:T(8,128)(2,1)S(1)}, u32[]{:S(2)}, u32[]{:S(2)}) async-start(bf16[8,2,64,768]{3,2,1,0:T(8,128)(2,1)} %get-tuple-element.24.refs_9_), calls=%async_computation | async-start | bytes 3145728 | tf_op jit(solution)/shard_map/all_to_all | solution.py:349
  12.4 22.1 %copy-start.12 = (s32[64]{0:T(128)S(1)}, s32[64]{0:T(128)}, u32[]{:S(2)}) copy-start(s32[64]{0:T(128)} %refs_0_.13) | copy-start | bytes 772
  12.4 22.1 %copy-start.13 = (s32[64]{0:T(128)S(1)}, s32[64]{0:T(128)}, u32[]{:S(2)}) copy-start(s32[64]{0:T(128)} %param.20) | copy-start | bytes 772
  30.8 20.7 %collective-permute-start.2 = (bf16[256,1536]{1,0:T(8,128)(2,1)}, bf16[256,1536]{1,0:T(8,128)(2,1)S(1)}, u32[]{:S(2)}, u32[]{:S(2)}) collective-permute-start(bf16[256,1536]{1,0:T(8,128)(2,1)} %get-tuple-element.26.refs_4_.refs_2_), channel_id=1, source_target_pairs={{0,4},{2,6},{4,0},{6,2},{1,5},{3,7},{5,1},{7,3},{8,12},{10,14},{12... | collective-permute-start | bytes 2359304 | tf_op jit(solution)/shard_map/ppermute | solution.py:453
  33.0 20.7 %collective-permute-start.1 = (bf16[256,1536]{1,0:T(8,128)(2,1)}, bf16[256,1536]{1,0:T(8,128)(2,1)}, u32[]{:S(2)}, u32[]{:S(2)}) collective-permute-start(bf16[256,1536]{1,0:T(8,128)(2,1)} %get-tuple-element.26.refs_4_.refs_2_), channel_id=1, source_target_pairs={{0,2},{2,0},{4,6},{6,4},{1,3},{3,1},{5,7},{7,5},{8,10},{10,8},{12,... | collective-permute-start | bytes 2359304 | tf_op jit(solution)/shard_map/ppermute | solution.py:453
  36.7 1.1 copy-start.2
  41.0 29.1 %all-to-all-start.1 = ((bf16[8,2,64,768]{3,2,1,0:T(8,128)(2,1)}), bf16[8,2,64,768]{3,2,1,0:T(8,128)(2,1)S(1)}, u32[]{:S(2)}, u32[]{:S(2)}) async-start(bf16[8,2,64,768]{3,2,1,0:T(8,128)(2,1)} %get-tuple-element.30), calls=%async_computation.1 | async-start | bytes 3145728 | tf_op jit(solution)/shard_map/all_to_all | solution.py:460
  44.6 44.0 %collective-permute-start.5 = (bf16[4,64,768]{2,1,0:T(8,128)(2,1)}, bf16[4,64,768]{2,1,0:T(8,128)(2,1)S(1)}, u32[]{:S(2)}, u32[]{:S(2)}) collective-permute-start(bf16[4,64,768]{2,1,0:T(8,128)(2,1)} %get-tuple-element.34), channel_id=1, source_target_pairs={{0,8},{8,16},{16,24},{24,0},{1,9},{9,17},{17,25},{25,1},{2,10},{10... | collective-permute-start | bytes 1179656 | tf_op jit(solution)/shard_map/ppermute | solution.py:462
  46.2 42.4 %collective-permute-start.6 = (bf16[4,64,768]{2,1,0:T(8,128)(2,1)}, bf16[4,64,768]{2,1,0:T(8,128)(2,1)S(1)}, u32[]{:S(2)}, u32[]{:S(2)}) collective-permute-start(bf16[4,64,768]{2,1,0:T(8,128)(2,1)} %get-tuple-element.35), channel_id=1, source_target_pairs={{0,16},{8,24},{16,0},{24,8},{1,17},{9,25},{17,1},{25,9},{2,18},{10... | collective-permute-start | bytes 1179656 | tf_op jit(solution)/shard_map/ppermute | solution.py:462
  48.8 39.8 %collective-permute-start.7 = (bf16[4,64,768]{2,1,0:T(8,128)(2,1)}, bf16[4,64,768]{2,1,0:T(8,128)(2,1)S(1)}, u32[]{:S(2)}, u32[]{:S(2)}) collective-permute-start(bf16[4,64,768]{2,1,0:T(8,128)(2,1)} %get-tuple-element.36), channel_id=1, source_target_pairs={{0,24},{8,0},{16,8},{24,16},{1,25},{9,1},{17,9},{25,17},{2,26},{10... | collective-permute-start | bytes 1179656 | tf_op jit(solution)/shard_map/ppermute | solution.py:462
  51.5 2.2 %copy-start.7 = (bf16[256,1536]{1,0:T(8,128)(2,1)}, bf16[256,1536]{1,0:T(8,128)(2,1)S(1)}, u32[]{:S(2)}) copy-start(bf16[256,1536]{1,0:T(8,128)(2,1)S(1)} %collective-permute-done.2.refs_1_.refs_3_) | copy-start | bytes 2359300
  56.0 20.4 %collective-permute-start.4 = (bf16[128,1536]{1,0:T(8,128)(2,1)}, bf16[128,1536]{1,0:T(8,128)(2,1)S(1)}, u32[]{:S(2)}, u32[]{:S(2)}) collective-permute-start(bf16[128,1536]{1,0:T(8,128)(2,1)} %get-tuple-element.31), channel_id=1, source_target_pairs={{0,4},{2,6},{4,0},{6,2},{1,5},{3,7},{5,1},{7,3},{8,12},{10,14},{12... | collective-permute-start | bytes 1179656 | tf_op jit(solution)/shard_map/ppermute | solution.py:453
  56.8 21.1 %collective-permute-start.3 = (bf16[128,1536]{1,0:T(8,128)(2,1)}, bf16[128,1536]{1,0:T(8,128)(2,1)S(1)}, u32[]{:S(2)}, u32[]{:S(2)}) collective-permute-start(bf16[128,1536]{1,0:T(8,128)(2,1)} %get-tuple-element.29.refs_3_), channel_id=1, source_target_pairs={{0,2},{2,0},{4,6},{6,4},{1,3},{3,1},{5,7},{7,5},{8,10},{10,8},{12,... | collective-permute-start | bytes 1179656 | tf_op jit(solution)/shard_map/ppermute | solution.py:453
  70.1 1.1 copy-start.3
  76.4 1.5 %copy-start.10 = (bf16[128,1536]{1,0:T(8,128)(2,1)}, bf16[128,1536]{1,0:T(8,128)(2,1)S(1)}, u32[]{:S(2)}) copy-start(bf16[128,1536]{1,0:T(8,128)(2,1)S(1)} %collective-permute-done.4.refs_6_.refs_3_) | copy-start | bytes 1179652
  77.9 0.7 copy-start.11
  88.6 0.7 copy-start.4
  88.6 0.9 copy-start.5
  88.6 1.0 copy-start.6
  89.6 5.0 %copy-start.9 = (bf16[256,1536]{1,0:T(8,128)(2,1)S(1)}, bf16[256,1536]{1,0:T(8,128)(2,1)}, u32[]{:S(2)}) copy-start(bf16[256,1536]{1,0:T(8,128)(2,1)} %get-tuple-element.37) | copy-start | bytes 2359300
  89.6 41.1 %all-to-all-start.2 = ((bf16[16,64,768]{2,1,0:T(8,128)(2,1)}), bf16[16,64,768]{2,1,0:T(8,128)(2,1)S(1)}, u32[]{:S(2)}, u32[]{:S(2)}) async-start(bf16[16,64,768]{2,1,0:T(8,128)(2,1)} %get-tuple-element.38.refs_4_), calls=%async_computation.2 | async-start | bytes 3145728 | tf_op jit(solution)/shard_map/all_to_all | solution.py:487
  94.6 20.5 %collective-permute-start.8 = (bf16[256,1536]{1,0:T(8,128)(2,1)S(1)}, bf16[256,1536]{1,0:T(8,128)(2,1)S(1)}, u32[]{:S(2)}, u32[]{:S(2)}) collective-permute-start(bf16[256,1536]{1,0:T(8,128)(2,1)S(1)} %copy-done.9), channel_id=1, source_target_pairs={{0,2},{2,0},{4,6},{6,4},{1,3},{3,1},{5,7},{7,5},{8,10},{10,8},{12,... | collective-permute-start | bytes 2359304 | tf_op jit(solution)/shard_map/ppermute | solution.py:453
  96.1 40.1 %collective-permute-start.9 = (bf16[256,1536]{1,0:T(8,128)(2,1)}, bf16[256,1536]{1,0:T(8,128)(2,1)}, u32[]{:S(2)}, u32[]{:S(2)}) collective-permute-start(bf16[256,1536]{1,0:T(8,128)(2,1)} %get-tuple-element.39), channel_id=1, source_target_pairs={{0,4},{2,6},{4,0},{6,2},{1,5},{3,7},{5,1},{7,3},{8,12},{10,14},{12... | collective-permute-start | bytes 2359304 | tf_op jit(solution)/shard_map/ppermute | solution.py:453
  103.7 32.4 %collective-permute-start.10 = (bf16[256,1536]{1,0:T(8,128)(2,1)}, bf16[256,1536]{1,0:T(8,128)(2,1)}, u32[]{:S(2)}, u32[]{:S(2)}) collective-permute-start(bf16[256,1536]{1,0:T(8,128)(2,1)} %shard_map.130.refs_6_), channel_id=1, source_target_pairs={{0,6},{2,4},{4,2},{6,0},{1,7},{3,5},{5,3},{7,1},{8,14},{10,12},{12... | collective-permute-start | bytes 2359304 | tf_op jit(solution)/shard_map/ppermute | solution.py:453
  115.1 0.9 copy-start.8
  116.0 14.8 %copy-start.1 = (s32[16]{0:T(128)S(1)}, s32[16]{0:T(128)}, u32[]{:S(2)}) copy-start(s32[16]{0:T(128)} %select_reduce_fusion.1.refs_4_.refs_0_) | copy-start | bytes 196
  130.7 1.4 %copy-start = (f32[2,128,1536]{2,1,0:T(8,128)S(1)}, f32[2,128,1536]{2,1,0:T(8,128)}, u32[]{:S(2)}) copy-start(f32[2,128,1536]{2,1,0:T(8,128)} %shard_map.132.refs_4_) | copy-start | bytes 4718596
